TPU v7x, 32 devices: a whole 2x2x4 slice. The times are simulated.
32 devices in a mesh: tx: 4 (over x, core), rx: 8 (over z, y).
Axes of the slice: x: 2, y: 2, z: 4, core: 2. Of those that a mesh axis runs over, the one named last changes fastest.
Arguments:
- records: bfloat16 [40, 256, 4096], P(None, 'tx', 'rx'), may hold values from -6 to 6
- active: int32 [256, 64], P('tx', 'rx'), may hold values 0 or 1
- green: bfloat16 [4, 2, 4096, 4096], P(None, None, 'rx', 'tx'), may hold values from -0.0625 to 0.0625
- background: bfloat16 [256, 4, 2, 4096], P('rx', None, None, 'tx'), may hold values from -0.125 to 0.125
Outputs:
- gradient: float32 [4096], P('tx')
All inputs are finite; a program needn't handle non-finite values. No bound on the sum of `active` on one device may be relied on, other than what follows from the above.
Results may differ from a plain program's by a relative error of at most 0.004.
Values may be sent and summed in bfloat16 or wider, within the bound.
No kernel may reach another device: no remote copies, remote signals or barrier semaphores. Data moves between devices by JAX's collectives and lax.ppermute only.
A program may use at most 128 MiB of HBM per device.

v0:
```python
import jax
import jax.numpy as jnp
from jax import lax
from jax.sharding import PartitionSpec as P


def cosine_table(gate_count, freq_count):
    gate_index = jnp.arange(gate_count, dtype=jnp.float32)
    freq_index = jnp.arange(freq_count, dtype=jnp.float32)
    phases = (
        jnp.pi
        * (2.0 * gate_index[None, :] + 1.0)
        * (1.0 + 3.0 * freq_index[:, None])
        / (2.0 * gate_count)
    )
    weight_scale = jnp.sqrt(2.0 / gate_count)
    stacked = jnp.stack([jnp.cos(phases) * weight_scale, -jnp.sin(phases) * weight_scale], axis=1)
    return stacked.reshape(2 * freq_count, gate_count).astype(jnp.bfloat16)


def shards(records, active, green, background):
    gate_count, local_trans, recv_rows = records.shape
    freq_count = green.shape[0]
    block_count = active.shape[1]
    table_bf16 = cosine_table(gate_count, freq_count)
    shaped = records.reshape(gate_count, local_trans, block_count, recv_rows // block_count)
    masked = (shaped * active.astype(records.dtype)[None, :, :, None]).reshape(
        gate_count, local_trans, recv_rows
    )
    shard_piece = lax.all_gather(masked, "tx", axis=1, tiled=True)
    trans_rows = shard_piece.shape[1]
    spectrum = jnp.einsum(
        "cg,gsr->scr", table_bf16, shard_piece, preferred_element_type=jnp.float32
    )
    spectra = spectrum.astype(jnp.bfloat16).reshape(trans_rows, freq_count, 2, recv_rows)
    real_real = jnp.einsum(
        "sfr,frm->sfm", spectra[:, :, 0], green[:, 0], preferred_element_type=jnp.float32
    )
    imag_imag = jnp.einsum(
        "sfr,frm->sfm", spectra[:, :, 1], green[:, 1], preferred_element_type=jnp.float32
    )
    real_imag = jnp.einsum(
        "sfr,frm->sfm", spectra[:, :, 0], green[:, 1], preferred_element_type=jnp.float32
    )
    imag_real = jnp.einsum(
        "sfr,frm->sfm", spectra[:, :, 1], green[:, 0], preferred_element_type=jnp.float32
    )
    partial_adjoint = jnp.stack([real_real - imag_imag, real_imag + imag_real], axis=2)
    fields_f32 = lax.all_gather(background, "rx", axis=0, tiled=True).astype(jnp.float32)
    products = (
        fields_f32[:, :, 0] * partial_adjoint[:, :, 0]
        - fields_f32[:, :, 1] * partial_adjoint[:, :, 1]
    )
    local_sum = jnp.sum(products, axis=(0, 1))
    return lax.psum(local_sum, "rx")


def solution(mesh):
    placed = (
        P(None, "tx", "rx"),
        P("tx", "rx"),
        P(None, None, "rx", "tx"),
        P("rx", None, None, "tx"),
    )
    return jax.shard_map(shards, mesh=mesh, in_specs=placed, out_specs=P("tx"), check_vma=False)
```

profile of v0, /device:TPU:0, one launch (start us, length us, event | category | flops | bytes accessed | tf_op | source)
XLA Modules:
  0.0 217.7 jit_solution(14812046161286827943)
XLA Ops:
  6.5 0.0 all-gather.3.cloned.1.call-start
  6.5 2.1 copy.26
  8.7 0.0 all-gather.3.cloned.1.call-update
  8.7 0.0 all-gather.5.cloned.1.call-start
  8.7 0.7 convert_element_type.17
  9.4 0.1 copy.27
  9.5 0.1 mul.105
  9.7 0.1 mul.106
  9.8 4.8 %copy_multiply_fusion = bf16[40,64,512]{2,0,1:T(8,128)(2,1)} fusion(bf16[40,64,512]{2,1,0:T(8,128)(2,1)} %param.4, bf16[64,512]{1,0:T(8,128)(2,1)S(1)} %mul.106), kind=kLoop, calls=%fused_computation.18 | loop fusion | flops 1310720 | bytes 5308416 | tf_op jit(solution)/shard_map/mul | solution.py:27
  14.6 0.0 all-gather.5.cloned.1.call-update
  14.7 0.1 multiply_convert_fusion.1
  14.8 70.9 %all-gather.3.cloned.1.call-done = bf16[256,4,2,1024]{3,0,1,2:T(8,128)(2,1)} async-done(((bf16[32,4,2,1024]{3,0,1,2:T(8,128)(2,1)}), bf16[256,4,2,1024]{3,0,1,2:T(8,128)(2,1)}) %all-gather.3.cloned.1.call-update) | async-done | bytes 4194320 | tf_op jit(solution)/shard_map/all_gather | solution.py:49
  85.7 6.6 %convert_element_type.16 = f32[256,4,2,1024]{3,0,1,2:T(8,128)} convert(bf16[256,4,2,1024]{3,0,1,2:T(8,128)(2,1)} %all-gather.3.cloned.1.call-done) | non-fusion elementwise | flops 2097152 | bytes 12582912 | tf_op jit(solution)/shard_map/convert_element_type | solution.py:49
  92.3 63.4 %all-gather.5.cloned.1.call-done = bf16[40,256,512]{2,0,1:T(8,128)(2,1)} async-done(((bf16[40,64,512]{2,0,1:T(8,128)(2,1)}), bf16[40,256,512]{2,0,1:T(8,128)(2,1)}) %all-gather.5.cloned.1.call-update) | async-done | bytes 10485776 | tf_op jit(solution)/shard_map/all_gather | solution.py:30
  155.7 6.9 %convert_bitcast_fusion = bf16[256,8,512]{2,1,0:T(8,128)(2,1)} fusion(bf16[40,256,512]{2,0,1:T(8,128)(2,1)} %all-gather.5.cloned.1.call-done, bf16[8,40,1]{1,0,2:T(8,128)(2,1)S(1)} %bitcast.53), kind=kOutput, calls=%fused_computation.19 | convolution fusion | flops 84934656 | bytes 12583552 | tf_op jit(solution)/shard_map/cg,gsr->scr/dot_general | solution.py:32
  162.6 2.7 %reshape.118 = bf16[256,4,2,512]{3,2,1,0:T(2,128)(2,1)S(1)} reshape(bf16[256,8,512]{2,1,0:T(8,128)(2,1)} %convert_bitcast_fusion) | data formatting | bytes 4194304 | tf_op jit(solution)/shard_map/reshape | solution.py:35
  165.4 0.0 slice-start
  165.4 3.0 %fusion.18 = (bf16[256,4,1,512]{3,2,1,0:T(2,128)(2,1)S(1)}, bf16[256,4,1,512]{3,2,1,0:T(2,128)(2,1)S(1)}) fusion(bf16[256,4,2,512]{3,2,1,0:T(2,128)(2,1)S(1)} %reshape.118), kind=kLoop, calls=%fused_computation.28 | loop fusion | bytes 4194304 | tf_op jit(solution)/shard_map/slice | solution.py:40
  168.4 0.0 copy-start
  168.4 0.0 slice-start.1
  168.4 6.4 %fusion.8 = f32[4,256,1024]{2,1,0:T(8,128)} fusion(bf16[4,2,512,1024]{3,2,1,0:T(8,128)(2,1)} %param.6, bf16[256,4,1,512]{3,2,1,0:T(2,128)(2,1)S(1)} %get-tuple-element.5), kind=kOutput, calls=%fused_computation.10 | convolution fusion | flops 1073741824 | bytes 9437184 | tf_op jit(solution)/shard_map/sfr,frm->sfm/dot_general | solution.py:45
  174.8 0.0 slice-done
  174.8 0.0 slice-done.1
  174.8 0.0 slice-start.2
  174.8 3.6 %fusion.6 = f32[4,256,1024]{2,1,0:T(8,128)} fusion(bf16[4,2,512,1024]{3,2,1,0:T(8,128)(2,1)S(1)} %bitcast.50, bf16[256,4,1,512]{3,2,1,0:T(2,128)(2,1)S(1)} %get-tuple-element.5), kind=kOutput, calls=%fused_computation.8 | convolution fusion | flops 1073741824 | bytes 10485760 | tf_op jit(solution)/shard_map/sfr,frm->sfm/dot_general | solution.py:39
  178.4 0.0 slice-start.3
  178.4 0.0 copy-done
  178.4 3.5 %fusion.4 = f32[4,256,1024]{2,1,0:T(8,128)} fusion(bf16[4,2,512,1024]{3,2,1,0:T(8,128)(2,1)S(1)} %bitcast.50, bf16[256,4,1,512]{3,2,1,0:T(2,128)(2,1)S(1)} %get-tuple-element.6), kind=kOutput, calls=%fused_computation.6 | convolution fusion | flops 1073741824 | bytes 10485760 | tf_op jit(solution)/shard_map/sfr,frm->sfm/dot_general | solution.py:42
  181.9 0.0 slice-done.2
  181.9 0.0 slice-done.3
  181.9 7.0 %fusion.2 = f32[1024]{0:T(1024)S(1)} fusion(f32[256,4,2,1024]{3,0,1,2:T(8,128)S(1)} %bitcast.52, f32[4,256,1024]{2,1,0:T(8,128)} %fusion.4, f32[4,256,1024]{2,1,0:T(8,128)} %fusion.8, f32[4,256,1024]{2,1,0:T(8,128)} %fusion.6, bf16[4,2,512,1024]{3,2,1,0:T(8,128)(2,1)S(1)} %bitcast.50, bf16[256,4,1,512]{3,2,1,0:T(2,128)(2,1)} %copy-done), kind=kOutput, calls=%fused_computation.3 | convolution fusion | flops 1080032256 | bytes 26218496 | tf_op jit(solution)/shard_map/sfr,frm->sfm/dot_general | solution.py:36
  188.9 22.0 %psum.7 = f32[1024]{0:T(1024)} all-reduce(f32[1024]{0:T(1024)S(1)} %fusion.2), channel_id=1, replica_groups=mesh['tx'=4,'rx'=8] {'rx'}, use_global_device_ids=true, to_apply=%region_1.0 | all-reduce | flops 1024 | bytes 8192 | tf_op jit(solution)/shard_map/psum | solution.py:55
  (6 shorter events, 0.0 us)
Async XLA Ops:
  6.5 79.1 %all-gather.3.cloned.1.call-start = ((), (), s32[]{:S(2)}) async-start(), calls=%async_computation | async-start | bytes 4718592 | tf_op jit(solution)/shard_map/all_gather | solution.py:49
  8.7 147.0 %all-gather.5.cloned.1.call-start = ((), (), s32[]{:S(2)}) async-start(), calls=%async_computation.1 | async-start | bytes 13107200 | tf_op jit(solution)/shard_map/all_gather | solution.py:30
  165.4 9.5 %slice-start = ((s8[8388608]{0:T(1024)(128)(4,1)}), s8[4194304]{0:T(1024)(128)(4,1)S(1)}, s32[]{:S(2)}) async-start(s8[8388608]{0:T(1024)(128)(4,1)} %bitcast.49), calls=%async_computation.2 | async-start | bytes 8388608
  168.4 10.1 %copy-start = (bf16[256,4,1,512]{3,2,1,0:T(2,128)(2,1)}, bf16[256,4,1,512]{3,2,1,0:T(2,128)(2,1)S(1)}, u32[]{:S(2)}) copy-start(bf16[256,4,1,512]{3,2,1,0:T(2,128)(2,1)S(1)} %get-tuple-element.6) | copy-start | bytes 3145732
  168.4 6.5 %slice-start.1 = ((s8[8388608]{0:T(1024)(128)(4,1)}), s8[4194304]{0:T(1024)(128)(4,1)S(1)}, s32[]{:S(2)}) async-start(s8[8388608]{0:T(1024)(128)(4,1)} %bitcast.49), calls=%async_computation.3 | async-start | bytes 8388608
  174.8 7.1 %slice-start.2 = ((s8[8388608]{0:T(1024)(128)(4,1)}), s8[4194304]{0:T(1024)(128)(4,1)S(1)}, s32[]{:S(2)}) async-start(s8[8388608]{0:T(1024)(128)(4,1)} %bitcast.51), calls=%async_computation.4 | async-start | bytes 8388608
  178.4 3.5 %slice-start.3 = ((s8[8388608]{0:T(1024)(128)(4,1)}), s8[4194304]{0:T(1024)(128)(4,1)S(1)}, s32[]{:S(2)}) async-start(s8[8388608]{0:T(1024)(128)(4,1)} %bitcast.51), calls=%async_computation.5 | async-start | bytes 8388608
Sparse Core Ops, SparseCore 0:
  9.5 76.0 all-gather.2
  87.2 68.4 all-gather.4
where the time goes:
time: 218 us
  waiting for transfers between devices  134 us (61%)
  matrix products  27.4 us (13%)
  blocking collectives  22 us (10%)
  between operations  13.5 us (6%)
  other arithmetic  12.3 us (6%)
  local copies, waits for them, and re-layouts  8.27 us (4%)
    all_gather x1, waiting for transfers between devices, shards(): lax.all_gather(background, 'rx', axis=0, tiled=True).astype(jnp.float32)  70.9 us
    all_gather x1, waiting for transfers between devices, shards(): shard_piece = lax.all_gather(masked, 'tx', axis=1, tiled=True)  63.4 us
    psum x1, blocking collectives, shards(): return lax.psum(local_sum, 'rx')  22 us
    dot_general x1, matrix products, shards(): jnp.einsum('sfr,frm->sfm', spectra[:, :, 0], green[:, 0], preferred_eleme...  7 us
    dot_general x1, matrix products, shards(): jnp.einsum('cg,gsr->scr', table_bf16, shard_piece, preferred_element_type...  6.9 us
    convert_element_type x1, other arithmetic, shards(): lax.all_gather(background, 'rx', axis=0, tiled=True).astype(jnp.float32)  6.65 us
    dot_general x1, matrix products, shards(): jnp.einsum('sfr,frm->sfm', spectra[:, :, 1], green[:, 0], preferred_eleme...  6.45 us
    mul x1, other arithmetic, shards(): shaped * active.astype(records.dtype)[None, :, :, None]  4.78 us
  transfers between devices with their start and end apart: 2, of which 2 were waited for; matrix products, arithmetic and copies ran while one was open for 6% of the time, Pallas kernels for 0%

commit v1 on v0

v1 whole, which is shorter than its diff:
```python
import functools

import jax
import jax.numpy as jnp
import numpy as np
from jax import lax
from jax.experimental import pallas as pl
from jax.experimental.pallas import tpu as pltpu
from jax.sharding import PartitionSpec as P

ROWS = 16


def spread_table(gate_count, freq_count):
    gates = np.arange(gate_count, dtype=np.float32)
    freqs = np.arange(freq_count, dtype=np.float32)
    phases = (
        np.float32(np.pi)
        * (np.float32(2) * gates[None, :] + np.float32(1))
        * (np.float32(1) + np.float32(3) * freqs[:, None])
        / np.float32(2 * gate_count)
    )
    scale = np.sqrt(np.float32(2.0 / gate_count))
    table = np.stack([np.cos(phases) * scale, -np.sin(phases) * scale], axis=1)
    table = table.reshape(2 * freq_count, gate_count).astype(jnp.bfloat16).astype(np.float32)
    return np.kron(table, np.eye(ROWS, dtype=np.float32)).astype(jnp.bfloat16)


def spectra_kernel(table_ref, active_ref, records_ref, out_ref):
    gates, rows, recv = records_ref.shape
    blocks = active_ref.shape[1]
    flat = records_ref[...].reshape(gates * rows, recv)
    sums = jnp.dot(table_ref[...], flat, preferred_element_type=jnp.float32)
    block_of = lax.broadcasted_iota(jnp.int32, (blocks, recv), 1) // (recv // blocks)
    spread = (block_of == lax.broadcasted_iota(jnp.int32, (blocks, recv), 0)).astype(jnp.float32)
    mask = jnp.dot(
        active_ref[...].astype(jnp.float32), spread, preferred_element_type=jnp.float32
    )
    channels = out_ref.shape[0]
    out_ref[...] = (sums.reshape(channels, rows, recv) * mask[None]).astype(out_ref.dtype)


def spectra_of(records, active, freq_count):
    gates, trans, recv = records.shape
    blocks = active.shape[1]
    channels = 2 * freq_count
    table = jnp.asarray(spread_table(gates, freq_count))
    return pl.pallas_call(
        spectra_kernel,
        grid=(trans // ROWS,),
        in_specs=[
            pl.BlockSpec(table.shape, lambda i: (0, 0)),
            pl.BlockSpec((ROWS, blocks), lambda i: (i, 0)),
            pl.BlockSpec((gates, ROWS, recv), lambda i: (0, i, 0)),
        ],
        out_specs=pl.BlockSpec((channels, ROWS, recv), lambda i: (0, i, 0)),
        out_shape=jax.ShapeDtypeStruct((channels, trans, recv), jnp.bfloat16),
        compiler_params=pltpu.CompilerParams(vmem_limit_bytes=24 << 20),
        cost_estimate=pl.CostEstimate(
            flops=2 * channels * ROWS * gates * trans * recv,
            bytes_accessed=2 * (gates + channels) * trans * recv,
            transcendentals=0,
        ),
        name="spectra",
    )(table, active, records)


def adjoint_kernel(*refs):
    spectra_refs, green_ref, out_ref = refs[:-2], refs[-2], refs[-1]
    rows = spectra_refs[0].shape[2]
    green = green_ref[0]
    real = jnp.concatenate([ref[0, 0] for ref in spectra_refs], axis=0)
    imag = jnp.concatenate([ref[0, 1] for ref in spectra_refs], axis=0)
    for part, left in enumerate(
        (jnp.concatenate([real, -imag], axis=1), jnp.concatenate([-imag, -real], axis=1))
    ):
        sums = jnp.dot(left, green, preferred_element_type=jnp.float32)
        for slot in range(len(spectra_refs)):
            out_ref[0, part, slot] = sums[slot * rows : (slot + 1) * rows]


def adjoint_of(pieces, green):
    freqs, _, recv, cells = green.shape
    rows = pieces[0].shape[1]
    pieces = [piece.reshape(freqs, 2, rows, recv) for piece in pieces]
    count = len(pieces)
    return pl.pallas_call(
        adjoint_kernel,
        grid=(freqs,),
        in_specs=[pl.BlockSpec((1, 2, rows, recv), lambda f: (f, 0, 0, 0))] * count
        + [pl.BlockSpec((1, 2 * recv, cells), lambda f: (f, 0, 0))],
        out_specs=pl.BlockSpec((1, 2, count, rows, cells), lambda f: (f, 0, 0, 0, 0)),
        out_shape=jax.ShapeDtypeStruct((freqs, 2, count, rows, cells), jnp.float32),
        compiler_params=pltpu.CompilerParams(vmem_limit_bytes=40 << 20),
        cost_estimate=pl.CostEstimate(
            flops=8 * freqs * count * rows * recv * cells,
            bytes_accessed=4 * freqs * recv * cells + 8 * freqs * count * rows * cells,
            transcendentals=0,
        ),
        name="adjoint",
    )(*pieces, green.reshape(freqs, 2 * recv, cells))


def weigh_kernel(last, place_ref, mine_ref, other_ref, field_ref, field_other_ref, sum_ref, out_ref, total):
    del place_ref
    step = pl.program_id(0)

    @pl.when(step == 0)
    def _():
        total[...] = sum_ref[...]

    cells = total.shape[1]
    sums = total[...]
    for adjoint, field in ((mine_ref, field_ref), (other_ref, field_other_ref)):
        terms = adjoint[0, :, 0].reshape(-1, cells) * field[0].reshape(-1, cells).astype(jnp.float32)
        sums = sums + jnp.sum(terms.reshape(-1, 8, cells), axis=0)
    total[...] = sums

    @pl.when(step == pl.num_programs(0) - 1)
    def _():
        if last:
            out_ref[...] = jnp.sum(total[...], axis=0, keepdims=True)
        else:
            out_ref[...] = total[...]


def weigh(adjoint, place, mine, other, sums, last):
    freqs, _, blocks, rows, cells = adjoint.shape
    field = pl.BlockSpec((1, 2, rows, cells), lambda f, place: (f, 0, 0, 0))
    out_rows = 1 if last else 8
    return pl.pallas_call(
        functools.partial(weigh_kernel, last),
        grid_spec=pltpu.PrefetchScalarGridSpec(
            num_scalar_prefetch=1,
            grid=(freqs,),
            in_specs=[
                pl.BlockSpec((1, 2, 1, rows, cells), lambda f, place: (f, 0, place[0], 0, 0)),
                pl.BlockSpec((1, 2, 1, rows, cells), lambda f, place: (f, 0, place[1], 0, 0)),
                field,
                field,
                pl.BlockSpec((8, cells), lambda f, place: (0, 0)),
            ],
            out_specs=pl.BlockSpec((out_rows, cells), lambda f, place: (0, 0)),
            scratch_shapes=[pltpu.VMEM((8, cells), jnp.float32)],
        ),
        out_shape=jax.ShapeDtypeStruct((out_rows, cells), jnp.float32),
        compiler_params=pltpu.CompilerParams(vmem_limit_bytes=16 << 20),
        cost_estimate=pl.CostEstimate(
            flops=8 * freqs * rows * cells,
            bytes_accessed=24 * freqs * rows * cells,
            transcendentals=0,
        ),
        name="weigh",
    )(place, adjoint, adjoint, mine, other, sums)


def box_shards(records, active, green, background):
    freqs = green.shape[0]
    along_y = [(r, r ^ 1) for r in range(8)]
    z_pairs = [(r, r ^ 2) for r in range(8)]
    z_middle = [(r, r ^ 6) for r in range(2, 6)]
    z_outward = [(2, 0), (3, 1), (4, 6), (5, 7)]
    core = [(t, t ^ 1) for t in range(4)]
    along_x = [(t, t ^ 2) for t in range(4)]
    send = lax.ppermute

    me_tx, me_rx = lax.axis_index("tx"), lax.axis_index("rx")
    me_z, me_y = me_rx // 2, me_rx % 2
    middle = (me_z == 1) | (me_z == 2)

    own = background.transpose(1, 2, 0, 3)
    near = send(own, "rx", z_pairs)
    across = send(own, "rx", z_middle)
    own_y = send(own, "rx", along_y)

    spectra = spectra_of(records, active, freqs)
    spectra_x = send(spectra, "tx", along_x)
    spectra_core = send(spectra, "tx", core)

    near_y = send(near, "rx", along_y)
    across_out = send(across, "rx", z_outward)
    far = send(near, "rx", z_middle)
    spectra_both = send(spectra_x, "tx", core)
    mid = jnp.where(middle, across, across_out)
    mid_y = send(mid, "rx", along_y)
    far_out = send(far, "rx", z_outward)
    end = jnp.where(middle, far, far_out)
    end_y = send(end, "rx", along_y)

    adjoint = adjoint_of([spectra, spectra_core, spectra_x, spectra_both], green)
    freqs, _, groups, rows, cells = adjoint.shape
    adjoint = adjoint.reshape(freqs, 2, 2 * groups, rows // 2, cells)

    lower = me_z < 2
    owners = (
        (me_z, own, own_y),
        (me_z ^ 1, near, near_y),
        (jnp.where(lower, 2, 1), mid, mid_y),
        (jnp.where(lower, 3, 0), end, end_y),
    )
    sums = jnp.zeros((8, cells), jnp.float32)
    for step, (owner, mine, other) in enumerate(owners):
        slot = (owner ^ me_tx) * 2
        place = jnp.stack([slot + me_y, slot + 1 - me_y]).astype(jnp.int32)
        sums = weigh(adjoint, place, mine, other, sums, step == len(owners) - 1)
    sums = sums.reshape(cells)
    for bit in (1, 2, 4):
        sums = sums + send(sums, "rx", [(r, r ^ bit) for r in range(8)])
    return sums


def plain_shards(records, active, green, background):
    freqs = green.shape[0]
    spectra = spectra_of(records, active, freqs)
    pieces = lax.all_gather(spectra, "tx", axis=0)
    adjoint = adjoint_of([pieces[t] for t in range(pieces.shape[0])], green)
    freqs, _, groups, rows, cells = adjoint.shape
    adjoint = adjoint.reshape(freqs, 2, groups * rows, cells)
    fields = lax.all_gather(background, "rx", axis=0, tiled=True)
    fields = fields.transpose(1, 2, 0, 3).astype(jnp.float32)
    return lax.psum(jnp.sum(adjoint * fields, axis=(0, 1, 2)), "rx")


def solution(mesh):
    placed = (
        P(None, "tx", "rx"),
        P("tx", "rx"),
        P(None, None, "rx", "tx"),
        P("rx", None, None, "tx"),
    )
    body = box_shards if (mesh.shape["tx"], mesh.shape["rx"]) == (4, 8) else plain_shards
    return jax.shard_map(body, mesh=mesh, in_specs=placed, out_specs=P("tx"), check_vma=False)
```

time: 218 us -> 97.3 us (0.45)
  waiting for transfers between devices: 134 us -> 40.7 us
  matrix products: 27.4 us -> 0 us
  starting transfers between devices: 0.04 us -> 27.4 us
  blocking collectives: 22 us -> 0 us
  Pallas kernels: 0 us -> 19.9 us
  between operations: 13.5 us -> 0.15 us
  other arithmetic: 12.3 us -> 3.1 us
  local copies, waits for them, and re-layouts: 8.27 us -> 5.57 us
    all_gather x2 -> x0, waiting for transfers between devices: 134 us -> none  [the longest x1 70.9 us: shards(): lax.all_gather(background, 'rx', axis=0, tiled=True).astype(jnp.float32)]
    ppermute x0 -> x15, waiting for transfers between devices: none -> 40.7 us  [the longest x1 11.3 us: box_shards(): near = send(own, 'rx', z_pairs)]
    dot_general x5 -> x0, matrix products: 27.4 us -> none  [the longest x1 7 us: shards(): jnp.einsum('sfr,frm->sfm', spectra[:, :, 0], green[:, 0], preferred_eleme...]
    ppermute x0 -> x15, starting transfers between devices: none -> 27.4 us  [the longest x3 12.7 us: box_shards(): sums = sums + send(sums, 'rx', [(r, r ^ bit) for r in range(8)])]
    psum x1 -> x0, blocking collectives: 22 us -> none  [shards(): return lax.psum(local_sum, 'rx')]
    pallas_call x0 -> x6, Pallas kernels: none -> 19.9 us  [the longest x4 11.2 us: weigh(): pl.pallas_call(functools.partial(weigh_kernel, last), grid_spec=pltpu.Pre...]
    convert_element_type x2 -> x0, other arithmetic: 7.34 us -> none  [the longest x1 6.65 us: shards(): lax.all_gather(background, 'rx', axis=0, tiled=True).astype(jnp.float32)]
    mul x2 -> x0, other arithmetic: 4.79 us -> none  [the longest x1 4.78 us: shards(): shaped * active.astype(records.dtype)[None, :, :, None]]
  transfers between devices with their start and end apart: 2 -> 15, of which waited for: 2 -> 8; matrix products, arithmetic and copies ran while one was open for 6% -> 3% of each run, Pallas kernels for 0% -> 18%
where the time goes in v1:
time: 97.3 us; the launch traced here: 96.7 us
  waiting for transfers between devices  40.7 us (42%)
  starting transfers between devices  27.4 us (28%)
  Pallas kernels  19.9 us (20%)
  local copies, waits for them, and re-layouts  5.57 us (6%)
  other arithmetic  3.1 us (3%)
    ppermute x3, starting transfers between devices, box_shards(): sums = sums + send(sums, 'rx', [(r, r ^ bit) for r in range(8)])  12.7 us
    ppermute x1, waiting for transfers between devices, box_shards(): near = send(own, 'rx', z_pairs)  11.3 us
    pallas_call x4, Pallas kernels, weigh(): pl.pallas_call(functools.partial(weigh_kernel, last), grid_spec=pltpu.Pre...  11.2 us
    pallas_call x1, Pallas kernels, adjoint_of(): pl.pallas_call(adjoint_kernel, grid=(freqs,), in_specs=[pl.BlockSpec((1,...  7.18 us
    ppermute x1, waiting for transfers between devices, box_shards(): far_out = send(far, 'rx', z_outward)  7.08 us
    ppermute x1, waiting for transfers between devices, box_shards(): spectra_x = send(spectra, 'tx', along_x)  7.04 us
    unnamed x8, local copies, waits for them, and re-layouts  5.56 us
    ppermute x3, waiting for transfers between devices, box_shards(): sums = sums + send(sums, 'rx', [(r, r ^ bit) for r in range(8)])  5.25 us
  transfers between devices with their start and end apart: 15, of which 8 were waited for; matrix products, arithmetic and copies ran while one was open for 3% of the time, Pallas kernels for 18%

profile of v1, /device:TPU:0, one launch (start us, length us, event | category | flops | bytes accessed | tf_op | source)
XLA Modules:
  0.0 96.7 jit_solution(10192007662689358576)
XLA Ops:
  0.0 1.3 %copy.9 = bf16[32,4,2,1024]{3,0,2,1:T(8,128)(2,1)S(1)} copy(bf16[32,4,2,1024]{3,2,1,0:T(2,128)(2,1)} %param.8) | data formatting | bytes 1048576 | tf_op args[3]
  1.3 3.1 %collective-permute-start.3 = (bf16[4,2,32,1024]{3,2,1,0:T(8,128)(2,1)S(1)}, bf16[4,2,32,1024]{3,2,1,0:T(8,128)(2,1)}, u32[]{:S(2)}, u32[]{:S(2)}) collective-permute-start(bf16[4,2,32,1024]{3,2,1,0:T(8,128)(2,1)S(1)} %bitcast.27), channel_id=1, source_target_pairs={{0,2},{1,3},{2,0},{3,1},{4,6},{5,7},{6,4},{7,5},{8,10},{9,11},{10,... | collective-permute-start | bytes 1572872 | tf_op jit(solution)/shard_map/ppermute | solution.py:172
  4.4 0.7 collective-permute-start.7
  5.1 11.3 %collective-permute-done.3.field_ref = bf16[4,2,32,1024]{3,2,1,0:T(8,128)(2,1)} collective-permute-done((bf16[4,2,32,1024]{3,2,1,0:T(8,128)(2,1)S(1)}, bf16[4,2,32,1024]{3,2,1,0:T(8,128)(2,1)}, u32[]{:S(2)}, u32[]{:S(2)}) %collective-permute-start.3) | collective-permute-done | bytes 524320 | tf_op jit(solution)/shard_map/ppermute | solution.py:172
  16.5 1.5 %collective-permute-start.4 = (bf16[4,2,32,1024]{3,2,1,0:T(8,128)(2,1)}, bf16[4,2,32,1024]{3,2,1,0:T(8,128)(2,1)}, u32[]{:S(2)}, u32[]{:S(2)}) collective-permute-start(bf16[4,2,32,1024]{3,2,1,0:T(8,128)(2,1)} %collective-permute-done.3.field_ref), channel_id=1, source_target_pairs={{2,4},{3,5},{4,2},{5,3},{10,12},{11,13},{12,10},{13,11},{18,20},{1... | collective-permute-start | bytes 1572872 | tf_op jit(solution)/shard_map/ppermute | solution.py:182
  17.9 0.8 copy.6.active_ref
  18.7 1.7 %copy-done = bf16[40,64,512]{2,1,0:T(8,128)(2,1)S(1)} copy-done((bf16[40,64,512]{2,1,0:T(8,128)(2,1)S(1)}, bf16[40,64,512]{2,1,0:T(8,128)(2,1)}, u32[]{:S(2)}) %copy-start) | copy-done | bytes 2621464
  20.4 0.9 copy-done.1
  21.4 1.4 %spectra.1 = bf16[8,64,512]{2,1,0:T(8,128)(2,1)S(1)} custom-call(bf16[128,640]{1,0:T(8,128)(2,1)S(1)} %copy-done.1, s32[64,8]{1,0:T(8,128)S(1)} %copy.6.active_ref, bf16[40,64,512]{2,1,0:T(8,128)(2,1)S(1)} %copy-done), custom_call_target="tpu_custom_call" | custom-call | flops 335544320 | bytes 3145728 | tf_op jit(solution)/shard_map/spectra/pallas_call | solution.py:48
  22.8 1.7 %collective-permute-start.1 = (bf16[8,64,512]{2,1,0:T(8,128)(2,1)S(1)}, bf16[8,64,512]{2,1,0:T(8,128)(2,1)S(1)}, u32[]{:S(2)}, u32[]{:S(2)}) collective-permute-start(bf16[8,64,512]{2,1,0:T(8,128)(2,1)S(1)} %spectra.1), channel_id=1, source_target_pairs={{0,16},{8,24},{16,0},{24,8},{1,17},{9,25},{17,1},{25,9},{2,18},{10... | collective-permute-start | bytes 1572872 | tf_op jit(solution)/shard_map/ppermute | solution.py:177
  24.5 0.0 collective-permute-done.7
  24.5 1.3 %collective-permute-start.8 = (bf16[4,2,32,1024]{3,2,1,0:T(8,128)(2,1)S(1)}, bf16[4,2,32,1024]{3,2,1,0:T(8,128)(2,1)S(1)}, u32[]{:S(2)}, u32[]{:S(2)}) collective-permute-start(bf16[4,2,32,1024]{3,2,1,0:T(8,128)(2,1)S(1)} %collective-permute-done.7), channel_id=1, source_target_pairs={{2,0},{3,1},{4,6},{5,7},{10,8},{11,9},{12,14},{13,15},{18,16},{19,... | collective-permute-start | bytes 1572872 | tf_op jit(solution)/shard_map/ppermute | solution.py:181
  25.8 0.0 collective-permute-done.4
  25.8 1.3 %collective-permute-start.5 = (bf16[4,2,32,1024]{3,2,1,0:T(8,128)(2,1)}, bf16[4,2,32,1024]{3,2,1,0:T(8,128)(2,1)}, u32[]{:S(2)}, u32[]{:S(2)}) collective-permute-start(bf16[4,2,32,1024]{3,2,1,0:T(8,128)(2,1)} %collective-permute-done.4), channel_id=1, source_target_pairs={{2,0},{3,1},{4,6},{5,7},{10,8},{11,9},{12,14},{13,15},{18,16},{19,... | collective-permute-start | bytes 1572872 | tf_op jit(solution)/shard_map/ppermute | solution.py:186
  27.1 0.1 collective-permute-start
  27.2 1.6 %collective-permute-start.11 = (bf16[4,2,32,1024]{3,2,1,0:T(8,128)(2,1)S(1)}, bf16[4,2,32,1024]{3,2,1,0:T(8,128)(2,1)}, u32[]{:S(2)}, u32[]{:S(2)}) collective-permute-start(bf16[4,2,32,1024]{3,2,1,0:T(8,128)(2,1)S(1)} %bitcast.29), channel_id=1, source_target_pairs={{0,1},{1,0},{2,3},{3,2},{4,5},{5,4},{6,7},{7,6},{8,9},{9,8},{10,11... | collective-permute-start | bytes 1572872 | tf_op jit(solution)/shard_map/ppermute | solution.py:174
  28.8 0.1 pad_add_fusion.3.place_ref
  28.9 0.1 pad_add_fusion.2.place_ref
  28.9 7.0 %collective-permute-done.1 = bf16[8,64,512]{2,1,0:T(8,128)(2,1)S(1)} collective-permute-done((bf16[8,64,512]{2,1,0:T(8,128)(2,1)S(1)}, bf16[8,64,512]{2,1,0:T(8,128)(2,1)S(1)}, u32[]{:S(2)}, u32[]{:S(2)}) %collective-permute-start.1) | collective-permute-done | bytes 524320 | tf_op jit(solution)/shard_map/ppermute | solution.py:177
  36.0 1.4 %collective-permute-start.10 = (bf16[4,2,32,1024]{3,2,1,0:T(8,128)(2,1)}, bf16[4,2,32,1024]{3,2,1,0:T(8,128)(2,1)}, u32[]{:S(2)}, u32[]{:S(2)}) collective-permute-start(bf16[4,2,32,1024]{3,2,1,0:T(8,128)(2,1)} %collective-permute-done.3.field_ref), channel_id=1, source_target_pairs={{0,1},{1,0},{2,3},{3,2},{4,5},{5,4},{6,7},{7,6},{8,9},{9,8},{10,11... | collective-permute-start | bytes 1572872 | tf_op jit(solution)/shard_map/ppermute | solution.py:180
  37.3 4.9 %collective-permute-done.8 = bf16[4,2,32,1024]{3,2,1,0:T(8,128)(2,1)S(1)} collective-permute-done((bf16[4,2,32,1024]{3,2,1,0:T(8,128)(2,1)S(1)}, bf16[4,2,32,1024]{3,2,1,0:T(8,128)(2,1)S(1)}, u32[]{:S(2)}, u32[]{:S(2)}) %collective-permute-start.8) | collective-permute-done | bytes 524320 | tf_op jit(solution)/shard_map/ppermute | solution.py:181
  42.2 0.8 copy-done.2
  43.0 0.0 collective-permute-start.2
  43.0 1.1 %broadcast_select_fusion.field_ref = bf16[4,2,32,1024]{3,2,1,0:T(8,128)(2,1)S(1)} fusion(bf16[4,2,32,1024]{3,2,1,0:T(8,128)(2,1)S(1)} %collective-permute-done.7, bf16[4,2,32,1024]{3,2,1,0:T(8,128)(2,1)} %copy-done.2, pred[]{:T(512)S(6)} %or.3), kind=kLoop, calls=%fused_computation.1 | loop fusion | flops 262144 | bytes 1572865 | tf_op jit(solution)/shard_map/jit(_where)/select_n | solution.py:184
  44.1 7.1 %collective-permute-done.5 = bf16[4,2,32,1024]{3,2,1,0:T(8,128)(2,1)} collective-permute-done((bf16[4,2,32,1024]{3,2,1,0:T(8,128)(2,1)}, bf16[4,2,32,1024]{3,2,1,0:T(8,128)(2,1)}, u32[]{:S(2)}, u32[]{:S(2)}) %collective-permute-start.5) | collective-permute-done | bytes 524320 | tf_op jit(solution)/shard_map/ppermute | solution.py:186
  51.2 1.5 %collective-permute-start.9 = (bf16[4,2,32,1024]{3,2,1,0:T(8,128)(2,1)S(1)}, bf16[4,2,32,1024]{3,2,1,0:T(8,128)(2,1)}, u32[]{:S(2)}, u32[]{:S(2)}) collective-permute-start(bf16[4,2,32,1024]{3,2,1,0:T(8,128)(2,1)S(1)} %broadcast_select_fusion.field_ref), channel_id=1, source_target_pairs={{0,1},{1,0},{2,3},{3,2},{4,5},{5,4},{6,7},{7,6},{8,9},{9,8},{10,11... | collective-permute-start | bytes 1572872 | tf_op jit(solution)/shard_map/ppermute | solution.py:185
  52.7 1.1 %broadcast_select_fusion.1.field_ref = bf16[4,2,32,1024]{3,2,1,0:T(8,128)(2,1)S(1)} fusion(bf16[4,2,32,1024]{3,2,1,0:T(8,128)(2,1)} %collective-permute-done.4, bf16[4,2,32,1024]{3,2,1,0:T(8,128)(2,1)} %collective-permute-done.5, pred[]{:T(512)S(6)} %or.3), kind=kLoop, calls=%fused_computation.2 | loop fusion | flops 262144 | bytes 1572865 | tf_op jit(solution)/shard_map/jit(_where)/select_n | solution.py:187
  53.8 0.0 collective-permute-done
  53.8 0.6 collective-permute-start.6
  54.4 0.1 pad_add_fusion.1.place_ref
  54.5 0.1 pad_add_fusion.place_ref
  54.6 0.0 collective-permute-done.2
  54.6 7.2 %adjoint.1 = f32[4,2,4,64,1024]{4,3,2,1,0:T(8,128)S(1)} custom-call(bf16[4,2,64,512]{3,2,1,0:T(8,128)(2,1)S(1)} %bitcast.26, bf16[4,2,64,512]{3,2,1,0:T(8,128)(2,1)S(1)} %bitcast.32, bf16[4,2,64,512]{3,2,1,0:T(8,128)(2,1)S(1)} %bitcast.31, bf16[4,2,64,512]{3,2,1,0:T(8,128)(2,1)} %bitcast.5.refs_3_, bf16[4,1024,1024]{2,1,0:T(8,128)(2,1)} %bitcast.35), custom_call_target="tpu_custom_call" | custom-call | flops 4294967296 | bytes 16777216 | tf_op jit(solution)/shard_map/adjoint/pallas_call | solution.py:87
  61.8 0.0 collective-permute-done.11.field_other_ref
  61.8 2.8 %weigh.4.sum_ref = f32[8,1024]{1,0:T(8,128)S(1)} custom-call(s32[2]{0:T(128)S(1)} %pad_add_fusion.3.place_ref, f32[4,2,8,32,1024]{4,3,2,1,0:T(8,128)S(1)} %bitcast.18, f32[4,2,8,32,1024]{4,3,2,1,0:T(8,128)S(1)} %bitcast.19, bf16[4,2,32,1024]{3,2,1,0:T(8,128)(2,1)S(1)} %bitcast.30, bf16[4,2,32,1024]{3,2,1,0:T(8,128)(2,1)} %collective-permute-done.11.field_other_ref, ...), custom_call_target="tpu_custom_call" | custom-call | flops 1048576 | bytes 3145728 | tf_op jit(solution)/shard_map/weigh/pallas_call | solution.py:131
  64.5 0.0 collective-permute-done.10.field_other_ref
  64.6 2.9 %weigh.5.sum_ref = f32[8,1024]{1,0:T(8,128)S(1)} custom-call(s32[2]{0:T(128)S(1)} %pad_add_fusion.2.place_ref, f32[4,2,8,32,1024]{4,3,2,1,0:T(8,128)S(1)} %bitcast.20, f32[4,2,8,32,1024]{4,3,2,1,0:T(8,128)S(1)} %bitcast.21, bf16[4,2,32,1024]{3,2,1,0:T(8,128)(2,1)} %collective-permute-done.3.field_ref, ...), custom_call_target="tpu_custom_call" | custom-call | flops 1048576 | bytes 3145728 | tf_op jit(solution)/shard_map/weigh/pallas_call | solution.py:131
  67.5 0.0 collective-permute-done.9.field_other_ref
  67.5 2.8 %weigh.6.sum_ref = f32[8,1024]{1,0:T(8,128)S(1)} custom-call(s32[2]{0:T(128)S(1)} %pad_add_fusion.1.place_ref, f32[4,2,8,32,1024]{4,3,2,1,0:T(8,128)S(1)} %bitcast.22, f32[4,2,8,32,1024]{4,3,2,1,0:T(8,128)S(1)} %bitcast.23, bf16[4,2,32,1024]{3,2,1,0:T(8,128)(2,1)S(1)} %broadcast_select_fusion.field_ref, ...), custom_call_target="tpu_custom_call" | custom-call | flops 1048576 | bytes 3145728 | tf_op jit(solution)/shard_map/weigh/pallas_call | solution.py:131
  70.3 5.1 %collective-permute-done.6.field_other_ref = bf16[4,2,32,1024]{3,2,1,0:T(8,128)(2,1)} collective-permute-done((bf16[4,2,32,1024]{3,2,1,0:T(8,128)(2,1)S(1)}, bf16[4,2,32,1024]{3,2,1,0:T(8,128)(2,1)}, u32[]{:S(2)}, u32[]{:S(2)}) %collective-permute-start.6) | collective-permute-done | bytes 524320 | tf_op jit(solution)/shard_map/ppermute | solution.py:188
  75.4 2.8 %weigh.7 = f32[1,1024]{1,0:T(1,128)S(1)} custom-call(s32[2]{0:T(128)S(1)} %pad_add_fusion.place_ref, f32[4,2,8,32,1024]{4,3,2,1,0:T(8,128)S(1)} %bitcast.24, f32[4,2,8,32,1024]{4,3,2,1,0:T(8,128)S(1)} %bitcast.25, bf16[4,2,32,1024]{3,2,1,0:T(8,128)(2,1)S(1)} %broadcast_select_fusion.1.field_ref, ...), custom_call_target="tpu_custom_call" | custom-call | flops 1048576 | bytes 3145728 | tf_op jit(solution)/shard_map/weigh/pallas_call | solution.py:131
  78.1 1.6 %collective-permute-start.12 = (f32[1024]{0:T(1024)S(1)}, f32[1024]{0:T(1024)S(1)}, u32[]{:S(2)}, u32[]{:S(2)}) collective-permute-start(f32[1024]{0:T(1024)S(1)} %bitcast.33), channel_id=1, source_target_pairs={{0,1},{1,0},{2,3},{3,2},{4,5},{5,4},{6,7},{7,6},{8,9},{9,8},{10,11... | collective-permute-start | bytes 12296 | tf_op jit(solution)/shard_map/ppermute | solution.py:208
  79.7 2.1 %collective-permute-done.12 = f32[1024]{0:T(1024)S(1)} collective-permute-done((f32[1024]{0:T(1024)S(1)}, f32[1024]{0:T(1024)S(1)}, u32[]{:S(2)}, u32[]{:S(2)}) %collective-permute-start.12) | collective-permute-done | bytes 4128 | tf_op jit(solution)/shard_map/ppermute | solution.py:208
  81.8 8.1 %collective-permute-start.13 = (f32[1024]{0:T(1024)S(1)}, f32[1024]{0:T(1024)S(1)}, u32[]{:S(2)}, u32[]{:S(2)}) collective-permute-start(f32[1024]{0:T(1024)S(1)} %add.47), channel_id=1, source_target_pairs={{0,2},{1,3},{2,0},{3,1},{4,6},{5,7},{6,4},{7,5},{8,10},{9,11},{10,... | collective-permute-start | bytes 12296 | tf_op jit(solution)/shard_map/ppermute | solution.py:208
  89.9 1.6 %collective-permute-done.13 = f32[1024]{0:T(1024)S(1)} collective-permute-done((f32[1024]{0:T(1024)S(1)}, f32[1024]{0:T(1024)S(1)}, u32[]{:S(2)}, u32[]{:S(2)}) %collective-permute-start.13) | collective-permute-done | bytes 4128 | tf_op jit(solution)/shard_map/ppermute | solution.py:208
  91.5 3.0 %collective-permute-start.14 = (f32[1024]{0:T(1024)S(1)}, f32[1024]{0:T(1024)S(1)}, u32[]{:S(2)}, u32[]{:S(2)}) collective-permute-start(f32[1024]{0:T(1024)S(1)} %add.48), channel_id=1, source_target_pairs={{0,4},{1,5},{2,6},{3,7},{4,0},{5,1},{6,2},{7,3},{8,12},{9,13},{10,... | collective-permute-start | bytes 12296 | tf_op jit(solution)/shard_map/ppermute | solution.py:208
  94.5 1.6 %collective-permute-done.14 = f32[1024]{0:T(1024)S(1)} collective-permute-done((f32[1024]{0:T(1024)S(1)}, f32[1024]{0:T(1024)S(1)}, u32[]{:S(2)}, u32[]{:S(2)}) %collective-permute-start.14) | collective-permute-done | bytes 4128 | tf_op jit(solution)/shard_map/ppermute | solution.py:208
  96.1 0.6 add.49
  (6 shorter events, 0.0 us)
Async XLA Ops:
  1.3 15.1 %collective-permute-start.3 = (bf16[4,2,32,1024]{3,2,1,0:T(8,128)(2,1)S(1)}, bf16[4,2,32,1024]{3,2,1,0:T(8,128)(2,1)}, u32[]{:S(2)}, u32[]{:S(2)}) collective-permute-start(bf16[4,2,32,1024]{3,2,1,0:T(8,128)(2,1)S(1)} %bitcast.27), channel_id=1, source_target_pairs={{0,2},{1,3},{2,0},{3,1},{4,6},{5,7},{6,4},{7,5},{8,10},{9,11},{10,... | collective-permute-start | bytes 1572872 | tf_op jit(solution)/shard_map/ppermute | solution.py:172
  4.4 20.1 %collective-permute-start.7 = (bf16[4,2,32,1024]{3,2,1,0:T(8,128)(2,1)S(1)}, bf16[4,2,32,1024]{3,2,1,0:T(8,128)(2,1)S(1)}, u32[]{:S(2)}, u32[]{:S(2)}) collective-permute-start(bf16[4,2,32,1024]{3,2,1,0:T(8,128)(2,1)S(1)} %bitcast.28), channel_id=1, source_target_pairs={{2,4},{3,5},{4,2},{5,3},{10,12},{11,13},{12,10},{13,11},{18,20},{1... | collective-permute-start | bytes 1572872 | tf_op jit(solution)/shard_map/ppermute | solution.py:173
  16.5 9.4 %collective-permute-start.4 = (bf16[4,2,32,1024]{3,2,1,0:T(8,128)(2,1)}, bf16[4,2,32,1024]{3,2,1,0:T(8,128)(2,1)}, u32[]{:S(2)}, u32[]{:S(2)}) collective-permute-start(bf16[4,2,32,1024]{3,2,1,0:T(8,128)(2,1)} %collective-permute-done.3.field_ref), channel_id=1, source_target_pairs={{2,4},{3,5},{4,2},{5,3},{10,12},{11,13},{12,10},{13,11},{18,20},{1... | collective-permute-start | bytes 1572872 | tf_op jit(solution)/shard_map/ppermute | solution.py:182
  18.7 1.7 %copy-start = (bf16[40,64,512]{2,1,0:T(8,128)(2,1)S(1)}, bf16[40,64,512]{2,1,0:T(8,128)(2,1)}, u32[]{:S(2)}) copy-start(bf16[40,64,512]{2,1,0:T(8,128)(2,1)} %records_ref.1) | copy-start | bytes 7864324
  20.4 0.9 copy-start.1
  22.8 13.2 %collective-permute-start.1 = (bf16[8,64,512]{2,1,0:T(8,128)(2,1)S(1)}, bf16[8,64,512]{2,1,0:T(8,128)(2,1)S(1)}, u32[]{:S(2)}, u32[]{:S(2)}) collective-permute-start(bf16[8,64,512]{2,1,0:T(8,128)(2,1)S(1)} %spectra.1), channel_id=1, source_target_pairs={{0,16},{8,24},{16,0},{24,8},{1,17},{9,25},{17,1},{25,9},{2,18},{10... | collective-permute-start | bytes 1572872 | tf_op jit(solution)/shard_map/ppermute | solution.py:177
  24.5 17.7 %collective-permute-start.8 = (bf16[4,2,32,1024]{3,2,1,0:T(8,128)(2,1)S(1)}, bf16[4,2,32,1024]{3,2,1,0:T(8,128)(2,1)S(1)}, u32[]{:S(2)}, u32[]{:S(2)}) collective-permute-start(bf16[4,2,32,1024]{3,2,1,0:T(8,128)(2,1)S(1)} %collective-permute-done.7), channel_id=1, source_target_pairs={{2,0},{3,1},{4,6},{5,7},{10,8},{11,9},{12,14},{13,15},{18,16},{19,... | collective-permute-start | bytes 1572872 | tf_op jit(solution)/shard_map/ppermute | solution.py:181
  25.8 25.4 %collective-permute-start.5 = (bf16[4,2,32,1024]{3,2,1,0:T(8,128)(2,1)}, bf16[4,2,32,1024]{3,2,1,0:T(8,128)(2,1)}, u32[]{:S(2)}, u32[]{:S(2)}) collective-permute-start(bf16[4,2,32,1024]{3,2,1,0:T(8,128)(2,1)} %collective-permute-done.4), channel_id=1, source_target_pairs={{2,0},{3,1},{4,6},{5,7},{10,8},{11,9},{12,14},{13,15},{18,16},{19,... | collective-permute-start | bytes 1572872 | tf_op jit(solution)/shard_map/ppermute | solution.py:186
  27.1 26.7 %collective-permute-start = (bf16[8,64,512]{2,1,0:T(8,128)(2,1)S(1)}, bf16[8,64,512]{2,1,0:T(8,128)(2,1)S(1)}, u32[]{:S(2)}, u32[]{:S(2)}) collective-permute-start(bf16[8,64,512]{2,1,0:T(8,128)(2,1)S(1)} %spectra.1), channel_id=1, source_target_pairs={{0,8},{8,0},{16,24},{24,16},{1,9},{9,1},{17,25},{25,17},{2,10},{10... | collective-permute-start | bytes 1572872 | tf_op jit(solution)/shard_map/ppermute | solution.py:178
  27.2 34.6 %collective-permute-start.11 = (bf16[4,2,32,1024]{3,2,1,0:T(8,128)(2,1)S(1)}, bf16[4,2,32,1024]{3,2,1,0:T(8,128)(2,1)}, u32[]{:S(2)}, u32[]{:S(2)}) collective-permute-start(bf16[4,2,32,1024]{3,2,1,0:T(8,128)(2,1)S(1)} %bitcast.29), channel_id=1, source_target_pairs={{0,1},{1,0},{2,3},{3,2},{4,5},{5,4},{6,7},{7,6},{8,9},{9,8},{10,11... | collective-permute-start | bytes 1572872 | tf_op jit(solution)/shard_map/ppermute | solution.py:174
  36.0 28.6 %collective-permute-start.10 = (bf16[4,2,32,1024]{3,2,1,0:T(8,128)(2,1)}, bf16[4,2,32,1024]{3,2,1,0:T(8,128)(2,1)}, u32[]{:S(2)}, u32[]{:S(2)}) collective-permute-start(bf16[4,2,32,1024]{3,2,1,0:T(8,128)(2,1)} %collective-permute-done.3.field_ref), channel_id=1, source_target_pairs={{0,1},{1,0},{2,3},{3,2},{4,5},{5,4},{6,7},{7,6},{8,9},{9,8},{10,11... | collective-permute-start | bytes 1572872 | tf_op jit(solution)/shard_map/ppermute | solution.py:180
  42.2 0.8 copy-start.2
  43.0 11.5 %collective-permute-start.2 = (bf16[8,64,512]{2,1,0:T(8,128)(2,1)S(1)}, bf16[8,64,512]{2,1,0:T(8,128)(2,1)}, u32[]{:S(2)}, u32[]{:S(2)}) collective-permute-start(bf16[8,64,512]{2,1,0:T(8,128)(2,1)S(1)} %collective-permute-done.1), channel_id=1, source_target_pairs={{0,8},{8,0},{16,24},{24,16},{1,9},{9,1},{17,25},{25,17},{2,10},{10... | collective-permute-start | bytes 1572872 | tf_op jit(solution)/shard_map/ppermute | solution.py:183
  51.2 16.3 %collective-permute-start.9 = (bf16[4,2,32,1024]{3,2,1,0:T(8,128)(2,1)S(1)}, bf16[4,2,32,1024]{3,2,1,0:T(8,128)(2,1)}, u32[]{:S(2)}, u32[]{:S(2)}) collective-permute-start(bf16[4,2,32,1024]{3,2,1,0:T(8,128)(2,1)S(1)} %broadcast_select_fusion.field_ref), channel_id=1, source_target_pairs={{0,1},{1,0},{2,3},{3,2},{4,5},{5,4},{6,7},{7,6},{8,9},{9,8},{10,11... | collective-permute-start | bytes 1572872 | tf_op jit(solution)/shard_map/ppermute | solution.py:185
  53.8 21.5 %collective-permute-start.6 = (bf16[4,2,32,1024]{3,2,1,0:T(8,128)(2,1)S(1)}, bf16[4,2,32,1024]{3,2,1,0:T(8,128)(2,1)}, u32[]{:S(2)}, u32[]{:S(2)}) collective-permute-start(bf16[4,2,32,1024]{3,2,1,0:T(8,128)(2,1)S(1)} %broadcast_select_fusion.1.field_ref), channel_id=1, source_target_pairs={{0,1},{1,0},{2,3},{3,2},{4,5},{5,4},{6,7},{7,6},{8,9},{9,8},{10,11... | collective-permute-start | bytes 1572872 | tf_op jit(solution)/shard_map/ppermute | solution.py:188
  78.1 3.7 %collective-permute-start.12 = (f32[1024]{0:T(1024)S(1)}, f32[1024]{0:T(1024)S(1)}, u32[]{:S(2)}, u32[]{:S(2)}) collective-permute-start(f32[1024]{0:T(1024)S(1)} %bitcast.33), channel_id=1, source_target_pairs={{0,1},{1,0},{2,3},{3,2},{4,5},{5,4},{6,7},{7,6},{8,9},{9,8},{10,11... | collective-permute-start | bytes 12296 | tf_op jit(solution)/shard_map/ppermute | solution.py:208
  81.8 9.7 %collective-permute-start.13 = (f32[1024]{0:T(1024)S(1)}, f32[1024]{0:T(1024)S(1)}, u32[]{:S(2)}, u32[]{:S(2)}) collective-permute-start(f32[1024]{0:T(1024)S(1)} %add.47), channel_id=1, source_target_pairs={{0,2},{1,3},{2,0},{3,1},{4,6},{5,7},{6,4},{7,5},{8,10},{9,11},{10,... | collective-permute-start | bytes 12296 | tf_op jit(solution)/shard_map/ppermute | solution.py:208
  91.5 4.6 %collective-permute-start.14 = (f32[1024]{0:T(1024)S(1)}, f32[1024]{0:T(1024)S(1)}, u32[]{:S(2)}, u32[]{:S(2)}) collective-permute-start(f32[1024]{0:T(1024)S(1)} %add.48), channel_id=1, source_target_pairs={{0,4},{1,5},{2,6},{3,7},{4,0},{5,1},{6,2},{7,3},{8,12},{9,13},{10,... | collective-permute-start | bytes 12296 | tf_op jit(solution)/shard_map/ppermute | solution.py:208

commit v2 on v1

--- a/solution.py
+++ b/solution.py
@@ -55,14 +55,14 @@
         ],
         out_specs=pl.BlockSpec((channels, ROWS, recv), lambda i: (0, i, 0)),
         out_shape=jax.ShapeDtypeStruct((channels, trans, recv), jnp.bfloat16),
-        compiler_params=pltpu.CompilerParams(vmem_limit_bytes=24 << 20),
+        compiler_params=pltpu.CompilerParams(vmem_limit_bytes=16 << 20),
         cost_estimate=pl.CostEstimate(
             flops=2 * channels * ROWS * gates * trans * recv,
             bytes_accessed=2 * (gates + channels) * trans * recv,
             transcendentals=0,
         ),
         name="spectra",
-    )(table, active, records)
+    )(table, active, pltpu.with_memory_space_constraint(records, pltpu.HBM))
 
 
 def adjoint_kernel(*refs):
@@ -90,68 +90,73 @@
         in_specs=[pl.BlockSpec((1, 2, rows, recv), lambda f: (f, 0, 0, 0))] * count
         + [pl.BlockSpec((1, 2 * recv, cells), lambda f: (f, 0, 0))],
         out_specs=pl.BlockSpec((1, 2, count, rows, cells), lambda f: (f, 0, 0, 0, 0)),
-        out_shape=jax.ShapeDtypeStruct((freqs, 2, count, rows, cells), jnp.float32),
-        compiler_params=pltpu.CompilerParams(vmem_limit_bytes=40 << 20),
+        out_shape=pltpu.VMEM((freqs, 2, count, rows, cells), jnp.float32),
+        compiler_params=pltpu.CompilerParams(vmem_limit_bytes=20 << 20),
         cost_estimate=pl.CostEstimate(
             flops=8 * freqs * count * rows * recv * cells,
             bytes_accessed=4 * freqs * recv * cells + 8 * freqs * count * rows * cells,
             transcendentals=0,
         ),
         name="adjoint",
-    )(*pieces, green.reshape(freqs, 2 * recv, cells))
-
-
-def weigh_kernel(last, place_ref, mine_ref, other_ref, field_ref, field_other_ref, sum_ref, out_ref, total):
-    del place_ref
-    step = pl.program_id(0)
-
-    @pl.when(step == 0)
-    def _():
-        total[...] = sum_ref[...]
-
-    cells = total.shape[1]
-    sums = total[...]
-    for adjoint, field in ((mine_ref, field_ref), (other_ref, field_other_ref)):
-        terms = adjoint[0, :, 0].reshape(-1, cells) * field[0].reshape(-1, cells).astype(jnp.float32)
-        sums = sums + jnp.sum(terms.reshape(-1, 8, cells), axis=0)
-    total[...] = sums
-
-    @pl.when(step == pl.num_programs(0) - 1)
-    def _():
-        if last:
-            out_ref[...] = jnp.sum(total[...], axis=0, keepdims=True)
-        else:
-            out_ref[...] = total[...]
-
-
-def weigh(adjoint, place, mine, other, sums, last):
-    freqs, _, blocks, rows, cells = adjoint.shape
-    field = pl.BlockSpec((1, 2, rows, cells), lambda f, place: (f, 0, 0, 0))
-    out_rows = 1 if last else 8
+    )(*pieces, pltpu.with_memory_space_constraint(green.reshape(freqs, 2 * recv, cells), pltpu.HBM))
+
+
+def in_vmem(kernel, scalars, operands, shape, dtype, name):
     return pl.pallas_call(
-        functools.partial(weigh_kernel, last),
-        grid_spec=pltpu.PrefetchScalarGridSpec(
-            num_scalar_prefetch=1,
-            grid=(freqs,),
-            in_specs=[
-                pl.BlockSpec((1, 2, 1, rows, cells), lambda f, place: (f, 0, place[0], 0, 0)),
-                pl.BlockSpec((1, 2, 1, rows, cells), lambda f, place: (f, 0, place[1], 0, 0)),
-                field,
-                field,
-                pl.BlockSpec((8, cells), lambda f, place: (0, 0)),
-            ],
-            out_specs=pl.BlockSpec((out_rows, cells), lambda f, place: (0, 0)),
-            scratch_shapes=[pltpu.VMEM((8, cells), jnp.float32)],
-        ),
-        out_shape=jax.ShapeDtypeStruct((out_rows, cells), jnp.float32),
+        kernel,
+        in_specs=[pl.BlockSpec(memory_space=pltpu.SMEM)]
+        + [pl.BlockSpec(memory_space=pltpu.VMEM)] * len(operands),
+        out_specs=pl.BlockSpec(memory_space=pltpu.VMEM),
+        out_shape=pltpu.VMEM(shape, dtype),
         compiler_params=pltpu.CompilerParams(vmem_limit_bytes=16 << 20),
         cost_estimate=pl.CostEstimate(
-            flops=8 * freqs * rows * cells,
-            bytes_accessed=24 * freqs * rows * cells,
+            flops=4 * sum(operand.size for operand in operands[1:]),
+            bytes_accessed=4 * sum(operand.size for operand in operands[1:]),
             transcendentals=0,
         ),
-        name="weigh",
-    )(place, adjoint, adjoint, mine, other, sums)
+        name=name,
+    )(
+        jnp.stack(scalars).astype(jnp.int32),
+        *[pltpu.with_memory_space_constraint(operand, pltpu.VMEM) for operand in operands],
+    )
+
+
+def weigh_kernel(count, paired, extra, last, place_ref, adjoint_ref, *refs):
+    field_refs, (sum_ref, out_ref) = list(refs[:-2]), refs[-2:]
+    extra_ref = field_refs.pop() if extra else None
+    freqs, parts, _, cells = field_refs[0].shape
+    second = place_ref[count] != 0
+    sums = sum_ref[...]
+    position = 0
+    for number in range(count):
+        place = place_ref[number]
+        for freq in range(freqs):
+            for part in range(parts):
+                weights = adjoint_ref[freq, part, place]
+                if extra and number == count - 1:
+                    weights = weights + extra_ref[freq, part].astype(jnp.float32)
+                field = field_refs[position][freq, part].astype(jnp.float32)
+                if number == paired:
+                    other = field_refs[position + 1][freq, part].astype(jnp.float32)
+                    field = jnp.where(second, other, field)
+                terms = weights * field
+                sums = sums + jnp.sum(terms.reshape(-1, 8, cells), axis=0)
+        position += 1 + (number == paired)
+    out_ref[...] = jnp.sum(sums, axis=0, keepdims=True) if last else sums
+
+
+def pick_kernel(flag_ref, first_ref, second_ref, out_ref):
+    @pl.when(flag_ref[0] == 0)
+    def _():
+        out_ref[...] = first_ref[...]
+
+    @pl.when(flag_ref[0] != 0)
+    def _():
+        out_ref[...] = second_ref[...]
+
+
+def block_kernel(place_ref, adjoint_ref, out_ref):
+    out_ref[...] = adjoint_ref[:, :, place_ref[0]].astype(out_ref.dtype)
 
 
 def box_shards(records, active, green, background):
@@ -160,13 +165,15 @@
     z_pairs = [(r, r ^ 2) for r in range(8)]
     z_middle = [(r, r ^ 6) for r in range(2, 6)]
     z_outward = [(2, 0), (3, 1), (4, 6), (5, 7)]
+    z_inward = [(there, here) for here, there in z_outward]
     core = [(t, t ^ 1) for t in range(4)]
     along_x = [(t, t ^ 2) for t in range(4)]
-    send = lax.ppermute
+    send, tie = lax.ppermute, lax.optimization_barrier
 
     me_tx, me_rx = lax.axis_index("tx"), lax.axis_index("rx")
     me_z, me_y = me_rx // 2, me_rx % 2
     middle = (me_z == 1) | (me_z == 2)
+    lower = me_z < 2
 
     own = background.transpose(1, 2, 0, 3)
     near = send(own, "rx", z_pairs)
@@ -177,32 +184,47 @@
     spectra_x = send(spectra, "tx", along_x)
     spectra_core = send(spectra, "tx", core)
 
-    near_y = send(near, "rx", along_y)
+    near, across, own_y, spectra_core = tie((near, across, own_y, spectra_core))
     across_out = send(across, "rx", z_outward)
     far = send(near, "rx", z_middle)
+    near_y = send(near, "rx", along_y)
+
     spectra_both = send(spectra_x, "tx", core)
-    mid = jnp.where(middle, across, across_out)
-    mid_y = send(mid, "rx", along_y)
-    far_out = send(far, "rx", z_outward)
-    end = jnp.where(middle, far, far_out)
-    end_y = send(end, "rx", along_y)
-
     adjoint = adjoint_of([spectra, spectra_core, spectra_x, spectra_both], green)
     freqs, _, groups, rows, cells = adjoint.shape
     adjoint = adjoint.reshape(freqs, 2, 2 * groups, rows // 2, cells)
 
-    lower = me_z < 2
-    owners = (
-        (me_z, own, own_y),
-        (me_z ^ 1, near, near_y),
-        (jnp.where(lower, 2, 1), mid, mid_y),
-        (jnp.where(lower, 3, 0), end, end_y),
-    )
-    sums = jnp.zeros((8, cells), jnp.float32)
-    for step, (owner, mine, other) in enumerate(owners):
-        slot = (owner ^ me_tx) * 2
-        place = jnp.stack([slot + me_y, slot + 1 - me_y]).astype(jnp.int32)
-        sums = weigh(adjoint, place, mine, other, sums, step == len(owners) - 1)
+    def place_of(z, y):
+        return (z ^ me_tx) * 2 + y
+
+    mid_z, far_z, other_y = jnp.where(lower, 2, 1), jnp.where(lower, 3, 0), 1 - me_y
+    far_place = place_of(far_z, other_y)
+    partial = in_vmem(block_kernel, [far_place], [adjoint], own.shape, own.dtype, "block")
+    partial, far, near_y, across_out = tie((partial, far, near_y, across_out))
+    partial = send(partial, "rx", z_inward)
+    far_out = send(far, "rx", z_outward)
+    far_both = send(near_y, "rx", z_middle)
+    mid = in_vmem(pick_kernel, [middle], [across_out, across], own.shape, own.dtype, "pick")
+    mid_y = send(mid, "rx", along_y)
+
+    zero = jnp.zeros((), jnp.int32)
+    places = [place_of(me_z, me_y), place_of(me_z, other_y), place_of(me_z ^ 1, me_y), place_of(me_z ^ 1, other_y)]
+    sums = in_vmem(
+        functools.partial(weigh_kernel, 5, -1, False, False),
+        places + [place_of(mid_z, me_y), zero],
+        [adjoint, own, own_y, near, near_y, mid, jnp.zeros((8, cells), jnp.float32)],
+        (8, cells),
+        jnp.float32,
+        "weigh",
+    )
+    sums = in_vmem(
+        functools.partial(weigh_kernel, 3, 1, True, True),
+        [place_of(mid_z, other_y), place_of(far_z, me_y), far_place, middle],
+        [adjoint, mid_y, far_out, far, far_both, partial, sums],
+        (1, cells),
+        jnp.float32,
+        "weigh",
+    )
     sums = sums.reshape(cells)
     for bit in (1, 2, 4):
         sums = sums + send(sums, "rx", [(r, r ^ bit) for r in range(8)])

time: 97.3 us -> 81.6 us (0.84)
  waiting for transfers between devices: 40.7 us -> 23.3 us
  local copies, waits for them, and re-layouts: 5.57 us -> 11.6 us
  Pallas kernels: 19.9 us -> 16 us
  other arithmetic: 3.1 us -> 0.68 us
  starting transfers between devices: 27.4 us -> 29.3 us
    ppermute x1 -> x2, starting transfers between devices: 0.57 us -> 10.2 us  [the longest x1 8.71 us: box_shards(): partial = send(partial, 'rx', z_inward)]
    ppermute x1, waiting for transfers between devices: 11.3 us -> 2.75 us  [box_shards(): near = send(own, 'rx', z_pairs)]
    ppermute x1, waiting for transfers between devices: 7.08 us -> 0.01 us  [box_shards(): far_out = send(far, 'rx', z_outward)]
    ppermute x3, starting transfers between devices: 12.7 us -> 6.09 us  [box_shards(): sums = sums + send(sums, 'rx', [(r, r ^ bit) for r in range(8)])]
    unnamed x8 -> x12, local copies, waits for them, and re-layouts: 5.56 us -> 11.5 us
    pallas_call x4, Pallas kernels: 11.2 us -> 5.51 us  [in_vmem(): pl.pallas_call(kernel, in_specs=[pl.BlockSpec(memory_space=pltpu.SMEM)] +...]
    ppermute x1, waiting for transfers between devices: 0.01 us -> 2.77 us  [box_shards(): own_y = send(own, 'rx', along_y)]
    ppermute x1, waiting for transfers between devices: 4.87 us -> 2.56 us  [box_shards(): across_out = send(across, 'rx', z_outward)]
  transfers between devices with their start and end apart: 15 -> 16, of which waited for: 8 -> 8; matrix products, arithmetic and copies ran while one was open for 3% -> 2% of each run, Pallas kernels for 18% -> 12%
where the time goes in v2:
time: 81.6 us; the launch traced here: 81 us
  starting transfers between devices  29.3 us (36%)
  waiting for transfers between devices  23.3 us (29%)
  Pallas kernels  16 us (20%)
  local copies, waits for them, and re-layouts  11.6 us (14%)
    unnamed x12, local copies, waits for them, and re-layouts  11.5 us
    ppermute x1, starting transfers between devices, box_shards(): partial = send(partial, 'rx', z_inward)  8.71 us
    pallas_call x1, Pallas kernels, adjoint_of(): pl.pallas_call(adjoint_kernel, grid=(freqs,), in_specs=[pl.BlockSpec((1,...  7.33 us
    ppermute x3, waiting for transfers between devices, box_shards(): sums = sums + send(sums, 'rx', [(r, r ^ bit) for r in range(8)])  6.15 us
    ppermute x3, starting transfers between devices, box_shards(): sums = sums + send(sums, 'rx', [(r, r ^ bit) for r in range(8)])  6.09 us
    ppermute x1, waiting for transfers between devices, box_shards(): spectra_x = send(spectra, 'tx', along_x)  6.05 us
    pallas_call x4, Pallas kernels, in_vmem(): pl.pallas_call(kernel, in_specs=[pl.BlockSpec(memory_space=pltpu.SMEM)] +...  5.51 us
    pallas_call x1, Pallas kernels, spectra_of(): pl.pallas_call(spectra_kernel, grid=(trans // ROWS,), in_specs=[pl.BlockS...  3.17 us
  transfers between devices with their start and end apart: 16, of which 8 were waited for; matrix products, arithmetic and copies ran while one was open for 2% of the time, Pallas kernels for 12%

profile of v2, /device:TPU:0, one launch (start us, length us, event | category | flops | bytes accessed | tf_op | source)
XLA Modules:
  0.0 81.0 jit_solution(11867720451915517434)
XLA Ops:
  0.0 0.8 copy.6.active_ref
  0.8 0.9 %copy-done.4 = bf16[128,640]{1,0:T(8,128)(2,1)S(1)} copy-done((bf16[128,640]{1,0:T(8,128)(2,1)S(1)}, bf16[128,640]{1,0:T(8,128)(2,1)}, u32[]{:S(2)}) %copy-start.4) | copy-done | bytes 163864
  1.7 3.2 %spectra.1 = bf16[8,64,512]{2,1,0:T(8,128)(2,1)S(1)} custom-call(bf16[128,640]{1,0:T(8,128)(2,1)S(1)} %copy-done.4, s32[64,8]{1,0:T(8,128)S(1)} %copy.6.active_ref, bf16[40,64,512]{2,1,0:T(8,128)(2,1)} %records_ref.1), custom_call_target="tpu_custom_call" | custom-call | flops 335544320 | bytes 3145728 | tf_op jit(solution)/shard_map/spectra/pallas_call | solution.py:48
  4.9 3.0 %collective-permute-start.4 = (bf16[8,64,512]{2,1,0:T(8,128)(2,1)S(1)}, bf16[8,64,512]{2,1,0:T(8,128)(2,1)}, u32[]{:S(2)}, u32[]{:S(2)}) collective-permute-start(bf16[8,64,512]{2,1,0:T(8,128)(2,1)S(1)} %spectra.1), channel_id=1, source_target_pairs={{0,16},{8,24},{16,0},{24,8},{1,17},{9,25},{17,1},{25,9},{2,18},{10... | collective-permute-start | bytes 1572872 | tf_op jit(solution)/shard_map/ppermute | solution.py:184
  7.9 1.3 %copy.9 = bf16[32,4,2,1024]{3,0,2,1:T(8,128)(2,1)S(1)} copy(bf16[32,4,2,1024]{3,2,1,0:T(2,128)(2,1)} %param.8) | data formatting | bytes 1048576 | tf_op args[3]
  9.2 1.6 %collective-permute-start = (bf16[4,2,32,1024]{3,2,1,0:T(8,128)(2,1)S(1)}, bf16[4,2,32,1024]{3,2,1,0:T(8,128)(2,1)S(1)}, u32[]{:S(2)}, u32[]{:S(2)}) collective-permute-start(bf16[4,2,32,1024]{3,2,1,0:T(8,128)(2,1)S(1)} %bitcast.23), channel_id=1, source_target_pairs={{0,2},{1,3},{2,0},{3,1},{4,6},{5,7},{6,4},{7,5},{8,10},{9,11},{10,... | collective-permute-start | bytes 1572872 | tf_op jit(solution)/shard_map/ppermute | solution.py:179
  10.8 1.5 %collective-permute-start.1 = (bf16[4,2,32,1024]{3,2,1,0:T(8,128)(2,1)S(1)}, bf16[4,2,32,1024]{3,2,1,0:T(8,128)(2,1)}, u32[]{:S(2)}, u32[]{:S(2)}) collective-permute-start(bf16[4,2,32,1024]{3,2,1,0:T(8,128)(2,1)S(1)} %bitcast.24), channel_id=1, source_target_pairs={{2,4},{3,5},{4,2},{5,3},{10,12},{11,13},{12,10},{13,11},{18,20},{1... | collective-permute-start | bytes 1572872 | tf_op jit(solution)/shard_map/ppermute | solution.py:180
  12.3 1.5 %collective-permute-start.2 = (bf16[4,2,32,1024]{3,2,1,0:T(8,128)(2,1)S(1)}, bf16[4,2,32,1024]{3,2,1,0:T(8,128)(2,1)S(1)}, u32[]{:S(2)}, u32[]{:S(2)}) collective-permute-start(bf16[4,2,32,1024]{3,2,1,0:T(8,128)(2,1)S(1)} %bitcast.25), channel_id=1, source_target_pairs={{0,1},{1,0},{2,3},{3,2},{4,5},{5,4},{6,7},{7,6},{8,9},{9,8},{10,11... | collective-permute-start | bytes 1572872 | tf_op jit(solution)/shard_map/ppermute | solution.py:181
  13.8 0.0 collective-permute-start.3
  13.8 6.1 %collective-permute-done.4 = bf16[8,64,512]{2,1,0:T(8,128)(2,1)} collective-permute-done((bf16[8,64,512]{2,1,0:T(8,128)(2,1)S(1)}, bf16[8,64,512]{2,1,0:T(8,128)(2,1)}, u32[]{:S(2)}, u32[]{:S(2)}) %collective-permute-start.4) | collective-permute-done | bytes 524320 | tf_op jit(solution)/shard_map/ppermute | solution.py:184
  19.9 0.0 collective-permute-start.5
  19.9 2.8 %collective-permute-done.refs_2_ = bf16[4,2,32,1024]{3,2,1,0:T(8,128)(2,1)S(1)} collective-permute-done((bf16[4,2,32,1024]{3,2,1,0:T(8,128)(2,1)S(1)}, bf16[4,2,32,1024]{3,2,1,0:T(8,128)(2,1)S(1)}, u32[]{:S(2)}, u32[]{:S(2)}) %collective-permute-start) | collective-permute-done | bytes 524320 | tf_op jit(solution)/shard_map/ppermute | solution.py:179
  22.7 0.0 collective-permute-done.1.second_ref
  22.7 2.8 %collective-permute-done.2.refs_1_ = bf16[4,2,32,1024]{3,2,1,0:T(8,128)(2,1)S(1)} collective-permute-done((bf16[4,2,32,1024]{3,2,1,0:T(8,128)(2,1)S(1)}, bf16[4,2,32,1024]{3,2,1,0:T(8,128)(2,1)S(1)}, u32[]{:S(2)}, u32[]{:S(2)}) %collective-permute-start.2) | collective-permute-done | bytes 524320 | tf_op jit(solution)/shard_map/ppermute | solution.py:181
  25.4 0.0 collective-permute-done.3
  25.4 0.8 %copy-done.2 = bf16[8,64,512]{2,1,0:T(8,128)(2,1)} copy-done((bf16[8,64,512]{2,1,0:T(8,128)(2,1)}, bf16[8,64,512]{2,1,0:T(8,128)(2,1)S(1)}, u32[]{:S(2)}) %copy-start.2) | copy-done | bytes 524312
  26.2 0.7 collective-permute-start.6
  26.9 1.6 %collective-permute-start.7 = (bf16[4,2,32,1024]{3,2,1,0:T(8,128)(2,1)S(1)}, bf16[4,2,32,1024]{3,2,1,0:T(8,128)(2,1)S(1)}, u32[]{:S(2)}, u32[]{:S(2)}) collective-permute-start(bf16[4,2,32,1024]{3,2,1,0:T(8,128)(2,1)S(1)} %collective-permute-done.refs_2_), channel_id=1, source_target_pairs={{0,1},{1,0},{2,3},{3,2},{4,5},{5,4},{6,7},{7,6},{8,9},{9,8},{10,11... | collective-permute-start | bytes 1572872 | tf_op jit(solution)/shard_map/ppermute | solution.py:190
  28.5 1.3 %collective-permute-start.8 = (bf16[4,2,32,1024]{3,2,1,0:T(8,128)(2,1)}, bf16[4,2,32,1024]{3,2,1,0:T(8,128)(2,1)}, u32[]{:S(2)}, u32[]{:S(2)}) collective-permute-start(bf16[4,2,32,1024]{3,2,1,0:T(8,128)(2,1)} %collective-permute-done.1.second_ref), channel_id=1, source_target_pairs={{2,0},{3,1},{4,6},{5,7},{10,8},{11,9},{12,14},{13,15},{18,16},{19,... | collective-permute-start | bytes 1572872 | tf_op jit(solution)/shard_map/ppermute | solution.py:188
  29.8 0.0 collective-permute-done.5
  29.9 1.0 %copy-done.3 = bf16[8,64,512]{2,1,0:T(8,128)(2,1)S(1)} copy-done((bf16[8,64,512]{2,1,0:T(8,128)(2,1)S(1)}, bf16[8,64,512]{2,1,0:T(8,128)(2,1)}, u32[]{:S(2)}) %copy-start.3) | copy-done | bytes 524312
  30.9 7.3 %adjoint.1 = f32[4,2,4,64,1024]{4,3,2,1,0:T(8,128)S(1)} custom-call(bf16[4,2,64,512]{3,2,1,0:T(8,128)(2,1)S(1)} %bitcast.22, bf16[4,2,64,512]{3,2,1,0:T(8,128)(2,1)S(1)} %bitcast.27, bf16[4,2,64,512]{3,2,1,0:T(8,128)(2,1)} %bitcast.7.refs_2_, bf16[4,2,64,512]{3,2,1,0:T(8,128)(2,1)} %bitcast.8.refs_3_, bf16[4,1024,1024]{2,1,0:T(8,128)(2,1)} %bitcast.30), custom_call_target="tpu_custom_call" | custom-call | flops 4294967296 | bytes 16777216 | tf_op jit(solution)/shard_map/adjoint/pallas_call | solution.py:87
  38.2 0.9 %block.1 = bf16[4,2,32,1024]{3,2,1,0:T(8,128)(2,1)} custom-call(s32[1]{0:T(128)} %bitcast.2.place_ref, f32[4,2,8,32,1024]{4,3,2,1,0:T(8,128)S(1)} %bitcast.19), custom_call_target="tpu_custom_call" | custom-call | tf_op jit(solution)/shard_map/block/pallas_call | solution.py:105
  39.2 3.2 %copy-done = f32[4,2,4,64,1024]{4,3,2,1,0:T(8,128)} copy-done((f32[4,2,4,64,1024]{4,3,2,1,0:T(8,128)}, f32[4,2,4,64,1024]{4,3,2,1,0:T(8,128)S(1)}, u32[]{:S(2)}) %copy-start) | copy-done | bytes 8388632
  42.4 0.0 collective-permute-done.6.refs_2_
  42.4 0.0 collective-permute-done.7.refs_3_
  42.4 2.6 %collective-permute-done.8.first_ref = bf16[4,2,32,1024]{3,2,1,0:T(8,128)(2,1)} collective-permute-done((bf16[4,2,32,1024]{3,2,1,0:T(8,128)(2,1)}, bf16[4,2,32,1024]{3,2,1,0:T(8,128)(2,1)}, u32[]{:S(2)}, u32[]{:S(2)}) %collective-permute-start.8) | collective-permute-done | bytes 524320 | tf_op jit(solution)/shard_map/ppermute | solution.py:188
  45.0 1.2 %pick.1.refs_4_ = bf16[4,2,32,1024]{3,2,1,0:T(8,128)(2,1)S(1)} custom-call(s32[1]{0:T(128)} %bitcast.3.flag_ref, bf16[4,2,32,1024]{3,2,1,0:T(8,128)(2,1)} %collective-permute-done.8.first_ref, bf16[4,2,32,1024]{3,2,1,0:T(8,128)(2,1)} %collective-permute-done.1.second_ref), custom_call_target="tpu_custom_call" | custom-call | flops 1048576 | bytes 1048576 | tf_op jit(solution)/shard_map/pick/pallas_call | solution.py:105
  46.2 0.6 collective-permute-start.9
  46.8 1.3 %collective-permute-start.10 = (bf16[4,2,32,1024]{3,2,1,0:T(8,128)(2,1)S(1)}, bf16[4,2,32,1024]{3,2,1,0:T(8,128)(2,1)}, u32[]{:S(2)}, u32[]{:S(2)}) collective-permute-start(bf16[4,2,32,1024]{3,2,1,0:T(8,128)(2,1)S(1)} %collective-permute-done.6.refs_2_), channel_id=1, source_target_pairs={{2,0},{3,1},{4,6},{5,7},{10,8},{11,9},{12,14},{13,15},{18,16},{19,... | collective-permute-start | bytes 1572872 | tf_op jit(solution)/shard_map/ppermute | solution.py:205
  48.1 1.5 %collective-permute-start.11 = (bf16[4,2,32,1024]{3,2,1,0:T(8,128)(2,1)S(1)}, bf16[4,2,32,1024]{3,2,1,0:T(8,128)(2,1)}, u32[]{:S(2)}, u32[]{:S(2)}) collective-permute-start(bf16[4,2,32,1024]{3,2,1,0:T(8,128)(2,1)S(1)} %collective-permute-done.7.refs_3_), channel_id=1, source_target_pairs={{2,4},{3,5},{4,2},{5,3},{10,12},{11,13},{12,10},{13,11},{18,20},{1... | collective-permute-start | bytes 1572872 | tf_op jit(solution)/shard_map/ppermute | solution.py:206
  49.6 8.7 %collective-permute-start.12 = (bf16[4,2,32,1024]{3,2,1,0:T(8,128)(2,1)}, bf16[4,2,32,1024]{3,2,1,0:T(8,128)(2,1)}, u32[]{:S(2)}, u32[]{:S(2)}) collective-permute-start(bf16[4,2,32,1024]{3,2,1,0:T(8,128)(2,1)} %block.1), channel_id=1, source_target_pairs={{0,2},{1,3},{6,4},{7,5},{8,10},{9,11},{14,12},{15,13},{16,18},{17,... | collective-permute-start | bytes 1572872 | tf_op jit(solution)/shard_map/ppermute | solution.py:204
  58.3 0.1 stack.49.place_ref
  58.4 0.1 pad_add_fusion.place_ref
  58.4 3.4 %copy-done.1 = f32[4,2,4,64,1024]{4,3,2,1,0:T(8,128)S(1)} copy-done((f32[4,2,4,64,1024]{4,3,2,1,0:T(8,128)S(1)}, f32[4,2,4,64,1024]{4,3,2,1,0:T(8,128)}, u32[]{:S(2)}) %copy-start.1) | copy-done | bytes 8388632
  61.8 1.4 %weigh.2.refs_5_ = f32[8,1024]{1,0:T(8,128)S(1)} custom-call(s32[6]{0:T(128)S(1)} %stack.49.place_ref, f32[4,2,8,32,1024]{4,3,2,1,0:T(8,128)S(1)} %bitcast.20, bf16[4,2,32,1024]{3,2,1,0:T(8,128)(2,1)S(1)} %bitcast.26, bf16[4,2,32,1024]{3,2,1,0:T(8,128)(2,1)S(1)} %collective-permute-done.2.refs_1_, bf16[4,2,32,1024]{3,2,1,0:T(8,128)(2,1)S(1)} %collective-permute-done.refs_2_, ...), custom_call_target="tpu_custom_call" | custom-call | flops 5275648 | bytes 5275648 | tf_op jit(solution)/shard_map/weigh/pallas_call | solution.py:105
  63.2 0.0 collective-permute-done.9.refs_0_
  63.2 0.0 collective-permute-done.10.refs_1_
  63.2 0.0 collective-permute-done.11.refs_3_
  63.2 3.0 %collective-permute-done.12.refs_4_ = bf16[4,2,32,1024]{3,2,1,0:T(8,128)(2,1)} collective-permute-done((bf16[4,2,32,1024]{3,2,1,0:T(8,128)(2,1)}, bf16[4,2,32,1024]{3,2,1,0:T(8,128)(2,1)}, u32[]{:S(2)}, u32[]{:S(2)}) %collective-permute-start.12) | collective-permute-done | bytes 524320 | tf_op jit(solution)/shard_map/ppermute | solution.py:204
  66.2 2.0 %weigh.3 = f32[1,1024]{1,0:T(1,128)S(1)} custom-call(s32[4]{0:T(128)S(1)} %pad_add_fusion.place_ref, f32[4,2,8,32,1024]{4,3,2,1,0:T(8,128)S(1)} %bitcast.21, bf16[4,2,32,1024]{3,2,1,0:T(8,128)(2,1)} %collective-permute-done.9.refs_0_, bf16[4,2,32,1024]{3,2,1,0:T(8,128)(2,1)} %collective-permute-done.10.refs_1_, ...), custom_call_target="tpu_custom_call" | custom-call | flops 5275648 | bytes 5275648 | tf_op jit(solution)/shard_map/weigh/pallas_call | solution.py:105
  68.2 1.6 %collective-permute-start.13 = (f32[1024]{0:T(1024)S(1)}, f32[1024]{0:T(1024)S(1)}, u32[]{:S(2)}, u32[]{:S(2)}) collective-permute-start(f32[1024]{0:T(1024)S(1)} %bitcast.28), channel_id=1, source_target_pairs={{0,1},{1,0},{2,3},{3,2},{4,5},{5,4},{6,7},{7,6},{8,9},{9,8},{10,11... | collective-permute-start | bytes 12296 | tf_op jit(solution)/shard_map/ppermute | solution.py:230
  69.8 2.1 %collective-permute-done.13 = f32[1024]{0:T(1024)S(1)} collective-permute-done((f32[1024]{0:T(1024)S(1)}, f32[1024]{0:T(1024)S(1)}, u32[]{:S(2)}, u32[]{:S(2)}) %collective-permute-start.13) | collective-permute-done | bytes 4128 | tf_op jit(solution)/shard_map/ppermute | solution.py:230
  71.9 2.5 %collective-permute-start.14 = (f32[1024]{0:T(1024)S(1)}, f32[1024]{0:T(1024)S(1)}, u32[]{:S(2)}, u32[]{:S(2)}) collective-permute-start(f32[1024]{0:T(1024)S(1)} %add.47), channel_id=1, source_target_pairs={{0,2},{1,3},{2,0},{3,1},{4,6},{5,7},{6,4},{7,5},{8,10},{9,11},{10,... | collective-permute-start | bytes 12296 | tf_op jit(solution)/shard_map/ppermute | solution.py:230
  74.3 1.6 %collective-permute-done.14 = f32[1024]{0:T(1024)S(1)} collective-permute-done((f32[1024]{0:T(1024)S(1)}, f32[1024]{0:T(1024)S(1)}, u32[]{:S(2)}, u32[]{:S(2)}) %collective-permute-start.14) | collective-permute-done | bytes 4128 | tf_op jit(solution)/shard_map/ppermute | solution.py:230
  75.9 2.0 %collective-permute-start.15 = (f32[1024]{0:T(1024)S(1)}, f32[1024]{0:T(1024)S(1)}, u32[]{:S(2)}, u32[]{:S(2)}) collective-permute-start(f32[1024]{0:T(1024)S(1)} %add.48), channel_id=1, source_target_pairs={{0,4},{1,5},{2,6},{3,7},{4,0},{5,1},{6,2},{7,3},{8,12},{9,13},{10,... | collective-permute-start | bytes 12296 | tf_op jit(solution)/shard_map/ppermute | solution.py:230
  78.0 2.5 %collective-permute-done.15 = f32[1024]{0:T(1024)S(1)} collective-permute-done((f32[1024]{0:T(1024)S(1)}, f32[1024]{0:T(1024)S(1)}, u32[]{:S(2)}, u32[]{:S(2)}) %collective-permute-start.15) | collective-permute-done | bytes 4128 | tf_op jit(solution)/shard_map/ppermute | solution.py:230
  80.4 0.6 add.49
  (8 shorter events, 0.0 us)
Async XLA Ops:
  0.8 0.9 %copy-start.4 = (bf16[128,640]{1,0:T(8,128)(2,1)S(1)}, bf16[128,640]{1,0:T(8,128)(2,1)}, u32[]{:S(2)}) copy-start(bf16[128,640]{1,0:T(8,128)(2,1)} %constant.42.clone.table_ref) | copy-start | bytes 491524
  4.9 15.0 %collective-permute-start.4 = (bf16[8,64,512]{2,1,0:T(8,128)(2,1)S(1)}, bf16[8,64,512]{2,1,0:T(8,128)(2,1)}, u32[]{:S(2)}, u32[]{:S(2)}) collective-permute-start(bf16[8,64,512]{2,1,0:T(8,128)(2,1)S(1)} %spectra.1), channel_id=1, source_target_pairs={{0,16},{8,24},{16,0},{24,8},{1,17},{9,25},{17,1},{25,9},{2,18},{10... | collective-permute-start | bytes 1572872 | tf_op jit(solution)/shard_map/ppermute | solution.py:184
  9.2 13.4 %collective-permute-start = (bf16[4,2,32,1024]{3,2,1,0:T(8,128)(2,1)S(1)}, bf16[4,2,32,1024]{3,2,1,0:T(8,128)(2,1)S(1)}, u32[]{:S(2)}, u32[]{:S(2)}) collective-permute-start(bf16[4,2,32,1024]{3,2,1,0:T(8,128)(2,1)S(1)} %bitcast.23), channel_id=1, source_target_pairs={{0,2},{1,3},{2,0},{3,1},{4,6},{5,7},{6,4},{7,5},{8,10},{9,11},{10,... | collective-permute-start | bytes 1572872 | tf_op jit(solution)/shard_map/ppermute | solution.py:179
  10.8 11.8 %collective-permute-start.1 = (bf16[4,2,32,1024]{3,2,1,0:T(8,128)(2,1)S(1)}, bf16[4,2,32,1024]{3,2,1,0:T(8,128)(2,1)}, u32[]{:S(2)}, u32[]{:S(2)}) collective-permute-start(bf16[4,2,32,1024]{3,2,1,0:T(8,128)(2,1)S(1)} %bitcast.24), channel_id=1, source_target_pairs={{2,4},{3,5},{4,2},{5,3},{10,12},{11,13},{12,10},{13,11},{18,20},{1... | collective-permute-start | bytes 1572872 | tf_op jit(solution)/shard_map/ppermute | solution.py:180
  12.3 13.1 %collective-permute-start.2 = (bf16[4,2,32,1024]{3,2,1,0:T(8,128)(2,1)S(1)}, bf16[4,2,32,1024]{3,2,1,0:T(8,128)(2,1)S(1)}, u32[]{:S(2)}, u32[]{:S(2)}) collective-permute-start(bf16[4,2,32,1024]{3,2,1,0:T(8,128)(2,1)S(1)} %bitcast.25), channel_id=1, source_target_pairs={{0,1},{1,0},{2,3},{3,2},{4,5},{5,4},{6,7},{7,6},{8,9},{9,8},{10,11... | collective-permute-start | bytes 1572872 | tf_op jit(solution)/shard_map/ppermute | solution.py:181
  13.8 11.6 %collective-permute-start.3 = (bf16[8,64,512]{2,1,0:T(8,128)(2,1)S(1)}, bf16[8,64,512]{2,1,0:T(8,128)(2,1)S(1)}, u32[]{:S(2)}, u32[]{:S(2)}) collective-permute-start(bf16[8,64,512]{2,1,0:T(8,128)(2,1)S(1)} %spectra.1), channel_id=1, source_target_pairs={{0,8},{8,0},{16,24},{24,16},{1,9},{9,1},{17,25},{25,17},{2,10},{10... | collective-permute-start | bytes 1572872 | tf_op jit(solution)/shard_map/ppermute | solution.py:185
  19.9 9.9 %collective-permute-start.5 = (bf16[8,64,512]{2,1,0:T(8,128)(2,1)}, bf16[8,64,512]{2,1,0:T(8,128)(2,1)}, u32[]{:S(2)}, u32[]{:S(2)}) collective-permute-start(bf16[8,64,512]{2,1,0:T(8,128)(2,1)} %collective-permute-done.4), channel_id=1, source_target_pairs={{0,8},{8,0},{16,24},{24,16},{1,9},{9,1},{17,25},{25,17},{2,10},{10... | collective-permute-start | bytes 1572872 | tf_op jit(solution)/shard_map/ppermute | solution.py:192
  25.4 0.8 %copy-start.2 = (bf16[8,64,512]{2,1,0:T(8,128)(2,1)}, bf16[8,64,512]{2,1,0:T(8,128)(2,1)S(1)}, u32[]{:S(2)}) copy-start(bf16[8,64,512]{2,1,0:T(8,128)(2,1)S(1)} %collective-permute-done.3) | copy-start | bytes 1572868
  26.2 16.1 %collective-permute-start.6 = (bf16[4,2,32,1024]{3,2,1,0:T(8,128)(2,1)S(1)}, bf16[4,2,32,1024]{3,2,1,0:T(8,128)(2,1)S(1)}, u32[]{:S(2)}, u32[]{:S(2)}) collective-permute-start(bf16[4,2,32,1024]{3,2,1,0:T(8,128)(2,1)S(1)} %collective-permute-done.refs_2_), channel_id=1, source_target_pairs={{2,4},{3,5},{4,2},{5,3},{10,12},{11,13},{12,10},{13,11},{18,20},{1... | collective-permute-start | bytes 1572872 | tf_op jit(solution)/shard_map/ppermute | solution.py:189
  26.9 15.5 %collective-permute-start.7 = (bf16[4,2,32,1024]{3,2,1,0:T(8,128)(2,1)S(1)}, bf16[4,2,32,1024]{3,2,1,0:T(8,128)(2,1)S(1)}, u32[]{:S(2)}, u32[]{:S(2)}) collective-permute-start(bf16[4,2,32,1024]{3,2,1,0:T(8,128)(2,1)S(1)} %collective-permute-done.refs_2_), channel_id=1, source_target_pairs={{0,1},{1,0},{2,3},{3,2},{4,5},{5,4},{6,7},{7,6},{8,9},{9,8},{10,11... | collective-permute-start | bytes 1572872 | tf_op jit(solution)/shard_map/ppermute | solution.py:190
  28.5 16.4 %collective-permute-start.8 = (bf16[4,2,32,1024]{3,2,1,0:T(8,128)(2,1)}, bf16[4,2,32,1024]{3,2,1,0:T(8,128)(2,1)}, u32[]{:S(2)}, u32[]{:S(2)}) collective-permute-start(bf16[4,2,32,1024]{3,2,1,0:T(8,128)(2,1)} %collective-permute-done.1.second_ref), channel_id=1, source_target_pairs={{2,0},{3,1},{4,6},{5,7},{10,8},{11,9},{12,14},{13,15},{18,16},{19,... | collective-permute-start | bytes 1572872 | tf_op jit(solution)/shard_map/ppermute | solution.py:188
  29.9 1.0 %copy-start.3 = (bf16[8,64,512]{2,1,0:T(8,128)(2,1)S(1)}, bf16[8,64,512]{2,1,0:T(8,128)(2,1)}, u32[]{:S(2)}) copy-start(bf16[8,64,512]{2,1,0:T(8,128)(2,1)} %copy-done.2) | copy-start | bytes 1572868
  39.2 3.2 %copy-start = (f32[4,2,4,64,1024]{4,3,2,1,0:T(8,128)}, f32[4,2,4,64,1024]{4,3,2,1,0:T(8,128)S(1)}, u32[]{:S(2)}) copy-start(f32[4,2,4,64,1024]{4,3,2,1,0:T(8,128)S(1)} %adjoint.1) | copy-start | bytes 25165828
  46.2 17.0 %collective-permute-start.9 = (bf16[4,2,32,1024]{3,2,1,0:T(8,128)(2,1)S(1)}, bf16[4,2,32,1024]{3,2,1,0:T(8,128)(2,1)}, u32[]{:S(2)}, u32[]{:S(2)}) collective-permute-start(bf16[4,2,32,1024]{3,2,1,0:T(8,128)(2,1)S(1)} %pick.1.refs_4_), channel_id=1, source_target_pairs={{0,1},{1,0},{2,3},{3,2},{4,5},{5,4},{6,7},{7,6},{8,9},{9,8},{10,11... | collective-permute-start | bytes 1572872 | tf_op jit(solution)/shard_map/ppermute | solution.py:208
  46.8 16.4 %collective-permute-start.10 = (bf16[4,2,32,1024]{3,2,1,0:T(8,128)(2,1)S(1)}, bf16[4,2,32,1024]{3,2,1,0:T(8,128)(2,1)}, u32[]{:S(2)}, u32[]{:S(2)}) collective-permute-start(bf16[4,2,32,1024]{3,2,1,0:T(8,128)(2,1)S(1)} %collective-permute-done.6.refs_2_), channel_id=1, source_target_pairs={{2,0},{3,1},{4,6},{5,7},{10,8},{11,9},{12,14},{13,15},{18,16},{19,... | collective-permute-start | bytes 1572872 | tf_op jit(solution)/shard_map/ppermute | solution.py:205
  48.1 15.1 %collective-permute-start.11 = (bf16[4,2,32,1024]{3,2,1,0:T(8,128)(2,1)S(1)}, bf16[4,2,32,1024]{3,2,1,0:T(8,128)(2,1)}, u32[]{:S(2)}, u32[]{:S(2)}) collective-permute-start(bf16[4,2,32,1024]{3,2,1,0:T(8,128)(2,1)S(1)} %collective-permute-done.7.refs_3_), channel_id=1, source_target_pairs={{2,4},{3,5},{4,2},{5,3},{10,12},{11,13},{12,10},{13,11},{18,20},{1... | collective-permute-start | bytes 1572872 | tf_op jit(solution)/shard_map/ppermute | solution.py:206
  49.6 16.6 %collective-permute-start.12 = (bf16[4,2,32,1024]{3,2,1,0:T(8,128)(2,1)}, bf16[4,2,32,1024]{3,2,1,0:T(8,128)(2,1)}, u32[]{:S(2)}, u32[]{:S(2)}) collective-permute-start(bf16[4,2,32,1024]{3,2,1,0:T(8,128)(2,1)} %block.1), channel_id=1, source_target_pairs={{0,2},{1,3},{6,4},{7,5},{8,10},{9,11},{14,12},{15,13},{16,18},{17,... | collective-permute-start | bytes 1572872 | tf_op jit(solution)/shard_map/ppermute | solution.py:204
  58.4 3.4 %copy-start.1 = (f32[4,2,4,64,1024]{4,3,2,1,0:T(8,128)S(1)}, f32[4,2,4,64,1024]{4,3,2,1,0:T(8,128)}, u32[]{:S(2)}) copy-start(f32[4,2,4,64,1024]{4,3,2,1,0:T(8,128)} %copy-done) | copy-start | bytes 25165828
  68.2 3.7 %collective-permute-start.13 = (f32[1024]{0:T(1024)S(1)}, f32[1024]{0:T(1024)S(1)}, u32[]{:S(2)}, u32[]{:S(2)}) collective-permute-start(f32[1024]{0:T(1024)S(1)} %bitcast.28), channel_id=1, source_target_pairs={{0,1},{1,0},{2,3},{3,2},{4,5},{5,4},{6,7},{7,6},{8,9},{9,8},{10,11... | collective-permute-start | bytes 12296 | tf_op jit(solution)/shard_map/ppermute | solution.py:230
  71.9 4.1 %collective-permute-start.14 = (f32[1024]{0:T(1024)S(1)}, f32[1024]{0:T(1024)S(1)}, u32[]{:S(2)}, u32[]{:S(2)}) collective-permute-start(f32[1024]{0:T(1024)S(1)} %add.47), channel_id=1, source_target_pairs={{0,2},{1,3},{2,0},{3,1},{4,6},{5,7},{6,4},{7,5},{8,10},{9,11},{10,... | collective-permute-start | bytes 12296 | tf_op jit(solution)/shard_map/ppermute | solution.py:230
  75.9 4.5 %collective-permute-start.15 = (f32[1024]{0:T(1024)S(1)}, f32[1024]{0:T(1024)S(1)}, u32[]{:S(2)}, u32[]{:S(2)}) collective-permute-start(f32[1024]{0:T(1024)S(1)} %add.48), channel_id=1, source_target_pairs={{0,4},{1,5},{2,6},{3,7},{4,0},{5,1},{6,2},{7,3},{8,12},{9,13},{10,... | collective-permute-start | bytes 12296 | tf_op jit(solution)/shard_map/ppermute | solution.py:230

commit v3 on v2

v3 whole, which is shorter than its diff:
```python
import functools

import jax
import jax.numpy as jnp
import numpy as np
from jax import lax
from jax.experimental import pallas as pl
from jax.experimental.pallas import tpu as pltpu
from jax.sharding import PartitionSpec as P

ROWS = 16


def spread_table(gate_count, freq_count):
    gates = np.arange(gate_count, dtype=np.float32)
    freqs = np.arange(freq_count, dtype=np.float32)
    phases = (
        np.float32(np.pi)
        * (np.float32(2) * gates[None, :] + np.float32(1))
        * (np.float32(1) + np.float32(3) * freqs[:, None])
        / np.float32(2 * gate_count)
    )
    scale = np.sqrt(np.float32(2.0 / gate_count))
    table = np.stack([np.cos(phases) * scale, -np.sin(phases) * scale], axis=1)
    table = table.reshape(2 * freq_count, gate_count).astype(jnp.bfloat16).astype(np.float32)
    return np.kron(table, np.eye(ROWS, dtype=np.float32)).astype(jnp.bfloat16)


def spectra_kernel(table_ref, active_ref, records_ref, out_ref, mask_ref):
    gates, rows, recv = records_ref.shape
    blocks = active_ref.shape[0]
    step = pl.program_id(0)

    @pl.when(step == 0)
    def _():
        block_of = lax.broadcasted_iota(jnp.int32, (blocks, recv), 1) // (recv // blocks)
        spread = (block_of == lax.broadcasted_iota(jnp.int32, (blocks, recv), 0)).astype(jnp.float32)
        mask_ref[...] = lax.dot_general(
            active_ref[...].astype(jnp.float32),
            spread,
            (((0,), (0,)), ((), ())),
            preferred_element_type=jnp.float32,
        )

    flat = records_ref[...].reshape(gates * rows, recv)
    sums = jnp.dot(table_ref[...], flat, preferred_element_type=jnp.float32)
    mask = mask_ref[pl.ds(pl.multiple_of(step * rows, rows), rows)]
    channels = out_ref.shape[0]
    out_ref[...] = (sums.reshape(channels, rows, recv) * mask[None]).astype(out_ref.dtype)


def in_hbm(array):
    return pltpu.with_memory_space_constraint(array, pltpu.HBM)


def spectra_of(records, active, freq_count):
    gates, trans, recv = records.shape
    blocks = active.shape[1]
    channels = 2 * freq_count
    table = jnp.asarray(spread_table(gates, freq_count))
    return pl.pallas_call(
        spectra_kernel,
        grid=(trans // ROWS,),
        in_specs=[
            pl.BlockSpec(table.shape, lambda i: (0, 0)),
            pl.BlockSpec((blocks, trans), lambda i: (0, 0)),
            pl.BlockSpec((gates, ROWS, recv), lambda i: (0, i, 0)),
        ],
        out_specs=pl.BlockSpec((channels, ROWS, recv), lambda i: (0, i, 0)),
        out_shape=jax.ShapeDtypeStruct((channels, trans, recv), jnp.bfloat16),
        scratch_shapes=[pltpu.VMEM((trans, recv), jnp.float32)],
        compiler_params=pltpu.CompilerParams(vmem_limit_bytes=16 << 20),
        cost_estimate=pl.CostEstimate(
            flops=2 * channels * ROWS * gates * trans * recv,
            bytes_accessed=2 * (gates + channels) * trans * recv,
            transcendentals=0,
        ),
        name="spectra",
    )(in_hbm(table), active.T, in_hbm(records))


def adjoint_kernel(count, *refs):
    spectra_refs, green_ref, out_ref = refs[:count], refs[count], refs[-1]
    rows = spectra_refs[0].shape[2]
    real = jnp.concatenate([ref[0, 0] for ref in spectra_refs], axis=0)
    imag = jnp.concatenate([ref[0, 1] for ref in spectra_refs], axis=0)
    left = jnp.concatenate(
        [jnp.concatenate([real, -imag], axis=1), jnp.concatenate([-imag, -real], axis=1)], axis=0
    )
    sums = jnp.dot(left, green_ref[0], preferred_element_type=jnp.float32)
    out_ref[0] = sums.reshape(2, count, rows, -1)


def adjoint_of(pieces, green, base=None, groups=None):
    freqs, _, recv, cells = green.shape
    rows = pieces[0].shape[1]
    pieces = [piece.reshape(freqs, 2, rows, recv) for piece in pieces]
    count = len(pieces)
    groups = groups or count
    place = 0 if base is None else 1
    shape = (freqs, 2, groups, rows, cells)
    bases = [] if base is None else [pltpu.with_memory_space_constraint(base, pltpu.VMEM)]
    return pl.pallas_call(
        functools.partial(adjoint_kernel, count),
        grid=(freqs,),
        in_specs=[pl.BlockSpec((1, 2, rows, recv), lambda f: (f, 0, 0, 0))] * count
        + [pl.BlockSpec((1, 2 * recv, cells), lambda f: (f, 0, 0))]
        + [pl.BlockSpec(memory_space=pl.ANY)] * len(bases),
        out_specs=pl.BlockSpec((1, 2, count, rows, cells), lambda f: (f, 0, place, 0, 0)),
        out_shape=pltpu.VMEM(shape, jnp.float32),
        input_output_aliases={count + 1: 0} if bases else {},
        compiler_params=pltpu.CompilerParams(vmem_limit_bytes=20 << 20),
        cost_estimate=pl.CostEstimate(
            flops=8 * freqs * count * rows * recv * cells,
            bytes_accessed=4 * freqs * recv * cells + 8 * freqs * count * rows * cells,
            transcendentals=0,
        ),
        name="adjoint",
    )(*pieces, in_hbm(green.reshape(freqs, 2 * recv, cells)), *bases)


def in_vmem(kernel, scalars, operands, shape, dtype, name):
    return pl.pallas_call(
        kernel,
        in_specs=[pl.BlockSpec(memory_space=pltpu.SMEM)]
        + [pl.BlockSpec(memory_space=pltpu.VMEM)] * len(operands),
        out_specs=pl.BlockSpec(memory_space=pltpu.VMEM),
        out_shape=pltpu.VMEM(shape, dtype),
        compiler_params=pltpu.CompilerParams(vmem_limit_bytes=16 << 20),
        cost_estimate=pl.CostEstimate(
            flops=4 * sum(operand.size for operand in operands[1:]),
            bytes_accessed=4 * sum(operand.size for operand in operands[1:]),
            transcendentals=0,
        ),
        name=name,
    )(scalars, *[pltpu.with_memory_space_constraint(operand, pltpu.VMEM) for operand in operands])


OWN, OWN_Y, NEAR, NEAR_Y, MID, MID_Y, FAR, FAR_Y, MIDDLE = range(9)


def weigh_kernel(terms, first, last, scalar_ref, adjoint_ref, *refs):
    refs, out_ref = list(refs[:-1]), refs[-1]
    sums = 0.0 if first else refs.pop()[...]
    freqs, parts, _, cells = refs[0].shape
    middle = scalar_ref[MIDDLE] != 0
    for number, choices in terms:
        block = scalar_ref[number]
        field_refs = [refs.pop(0) for _ in range(choices)]
        extra_ref = refs.pop(0) if number == FAR_Y else None
        for freq in range(freqs):
            for part in range(parts):
                weights = adjoint_ref[freq, part, block]
                if extra_ref is not None:
                    weights = weights + extra_ref[freq, part].astype(jnp.float32)
                field = field_refs[0][freq, part].astype(jnp.float32)
                if choices == 2:
                    other = field_refs[1][freq, part].astype(jnp.float32)
                    field = jnp.where(middle, other, field)
                sums = sums + jnp.sum((weights * field).reshape(-1, 8, cells), axis=0)
    out_ref[...] = jnp.sum(sums, axis=0, keepdims=True) if last else sums


def pick_kernel(scalar_ref, first_ref, second_ref, out_ref):
    @pl.when(scalar_ref[MIDDLE] == 0)
    def _():
        out_ref[...] = first_ref[...]

    @pl.when(scalar_ref[MIDDLE] != 0)
    def _():
        out_ref[...] = second_ref[...]


def block_kernel(scalar_ref, adjoint_ref, out_ref):
    out_ref[...] = adjoint_ref[:, :, scalar_ref[FAR_Y]].astype(out_ref.dtype)


def box_shards(records, active, green, background):
    freqs, _, _, cells = green.shape
    along_y = [(r, r ^ 1) for r in range(8)]
    z_pairs = [(r, r ^ 2) for r in range(8)]
    z_middle = [(r, r ^ 6) for r in range(2, 6)]
    z_outward = [(2, 0), (3, 1), (4, 6), (5, 7)]
    z_inward = [(there, here) for here, there in z_outward]
    core = [(t, t ^ 1) for t in range(4)]
    along_x = [(t, t ^ 2) for t in range(4)]
    send, tie = lax.ppermute, lax.optimization_barrier

    me_tx, me_rx = lax.axis_index("tx"), lax.axis_index("rx")
    me_z, me_y = me_rx // 2, me_rx % 2
    lower = me_z < 2
    mid_z, far_z = jnp.where(lower, 2, 1), jnp.where(lower, 3, 0)
    scalars = jnp.stack(
        [(z ^ me_tx) * 2 + y for z in (me_z, me_z ^ 1, mid_z, far_z) for y in (me_y, 1 - me_y)]
        + [(me_z == 1) | (me_z == 2)]
    ).astype(jnp.int32)

    own = background.transpose(1, 2, 0, 3)
    own, scalars, records = tie((own, scalars, records))
    near = send(own, "rx", z_pairs)
    across = send(own, "rx", z_middle)
    own_y = send(own, "rx", along_y)

    spectra = spectra_of(records, active, freqs)
    spectra_x = send(spectra, "tx", along_x)
    spectra_core = send(spectra, "tx", core)

    near, across, own_y, spectra_core = tie((near, across, own_y, spectra_core))
    across_out = send(across, "rx", z_outward)
    far = send(near, "rx", z_middle)
    near_y = send(near, "rx", along_y)

    adjoint = adjoint_of([spectra, spectra_core], green, groups=4)
    spectra_x, adjoint = tie((spectra_x, adjoint))
    spectra_both = send(spectra_x, "tx", core)
    adjoint = adjoint_of([spectra_x, spectra_both], green, adjoint, groups=4)
    adjoint = adjoint.reshape((freqs, 2, 8) + own.shape[2:])

    partial = in_vmem(block_kernel, scalars, [adjoint], own.shape, own.dtype, "block")
    partial, far, near_y, across_out = tie((partial, far, near_y, across_out))
    partial = send(partial, "rx", z_inward)
    far_out = send(far, "rx", z_outward)
    far_both = send(near_y, "rx", z_middle)
    mid = in_vmem(pick_kernel, scalars, [across_out, across], own.shape, own.dtype, "pick")
    mid_y = send(mid, "rx", along_y)

    sums = in_vmem(
        functools.partial(weigh_kernel, ((OWN, 1), (OWN_Y, 1), (NEAR, 1), (NEAR_Y, 1), (MID, 1)), True, False),
        scalars,
        [adjoint, own, own_y, near, near_y, mid],
        (8, cells),
        jnp.float32,
        "weigh",
    )
    sums = in_vmem(
        functools.partial(weigh_kernel, ((MID_Y, 1), (FAR, 2), (FAR_Y, 1)), False, True),
        scalars,
        [adjoint, mid_y, far_out, far, far_both, partial, sums],
        (1, cells),
        jnp.float32,
        "weigh",
    )
    sums = sums.reshape(cells)
    for bit in (1, 2, 4):
        sums = sums + send(sums, "rx", [(r, r ^ bit) for r in range(8)])
    return sums


def plain_shards(records, active, green, background):
    freqs = green.shape[0]
    spectra = spectra_of(records, active, freqs)
    pieces = lax.all_gather(spectra, "tx", axis=0)
    adjoint = adjoint_of([pieces[t] for t in range(pieces.shape[0])], green)
    freqs, _, groups, rows, cells = adjoint.shape
    adjoint = adjoint.reshape(freqs, 2, groups * rows, cells)
    fields = lax.all_gather(background, "rx", axis=0, tiled=True)
    fields = fields.transpose(1, 2, 0, 3).astype(jnp.float32)
    return lax.psum(jnp.sum(adjoint * fields, axis=(0, 1, 2)), "rx")


def solution(mesh):
    placed = (
        P(None, "tx", "rx"),
        P("tx", "rx"),
        P(None, None, "rx", "tx"),
        P("rx", None, None, "tx"),
    )
    body = box_shards if (mesh.shape["tx"], mesh.shape["rx"]) == (4, 8) else plain_shards
    return jax.shard_map(body, mesh=mesh, in_specs=placed, out_specs=P("tx"), check_vma=False)
```

time: 81.6 us -> 81.5 us (level)
  waiting for transfers between devices: 23.3 us -> 33.9 us
  local copies, waits for them, and re-layouts: 11.6 us -> 2.11 us
  starting transfers between devices: 29.3 us -> 25.9 us
  Pallas kernels: 16 us -> 18.5 us
    unnamed x12 -> x3, local copies, waits for them, and re-layouts: 11.5 us -> 2.02 us
    ppermute x1, waiting for transfers between devices: 0.01 us -> 6.01 us  [box_shards(): near_y = send(near, 'rx', along_y)]
    ppermute x1, waiting for transfers between devices: 6.05 us -> 0.92 us  [box_shards(): spectra_x = send(spectra, 'tx', along_x)]
    pallas_call x1 -> x2, Pallas kernels: 7.33 us -> 11.4 us  [adjoint_of(): pl.pallas_call(functools.partial(adjoint_kernel, count), grid=(freqs,), i...]
    ppermute x1, waiting for transfers between devices: 0.01 us -> 3.34 us  [box_shards(): far_out = send(far, 'rx', z_outward)]
    ppermute x1, waiting for transfers between devices: 2.56 us -> 5.34 us  [box_shards(): across_out = send(across, 'rx', z_outward)]
    pallas_call x4, Pallas kernels: 5.51 us -> 3.72 us  [in_vmem(): pl.pallas_call(kernel, in_specs=[pl.BlockSpec(memory_space=pltpu.SMEM)] +...]
    ppermute x1, starting transfers between devices: 3 us -> 1.56 us  [box_shards(): spectra_x = send(spectra, 'tx', along_x)]
  transfers between devices with their start and end apart: 16 -> 16, of which waited for: 8 -> 11; matrix products, arithmetic and copies ran while one was open for 2% -> 0% of each run, Pallas kernels for 12% -> 21%
where the time goes in v3:
time: 81.5 us; the launch traced here: 81.1 us
  waiting for transfers between devices  33.9 us (42%)
  starting transfers between devices  25.9 us (32%)
  Pallas kernels  18.5 us (23%)
  local copies, waits for them, and re-layouts  2.11 us (3%)
    pallas_call x2, Pallas kernels, adjoint_of(): pl.pallas_call(functools.partial(adjoint_kernel, count), grid=(freqs,), i...  11.4 us
    ppermute x1, starting transfers between devices, box_shards(): partial = send(partial, 'rx', z_inward)  7.56 us
    ppermute x3, waiting for transfers between devices, box_shards(): sums = sums + send(sums, 'rx', [(r, r ^ bit) for r in range(8)])  7.12 us
    ppermute x1, waiting for transfers between devices, box_shards(): near_y = send(near, 'rx', along_y)  6.01 us
    ppermute x1, waiting for transfers between devices, box_shards(): across_out = send(across, 'rx', z_outward)  5.34 us
    ppermute x3, starting transfers between devices, box_shards(): sums = sums + send(sums, 'rx', [(r, r ^ bit) for r in range(8)])  5.12 us
    ppermute x1, waiting for transfers between devices, box_shards(): partial = send(partial, 'rx', z_inward)  4.26 us
    ppermute x1, waiting for transfers between devices, box_shards(): near = send(own, 'rx', z_pairs)  3.96 us
  transfers between devices with their start and end apart: 16, of which 11 were waited for; matrix products, arithmetic and copies ran while one was open for 0% of the time, Pallas kernels for 21%

profile of v3, /device:TPU:0, one launch (start us, length us, event | category | flops | bytes accessed | tf_op | source)
XLA Modules:
  0.0 81.1 jit_solution(9108425020048431598)
XLA Ops:
  0.0 1.3 %copy.9 = bf16[32,4,2,1024]{3,0,2,1:T(8,128)(2,1)S(1)} copy(bf16[32,4,2,1024]{3,2,1,0:T(2,128)(2,1)} %param.8) | data formatting | bytes 1048576 | tf_op args[3]
  1.3 0.1 stack.43.scalar_ref
  1.4 3.0 %collective-permute-start.1 = (bf16[4,2,32,1024]{3,2,1,0:T(8,128)(2,1)S(1)}, bf16[4,2,32,1024]{3,2,1,0:T(8,128)(2,1)S(1)}, u32[]{:S(2)}, u32[]{:S(2)}) collective-permute-start(bf16[4,2,32,1024]{3,2,1,0:T(8,128)(2,1)S(1)} %bitcast.24), channel_id=1, source_target_pairs={{0,2},{1,3},{2,0},{3,1},{4,6},{5,7},{6,4},{7,5},{8,10},{9,11},{10,... | collective-permute-start | bytes 1572872 | tf_op jit(solution)/shard_map/ppermute | solution.py:200
  4.5 0.7 collective-permute-start.2
  5.2 1.6 %collective-permute-start.3 = (bf16[4,2,32,1024]{3,2,1,0:T(8,128)(2,1)S(1)}, bf16[4,2,32,1024]{3,2,1,0:T(8,128)(2,1)S(1)}, u32[]{:S(2)}, u32[]{:S(2)}) collective-permute-start(bf16[4,2,32,1024]{3,2,1,0:T(8,128)(2,1)S(1)} %bitcast.26), channel_id=1, source_target_pairs={{0,1},{1,0},{2,3},{3,2},{4,5},{5,4},{6,7},{7,6},{8,9},{9,8},{10,11... | collective-permute-start | bytes 1572872 | tf_op jit(solution)/shard_map/ppermute | solution.py:202
  6.7 0.0 copy-start
  6.7 0.7 copy-done
  7.4 3.4 %spectra.1 = bf16[8,64,512]{2,1,0:T(8,128)(2,1)S(1)} custom-call(bf16[128,640]{1,0:T(8,128)(2,1)} %constant.38.clone.table_ref, s32[8,64]{1,0:T(8,128)S(1)} %bitcast.33, bf16[40,64,512]{2,1,0:T(8,128)(2,1)} %records_ref), custom_call_target="tpu_custom_call" | custom-call | flops 335544320 | bytes 3145728 | tf_op jit(solution)/shard_map/spectra/pallas_call | solution.py:61
  10.8 0.1 collective-permute-start.4
  10.9 1.6 %collective-permute-start = (bf16[8,64,512]{2,1,0:T(8,128)(2,1)S(1)}, bf16[8,64,512]{2,1,0:T(8,128)(2,1)S(1)}, u32[]{:S(2)}, u32[]{:S(2)}) collective-permute-start(bf16[8,64,512]{2,1,0:T(8,128)(2,1)S(1)} %spectra.1), channel_id=1, source_target_pairs={{0,16},{8,24},{16,0},{24,8},{1,17},{9,25},{17,1},{25,9},{2,18},{10... | collective-permute-start | bytes 1572872 | tf_op jit(solution)/shard_map/ppermute | solution.py:205
  12.4 4.0 %collective-permute-done.1.refs_2_ = bf16[4,2,32,1024]{3,2,1,0:T(8,128)(2,1)S(1)} collective-permute-done((bf16[4,2,32,1024]{3,2,1,0:T(8,128)(2,1)S(1)}, bf16[4,2,32,1024]{3,2,1,0:T(8,128)(2,1)S(1)}, u32[]{:S(2)}, u32[]{:S(2)}) %collective-permute-start.1) | collective-permute-done | bytes 524320 | tf_op jit(solution)/shard_map/ppermute | solution.py:200
  16.4 0.0 collective-permute-done.2.second_ref
  16.4 2.2 %collective-permute-done.3.refs_1_ = bf16[4,2,32,1024]{3,2,1,0:T(8,128)(2,1)S(1)} collective-permute-done((bf16[4,2,32,1024]{3,2,1,0:T(8,128)(2,1)S(1)}, bf16[4,2,32,1024]{3,2,1,0:T(8,128)(2,1)S(1)}, u32[]{:S(2)}, u32[]{:S(2)}) %collective-permute-start.3) | collective-permute-done | bytes 524320 | tf_op jit(solution)/shard_map/ppermute | solution.py:202
  18.6 0.0 collective-permute-done.4
  18.6 5.7 %adjoint.2.refs_3_ = f32[4,2,4,64,1024]{4,3,2,1,0:T(8,128)S(1)} custom-call(bf16[4,2,64,512]{3,2,1,0:T(8,128)(2,1)S(1)} %bitcast.23, bf16[4,2,64,512]{3,2,1,0:T(8,128)(2,1)S(1)} %bitcast.30, bf16[4,1024,1024]{2,1,0:T(8,128)(2,1)} %bitcast.34), custom_call_target="tpu_custom_call" | custom-call | flops 2147483648 | bytes 12582912 | tf_op jit(solution)/shard_map/adjoint/pallas_call | solution.py:103
  24.3 0.9 %collective-permute-done = bf16[8,64,512]{2,1,0:T(8,128)(2,1)S(1)} collective-permute-done((bf16[8,64,512]{2,1,0:T(8,128)(2,1)S(1)}, bf16[8,64,512]{2,1,0:T(8,128)(2,1)S(1)}, u32[]{:S(2)}, u32[]{:S(2)}) %collective-permute-start) | collective-permute-done | bytes 524320 | tf_op jit(solution)/shard_map/ppermute | solution.py:205
  25.2 0.0 collective-permute-start.5
  25.2 0.7 collective-permute-start.6
  25.9 0.8 collective-permute-start.7
  26.7 1.3 %collective-permute-start.8 = (bf16[4,2,32,1024]{3,2,1,0:T(8,128)(2,1)S(1)}, bf16[4,2,32,1024]{3,2,1,0:T(8,128)(2,1)S(1)}, u32[]{:S(2)}, u32[]{:S(2)}) collective-permute-start(bf16[4,2,32,1024]{3,2,1,0:T(8,128)(2,1)S(1)} %collective-permute-done.2.second_ref), channel_id=1, source_target_pairs={{2,0},{3,1},{4,6},{5,7},{10,8},{11,9},{12,14},{13,15},{18,16},{19,... | collective-permute-start | bytes 1572872 | tf_op jit(solution)/shard_map/ppermute | solution.py:209
  27.9 0.0 collective-permute-done.5
  28.0 5.7 %adjoint.3 = f32[4,2,4,64,1024]{4,3,2,1,0:T(8,128)S(1)} custom-call(bf16[4,2,64,512]{3,2,1,0:T(8,128)(2,1)S(1)} %bitcast.28, bf16[4,2,64,512]{3,2,1,0:T(8,128)(2,1)S(1)} %bitcast.29, bf16[4,1024,1024]{2,1,0:T(8,128)(2,1)} %bitcast.35, f32[4,2,4,64,1024]{4,3,2,1,0:T(8,128)S(1)} %adjoint.2.refs_3_), custom_call_target="tpu_custom_call", output_to_operand_aliasing={{}: (3, {})} | custom-call | flops 2147483648 | bytes 12582912 | tf_op jit(solution)/shard_map/adjoint/pallas_call | solution.py:103
  33.7 0.6 block.1
  34.3 0.0 collective-permute-done.6.refs_2_
  34.3 6.0 %collective-permute-done.7.refs_3_ = bf16[4,2,32,1024]{3,2,1,0:T(8,128)(2,1)S(1)} collective-permute-done((bf16[4,2,32,1024]{3,2,1,0:T(8,128)(2,1)S(1)}, bf16[4,2,32,1024]{3,2,1,0:T(8,128)(2,1)S(1)}, u32[]{:S(2)}, u32[]{:S(2)}) %collective-permute-start.7) | collective-permute-done | bytes 524320 | tf_op jit(solution)/shard_map/ppermute | solution.py:211
  40.3 5.3 %collective-permute-done.8.first_ref = bf16[4,2,32,1024]{3,2,1,0:T(8,128)(2,1)S(1)} collective-permute-done((bf16[4,2,32,1024]{3,2,1,0:T(8,128)(2,1)S(1)}, bf16[4,2,32,1024]{3,2,1,0:T(8,128)(2,1)S(1)}, u32[]{:S(2)}, u32[]{:S(2)}) %collective-permute-start.8) | collective-permute-done | bytes 524320 | tf_op jit(solution)/shard_map/ppermute | solution.py:209
  45.6 0.6 pick.1.refs_4_
  46.2 1.6 %collective-permute-start.9 = (bf16[4,2,32,1024]{3,2,1,0:T(8,128)(2,1)S(1)}, bf16[4,2,32,1024]{3,2,1,0:T(8,128)(2,1)S(1)}, u32[]{:S(2)}, u32[]{:S(2)}) collective-permute-start(bf16[4,2,32,1024]{3,2,1,0:T(8,128)(2,1)S(1)} %pick.1.refs_4_), channel_id=1, source_target_pairs={{0,1},{1,0},{2,3},{3,2},{4,5},{5,4},{6,7},{7,6},{8,9},{9,8},{10,11... | collective-permute-start | bytes 1572872 | tf_op jit(solution)/shard_map/ppermute | solution.py:225
  47.8 1.3 %collective-permute-start.10 = (bf16[4,2,32,1024]{3,2,1,0:T(8,128)(2,1)S(1)}, bf16[4,2,32,1024]{3,2,1,0:T(8,128)(2,1)S(1)}, u32[]{:S(2)}, u32[]{:S(2)}) collective-permute-start(bf16[4,2,32,1024]{3,2,1,0:T(8,128)(2,1)S(1)} %collective-permute-done.6.refs_2_), channel_id=1, source_target_pairs={{2,0},{3,1},{4,6},{5,7},{10,8},{11,9},{12,14},{13,15},{18,16},{19,... | collective-permute-start | bytes 1572872 | tf_op jit(solution)/shard_map/ppermute | solution.py:222
  49.1 0.7 collective-permute-start.11
  49.8 7.6 %collective-permute-start.12 = (bf16[4,2,32,1024]{3,2,1,0:T(8,128)(2,1)S(1)}, bf16[4,2,32,1024]{3,2,1,0:T(8,128)(2,1)S(1)}, u32[]{:S(2)}, u32[]{:S(2)}) collective-permute-start(bf16[4,2,32,1024]{3,2,1,0:T(8,128)(2,1)S(1)} %block.1), channel_id=1, source_target_pairs={{0,2},{1,3},{6,4},{7,5},{8,10},{9,11},{14,12},{15,13},{16,18},{17,... | collective-permute-start | bytes 1572872 | tf_op jit(solution)/shard_map/ppermute | solution.py:221
  57.4 1.5 %weigh.2.refs_5_ = f32[8,1024]{1,0:T(8,128)S(1)} custom-call(s32[9]{0:T(128)S(1)} %stack.43.scalar_ref, f32[4,2,8,32,1024]{4,3,2,1,0:T(8,128)S(1)} %bitcast.21, bf16[4,2,32,1024]{3,2,1,0:T(8,128)(2,1)S(1)} %bitcast.27, bf16[4,2,32,1024]{3,2,1,0:T(8,128)(2,1)S(1)} %collective-permute-done.3.refs_1_, ...), custom_call_target="tpu_custom_call" | custom-call | flops 5242880 | bytes 5242880 | tf_op jit(solution)/shard_map/weigh/pallas_call | solution.py:123
  58.9 0.8 collective-permute-done.9.refs_0_
  59.6 3.3 %collective-permute-done.10.refs_1_ = bf16[4,2,32,1024]{3,2,1,0:T(8,128)(2,1)S(1)} collective-permute-done((bf16[4,2,32,1024]{3,2,1,0:T(8,128)(2,1)S(1)}, bf16[4,2,32,1024]{3,2,1,0:T(8,128)(2,1)S(1)}, u32[]{:S(2)}, u32[]{:S(2)}) %collective-permute-start.10) | collective-permute-done | bytes 524320 | tf_op jit(solution)/shard_map/ppermute | solution.py:222
  63.0 0.0 collective-permute-done.11.refs_3_
  63.0 4.3 %collective-permute-done.12.refs_4_ = bf16[4,2,32,1024]{3,2,1,0:T(8,128)(2,1)S(1)} collective-permute-done((bf16[4,2,32,1024]{3,2,1,0:T(8,128)(2,1)S(1)}, bf16[4,2,32,1024]{3,2,1,0:T(8,128)(2,1)S(1)}, u32[]{:S(2)}, u32[]{:S(2)}) %collective-permute-start.12) | collective-permute-done | bytes 524320 | tf_op jit(solution)/shard_map/ppermute | solution.py:221
  67.2 1.0 %weigh.3 = f32[1,1024]{1,0:T(1,128)S(1)} custom-call(s32[9]{0:T(128)S(1)} %stack.43.scalar_ref, f32[4,2,8,32,1024]{4,3,2,1,0:T(8,128)S(1)} %bitcast.22, bf16[4,2,32,1024]{3,2,1,0:T(8,128)(2,1)S(1)} %collective-permute-done.9.refs_0_, bf16[4,2,32,1024]{3,2,1,0:T(8,128)(2,1)S(1)} %collective-permute-done.10.refs_1_, ...), custom_call_target="tpu_custom_call" | custom-call | flops 5275648 | bytes 5275648 | tf_op jit(solution)/shard_map/weigh/pallas_call | solution.py:123
  68.3 0.6 collective-permute-start.13
  68.8 3.1 %collective-permute-done.13 = f32[1024]{0:T(1024)S(1)} collective-permute-done((f32[1024]{0:T(1024)S(1)}, f32[1024]{0:T(1024)S(1)}, u32[]{:S(2)}, u32[]{:S(2)}) %collective-permute-start.13) | collective-permute-done | bytes 4128 | tf_op jit(solution)/shard_map/ppermute | solution.py:245
  72.0 2.5 %collective-permute-start.14 = (f32[1024]{0:T(1024)S(1)}, f32[1024]{0:T(1024)S(1)}, u32[]{:S(2)}, u32[]{:S(2)}) collective-permute-start(f32[1024]{0:T(1024)S(1)} %add.47), channel_id=1, source_target_pairs={{0,2},{1,3},{2,0},{3,1},{4,6},{5,7},{6,4},{7,5},{8,10},{9,11},{10,... | collective-permute-start | bytes 12296 | tf_op jit(solution)/shard_map/ppermute | solution.py:245
  74.4 1.6 %collective-permute-done.14 = f32[1024]{0:T(1024)S(1)} collective-permute-done((f32[1024]{0:T(1024)S(1)}, f32[1024]{0:T(1024)S(1)}, u32[]{:S(2)}, u32[]{:S(2)}) %collective-permute-start.14) | collective-permute-done | bytes 4128 | tf_op jit(solution)/shard_map/ppermute | solution.py:245
  76.0 2.1 %collective-permute-start.15 = (f32[1024]{0:T(1024)S(1)}, f32[1024]{0:T(1024)S(1)}, u32[]{:S(2)}, u32[]{:S(2)}) collective-permute-start(f32[1024]{0:T(1024)S(1)} %add.48), channel_id=1, source_target_pairs={{0,4},{1,5},{2,6},{3,7},{4,0},{5,1},{6,2},{7,3},{8,12},{9,13},{10,... | collective-permute-start | bytes 12296 | tf_op jit(solution)/shard_map/ppermute | solution.py:245
  78.1 2.4 %collective-permute-done.15 = f32[1024]{0:T(1024)S(1)} collective-permute-done((f32[1024]{0:T(1024)S(1)}, f32[1024]{0:T(1024)S(1)}, u32[]{:S(2)}, u32[]{:S(2)}) %collective-permute-start.15) | collective-permute-done | bytes 4128 | tf_op jit(solution)/shard_map/ppermute | solution.py:245
  80.5 0.6 add.49
  (2 shorter events, 0.0 us)
Async XLA Ops:
  1.4 15.0 %collective-permute-start.1 = (bf16[4,2,32,1024]{3,2,1,0:T(8,128)(2,1)S(1)}, bf16[4,2,32,1024]{3,2,1,0:T(8,128)(2,1)S(1)}, u32[]{:S(2)}, u32[]{:S(2)}) collective-permute-start(bf16[4,2,32,1024]{3,2,1,0:T(8,128)(2,1)S(1)} %bitcast.24), channel_id=1, source_target_pairs={{0,2},{1,3},{2,0},{3,1},{4,6},{5,7},{6,4},{7,5},{8,10},{9,11},{10,... | collective-permute-start | bytes 1572872 | tf_op jit(solution)/shard_map/ppermute | solution.py:200
  4.5 11.9 %collective-permute-start.2 = (bf16[4,2,32,1024]{3,2,1,0:T(8,128)(2,1)S(1)}, bf16[4,2,32,1024]{3,2,1,0:T(8,128)(2,1)S(1)}, u32[]{:S(2)}, u32[]{:S(2)}) collective-permute-start(bf16[4,2,32,1024]{3,2,1,0:T(8,128)(2,1)S(1)} %bitcast.25), channel_id=1, source_target_pairs={{2,4},{3,5},{4,2},{5,3},{10,12},{11,13},{12,10},{13,11},{18,20},{1... | collective-permute-start | bytes 1572872 | tf_op jit(solution)/shard_map/ppermute | solution.py:201
  5.2 13.4 %collective-permute-start.3 = (bf16[4,2,32,1024]{3,2,1,0:T(8,128)(2,1)S(1)}, bf16[4,2,32,1024]{3,2,1,0:T(8,128)(2,1)S(1)}, u32[]{:S(2)}, u32[]{:S(2)}) collective-permute-start(bf16[4,2,32,1024]{3,2,1,0:T(8,128)(2,1)S(1)} %bitcast.26), channel_id=1, source_target_pairs={{0,1},{1,0},{2,3},{3,2},{4,5},{5,4},{6,7},{7,6},{8,9},{9,8},{10,11... | collective-permute-start | bytes 1572872 | tf_op jit(solution)/shard_map/ppermute | solution.py:202
  6.7 0.7 copy-start
  10.8 7.8 %collective-permute-start.4 = (bf16[8,64,512]{2,1,0:T(8,128)(2,1)S(1)}, bf16[8,64,512]{2,1,0:T(8,128)(2,1)S(1)}, u32[]{:S(2)}, u32[]{:S(2)}) collective-permute-start(bf16[8,64,512]{2,1,0:T(8,128)(2,1)S(1)} %spectra.1), channel_id=1, source_target_pairs={{0,8},{8,0},{16,24},{24,16},{1,9},{9,1},{17,25},{25,17},{2,10},{10... | collective-permute-start | bytes 1572872 | tf_op jit(solution)/shard_map/ppermute | solution.py:206
  10.9 14.3 %collective-permute-start = (bf16[8,64,512]{2,1,0:T(8,128)(2,1)S(1)}, bf16[8,64,512]{2,1,0:T(8,128)(2,1)S(1)}, u32[]{:S(2)}, u32[]{:S(2)}) collective-permute-start(bf16[8,64,512]{2,1,0:T(8,128)(2,1)S(1)} %spectra.1), channel_id=1, source_target_pairs={{0,16},{8,24},{16,0},{24,8},{1,17},{9,25},{17,1},{25,9},{2,18},{10... | collective-permute-start | bytes 1572872 | tf_op jit(solution)/shard_map/ppermute | solution.py:205
  25.2 2.7 %collective-permute-start.5 = (bf16[8,64,512]{2,1,0:T(8,128)(2,1)S(1)}, bf16[8,64,512]{2,1,0:T(8,128)(2,1)S(1)}, u32[]{:S(2)}, u32[]{:S(2)}) collective-permute-start(bf16[8,64,512]{2,1,0:T(8,128)(2,1)S(1)} %collective-permute-done), channel_id=1, source_target_pairs={{0,8},{8,0},{16,24},{24,16},{1,9},{9,1},{17,25},{25,17},{2,10},{10... | collective-permute-start | bytes 1572872 | tf_op jit(solution)/shard_map/ppermute | solution.py:215
  25.2 9.1 %collective-permute-start.6 = (bf16[4,2,32,1024]{3,2,1,0:T(8,128)(2,1)S(1)}, bf16[4,2,32,1024]{3,2,1,0:T(8,128)(2,1)S(1)}, u32[]{:S(2)}, u32[]{:S(2)}) collective-permute-start(bf16[4,2,32,1024]{3,2,1,0:T(8,128)(2,1)S(1)} %collective-permute-done.1.refs_2_), channel_id=1, source_target_pairs={{2,4},{3,5},{4,2},{5,3},{10,12},{11,13},{12,10},{13,11},{18,20},{1... | collective-permute-start | bytes 1572872 | tf_op jit(solution)/shard_map/ppermute | solution.py:210
  25.9 14.4 %collective-permute-start.7 = (bf16[4,2,32,1024]{3,2,1,0:T(8,128)(2,1)S(1)}, bf16[4,2,32,1024]{3,2,1,0:T(8,128)(2,1)S(1)}, u32[]{:S(2)}, u32[]{:S(2)}) collective-permute-start(bf16[4,2,32,1024]{3,2,1,0:T(8,128)(2,1)S(1)} %collective-permute-done.1.refs_2_), channel_id=1, source_target_pairs={{0,1},{1,0},{2,3},{3,2},{4,5},{5,4},{6,7},{7,6},{8,9},{9,8},{10,11... | collective-permute-start | bytes 1572872 | tf_op jit(solution)/shard_map/ppermute | solution.py:211
  26.7 19.0 %collective-permute-start.8 = (bf16[4,2,32,1024]{3,2,1,0:T(8,128)(2,1)S(1)}, bf16[4,2,32,1024]{3,2,1,0:T(8,128)(2,1)S(1)}, u32[]{:S(2)}, u32[]{:S(2)}) collective-permute-start(bf16[4,2,32,1024]{3,2,1,0:T(8,128)(2,1)S(1)} %collective-permute-done.2.second_ref), channel_id=1, source_target_pairs={{2,0},{3,1},{4,6},{5,7},{10,8},{11,9},{12,14},{13,15},{18,16},{19,... | collective-permute-start | bytes 1572872 | tf_op jit(solution)/shard_map/ppermute | solution.py:209
  46.2 13.4 %collective-permute-start.9 = (bf16[4,2,32,1024]{3,2,1,0:T(8,128)(2,1)S(1)}, bf16[4,2,32,1024]{3,2,1,0:T(8,128)(2,1)S(1)}, u32[]{:S(2)}, u32[]{:S(2)}) collective-permute-start(bf16[4,2,32,1024]{3,2,1,0:T(8,128)(2,1)S(1)} %pick.1.refs_4_), channel_id=1, source_target_pairs={{0,1},{1,0},{2,3},{3,2},{4,5},{5,4},{6,7},{7,6},{8,9},{9,8},{10,11... | collective-permute-start | bytes 1572872 | tf_op jit(solution)/shard_map/ppermute | solution.py:225
  47.8 15.2 %collective-permute-start.10 = (bf16[4,2,32,1024]{3,2,1,0:T(8,128)(2,1)S(1)}, bf16[4,2,32,1024]{3,2,1,0:T(8,128)(2,1)S(1)}, u32[]{:S(2)}, u32[]{:S(2)}) collective-permute-start(bf16[4,2,32,1024]{3,2,1,0:T(8,128)(2,1)S(1)} %collective-permute-done.6.refs_2_), channel_id=1, source_target_pairs={{2,0},{3,1},{4,6},{5,7},{10,8},{11,9},{12,14},{13,15},{18,16},{19,... | collective-permute-start | bytes 1572872 | tf_op jit(solution)/shard_map/ppermute | solution.py:222
  49.1 13.9 %collective-permute-start.11 = (bf16[4,2,32,1024]{3,2,1,0:T(8,128)(2,1)S(1)}, bf16[4,2,32,1024]{3,2,1,0:T(8,128)(2,1)S(1)}, u32[]{:S(2)}, u32[]{:S(2)}) collective-permute-start(bf16[4,2,32,1024]{3,2,1,0:T(8,128)(2,1)S(1)} %collective-permute-done.7.refs_3_), channel_id=1, source_target_pairs={{2,4},{3,5},{4,2},{5,3},{10,12},{11,13},{12,10},{13,11},{18,20},{1... | collective-permute-start | bytes 1572872 | tf_op jit(solution)/shard_map/ppermute | solution.py:223
  49.8 17.4 %collective-permute-start.12 = (bf16[4,2,32,1024]{3,2,1,0:T(8,128)(2,1)S(1)}, bf16[4,2,32,1024]{3,2,1,0:T(8,128)(2,1)S(1)}, u32[]{:S(2)}, u32[]{:S(2)}) collective-permute-start(bf16[4,2,32,1024]{3,2,1,0:T(8,128)(2,1)S(1)} %block.1), channel_id=1, source_target_pairs={{0,2},{1,3},{6,4},{7,5},{8,10},{9,11},{14,12},{15,13},{16,18},{17,... | collective-permute-start | bytes 1572872 | tf_op jit(solution)/shard_map/ppermute | solution.py:221
  68.3 3.7 %collective-permute-start.13 = (f32[1024]{0:T(1024)S(1)}, f32[1024]{0:T(1024)S(1)}, u32[]{:S(2)}, u32[]{:S(2)}) collective-permute-start(f32[1024]{0:T(1024)S(1)} %bitcast.31), channel_id=1, source_target_pairs={{0,1},{1,0},{2,3},{3,2},{4,5},{5,4},{6,7},{7,6},{8,9},{9,8},{10,11... | collective-permute-start | bytes 12296 | tf_op jit(solution)/shard_map/ppermute | solution.py:245
  72.0 4.1 %collective-permute-start.14 = (f32[1024]{0:T(1024)S(1)}, f32[1024]{0:T(1024)S(1)}, u32[]{:S(2)}, u32[]{:S(2)}) collective-permute-start(f32[1024]{0:T(1024)S(1)} %add.47), channel_id=1, source_target_pairs={{0,2},{1,3},{2,0},{3,1},{4,6},{5,7},{6,4},{7,5},{8,10},{9,11},{10,... | collective-permute-start | bytes 12296 | tf_op jit(solution)/shard_map/ppermute | solution.py:245
  76.0 4.5 %collective-permute-start.15 = (f32[1024]{0:T(1024)S(1)}, f32[1024]{0:T(1024)S(1)}, u32[]{:S(2)}, u32[]{:S(2)}) collective-permute-start(f32[1024]{0:T(1024)S(1)} %add.48), channel_id=1, source_target_pairs={{0,4},{1,5},{2,6},{3,7},{4,0},{5,1},{6,2},{7,3},{8,12},{9,13},{10,... | collective-permute-start | bytes 12296 | tf_op jit(solution)/shard_map/ppermute | solution.py:245

commit v4 on v3

--- a/solution.py
+++ b/solution.py
@@ -76,7 +76,7 @@
             transcendentals=0,
         ),
         name="spectra",
-    )(in_hbm(table), active.T, in_hbm(records))
+    )(in_hbm(table), in_hbm(active.T), in_hbm(records))
 
 
 def adjoint_kernel(count, *refs):
@@ -197,27 +197,26 @@
 
     own = background.transpose(1, 2, 0, 3)
     own, scalars, records = tie((own, scalars, records))
+    spectra = spectra_of(records, active, freqs)
+    spectra_x = send(spectra, "tx", along_x)
+    spectra_core = send(spectra, "tx", core)
+
+    own, _ = tie((own, spectra))
     near = send(own, "rx", z_pairs)
     across = send(own, "rx", z_middle)
     own_y = send(own, "rx", along_y)
-
-    spectra = spectra_of(records, active, freqs)
-    spectra_x = send(spectra, "tx", along_x)
-    spectra_core = send(spectra, "tx", core)
-
-    near, across, own_y, spectra_core = tie((near, across, own_y, spectra_core))
+    adjoint = adjoint_of([spectra, spectra_core], green, groups=4)
+    near, across, own_y, adjoint, spectra_x = tie((near, across, own_y, adjoint, spectra_x))
+
+    spectra_both = send(spectra_x, "tx", core)
     across_out = send(across, "rx", z_outward)
     far = send(near, "rx", z_middle)
     near_y = send(near, "rx", along_y)
 
-    adjoint = adjoint_of([spectra, spectra_core], green, groups=4)
-    spectra_x, adjoint = tie((spectra_x, adjoint))
-    spectra_both = send(spectra_x, "tx", core)
     adjoint = adjoint_of([spectra_x, spectra_both], green, adjoint, groups=4)
     adjoint = adjoint.reshape((freqs, 2, 8) + own.shape[2:])
 
     partial = in_vmem(block_kernel, scalars, [adjoint], own.shape, own.dtype, "block")
-    partial, far, near_y, across_out = tie((partial, far, near_y, across_out))
     partial = send(partial, "rx", z_inward)
     far_out = send(far, "rx", z_outward)
     far_both = send(near_y, "rx", z_middle)

time: 81.5 us -> 73.6 us (0.903)
  waiting for transfers between devices: 33.9 us -> 29.2 us
  starting transfers between devices: 25.9 us -> 23.4 us
    ppermute x1, waiting for transfers between devices: 6.01 us -> 0.01 us  [box_shards(): near_y = send(near, 'rx', along_y)]
    ppermute x1, waiting for transfers between devices: 5.34 us -> 1.07 us  [box_shards(): across_out = send(across, 'rx', z_outward)]
    ppermute x1, waiting for transfers between devices: 0.76 us -> 4.32 us  [box_shards(): mid_y = send(mid, 'rx', along_y)]
    ppermute x3, starting transfers between devices: 5.12 us -> 2.28 us  [box_shards(): sums = sums + send(sums, 'rx', [(r, r ^ bit) for r in range(8)])]
    ppermute x3, waiting for transfers between devices: 7.12 us -> 9.51 us  [box_shards(): sums = sums + send(sums, 'rx', [(r, r ^ bit) for r in range(8)])]
    ppermute x1, waiting for transfers between devices: 2.21 us -> 0.23 us  [box_shards(): own_y = send(own, 'rx', along_y)]
    ppermute x1, starting transfers between devices: 3.03 us -> 4.43 us  [box_shards(): near = send(own, 'rx', z_pairs)]
    ppermute x1, starting transfers between devices: 7.56 us -> 6.27 us  [box_shards(): partial = send(partial, 'rx', z_inward)]
  transfers between devices with their start and end apart: 16 -> 16, of which waited for: 11 -> 10; matrix products, arithmetic and copies ran while one was open for 0% -> 0% of each run, Pallas kernels for 21% -> 19%
where the time goes in v4:
time: 73.6 us; the launch traced here: 73.2 us
  waiting for transfers between devices  29.2 us (40%)
  starting transfers between devices  23.4 us (32%)
  Pallas kernels  18.5 us (25%)
  local copies, waits for them, and re-layouts  1.42 us (2%)
    pallas_call x2, Pallas kernels, adjoint_of(): pl.pallas_call(functools.partial(adjoint_kernel, count), grid=(freqs,), i...  11.4 us
    ppermute x3, waiting for transfers between devices, box_shards(): sums = sums + send(sums, 'rx', [(r, r ^ bit) for r in range(8)])  9.51 us
    ppermute x1, starting transfers between devices, box_shards(): partial = send(partial, 'rx', z_inward)  6.27 us
    ppermute x1, waiting for transfers between devices, box_shards(): partial = send(partial, 'rx', z_inward)  5.22 us
    ppermute x1, waiting for transfers between devices, box_shards(): near = send(own, 'rx', z_pairs)  4.58 us
    ppermute x1, starting transfers between devices, box_shards(): near = send(own, 'rx', z_pairs)  4.43 us
    ppermute x1, waiting for transfers between devices, box_shards(): mid_y = send(mid, 'rx', along_y)  4.32 us
    pallas_call x4, Pallas kernels, in_vmem(): pl.pallas_call(kernel, in_specs=[pl.BlockSpec(memory_space=pltpu.SMEM)] +...  3.74 us
  transfers between devices with their start and end apart: 16, of which 10 were waited for; matrix products, arithmetic and copies ran while one was open for 0% of the time, Pallas kernels for 19%

profile of v4, /device:TPU:0, one launch (start us, length us, event | category | flops | bytes accessed | tf_op | source)
XLA Modules:
  0.0 73.2 jit_solution(14918121490924030619)
XLA Ops:
  0.0 1.3 %copy.9 = bf16[32,4,2,1024]{3,0,2,1:T(8,128)(2,1)S(1)} copy(bf16[32,4,2,1024]{3,2,1,0:T(2,128)(2,1)} %param.8) | data formatting | bytes 1048576 | tf_op args[3]
  1.3 0.1 stack.43.scalar_ref
  1.4 3.4 %spectra.1 = bf16[8,64,512]{2,1,0:T(8,128)(2,1)S(1)} custom-call(bf16[128,640]{1,0:T(8,128)(2,1)} %constant.38.clone.table_ref, s32[8,64]{1,0:T(8,128)} %bitcast.35, bf16[40,64,512]{2,1,0:T(8,128)(2,1)} %records_ref), custom_call_target="tpu_custom_call" | custom-call | flops 335544320 | bytes 3145728 | tf_op jit(solution)/shard_map/spectra/pallas_call | solution.py:61
  4.8 0.5 collective-permute-start.3
  5.3 2.6 %collective-permute-start.2 = (bf16[4,2,32,1024]{3,2,1,0:T(8,128)(2,1)S(1)}, bf16[4,2,32,1024]{3,2,1,0:T(8,128)(2,1)S(1)}, u32[]{:S(2)}, u32[]{:S(2)}) collective-permute-start(bf16[4,2,32,1024]{3,2,1,0:T(8,128)(2,1)S(1)} %bitcast.24), channel_id=1, source_target_pairs={{0,1},{1,0},{2,3},{3,2},{4,5},{5,4},{6,7},{7,6},{8,9},{9,8},{10,11... | collective-permute-start | bytes 1572872 | tf_op jit(solution)/shard_map/ppermute | solution.py:207
  7.9 0.7 collective-permute-start.1
  8.6 4.4 %collective-permute-start = (bf16[4,2,32,1024]{3,2,1,0:T(8,128)(2,1)S(1)}, bf16[4,2,32,1024]{3,2,1,0:T(8,128)(2,1)S(1)}, u32[]{:S(2)}, u32[]{:S(2)}) collective-permute-start(bf16[4,2,32,1024]{3,2,1,0:T(8,128)(2,1)S(1)} %bitcast.26), channel_id=1, source_target_pairs={{0,2},{1,3},{2,0},{3,1},{4,6},{5,7},{6,4},{7,5},{8,10},{9,11},{10,... | collective-permute-start | bytes 1572872 | tf_op jit(solution)/shard_map/ppermute | solution.py:205
  13.0 1.5 %collective-permute-start.4 = (bf16[8,64,512]{2,1,0:T(8,128)(2,1)S(1)}, bf16[8,64,512]{2,1,0:T(8,128)(2,1)S(1)}, u32[]{:S(2)}, u32[]{:S(2)}) collective-permute-start(bf16[8,64,512]{2,1,0:T(8,128)(2,1)S(1)} %spectra.1), channel_id=1, source_target_pairs={{0,16},{8,24},{16,0},{24,8},{1,17},{9,25},{17,1},{25,9},{2,18},{10... | collective-permute-start | bytes 1572872 | tf_op jit(solution)/shard_map/ppermute | solution.py:201
  14.5 0.0 collective-permute-done.3
  14.5 5.7 %adjoint.2.refs_3_ = f32[4,2,4,64,1024]{4,3,2,1,0:T(8,128)S(1)} custom-call(bf16[4,2,64,512]{3,2,1,0:T(8,128)(2,1)S(1)} %bitcast.23, bf16[4,2,64,512]{3,2,1,0:T(8,128)(2,1)S(1)} %bitcast.29, bf16[4,1024,1024]{2,1,0:T(8,128)(2,1)} %bitcast.33), custom_call_target="tpu_custom_call" | custom-call | flops 2147483648 | bytes 12582912 | tf_op jit(solution)/shard_map/adjoint/pallas_call | solution.py:103
  20.2 0.2 collective-permute-done.2.refs_1_
  20.4 0.0 collective-permute-done.1.second_ref
  20.4 4.6 %collective-permute-done.refs_2_ = bf16[4,2,32,1024]{3,2,1,0:T(8,128)(2,1)S(1)} collective-permute-done((bf16[4,2,32,1024]{3,2,1,0:T(8,128)(2,1)S(1)}, bf16[4,2,32,1024]{3,2,1,0:T(8,128)(2,1)S(1)}, u32[]{:S(2)}, u32[]{:S(2)}) %collective-permute-start) | collective-permute-done | bytes 524320 | tf_op jit(solution)/shard_map/ppermute | solution.py:205
  25.0 1.5 %collective-permute-done.4 = bf16[8,64,512]{2,1,0:T(8,128)(2,1)S(1)} collective-permute-done((bf16[8,64,512]{2,1,0:T(8,128)(2,1)S(1)}, bf16[8,64,512]{2,1,0:T(8,128)(2,1)S(1)}, u32[]{:S(2)}, u32[]{:S(2)}) %collective-permute-start.4) | collective-permute-done | bytes 524320 | tf_op jit(solution)/shard_map/ppermute | solution.py:201
  26.5 0.0 collective-permute-start.5
  26.5 1.3 %collective-permute-start.6 = (bf16[4,2,32,1024]{3,2,1,0:T(8,128)(2,1)S(1)}, bf16[4,2,32,1024]{3,2,1,0:T(8,128)(2,1)S(1)}, u32[]{:S(2)}, u32[]{:S(2)}) collective-permute-start(bf16[4,2,32,1024]{3,2,1,0:T(8,128)(2,1)S(1)} %collective-permute-done.1.second_ref), channel_id=1, source_target_pairs={{2,0},{3,1},{4,6},{5,7},{10,8},{11,9},{12,14},{13,15},{18,16},{19,... | collective-permute-start | bytes 1572872 | tf_op jit(solution)/shard_map/ppermute | solution.py:212
  27.8 0.6 collective-permute-start.10
  28.3 0.7 collective-permute-start.8
  29.0 0.0 collective-permute-done.5
  29.0 5.7 %adjoint.3 = f32[4,2,4,64,1024]{4,3,2,1,0:T(8,128)S(1)} custom-call(bf16[4,2,64,512]{3,2,1,0:T(8,128)(2,1)S(1)} %bitcast.28, bf16[4,2,64,512]{3,2,1,0:T(8,128)(2,1)S(1)} %bitcast.30, bf16[4,1024,1024]{2,1,0:T(8,128)(2,1)} %bitcast.34, f32[4,2,4,64,1024]{4,3,2,1,0:T(8,128)S(1)} %adjoint.2.refs_3_), custom_call_target="tpu_custom_call", output_to_operand_aliasing={{}: (3, {})} | custom-call | flops 2147483648 | bytes 12582912 | tf_op jit(solution)/shard_map/adjoint/pallas_call | solution.py:103
  34.7 0.6 block.1
  35.4 6.3 %collective-permute-start.12 = (bf16[4,2,32,1024]{3,2,1,0:T(8,128)(2,1)S(1)}, bf16[4,2,32,1024]{3,2,1,0:T(8,128)(2,1)S(1)}, u32[]{:S(2)}, u32[]{:S(2)}) collective-permute-start(bf16[4,2,32,1024]{3,2,1,0:T(8,128)(2,1)S(1)} %block.1), channel_id=1, source_target_pairs={{0,2},{1,3},{6,4},{7,5},{8,10},{9,11},{14,12},{15,13},{16,18},{17,... | collective-permute-start | bytes 1572872 | tf_op jit(solution)/shard_map/ppermute | solution.py:220
  41.6 1.1 %collective-permute-done.6.first_ref = bf16[4,2,32,1024]{3,2,1,0:T(8,128)(2,1)S(1)} collective-permute-done((bf16[4,2,32,1024]{3,2,1,0:T(8,128)(2,1)S(1)}, bf16[4,2,32,1024]{3,2,1,0:T(8,128)(2,1)S(1)}, u32[]{:S(2)}, u32[]{:S(2)}) %collective-permute-start.6) | collective-permute-done | bytes 524320 | tf_op jit(solution)/shard_map/ppermute | solution.py:212
  42.7 0.6 pick.1.refs_4_
  43.3 0.6 collective-permute-start.7
  43.9 0.0 collective-permute-done.10.refs_3_
  43.9 0.7 collective-permute-start.11
  44.6 0.0 collective-permute-done.8.refs_2_
  44.6 1.3 %collective-permute-start.9 = (bf16[4,2,32,1024]{3,2,1,0:T(8,128)(2,1)S(1)}, bf16[4,2,32,1024]{3,2,1,0:T(8,128)(2,1)S(1)}, u32[]{:S(2)}, u32[]{:S(2)}) collective-permute-start(bf16[4,2,32,1024]{3,2,1,0:T(8,128)(2,1)S(1)} %collective-permute-done.8.refs_2_), channel_id=1, source_target_pairs={{2,0},{3,1},{4,6},{5,7},{10,8},{11,9},{12,14},{13,15},{18,16},{19,... | collective-permute-start | bytes 1572872 | tf_op jit(solution)/shard_map/ppermute | solution.py:221
  45.9 1.5 %weigh.2.refs_5_ = f32[8,1024]{1,0:T(8,128)S(1)} custom-call(s32[9]{0:T(128)S(1)} %stack.43.scalar_ref, f32[4,2,8,32,1024]{4,3,2,1,0:T(8,128)S(1)} %bitcast.21, bf16[4,2,32,1024]{3,2,1,0:T(8,128)(2,1)S(1)} %bitcast.27, bf16[4,2,32,1024]{3,2,1,0:T(8,128)(2,1)S(1)} %collective-permute-done.2.refs_1_, ...), custom_call_target="tpu_custom_call" | custom-call | flops 5242880 | bytes 5242880 | tf_op jit(solution)/shard_map/weigh/pallas_call | solution.py:123
  47.4 5.2 %collective-permute-done.12.refs_4_ = bf16[4,2,32,1024]{3,2,1,0:T(8,128)(2,1)S(1)} collective-permute-done((bf16[4,2,32,1024]{3,2,1,0:T(8,128)(2,1)S(1)}, bf16[4,2,32,1024]{3,2,1,0:T(8,128)(2,1)S(1)}, u32[]{:S(2)}, u32[]{:S(2)}) %collective-permute-start.12) | collective-permute-done | bytes 524320 | tf_op jit(solution)/shard_map/ppermute | solution.py:220
  52.6 4.3 %collective-permute-done.7.refs_0_ = bf16[4,2,32,1024]{3,2,1,0:T(8,128)(2,1)S(1)} collective-permute-done((bf16[4,2,32,1024]{3,2,1,0:T(8,128)(2,1)S(1)}, bf16[4,2,32,1024]{3,2,1,0:T(8,128)(2,1)S(1)}, u32[]{:S(2)}, u32[]{:S(2)}) %collective-permute-start.7) | collective-permute-done | bytes 524320 | tf_op jit(solution)/shard_map/ppermute | solution.py:224
  56.9 0.0 collective-permute-done.11.refs_3_
  56.9 2.8 %collective-permute-done.9.refs_1_ = bf16[4,2,32,1024]{3,2,1,0:T(8,128)(2,1)S(1)} collective-permute-done((bf16[4,2,32,1024]{3,2,1,0:T(8,128)(2,1)S(1)}, bf16[4,2,32,1024]{3,2,1,0:T(8,128)(2,1)S(1)}, u32[]{:S(2)}, u32[]{:S(2)}) %collective-permute-start.9) | collective-permute-done | bytes 524320 | tf_op jit(solution)/shard_map/ppermute | solution.py:221
  59.7 1.1 %weigh.3 = f32[1,1024]{1,0:T(1,128)S(1)} custom-call(s32[9]{0:T(128)S(1)} %stack.43.scalar_ref, f32[4,2,8,32,1024]{4,3,2,1,0:T(8,128)S(1)} %bitcast.22, bf16[4,2,32,1024]{3,2,1,0:T(8,128)(2,1)S(1)} %collective-permute-done.7.refs_0_, bf16[4,2,32,1024]{3,2,1,0:T(8,128)(2,1)S(1)} %collective-permute-done.9.refs_1_, ...), custom_call_target="tpu_custom_call" | custom-call | flops 5275648 | bytes 5275648 | tf_op jit(solution)/shard_map/weigh/pallas_call | solution.py:123
  60.8 1.6 %collective-permute-start.13 = (f32[1024]{0:T(1024)S(1)}, f32[1024]{0:T(1024)S(1)}, u32[]{:S(2)}, u32[]{:S(2)}) collective-permute-start(f32[1024]{0:T(1024)S(1)} %bitcast.31), channel_id=1, source_target_pairs={{0,1},{1,0},{2,3},{3,2},{4,5},{5,4},{6,7},{7,6},{8,9},{9,8},{10,11... | collective-permute-start | bytes 12296 | tf_op jit(solution)/shard_map/ppermute | solution.py:244
  62.4 2.1 %collective-permute-done.13 = f32[1024]{0:T(1024)S(1)} collective-permute-done((f32[1024]{0:T(1024)S(1)}, f32[1024]{0:T(1024)S(1)}, u32[]{:S(2)}, u32[]{:S(2)}) %collective-permute-start.13) | collective-permute-done | bytes 4128 | tf_op jit(solution)/shard_map/ppermute | solution.py:244
  64.5 0.0 collective-permute-start.14
  64.5 3.6 %collective-permute-done.14 = f32[1024]{0:T(1024)S(1)} collective-permute-done((f32[1024]{0:T(1024)S(1)}, f32[1024]{0:T(1024)S(1)}, u32[]{:S(2)}, u32[]{:S(2)}) %collective-permute-start.14) | collective-permute-done | bytes 4128 | tf_op jit(solution)/shard_map/ppermute | solution.py:244
  68.1 0.7 collective-permute-start.15
  68.8 3.8 %collective-permute-done.15 = f32[1024]{0:T(1024)S(1)} collective-permute-done((f32[1024]{0:T(1024)S(1)}, f32[1024]{0:T(1024)S(1)}, u32[]{:S(2)}, u32[]{:S(2)}) %collective-permute-start.15) | collective-permute-done | bytes 4128 | tf_op jit(solution)/shard_map/ppermute | solution.py:244
  72.6 0.6 add.49
  (2 shorter events, 0.0 us)
Async XLA Ops:
  4.8 9.7 %collective-permute-start.3 = (bf16[8,64,512]{2,1,0:T(8,128)(2,1)S(1)}, bf16[8,64,512]{2,1,0:T(8,128)(2,1)S(1)}, u32[]{:S(2)}, u32[]{:S(2)}) collective-permute-start(bf16[8,64,512]{2,1,0:T(8,128)(2,1)S(1)} %spectra.1), channel_id=1, source_target_pairs={{0,8},{8,0},{16,24},{24,16},{1,9},{9,1},{17,25},{25,17},{2,10},{10... | collective-permute-start | bytes 1572872 | tf_op jit(solution)/shard_map/ppermute | solution.py:202
  5.3 15.1 %collective-permute-start.2 = (bf16[4,2,32,1024]{3,2,1,0:T(8,128)(2,1)S(1)}, bf16[4,2,32,1024]{3,2,1,0:T(8,128)(2,1)S(1)}, u32[]{:S(2)}, u32[]{:S(2)}) collective-permute-start(bf16[4,2,32,1024]{3,2,1,0:T(8,128)(2,1)S(1)} %bitcast.24), channel_id=1, source_target_pairs={{0,1},{1,0},{2,3},{3,2},{4,5},{5,4},{6,7},{7,6},{8,9},{9,8},{10,11... | collective-permute-start | bytes 1572872 | tf_op jit(solution)/shard_map/ppermute | solution.py:207
  7.9 12.5 %collective-permute-start.1 = (bf16[4,2,32,1024]{3,2,1,0:T(8,128)(2,1)S(1)}, bf16[4,2,32,1024]{3,2,1,0:T(8,128)(2,1)S(1)}, u32[]{:S(2)}, u32[]{:S(2)}) collective-permute-start(bf16[4,2,32,1024]{3,2,1,0:T(8,128)(2,1)S(1)} %bitcast.25), channel_id=1, source_target_pairs={{2,4},{3,5},{4,2},{5,3},{10,12},{11,13},{12,10},{13,11},{18,20},{1... | collective-permute-start | bytes 1572872 | tf_op jit(solution)/shard_map/ppermute | solution.py:206
  8.6 16.4 %collective-permute-start = (bf16[4,2,32,1024]{3,2,1,0:T(8,128)(2,1)S(1)}, bf16[4,2,32,1024]{3,2,1,0:T(8,128)(2,1)S(1)}, u32[]{:S(2)}, u32[]{:S(2)}) collective-permute-start(bf16[4,2,32,1024]{3,2,1,0:T(8,128)(2,1)S(1)} %bitcast.26), channel_id=1, source_target_pairs={{0,2},{1,3},{2,0},{3,1},{4,6},{5,7},{6,4},{7,5},{8,10},{9,11},{10,... | collective-permute-start | bytes 1572872 | tf_op jit(solution)/shard_map/ppermute | solution.py:205
  13.0 13.4 %collective-permute-start.4 = (bf16[8,64,512]{2,1,0:T(8,128)(2,1)S(1)}, bf16[8,64,512]{2,1,0:T(8,128)(2,1)S(1)}, u32[]{:S(2)}, u32[]{:S(2)}) collective-permute-start(bf16[8,64,512]{2,1,0:T(8,128)(2,1)S(1)} %spectra.1), channel_id=1, source_target_pairs={{0,16},{8,24},{16,0},{24,8},{1,17},{9,25},{17,1},{25,9},{2,18},{10... | collective-permute-start | bytes 1572872 | tf_op jit(solution)/shard_map/ppermute | solution.py:201
  26.5 2.6 %collective-permute-start.5 = (bf16[8,64,512]{2,1,0:T(8,128)(2,1)S(1)}, bf16[8,64,512]{2,1,0:T(8,128)(2,1)S(1)}, u32[]{:S(2)}, u32[]{:S(2)}) collective-permute-start(bf16[8,64,512]{2,1,0:T(8,128)(2,1)S(1)} %collective-permute-done.4), channel_id=1, source_target_pairs={{0,8},{8,0},{16,24},{24,16},{1,9},{9,1},{17,25},{25,17},{2,10},{10... | collective-permute-start | bytes 1572872 | tf_op jit(solution)/shard_map/ppermute | solution.py:211
  26.5 16.2 %collective-permute-start.6 = (bf16[4,2,32,1024]{3,2,1,0:T(8,128)(2,1)S(1)}, bf16[4,2,32,1024]{3,2,1,0:T(8,128)(2,1)S(1)}, u32[]{:S(2)}, u32[]{:S(2)}) collective-permute-start(bf16[4,2,32,1024]{3,2,1,0:T(8,128)(2,1)S(1)} %collective-permute-done.1.second_ref), channel_id=1, source_target_pairs={{2,0},{3,1},{4,6},{5,7},{10,8},{11,9},{12,14},{13,15},{18,16},{19,... | collective-permute-start | bytes 1572872 | tf_op jit(solution)/shard_map/ppermute | solution.py:212
  27.8 16.1 %collective-permute-start.10 = (bf16[4,2,32,1024]{3,2,1,0:T(8,128)(2,1)S(1)}, bf16[4,2,32,1024]{3,2,1,0:T(8,128)(2,1)S(1)}, u32[]{:S(2)}, u32[]{:S(2)}) collective-permute-start(bf16[4,2,32,1024]{3,2,1,0:T(8,128)(2,1)S(1)} %collective-permute-done.refs_2_), channel_id=1, source_target_pairs={{0,1},{1,0},{2,3},{3,2},{4,5},{5,4},{6,7},{7,6},{8,9},{9,8},{10,11... | collective-permute-start | bytes 1572872 | tf_op jit(solution)/shard_map/ppermute | solution.py:214
  28.3 16.2 %collective-permute-start.8 = (bf16[4,2,32,1024]{3,2,1,0:T(8,128)(2,1)S(1)}, bf16[4,2,32,1024]{3,2,1,0:T(8,128)(2,1)S(1)}, u32[]{:S(2)}, u32[]{:S(2)}) collective-permute-start(bf16[4,2,32,1024]{3,2,1,0:T(8,128)(2,1)S(1)} %collective-permute-done.refs_2_), channel_id=1, source_target_pairs={{2,4},{3,5},{4,2},{5,3},{10,12},{11,13},{12,10},{13,11},{18,20},{1... | collective-permute-start | bytes 1572872 | tf_op jit(solution)/shard_map/ppermute | solution.py:213
  35.4 17.2 %collective-permute-start.12 = (bf16[4,2,32,1024]{3,2,1,0:T(8,128)(2,1)S(1)}, bf16[4,2,32,1024]{3,2,1,0:T(8,128)(2,1)S(1)}, u32[]{:S(2)}, u32[]{:S(2)}) collective-permute-start(bf16[4,2,32,1024]{3,2,1,0:T(8,128)(2,1)S(1)} %block.1), channel_id=1, source_target_pairs={{0,2},{1,3},{6,4},{7,5},{8,10},{9,11},{14,12},{15,13},{16,18},{17,... | collective-permute-start | bytes 1572872 | tf_op jit(solution)/shard_map/ppermute | solution.py:220
  43.3 13.6 %collective-permute-start.7 = (bf16[4,2,32,1024]{3,2,1,0:T(8,128)(2,1)S(1)}, bf16[4,2,32,1024]{3,2,1,0:T(8,128)(2,1)S(1)}, u32[]{:S(2)}, u32[]{:S(2)}) collective-permute-start(bf16[4,2,32,1024]{3,2,1,0:T(8,128)(2,1)S(1)} %pick.1.refs_4_), channel_id=1, source_target_pairs={{0,1},{1,0},{2,3},{3,2},{4,5},{5,4},{6,7},{7,6},{8,9},{9,8},{10,11... | collective-permute-start | bytes 1572872 | tf_op jit(solution)/shard_map/ppermute | solution.py:224
  43.9 13.0 %collective-permute-start.11 = (bf16[4,2,32,1024]{3,2,1,0:T(8,128)(2,1)S(1)}, bf16[4,2,32,1024]{3,2,1,0:T(8,128)(2,1)S(1)}, u32[]{:S(2)}, u32[]{:S(2)}) collective-permute-start(bf16[4,2,32,1024]{3,2,1,0:T(8,128)(2,1)S(1)} %collective-permute-done.10.refs_3_), channel_id=1, source_target_pairs={{2,4},{3,5},{4,2},{5,3},{10,12},{11,13},{12,10},{13,11},{18,20},{1... | collective-permute-start | bytes 1572872 | tf_op jit(solution)/shard_map/ppermute | solution.py:222
  44.6 15.2 %collective-permute-start.9 = (bf16[4,2,32,1024]{3,2,1,0:T(8,128)(2,1)S(1)}, bf16[4,2,32,1024]{3,2,1,0:T(8,128)(2,1)S(1)}, u32[]{:S(2)}, u32[]{:S(2)}) collective-permute-start(bf16[4,2,32,1024]{3,2,1,0:T(8,128)(2,1)S(1)} %collective-permute-done.8.refs_2_), channel_id=1, source_target_pairs={{2,0},{3,1},{4,6},{5,7},{10,8},{11,9},{12,14},{13,15},{18,16},{19,... | collective-permute-start | bytes 1572872 | tf_op jit(solution)/shard_map/ppermute | solution.py:221
  60.8 3.7 %collective-permute-start.13 = (f32[1024]{0:T(1024)S(1)}, f32[1024]{0:T(1024)S(1)}, u32[]{:S(2)}, u32[]{:S(2)}) collective-permute-start(f32[1024]{0:T(1024)S(1)} %bitcast.31), channel_id=1, source_target_pairs={{0,1},{1,0},{2,3},{3,2},{4,5},{5,4},{6,7},{7,6},{8,9},{9,8},{10,11... | collective-permute-start | bytes 12296 | tf_op jit(solution)/shard_map/ppermute | solution.py:244
  64.5 3.6 %collective-permute-start.14 = (f32[1024]{0:T(1024)S(1)}, f32[1024]{0:T(1024)S(1)}, u32[]{:S(2)}, u32[]{:S(2)}) collective-permute-start(f32[1024]{0:T(1024)S(1)} %add.47), channel_id=1, source_target_pairs={{0,2},{1,3},{2,0},{3,1},{4,6},{5,7},{6,4},{7,5},{8,10},{9,11},{10,... | collective-permute-start | bytes 12296 | tf_op jit(solution)/shard_map/ppermute | solution.py:244
  68.1 4.5 %collective-permute-start.15 = (f32[1024]{0:T(1024)S(1)}, f32[1024]{0:T(1024)S(1)}, u32[]{:S(2)}, u32[]{:S(2)}) collective-permute-start(f32[1024]{0:T(1024)S(1)} %add.48), channel_id=1, source_target_pairs={{0,4},{1,5},{2,6},{3,7},{4,0},{5,1},{6,2},{7,3},{8,12},{9,13},{10,... | collective-permute-start | bytes 12296 | tf_op jit(solution)/shard_map/ppermute | solution.py:244

commit v5 on v3

--- a/solution.py
+++ b/solution.py
@@ -76,47 +76,101 @@
             transcendentals=0,
         ),
         name="spectra",
-    )(in_hbm(table), active.T, in_hbm(records))
-
-
-def adjoint_kernel(count, *refs):
-    spectra_refs, green_ref, out_ref = refs[:count], refs[count], refs[-1]
-    rows = spectra_refs[0].shape[2]
-    real = jnp.concatenate([ref[0, 0] for ref in spectra_refs], axis=0)
-    imag = jnp.concatenate([ref[0, 1] for ref in spectra_refs], axis=0)
-    left = jnp.concatenate(
+    )(in_hbm(table), in_hbm(active.T), in_hbm(records))
+
+
+def complex_rows(spectra_refs, freq):
+    real = jnp.concatenate([ref[freq, 0] for ref in spectra_refs], axis=0)
+    imag = jnp.concatenate([ref[freq, 1] for ref in spectra_refs], axis=0)
+    return jnp.concatenate(
         [jnp.concatenate([real, -imag], axis=1), jnp.concatenate([-imag, -real], axis=1)], axis=0
     )
-    sums = jnp.dot(left, green_ref[0], preferred_element_type=jnp.float32)
-    out_ref[0] = sums.reshape(2, count, rows, -1)
-
-
-def adjoint_of(pieces, green, base=None, groups=None):
+
+
+def adjoint_kernel(count, green_hbm_ref, *refs):
+    spectra_refs, (out_ref, green_ref, arrived) = refs[:count], refs[count:]
+    freqs, _, rows, _ = spectra_refs[0].shape
+
+    def fetch(freq):
+        return pltpu.make_async_copy(green_hbm_ref.at[freq], green_ref.at[freq], arrived.at[freq])
+
+    for freq in range(freqs):
+        fetch(freq).start()
+
+    @pl.loop(0, freqs)
+    def _(freq):
+        fetch(freq).wait()
+        left = complex_rows(spectra_refs, freq)
+        sums = jnp.dot(left, green_ref[freq], preferred_element_type=jnp.float32)
+        out_ref[freq, :, :count] = sums.reshape(2, count, rows, -1)
+
+
+def adjoint_rest_kernel(count, half, scalar_ref, green_ref, base_ref, *refs):
+    spectra_refs, (out_ref, block_ref) = refs[:count], refs[count:]
+    del base_ref
+    freqs, _, rows, _ = spectra_refs[0].shape
+    block = scalar_ref[FAR_Y]
+    group, first = block // 2, pl.multiple_of((block % 2) * half, half)
+
+    @pl.loop(0, freqs)
+    def _(freq):
+        left = complex_rows(spectra_refs, freq)
+        sums = jnp.dot(left, green_ref[freq], preferred_element_type=jnp.float32)
+        out_ref[freq, :, count:] = sums.reshape(2, count, rows, -1)
+        block_ref[freq] = out_ref[freq, :, group, pl.ds(first, half)].astype(block_ref.dtype)
+
+
+def in_vmem_all(arrays):
+    return [pltpu.with_memory_space_constraint(array, pltpu.VMEM) for array in arrays]
+
+
+def adjoint_of(pieces, green, groups):
     freqs, _, recv, cells = green.shape
-    rows = pieces[0].shape[1]
-    pieces = [piece.reshape(freqs, 2, rows, recv) for piece in pieces]
-    count = len(pieces)
-    groups = groups or count
-    place = 0 if base is None else 1
-    shape = (freqs, 2, groups, rows, cells)
-    bases = [] if base is None else [pltpu.with_memory_space_constraint(base, pltpu.VMEM)]
+    rows, count = pieces[0].shape[1], len(pieces)
+    green = green.reshape(freqs, 2 * recv, cells)
     return pl.pallas_call(
         functools.partial(adjoint_kernel, count),
-        grid=(freqs,),
-        in_specs=[pl.BlockSpec((1, 2, rows, recv), lambda f: (f, 0, 0, 0))] * count
-        + [pl.BlockSpec((1, 2 * recv, cells), lambda f: (f, 0, 0))]
-        + [pl.BlockSpec(memory_space=pl.ANY)] * len(bases),
-        out_specs=pl.BlockSpec((1, 2, count, rows, cells), lambda f: (f, 0, place, 0, 0)),
-        out_shape=pltpu.VMEM(shape, jnp.float32),
-        input_output_aliases={count + 1: 0} if bases else {},
-        compiler_params=pltpu.CompilerParams(vmem_limit_bytes=20 << 20),
+        in_specs=[pl.BlockSpec(memory_space=pltpu.HBM)]
+        + [pl.BlockSpec(memory_space=pltpu.VMEM)] * count,
+        out_specs=[pl.BlockSpec(memory_space=pltpu.VMEM)] * 2,
+        out_shape=[
+            pltpu.VMEM((freqs, 2, groups, rows, cells), jnp.float32),
+            pltpu.VMEM(green.shape, green.dtype),
+        ],
+        scratch_shapes=[pltpu.SemaphoreType.DMA((freqs,))],
+        compiler_params=pltpu.CompilerParams(vmem_limit_bytes=4 * count << 20),
         cost_estimate=pl.CostEstimate(
             flops=8 * freqs * count * rows * recv * cells,
-            bytes_accessed=4 * freqs * recv * cells + 8 * freqs * count * rows * cells,
+            bytes_accessed=4 * freqs * recv * cells,
             transcendentals=0,
         ),
         name="adjoint",
-    )(*pieces, in_hbm(green.reshape(freqs, 2 * recv, cells)), *bases)
+    )(in_hbm(green), *in_vmem_all([piece.reshape(freqs, 2, rows, recv) for piece in pieces]))
+
+
+def adjoint_rest(scalars, pieces, green, base):
+    freqs, _, groups, rows, cells = base.shape
+    recv, count = pieces[0].shape[2], len(pieces)
+    half = rows // 2
+    pieces = [piece.reshape(freqs, 2, rows, recv) for piece in pieces]
+    return pl.pallas_call(
+        functools.partial(adjoint_rest_kernel, count, half),
+        in_specs=[pl.BlockSpec(memory_space=pltpu.SMEM)]
+        + [pl.BlockSpec(memory_space=pltpu.VMEM)] * (count + 2),
+        out_specs=[pl.BlockSpec(memory_space=pltpu.VMEM)] * 2,
+        out_shape=[
+            pltpu.VMEM(base.shape, base.dtype),
+            pltpu.VMEM((freqs, 2, half, cells), jnp.bfloat16),
+        ],
+        input_output_aliases={2: 0},
+        compiler_params=pltpu.CompilerParams(vmem_limit_bytes=8 << 20),
+        cost_estimate=pl.CostEstimate(
+            flops=8 * freqs * count * rows * recv * cells,
+            bytes_accessed=4 * freqs * recv * cells,
+            transcendentals=0,
+        ),
+        name="adjoint_rest",
+    )(scalars, *in_vmem_all([green, base, *pieces]))
 
 
 def in_vmem(kernel, scalars, operands, shape, dtype, name):
@@ -126,14 +180,14 @@
         + [pl.BlockSpec(memory_space=pltpu.VMEM)] * len(operands),
         out_specs=pl.BlockSpec(memory_space=pltpu.VMEM),
         out_shape=pltpu.VMEM(shape, dtype),
-        compiler_params=pltpu.CompilerParams(vmem_limit_bytes=16 << 20),
+        compiler_params=pltpu.CompilerParams(vmem_limit_bytes=4 << 20),
         cost_estimate=pl.CostEstimate(
             flops=4 * sum(operand.size for operand in operands[1:]),
             bytes_accessed=4 * sum(operand.size for operand in operands[1:]),
             transcendentals=0,
         ),
         name=name,
-    )(scalars, *[pltpu.with_memory_space_constraint(operand, pltpu.VMEM) for operand in operands])
+    )(scalars, *in_vmem_all(operands))
 
 
 OWN, OWN_Y, NEAR, NEAR_Y, MID, MID_Y, FAR, FAR_Y, MIDDLE = range(9)
@@ -171,10 +225,6 @@
         out_ref[...] = second_ref[...]
 
 
-def block_kernel(scalar_ref, adjoint_ref, out_ref):
-    out_ref[...] = adjoint_ref[:, :, scalar_ref[FAR_Y]].astype(out_ref.dtype)
-
-
 def box_shards(records, active, green, background):
     freqs, _, _, cells = green.shape
     along_y = [(r, r ^ 1) for r in range(8)]
@@ -184,6 +234,7 @@
     z_inward = [(there, here) for here, there in z_outward]
     core = [(t, t ^ 1) for t in range(4)]
     along_x = [(t, t ^ 2) for t in range(4)]
+    along_both = [(t, t ^ 3) for t in range(4)]
     send, tie = lax.ppermute, lax.optimization_barrier
 
     me_tx, me_rx = lax.axis_index("tx"), lax.axis_index("rx")
@@ -204,20 +255,17 @@
     spectra = spectra_of(records, active, freqs)
     spectra_x = send(spectra, "tx", along_x)
     spectra_core = send(spectra, "tx", core)
-
-    near, across, own_y, spectra_core = tie((near, across, own_y, spectra_core))
+    spectra_both = send(spectra, "tx", along_both)
+    adjoint, green_kept = adjoint_of([spectra, spectra_core], green, 4)
+    near, across, own_y, adjoint = tie((near, across, own_y, adjoint))
+
     across_out = send(across, "rx", z_outward)
     far = send(near, "rx", z_middle)
     near_y = send(near, "rx", along_y)
 
-    adjoint = adjoint_of([spectra, spectra_core], green, groups=4)
-    spectra_x, adjoint = tie((spectra_x, adjoint))
-    spectra_both = send(spectra_x, "tx", core)
-    adjoint = adjoint_of([spectra_x, spectra_both], green, adjoint, groups=4)
+    adjoint, partial = adjoint_rest(scalars, [spectra_x, spectra_both], green_kept, adjoint)
     adjoint = adjoint.reshape((freqs, 2, 8) + own.shape[2:])
 
-    partial = in_vmem(block_kernel, scalars, [adjoint], own.shape, own.dtype, "block")
-    partial, far, near_y, across_out = tie((partial, far, near_y, across_out))
     partial = send(partial, "rx", z_inward)
     far_out = send(far, "rx", z_outward)
     far_both = send(near_y, "rx", z_middle)
@@ -250,7 +298,7 @@
     freqs = green.shape[0]
     spectra = spectra_of(records, active, freqs)
     pieces = lax.all_gather(spectra, "tx", axis=0)
-    adjoint = adjoint_of([pieces[t] for t in range(pieces.shape[0])], green)
+    adjoint, _ = adjoint_of([pieces[t] for t in range(pieces.shape[0])], green, pieces.shape[0])
     freqs, _, groups, rows, cells = adjoint.shape
     adjoint = adjoint.reshape(freqs, 2, groups * rows, cells)
     fields = lax.all_gather(background, "rx", axis=0, tiled=True)

time: 81.5 us -> 74.8 us (0.918)
  starting transfers between devices: 25.9 us -> 18.4 us
  waiting for transfers between devices: 33.9 us -> 39.5 us
  Pallas kernels: 18.5 us -> 14.5 us
    ppermute x1, waiting for transfers between devices: 0.92 us -> 10.9 us  [box_shards(): spectra_x = send(spectra, 'tx', along_x)]
    ppermute x1, waiting for transfers between devices: 6.01 us -> 0.01 us  [box_shards(): near_y = send(near, 'rx', along_y)]
    ppermute x1, starting transfers between devices: 7.56 us -> 2.02 us  [box_shards(): partial = send(partial, 'rx', z_inward)]
    ppermute x1, waiting for transfers between devices: 5.34 us -> 0.01 us  [box_shards(): across_out = send(across, 'rx', z_outward)]
    ppermute x3, starting transfers between devices: 5.12 us -> 1.59 us  [box_shards(): sums = sums + send(sums, 'rx', [(r, r ^ bit) for r in range(8)])]
    pallas_call x2, Pallas kernels: 11.4 us -> 7.94 us  [the longest x1 4.47 us: adjoint_of(): pl.pallas_call(functools.partial(adjoint_kernel, count), in_specs=[pl.Blo...]
    ppermute x3, waiting for transfers between devices: 7.12 us -> 10.2 us  [box_shards(): sums = sums + send(sums, 'rx', [(r, r ^ bit) for r in range(8)])]
    ppermute x1, waiting for transfers between devices: 4.26 us -> 6.63 us  [box_shards(): partial = send(partial, 'rx', z_inward)]
  transfers between devices with their start and end apart: 16 -> 16, of which waited for: 11 -> 9; matrix products, arithmetic and copies ran while one was open for 0% -> 0% of each run, Pallas kernels for 21% -> 13%
where the time goes in v5:
time: 74.8 us; the launch traced here: 74.5 us
  waiting for transfers between devices  39.5 us (53%)
  starting transfers between devices  18.4 us (25%)
  Pallas kernels  14.5 us (19%)
  local copies, waits for them, and re-layouts  1.42 us (2%)
    ppermute x1, waiting for transfers between devices, box_shards(): spectra_x = send(spectra, 'tx', along_x)  10.9 us
    ppermute x3, waiting for transfers between devices, box_shards(): sums = sums + send(sums, 'rx', [(r, r ^ bit) for r in range(8)])  10.2 us
    ppermute x1, waiting for transfers between devices, box_shards(): partial = send(partial, 'rx', z_inward)  6.63 us
    ppermute x1, waiting for transfers between devices, box_shards(): near = send(own, 'rx', z_pairs)  4.58 us
    pallas_call x1, Pallas kernels, adjoint_of(): pl.pallas_call(functools.partial(adjoint_kernel, count), in_specs=[pl.Blo...  4.47 us
    ppermute x1, starting transfers between devices, box_shards(): near = send(own, 'rx', z_pairs)  4.43 us
    pallas_call x1, Pallas kernels, adjoint_rest(): pl.pallas_call(functools.partial(adjoint_rest_kernel, count, half), in_sp...  3.47 us
    pallas_call x1, Pallas kernels, spectra_of(): pl.pallas_call(spectra_kernel, grid=(trans // ROWS,), in_specs=[pl.BlockS...  3.37 us
  transfers between devices with their start and end apart: 16, of which 9 were waited for; matrix products, arithmetic and copies ran while one was open for 0% of the time, Pallas kernels for 13%

profile of v5, /device:TPU:0, one launch (start us, length us, event | category | flops | bytes accessed | tf_op | source)
XLA Modules:
  0.0 74.5 jit_solution(10699822826708850613)
XLA Ops:
  0.0 1.3 %copy.9 = bf16[32,4,2,1024]{3,0,2,1:T(8,128)(2,1)S(1)} copy(bf16[32,4,2,1024]{3,2,1,0:T(2,128)(2,1)} %param.8) | data formatting | bytes 1048576 | tf_op args[3]
  1.3 0.1 stack.43.scalar_ref
  1.4 3.4 %spectra.1 = bf16[8,64,512]{2,1,0:T(8,128)(2,1)S(1)} custom-call(bf16[128,640]{1,0:T(8,128)(2,1)} %constant.38.clone.table_ref, s32[8,64]{1,0:T(8,128)} %bitcast.33, bf16[40,64,512]{2,1,0:T(8,128)(2,1)} %records_ref), custom_call_target="tpu_custom_call" | custom-call | flops 335544320 | bytes 3145728 | tf_op jit(solution)/shard_map/spectra/pallas_call | solution.py:61
  4.8 0.5 collective-permute-start
  5.3 2.6 %collective-permute-start.3 = (bf16[4,2,32,1024]{3,2,1,0:T(8,128)(2,1)S(1)}, bf16[4,2,32,1024]{3,2,1,0:T(8,128)(2,1)S(1)}, u32[]{:S(2)}, u32[]{:S(2)}) collective-permute-start(bf16[4,2,32,1024]{3,2,1,0:T(8,128)(2,1)S(1)} %bitcast.23), channel_id=1, source_target_pairs={{0,1},{1,0},{2,3},{3,2},{4,5},{5,4},{6,7},{7,6},{8,9},{9,8},{10,11... | collective-permute-start | bytes 1572872 | tf_op jit(solution)/shard_map/ppermute | solution.py:253
  7.9 0.7 collective-permute-start.2
  8.6 4.4 %collective-permute-start.1 = (bf16[4,2,32,1024]{3,2,1,0:T(8,128)(2,1)S(1)}, bf16[4,2,32,1024]{3,2,1,0:T(8,128)(2,1)S(1)}, u32[]{:S(2)}, u32[]{:S(2)}) collective-permute-start(bf16[4,2,32,1024]{3,2,1,0:T(8,128)(2,1)S(1)} %bitcast.25), channel_id=1, source_target_pairs={{0,2},{1,3},{2,0},{3,1},{4,6},{5,7},{6,4},{7,5},{8,10},{9,11},{10,... | collective-permute-start | bytes 1572872 | tf_op jit(solution)/shard_map/ppermute | solution.py:251
  13.0 0.7 collective-permute-start.5
  13.7 0.0 collective-permute-done
  13.7 0.8 %collective-permute-start.4 = (bf16[8,64,512]{2,1,0:T(8,128)(2,1)S(1)}, bf16[8,64,512]{2,1,0:T(8,128)(2,1)S(1)}, u32[]{:S(2)}, u32[]{:S(2)}) collective-permute-start(bf16[8,64,512]{2,1,0:T(8,128)(2,1)S(1)} %spectra.1), channel_id=1, source_target_pairs={{0,16},{8,24},{16,0},{24,8},{1,17},{9,25},{17,1},{25,9},{2,18},{10... | collective-permute-start | bytes 1572872 | tf_op jit(solution)/shard_map/ppermute | solution.py:256
  14.6 4.5 %adjoint.1 = (f32[4,2,4,64,1024]{4,3,2,1,0:T(8,128)S(1)}, bf16[4,1024,1024]{2,1,0:T(8,128)(2,1)S(1)}) custom-call(bf16[4,1024,1024]{2,1,0:T(8,128)(2,1)} %bitcast.32, bf16[4,2,64,512]{3,2,1,0:T(8,128)(2,1)S(1)} %bitcast.22, bf16[4,2,64,512]{3,2,1,0:T(8,128)(2,1)S(1)} %bitcast.29), custom_call_target="tpu_custom_call" | custom-call | flops 2147483648 | bytes 8388608 | tf_op jit(solution)/shard_map/adjoint/pallas_call | solution.py:131
  19.0 1.4 %collective-permute-done.3.refs_1_ = bf16[4,2,32,1024]{3,2,1,0:T(8,128)(2,1)S(1)} collective-permute-done((bf16[4,2,32,1024]{3,2,1,0:T(8,128)(2,1)S(1)}, bf16[4,2,32,1024]{3,2,1,0:T(8,128)(2,1)S(1)}, u32[]{:S(2)}, u32[]{:S(2)}) %collective-permute-start.3) | collective-permute-done | bytes 524320 | tf_op jit(solution)/shard_map/ppermute | solution.py:253
  20.4 0.0 collective-permute-done.2.second_ref
  20.4 4.6 %collective-permute-done.1.refs_2_ = bf16[4,2,32,1024]{3,2,1,0:T(8,128)(2,1)S(1)} collective-permute-done((bf16[4,2,32,1024]{3,2,1,0:T(8,128)(2,1)S(1)}, bf16[4,2,32,1024]{3,2,1,0:T(8,128)(2,1)S(1)}, u32[]{:S(2)}, u32[]{:S(2)}) %collective-permute-start.1) | collective-permute-done | bytes 524320 | tf_op jit(solution)/shard_map/ppermute | solution.py:251
  25.0 1.3 %collective-permute-start.6 = (bf16[4,2,32,1024]{3,2,1,0:T(8,128)(2,1)S(1)}, bf16[4,2,32,1024]{3,2,1,0:T(8,128)(2,1)S(1)}, u32[]{:S(2)}, u32[]{:S(2)}) collective-permute-start(bf16[4,2,32,1024]{3,2,1,0:T(8,128)(2,1)S(1)} %collective-permute-done.2.second_ref), channel_id=1, source_target_pairs={{2,0},{3,1},{4,6},{5,7},{10,8},{11,9},{12,14},{13,15},{18,16},{19,... | collective-permute-start | bytes 1572872 | tf_op jit(solution)/shard_map/ppermute | solution.py:262
  26.3 0.6 collective-permute-start.10
  26.9 0.7 collective-permute-start.8
  27.6 0.0 collective-permute-done.5
  27.6 10.9 %collective-permute-done.4 = bf16[8,64,512]{2,1,0:T(8,128)(2,1)S(1)} collective-permute-done((bf16[8,64,512]{2,1,0:T(8,128)(2,1)S(1)}, bf16[8,64,512]{2,1,0:T(8,128)(2,1)S(1)}, u32[]{:S(2)}, u32[]{:S(2)}) %collective-permute-start.4) | collective-permute-done | bytes 524320 | tf_op jit(solution)/shard_map/ppermute | solution.py:256
  38.5 3.5 %adjoint_rest.1 = (f32[4,2,4,64,1024]{4,3,2,1,0:T(8,128)S(1)}, bf16[4,2,32,1024]{3,2,1,0:T(8,128)(2,1)S(1)}) custom-call(s32[9]{0:T(128)S(1)} %stack.43.scalar_ref, bf16[4,1024,1024]{2,1,0:T(8,128)(2,1)S(1)} %get-tuple-element.18.green_ref, f32[4,2,4,64,1024]{4,3,2,1,0:T(8,128)S(1)} %get-tuple-element.21.base_ref, ...), custom_call_target="tpu_custom_call", output_to_operand_aliasing={{0}: (2, {})} | custom-call | flops 2147483648 | bytes 8388608 | tf_op jit(solution)/shard_map/adjoint_rest/pallas_call | solution.py:156
  42.0 2.0 %collective-permute-start.12 = (bf16[4,2,32,1024]{3,2,1,0:T(8,128)(2,1)S(1)}, bf16[4,2,32,1024]{3,2,1,0:T(8,128)(2,1)S(1)}, u32[]{:S(2)}, u32[]{:S(2)}) collective-permute-start(bf16[4,2,32,1024]{3,2,1,0:T(8,128)(2,1)S(1)} %get-tuple-element.25), channel_id=1, source_target_pairs={{0,2},{1,3},{6,4},{7,5},{8,10},{9,11},{14,12},{15,13},{16,18},{17,... | collective-permute-start | bytes 1572872 | tf_op jit(solution)/shard_map/ppermute | solution.py:269
  44.0 0.0 collective-permute-done.6.first_ref
  44.0 0.6 pick.1.refs_4_
  44.6 0.6 collective-permute-start.7
  45.2 0.0 collective-permute-done.10.refs_3_
  45.2 0.7 collective-permute-start.11
  45.9 0.0 collective-permute-done.8.refs_2_
  45.9 1.3 %collective-permute-start.9 = (bf16[4,2,32,1024]{3,2,1,0:T(8,128)(2,1)S(1)}, bf16[4,2,32,1024]{3,2,1,0:T(8,128)(2,1)S(1)}, u32[]{:S(2)}, u32[]{:S(2)}) collective-permute-start(bf16[4,2,32,1024]{3,2,1,0:T(8,128)(2,1)S(1)} %collective-permute-done.8.refs_2_), channel_id=1, source_target_pairs={{2,0},{3,1},{4,6},{5,7},{10,8},{11,9},{12,14},{13,15},{18,16},{19,... | collective-permute-start | bytes 1572872 | tf_op jit(solution)/shard_map/ppermute | solution.py:270
  47.2 1.5 %weigh.2.refs_5_ = f32[8,1024]{1,0:T(8,128)S(1)} custom-call(s32[9]{0:T(128)S(1)} %stack.43.scalar_ref, f32[4,2,8,32,1024]{4,3,2,1,0:T(8,128)S(1)} %bitcast.20, bf16[4,2,32,1024]{3,2,1,0:T(8,128)(2,1)S(1)} %bitcast.26, bf16[4,2,32,1024]{3,2,1,0:T(8,128)(2,1)S(1)} %collective-permute-done.3.refs_1_, ...), custom_call_target="tpu_custom_call" | custom-call | flops 5242880 | bytes 5242880 | tf_op jit(solution)/shard_map/weigh/pallas_call | solution.py:177
  48.7 6.6 %collective-permute-done.12.refs_4_ = bf16[4,2,32,1024]{3,2,1,0:T(8,128)(2,1)S(1)} collective-permute-done((bf16[4,2,32,1024]{3,2,1,0:T(8,128)(2,1)S(1)}, bf16[4,2,32,1024]{3,2,1,0:T(8,128)(2,1)S(1)}, u32[]{:S(2)}, u32[]{:S(2)}) %collective-permute-start.12) | collective-permute-done | bytes 524320 | tf_op jit(solution)/shard_map/ppermute | solution.py:269
  55.4 2.9 %collective-permute-done.7.refs_0_ = bf16[4,2,32,1024]{3,2,1,0:T(8,128)(2,1)S(1)} collective-permute-done((bf16[4,2,32,1024]{3,2,1,0:T(8,128)(2,1)S(1)}, bf16[4,2,32,1024]{3,2,1,0:T(8,128)(2,1)S(1)}, u32[]{:S(2)}, u32[]{:S(2)}) %collective-permute-start.7) | collective-permute-done | bytes 524320 | tf_op jit(solution)/shard_map/ppermute | solution.py:273
  58.3 0.0 collective-permute-done.11.refs_3_
  58.3 2.8 %collective-permute-done.9.refs_1_ = bf16[4,2,32,1024]{3,2,1,0:T(8,128)(2,1)S(1)} collective-permute-done((bf16[4,2,32,1024]{3,2,1,0:T(8,128)(2,1)S(1)}, bf16[4,2,32,1024]{3,2,1,0:T(8,128)(2,1)S(1)}, u32[]{:S(2)}, u32[]{:S(2)}) %collective-permute-start.9) | collective-permute-done | bytes 524320 | tf_op jit(solution)/shard_map/ppermute | solution.py:270
  61.1 1.0 %weigh.3 = f32[1,1024]{1,0:T(1,128)S(1)} custom-call(s32[9]{0:T(128)S(1)} %stack.43.scalar_ref, f32[4,2,8,32,1024]{4,3,2,1,0:T(8,128)S(1)} %bitcast.21, bf16[4,2,32,1024]{3,2,1,0:T(8,128)(2,1)S(1)} %collective-permute-done.7.refs_0_, bf16[4,2,32,1024]{3,2,1,0:T(8,128)(2,1)S(1)} %collective-permute-done.9.refs_1_, ...), custom_call_target="tpu_custom_call" | custom-call | flops 5275648 | bytes 5275648 | tf_op jit(solution)/shard_map/weigh/pallas_call | solution.py:177
  62.1 1.6 %collective-permute-start.13 = (f32[1024]{0:T(1024)S(1)}, f32[1024]{0:T(1024)S(1)}, u32[]{:S(2)}, u32[]{:S(2)}) collective-permute-start(f32[1024]{0:T(1024)S(1)} %bitcast.30), channel_id=1, source_target_pairs={{0,1},{1,0},{2,3},{3,2},{4,5},{5,4},{6,7},{7,6},{8,9},{9,8},{10,11... | collective-permute-start | bytes 12296 | tf_op jit(solution)/shard_map/ppermute | solution.py:293
  63.7 2.1 %collective-permute-done.13 = f32[1024]{0:T(1024)S(1)} collective-permute-done((f32[1024]{0:T(1024)S(1)}, f32[1024]{0:T(1024)S(1)}, u32[]{:S(2)}, u32[]{:S(2)}) %collective-permute-start.13) | collective-permute-done | bytes 4128 | tf_op jit(solution)/shard_map/ppermute | solution.py:293
  65.8 0.0 collective-permute-start.14
  65.8 3.6 %collective-permute-done.14 = f32[1024]{0:T(1024)S(1)} collective-permute-done((f32[1024]{0:T(1024)S(1)}, f32[1024]{0:T(1024)S(1)}, u32[]{:S(2)}, u32[]{:S(2)}) %collective-permute-start.14) | collective-permute-done | bytes 4128 | tf_op jit(solution)/shard_map/ppermute | solution.py:293
  69.4 0.0 collective-permute-start.15
  69.4 4.5 %collective-permute-done.15 = f32[1024]{0:T(1024)S(1)} collective-permute-done((f32[1024]{0:T(1024)S(1)}, f32[1024]{0:T(1024)S(1)}, u32[]{:S(2)}, u32[]{:S(2)}) %collective-permute-start.15) | collective-permute-done | bytes 4128 | tf_op jit(solution)/shard_map/ppermute | solution.py:293
  73.9 0.6 add.49
  (2 shorter events, 0.0 us)
Async XLA Ops:
  4.8 8.9 %collective-permute-start = (bf16[8,64,512]{2,1,0:T(8,128)(2,1)S(1)}, bf16[8,64,512]{2,1,0:T(8,128)(2,1)S(1)}, u32[]{:S(2)}, u32[]{:S(2)}) collective-permute-start(bf16[8,64,512]{2,1,0:T(8,128)(2,1)S(1)} %spectra.1), channel_id=1, source_target_pairs={{0,8},{8,0},{16,24},{24,16},{1,9},{9,1},{17,25},{25,17},{2,10},{10... | collective-permute-start | bytes 1572872 | tf_op jit(solution)/shard_map/ppermute | solution.py:257
  5.3 15.1 %collective-permute-start.3 = (bf16[4,2,32,1024]{3,2,1,0:T(8,128)(2,1)S(1)}, bf16[4,2,32,1024]{3,2,1,0:T(8,128)(2,1)S(1)}, u32[]{:S(2)}, u32[]{:S(2)}) collective-permute-start(bf16[4,2,32,1024]{3,2,1,0:T(8,128)(2,1)S(1)} %bitcast.23), channel_id=1, source_target_pairs={{0,1},{1,0},{2,3},{3,2},{4,5},{5,4},{6,7},{7,6},{8,9},{9,8},{10,11... | collective-permute-start | bytes 1572872 | tf_op jit(solution)/shard_map/ppermute | solution.py:253
  7.9 12.5 %collective-permute-start.2 = (bf16[4,2,32,1024]{3,2,1,0:T(8,128)(2,1)S(1)}, bf16[4,2,32,1024]{3,2,1,0:T(8,128)(2,1)S(1)}, u32[]{:S(2)}, u32[]{:S(2)}) collective-permute-start(bf16[4,2,32,1024]{3,2,1,0:T(8,128)(2,1)S(1)} %bitcast.24), channel_id=1, source_target_pairs={{2,4},{3,5},{4,2},{5,3},{10,12},{11,13},{12,10},{13,11},{18,20},{1... | collective-permute-start | bytes 1572872 | tf_op jit(solution)/shard_map/ppermute | solution.py:252
  8.6 16.4 %collective-permute-start.1 = (bf16[4,2,32,1024]{3,2,1,0:T(8,128)(2,1)S(1)}, bf16[4,2,32,1024]{3,2,1,0:T(8,128)(2,1)S(1)}, u32[]{:S(2)}, u32[]{:S(2)}) collective-permute-start(bf16[4,2,32,1024]{3,2,1,0:T(8,128)(2,1)S(1)} %bitcast.25), channel_id=1, source_target_pairs={{0,2},{1,3},{2,0},{3,1},{4,6},{5,7},{6,4},{7,5},{8,10},{9,11},{10,... | collective-permute-start | bytes 1572872 | tf_op jit(solution)/shard_map/ppermute | solution.py:251
  13.0 14.5 %collective-permute-start.5 = (bf16[8,64,512]{2,1,0:T(8,128)(2,1)S(1)}, bf16[8,64,512]{2,1,0:T(8,128)(2,1)S(1)}, u32[]{:S(2)}, u32[]{:S(2)}) collective-permute-start(bf16[8,64,512]{2,1,0:T(8,128)(2,1)S(1)} %spectra.1), channel_id=1, source_target_pairs={{0,24},{8,16},{16,8},{24,0},{1,25},{9,17},{17,9},{25,1},{2,26},{10... | collective-permute-start | bytes 1572872 | tf_op jit(solution)/shard_map/ppermute | solution.py:258
  13.7 24.8 %collective-permute-start.4 = (bf16[8,64,512]{2,1,0:T(8,128)(2,1)S(1)}, bf16[8,64,512]{2,1,0:T(8,128)(2,1)S(1)}, u32[]{:S(2)}, u32[]{:S(2)}) collective-permute-start(bf16[8,64,512]{2,1,0:T(8,128)(2,1)S(1)} %spectra.1), channel_id=1, source_target_pairs={{0,16},{8,24},{16,0},{24,8},{1,17},{9,25},{17,1},{25,9},{2,18},{10... | collective-permute-start | bytes 1572872 | tf_op jit(solution)/shard_map/ppermute | solution.py:256
  25.0 19.0 %collective-permute-start.6 = (bf16[4,2,32,1024]{3,2,1,0:T(8,128)(2,1)S(1)}, bf16[4,2,32,1024]{3,2,1,0:T(8,128)(2,1)S(1)}, u32[]{:S(2)}, u32[]{:S(2)}) collective-permute-start(bf16[4,2,32,1024]{3,2,1,0:T(8,128)(2,1)S(1)} %collective-permute-done.2.second_ref), channel_id=1, source_target_pairs={{2,0},{3,1},{4,6},{5,7},{10,8},{11,9},{12,14},{13,15},{18,16},{19,... | collective-permute-start | bytes 1572872 | tf_op jit(solution)/shard_map/ppermute | solution.py:262
  26.3 18.9 %collective-permute-start.10 = (bf16[4,2,32,1024]{3,2,1,0:T(8,128)(2,1)S(1)}, bf16[4,2,32,1024]{3,2,1,0:T(8,128)(2,1)S(1)}, u32[]{:S(2)}, u32[]{:S(2)}) collective-permute-start(bf16[4,2,32,1024]{3,2,1,0:T(8,128)(2,1)S(1)} %collective-permute-done.1.refs_2_), channel_id=1, source_target_pairs={{0,1},{1,0},{2,3},{3,2},{4,5},{5,4},{6,7},{7,6},{8,9},{9,8},{10,11... | collective-permute-start | bytes 1572872 | tf_op jit(solution)/shard_map/ppermute | solution.py:264
  26.9 19.0 %collective-permute-start.8 = (bf16[4,2,32,1024]{3,2,1,0:T(8,128)(2,1)S(1)}, bf16[4,2,32,1024]{3,2,1,0:T(8,128)(2,1)S(1)}, u32[]{:S(2)}, u32[]{:S(2)}) collective-permute-start(bf16[4,2,32,1024]{3,2,1,0:T(8,128)(2,1)S(1)} %collective-permute-done.1.refs_2_), channel_id=1, source_target_pairs={{2,4},{3,5},{4,2},{5,3},{10,12},{11,13},{12,10},{13,11},{18,20},{1... | collective-permute-start | bytes 1572872 | tf_op jit(solution)/shard_map/ppermute | solution.py:263
  42.0 13.4 %collective-permute-start.12 = (bf16[4,2,32,1024]{3,2,1,0:T(8,128)(2,1)S(1)}, bf16[4,2,32,1024]{3,2,1,0:T(8,128)(2,1)S(1)}, u32[]{:S(2)}, u32[]{:S(2)}) collective-permute-start(bf16[4,2,32,1024]{3,2,1,0:T(8,128)(2,1)S(1)} %get-tuple-element.25), channel_id=1, source_target_pairs={{0,2},{1,3},{6,4},{7,5},{8,10},{9,11},{14,12},{15,13},{16,18},{17,... | collective-permute-start | bytes 1572872 | tf_op jit(solution)/shard_map/ppermute | solution.py:269
  44.6 13.7 %collective-permute-start.7 = (bf16[4,2,32,1024]{3,2,1,0:T(8,128)(2,1)S(1)}, bf16[4,2,32,1024]{3,2,1,0:T(8,128)(2,1)S(1)}, u32[]{:S(2)}, u32[]{:S(2)}) collective-permute-start(bf16[4,2,32,1024]{3,2,1,0:T(8,128)(2,1)S(1)} %pick.1.refs_4_), channel_id=1, source_target_pairs={{0,1},{1,0},{2,3},{3,2},{4,5},{5,4},{6,7},{7,6},{8,9},{9,8},{10,11... | collective-permute-start | bytes 1572872 | tf_op jit(solution)/shard_map/ppermute | solution.py:273
  45.2 13.1 %collective-permute-start.11 = (bf16[4,2,32,1024]{3,2,1,0:T(8,128)(2,1)S(1)}, bf16[4,2,32,1024]{3,2,1,0:T(8,128)(2,1)S(1)}, u32[]{:S(2)}, u32[]{:S(2)}) collective-permute-start(bf16[4,2,32,1024]{3,2,1,0:T(8,128)(2,1)S(1)} %collective-permute-done.10.refs_3_), channel_id=1, source_target_pairs={{2,4},{3,5},{4,2},{5,3},{10,12},{11,13},{12,10},{13,11},{18,20},{1... | collective-permute-start | bytes 1572872 | tf_op jit(solution)/shard_map/ppermute | solution.py:271
  45.9 15.2 %collective-permute-start.9 = (bf16[4,2,32,1024]{3,2,1,0:T(8,128)(2,1)S(1)}, bf16[4,2,32,1024]{3,2,1,0:T(8,128)(2,1)S(1)}, u32[]{:S(2)}, u32[]{:S(2)}) collective-permute-start(bf16[4,2,32,1024]{3,2,1,0:T(8,128)(2,1)S(1)} %collective-permute-done.8.refs_2_), channel_id=1, source_target_pairs={{2,0},{3,1},{4,6},{5,7},{10,8},{11,9},{12,14},{13,15},{18,16},{19,... | collective-permute-start | bytes 1572872 | tf_op jit(solution)/shard_map/ppermute | solution.py:270
  62.1 3.7 %collective-permute-start.13 = (f32[1024]{0:T(1024)S(1)}, f32[1024]{0:T(1024)S(1)}, u32[]{:S(2)}, u32[]{:S(2)}) collective-permute-start(f32[1024]{0:T(1024)S(1)} %bitcast.30), channel_id=1, source_target_pairs={{0,1},{1,0},{2,3},{3,2},{4,5},{5,4},{6,7},{7,6},{8,9},{9,8},{10,11... | collective-permute-start | bytes 12296 | tf_op jit(solution)/shard_map/ppermute | solution.py:293
  65.8 3.6 %collective-permute-start.14 = (f32[1024]{0:T(1024)S(1)}, f32[1024]{0:T(1024)S(1)}, u32[]{:S(2)}, u32[]{:S(2)}) collective-permute-start(f32[1024]{0:T(1024)S(1)} %add.47), channel_id=1, source_target_pairs={{0,2},{1,3},{2,0},{3,1},{4,6},{5,7},{6,4},{7,5},{8,10},{9,11},{10,... | collective-permute-start | bytes 12296 | tf_op jit(solution)/shard_map/ppermute | solution.py:293
  69.4 4.5 %collective-permute-start.15 = (f32[1024]{0:T(1024)S(1)}, f32[1024]{0:T(1024)S(1)}, u32[]{:S(2)}, u32[]{:S(2)}) collective-permute-start(f32[1024]{0:T(1024)S(1)} %add.48), channel_id=1, source_target_pairs={{0,4},{1,5},{2,6},{3,7},{4,0},{5,1},{6,2},{7,3},{8,12},{9,13},{10,... | collective-permute-start | bytes 12296 | tf_op jit(solution)/shard_map/ppermute | solution.py:293

commit v6 on v5

--- a/solution.py
+++ b/solution.py
@@ -26,27 +26,44 @@
     return np.kron(table, np.eye(ROWS, dtype=np.float32)).astype(jnp.bfloat16)
 
 
-def spectra_kernel(table_ref, active_ref, records_ref, out_ref, mask_ref):
-    gates, rows, recv = records_ref.shape
-    blocks = active_ref.shape[0]
-    step = pl.program_id(0)
-
-    @pl.when(step == 0)
-    def _():
-        block_of = lax.broadcasted_iota(jnp.int32, (blocks, recv), 1) // (recv // blocks)
-        spread = (block_of == lax.broadcasted_iota(jnp.int32, (blocks, recv), 0)).astype(jnp.float32)
-        mask_ref[...] = lax.dot_general(
-            active_ref[...].astype(jnp.float32),
-            spread,
-            (((0,), (0,)), ((), ())),
-            preferred_element_type=jnp.float32,
+def spectra_kernel(table_hbm, active_hbm, records_hbm, out_ref, table_ref, active_ref, records_ref, mask_ref, arrived):
+    gates, trans, recv = records_ref.shape
+    blocks, channels = active_ref.shape[0], out_ref.shape[0]
+    steps = trans // ROWS
+
+    def rows(step):
+        return pl.ds(pl.multiple_of(step * ROWS, ROWS), ROWS)
+
+    def fetch(step):
+        return pltpu.make_async_copy(
+            records_hbm.at[:, rows(step)], records_ref.at[:, rows(step)], arrived.at[step]
         )
 
-    flat = records_ref[...].reshape(gates * rows, recv)
-    sums = jnp.dot(table_ref[...], flat, preferred_element_type=jnp.float32)
-    mask = mask_ref[pl.ds(pl.multiple_of(step * rows, rows), rows)]
-    channels = out_ref.shape[0]
-    out_ref[...] = (sums.reshape(channels, rows, recv) * mask[None]).astype(out_ref.dtype)
+    fetch_active = pltpu.make_async_copy(active_hbm, active_ref, arrived.at[steps])
+    fetch_table = pltpu.make_async_copy(table_hbm, table_ref, arrived.at[steps + 1])
+    fetch_active.start()
+    fetch_table.start()
+    for step in range(steps):
+        fetch(step).start()
+
+    fetch_active.wait()
+    block_of = lax.broadcasted_iota(jnp.int32, (blocks, recv), 1) // (recv // blocks)
+    spread = (block_of == lax.broadcasted_iota(jnp.int32, (blocks, recv), 0)).astype(jnp.float32)
+    mask_ref[...] = lax.dot_general(
+        active_ref[...].astype(jnp.float32),
+        spread,
+        (((0,), (0,)), ((), ())),
+        preferred_element_type=jnp.float32,
+    )
+    fetch_table.wait()
+
+    @pl.loop(0, steps)
+    def _(step):
+        fetch(step).wait()
+        flat = records_ref[:, rows(step)].reshape(gates * ROWS, recv)
+        sums = jnp.dot(table_ref[...], flat, preferred_element_type=jnp.float32)
+        masked = sums.reshape(channels, ROWS, recv) * mask_ref[rows(step)][None]
+        out_ref[:, rows(step)] = masked.astype(out_ref.dtype)
 
 
 def in_hbm(array):
@@ -60,15 +77,16 @@
     table = jnp.asarray(spread_table(gates, freq_count))
     return pl.pallas_call(
         spectra_kernel,
-        grid=(trans // ROWS,),
-        in_specs=[
-            pl.BlockSpec(table.shape, lambda i: (0, 0)),
-            pl.BlockSpec((blocks, trans), lambda i: (0, 0)),
-            pl.BlockSpec((gates, ROWS, recv), lambda i: (0, i, 0)),
+        in_specs=[pl.BlockSpec(memory_space=pltpu.HBM)] * 3,
+        out_specs=pl.BlockSpec(memory_space=pltpu.VMEM),
+        out_shape=pltpu.VMEM((channels, trans, recv), jnp.bfloat16),
+        scratch_shapes=[
+            pltpu.VMEM(table.shape, table.dtype),
+            pltpu.VMEM((blocks, trans), jnp.int32),
+            pltpu.VMEM(records.shape, records.dtype),
+            pltpu.VMEM((trans, recv), jnp.float32),
+            pltpu.SemaphoreType.DMA((trans // ROWS + 2,)),
         ],
-        out_specs=pl.BlockSpec((channels, ROWS, recv), lambda i: (0, i, 0)),
-        out_shape=jax.ShapeDtypeStruct((channels, trans, recv), jnp.bfloat16),
-        scratch_shapes=[pltpu.VMEM((trans, recv), jnp.float32)],
         compiler_params=pltpu.CompilerParams(vmem_limit_bytes=16 << 20),
         cost_estimate=pl.CostEstimate(
             flops=2 * channels * ROWS * gates * trans * recv,
@@ -87,12 +105,14 @@
     )
 
 
-def adjoint_kernel(count, green_hbm_ref, *refs):
-    spectra_refs, (out_ref, green_ref, arrived) = refs[:count], refs[count:]
+def adjoint_kernel(count, half, scalar_ref, green_hbm, *refs):
+    spectra_refs, (out_ref, block_ref, green_ref, arrived) = refs[:count], refs[count:]
     freqs, _, rows, _ = spectra_refs[0].shape
+    block = scalar_ref[FAR_Y]
+    group, first = block // 2, pl.multiple_of((block % 2) * half, half)
 
     def fetch(freq):
-        return pltpu.make_async_copy(green_hbm_ref.at[freq], green_ref.at[freq], arrived.at[freq])
+        return pltpu.make_async_copy(green_hbm.at[freq], green_ref.at[freq], arrived.at[freq])
 
     for freq in range(freqs):
         fetch(freq).start()
@@ -102,21 +122,7 @@
         fetch(freq).wait()
         left = complex_rows(spectra_refs, freq)
         sums = jnp.dot(left, green_ref[freq], preferred_element_type=jnp.float32)
-        out_ref[freq, :, :count] = sums.reshape(2, count, rows, -1)
-
-
-def adjoint_rest_kernel(count, half, scalar_ref, green_ref, base_ref, *refs):
-    spectra_refs, (out_ref, block_ref) = refs[:count], refs[count:]
-    del base_ref
-    freqs, _, rows, _ = spectra_refs[0].shape
-    block = scalar_ref[FAR_Y]
-    group, first = block // 2, pl.multiple_of((block % 2) * half, half)
-
-    @pl.loop(0, freqs)
-    def _(freq):
-        left = complex_rows(spectra_refs, freq)
-        sums = jnp.dot(left, green_ref[freq], preferred_element_type=jnp.float32)
-        out_ref[freq, :, count:] = sums.reshape(2, count, rows, -1)
+        out_ref[freq] = sums.reshape(2, count, rows, -1)
         block_ref[freq] = out_ref[freq, :, group, pl.ds(first, half)].astype(block_ref.dtype)
 
 
@@ -124,53 +130,29 @@
     return [pltpu.with_memory_space_constraint(array, pltpu.VMEM) for array in arrays]
 
 
-def adjoint_of(pieces, green, groups):
+def adjoint_of(scalars, pieces, green):
     freqs, _, recv, cells = green.shape
     rows, count = pieces[0].shape[1], len(pieces)
+    half = rows // 2
     green = green.reshape(freqs, 2 * recv, cells)
     return pl.pallas_call(
-        functools.partial(adjoint_kernel, count),
-        in_specs=[pl.BlockSpec(memory_space=pltpu.HBM)]
+        functools.partial(adjoint_kernel, count, half),
+        in_specs=[pl.BlockSpec(memory_space=pltpu.SMEM), pl.BlockSpec(memory_space=pltpu.HBM)]
         + [pl.BlockSpec(memory_space=pltpu.VMEM)] * count,
         out_specs=[pl.BlockSpec(memory_space=pltpu.VMEM)] * 2,
         out_shape=[
-            pltpu.VMEM((freqs, 2, groups, rows, cells), jnp.float32),
-            pltpu.VMEM(green.shape, green.dtype),
+            pltpu.VMEM((freqs, 2, count, rows, cells), jnp.float32),
+            pltpu.VMEM((freqs, 2, half, cells), jnp.bfloat16),
         ],
-        scratch_shapes=[pltpu.SemaphoreType.DMA((freqs,))],
-        compiler_params=pltpu.CompilerParams(vmem_limit_bytes=4 * count << 20),
+        scratch_shapes=[pltpu.VMEM(green.shape, green.dtype), pltpu.SemaphoreType.DMA((freqs,))],
+        compiler_params=pltpu.CompilerParams(vmem_limit_bytes=24 << 20),
         cost_estimate=pl.CostEstimate(
             flops=8 * freqs * count * rows * recv * cells,
             bytes_accessed=4 * freqs * recv * cells,
             transcendentals=0,
         ),
         name="adjoint",
-    )(in_hbm(green), *in_vmem_all([piece.reshape(freqs, 2, rows, recv) for piece in pieces]))
-
-
-def adjoint_rest(scalars, pieces, green, base):
-    freqs, _, groups, rows, cells = base.shape
-    recv, count = pieces[0].shape[2], len(pieces)
-    half = rows // 2
-    pieces = [piece.reshape(freqs, 2, rows, recv) for piece in pieces]
-    return pl.pallas_call(
-        functools.partial(adjoint_rest_kernel, count, half),
-        in_specs=[pl.BlockSpec(memory_space=pltpu.SMEM)]
-        + [pl.BlockSpec(memory_space=pltpu.VMEM)] * (count + 2),
-        out_specs=[pl.BlockSpec(memory_space=pltpu.VMEM)] * 2,
-        out_shape=[
-            pltpu.VMEM(base.shape, base.dtype),
-            pltpu.VMEM((freqs, 2, half, cells), jnp.bfloat16),
-        ],
-        input_output_aliases={2: 0},
-        compiler_params=pltpu.CompilerParams(vmem_limit_bytes=8 << 20),
-        cost_estimate=pl.CostEstimate(
-            flops=8 * freqs * count * rows * recv * cells,
-            bytes_accessed=4 * freqs * recv * cells,
-            transcendentals=0,
-        ),
-        name="adjoint_rest",
-    )(scalars, *in_vmem_all([green, base, *pieces]))
+    )(scalars, in_hbm(green), *in_vmem_all([piece.reshape(freqs, 2, rows, recv) for piece in pieces]))
 
 
 def in_vmem(kernel, scalars, operands, shape, dtype, name):
@@ -234,7 +216,6 @@
     z_inward = [(there, here) for here, there in z_outward]
     core = [(t, t ^ 1) for t in range(4)]
     along_x = [(t, t ^ 2) for t in range(4)]
-    along_both = [(t, t ^ 3) for t in range(4)]
     send, tie = lax.ppermute, lax.optimization_barrier
 
     me_tx, me_rx = lax.axis_index("tx"), lax.axis_index("rx")
@@ -248,22 +229,23 @@
 
     own = background.transpose(1, 2, 0, 3)
     own, scalars, records = tie((own, scalars, records))
+    spectra = spectra_of(records, active, freqs)
+    spectra_x = send(spectra, "tx", along_x)
+    spectra_core = send(spectra, "tx", core)
+    spectra_both = send(spectra_x, "tx", core)
+
+    own, _ = tie((own, spectra))
     near = send(own, "rx", z_pairs)
     across = send(own, "rx", z_middle)
     own_y = send(own, "rx", along_y)
-
-    spectra = spectra_of(records, active, freqs)
-    spectra_x = send(spectra, "tx", along_x)
-    spectra_core = send(spectra, "tx", core)
-    spectra_both = send(spectra, "tx", along_both)
-    adjoint, green_kept = adjoint_of([spectra, spectra_core], green, 4)
-    near, across, own_y, adjoint = tie((near, across, own_y, adjoint))
+    near, across, own_y, spectra_core = tie((near, across, own_y, spectra_core))
 
     across_out = send(across, "rx", z_outward)
     far = send(near, "rx", z_middle)
     near_y = send(near, "rx", along_y)
 
-    adjoint, partial = adjoint_rest(scalars, [spectra_x, spectra_both], green_kept, adjoint)
+    adjoint, partial = adjoint_of(scalars, [spectra, spectra_core, spectra_x, spectra_both], green)
+    across_out, partial = tie((across_out, partial))
     adjoint = adjoint.reshape((freqs, 2, 8) + own.shape[2:])
 
     partial = send(partial, "rx", z_inward)
@@ -298,7 +280,8 @@
     freqs = green.shape[0]
     spectra = spectra_of(records, active, freqs)
     pieces = lax.all_gather(spectra, "tx", axis=0)
-    adjoint, _ = adjoint_of([pieces[t] for t in range(pieces.shape[0])], green, pieces.shape[0])
+    scalars = jnp.zeros(MIDDLE + 1, jnp.int32)
+    adjoint, _ = adjoint_of(scalars, [pieces[t] for t in range(pieces.shape[0])], green)
     freqs, _, groups, rows, cells = adjoint.shape
     adjoint = adjoint.reshape(freqs, 2, groups * rows, cells)
     fields = lax.all_gather(background, "rx", axis=0, tiled=True)

time: 74.8 us -> 69.2 us (0.925)
  waiting for transfers between devices: 39.5 us -> 35.7 us
  Pallas kernels: 14.5 us -> 12.7 us
    ppermute x1, waiting for transfers between devices: 6.63 us -> 0.99 us  [box_shards(): partial = send(partial, 'rx', z_inward)]
    ppermute x1, waiting for transfers between devices: 0.01 us -> 4.64 us  [box_shards(): across_out = send(across, 'rx', z_outward)]
    ppermute x1, waiting for transfers between devices: 4.58 us -> 1.46 us  [box_shards(): near = send(own, 'rx', z_pairs)]
    ppermute x1, waiting for transfers between devices: 10.9 us -> 8.07 us  [box_shards(): spectra_x = send(spectra, 'tx', along_x)]
    ppermute x1, starting transfers between devices: 4.43 us -> 1.59 us  [box_shards(): near = send(own, 'rx', z_pairs)]
    ppermute x1, starting transfers between devices: 0.82 us -> 2.99 us  [box_shards(): spectra_x = send(spectra, 'tx', along_x)]
    ppermute x1, waiting for transfers between devices: 2.83 us -> 4.87 us  [box_shards(): far_out = send(far, 'rx', z_outward)]
    pallas_call x3 -> x2, Pallas kernels: 11.3 us -> 9.65 us  [the longest x1 7.3 us: adjoint_of(): pl.pallas_call(functools.partial(adjoint_kernel, count, half), in_specs=[...]
  transfers between devices with their start and end apart: 16 -> 16, of which waited for: 9 -> 10; matrix products, arithmetic and copies ran while one was open for 0% -> 0% of each run, Pallas kernels for 13% -> 14%
where the time goes in v6:
time: 69.2 us; the launch traced here: 68.9 us
  waiting for transfers between devices  35.7 us (52%)
  starting transfers between devices  18.4 us (27%)
  Pallas kernels  12.7 us (18%)
  local copies, waits for them, and re-layouts  1.42 us (2%)
    ppermute x3, waiting for transfers between devices, box_shards(): sums = sums + send(sums, 'rx', [(r, r ^ bit) for r in range(8)])  9.31 us
    ppermute x1, waiting for transfers between devices, box_shards(): spectra_x = send(spectra, 'tx', along_x)  8.07 us
    pallas_call x1, Pallas kernels, adjoint_of(): pl.pallas_call(functools.partial(adjoint_kernel, count, half), in_specs=[...  7.3 us
    ppermute x1, waiting for transfers between devices, box_shards(): far_out = send(far, 'rx', z_outward)  4.87 us
    ppermute x1, waiting for transfers between devices, box_shards(): across_out = send(across, 'rx', z_outward)  4.64 us
    ppermute x1, waiting for transfers between devices, box_shards(): mid_y = send(mid, 'rx', along_y)  4.33 us
    pallas_call x3, Pallas kernels, in_vmem(): pl.pallas_call(kernel, in_specs=[pl.BlockSpec(memory_space=pltpu.SMEM)] +...  3.08 us
    ppermute x1, starting transfers between devices, box_shards(): spectra_x = send(spectra, 'tx', along_x)  2.99 us
  transfers between devices with their start and end apart: 16, of which 10 were waited for; matrix products, arithmetic and copies ran while one was open for 0% of the time, Pallas kernels for 14%

profile of v6, /device:TPU:0, one launch (start us, length us, event | category | flops | bytes accessed | tf_op | source)
XLA Modules:
  0.0 68.9 jit_solution(16647747352192178470)
XLA Ops:
  0.0 1.3 %copy.8 = bf16[32,4,2,1024]{3,0,2,1:T(8,128)(2,1)S(1)} copy(bf16[32,4,2,1024]{3,2,1,0:T(2,128)(2,1)} %param.8) | data formatting | bytes 1048576 | tf_op args[3]
  1.3 0.1 stack.43.scalar_ref
  1.4 2.3 %spectra.1 = bf16[8,64,512]{2,1,0:T(8,128)(2,1)S(1)} custom-call(bf16[128,640]{1,0:T(8,128)(2,1)} %constant.38.clone.table_hbm, s32[8,64]{1,0:T(8,128)} %bitcast.32, bf16[40,64,512]{2,1,0:T(8,128)(2,1)} %records_hbm), custom_call_target="tpu_custom_call" | custom-call | flops 335544320 | bytes 3145728 | tf_op jit(solution)/shard_map/spectra/pallas_call | solution.py:78
  3.8 3.0 %collective-permute-start.4 = (bf16[8,64,512]{2,1,0:T(8,128)(2,1)S(1)}, bf16[8,64,512]{2,1,0:T(8,128)(2,1)S(1)}, u32[]{:S(2)}, u32[]{:S(2)}) collective-permute-start(bf16[8,64,512]{2,1,0:T(8,128)(2,1)S(1)} %spectra.1), channel_id=1, source_target_pairs={{0,16},{8,24},{16,0},{24,8},{1,17},{9,25},{17,1},{25,9},{2,18},{10... | collective-permute-start | bytes 1572872 | tf_op jit(solution)/shard_map/ppermute | solution.py:233
  6.8 1.6 %collective-permute-start = (bf16[4,2,32,1024]{3,2,1,0:T(8,128)(2,1)S(1)}, bf16[4,2,32,1024]{3,2,1,0:T(8,128)(2,1)S(1)}, u32[]{:S(2)}, u32[]{:S(2)}) collective-permute-start(bf16[4,2,32,1024]{3,2,1,0:T(8,128)(2,1)S(1)} %bitcast.22), channel_id=1, source_target_pairs={{0,2},{1,3},{2,0},{3,1},{4,6},{5,7},{6,4},{7,5},{8,10},{9,11},{10,... | collective-permute-start | bytes 1572872 | tf_op jit(solution)/shard_map/ppermute | solution.py:238
  8.4 0.7 collective-permute-start.1
  9.1 1.6 %collective-permute-start.2 = (bf16[4,2,32,1024]{3,2,1,0:T(8,128)(2,1)S(1)}, bf16[4,2,32,1024]{3,2,1,0:T(8,128)(2,1)S(1)}, u32[]{:S(2)}, u32[]{:S(2)}) collective-permute-start(bf16[4,2,32,1024]{3,2,1,0:T(8,128)(2,1)S(1)} %bitcast.24), channel_id=1, source_target_pairs={{0,1},{1,0},{2,3},{3,2},{4,5},{5,4},{6,7},{7,6},{8,9},{9,8},{10,11... | collective-permute-start | bytes 1572872 | tf_op jit(solution)/shard_map/ppermute | solution.py:240
  10.6 0.0 collective-permute-start.3
  10.6 8.1 %collective-permute-done.4 = bf16[8,64,512]{2,1,0:T(8,128)(2,1)S(1)} collective-permute-done((bf16[8,64,512]{2,1,0:T(8,128)(2,1)S(1)}, bf16[8,64,512]{2,1,0:T(8,128)(2,1)S(1)}, u32[]{:S(2)}, u32[]{:S(2)}) %collective-permute-start.4) | collective-permute-done | bytes 524320 | tf_op jit(solution)/shard_map/ppermute | solution.py:233
  18.7 0.0 collective-permute-start.5
  18.7 1.5 %collective-permute-done.refs_2_ = bf16[4,2,32,1024]{3,2,1,0:T(8,128)(2,1)S(1)} collective-permute-done((bf16[4,2,32,1024]{3,2,1,0:T(8,128)(2,1)S(1)}, bf16[4,2,32,1024]{3,2,1,0:T(8,128)(2,1)S(1)}, u32[]{:S(2)}, u32[]{:S(2)}) %collective-permute-start) | collective-permute-done | bytes 524320 | tf_op jit(solution)/shard_map/ppermute | solution.py:238
  20.2 0.0 collective-permute-done.1.second_ref
  20.2 2.1 %collective-permute-done.2.refs_1_ = bf16[4,2,32,1024]{3,2,1,0:T(8,128)(2,1)S(1)} collective-permute-done((bf16[4,2,32,1024]{3,2,1,0:T(8,128)(2,1)S(1)}, bf16[4,2,32,1024]{3,2,1,0:T(8,128)(2,1)S(1)}, u32[]{:S(2)}, u32[]{:S(2)}) %collective-permute-start.2) | collective-permute-done | bytes 524320 | tf_op jit(solution)/shard_map/ppermute | solution.py:240
  22.2 0.0 collective-permute-done.3
  22.2 1.3 %collective-permute-start.6 = (bf16[4,2,32,1024]{3,2,1,0:T(8,128)(2,1)S(1)}, bf16[4,2,32,1024]{3,2,1,0:T(8,128)(2,1)S(1)}, u32[]{:S(2)}, u32[]{:S(2)}) collective-permute-start(bf16[4,2,32,1024]{3,2,1,0:T(8,128)(2,1)S(1)} %collective-permute-done.1.second_ref), channel_id=1, source_target_pairs={{2,0},{3,1},{4,6},{5,7},{10,8},{11,9},{12,14},{13,15},{18,16},{19,... | collective-permute-start | bytes 1572872 | tf_op jit(solution)/shard_map/ppermute | solution.py:243
  23.5 1.6 %collective-permute-start.10 = (bf16[4,2,32,1024]{3,2,1,0:T(8,128)(2,1)S(1)}, bf16[4,2,32,1024]{3,2,1,0:T(8,128)(2,1)S(1)}, u32[]{:S(2)}, u32[]{:S(2)}) collective-permute-start(bf16[4,2,32,1024]{3,2,1,0:T(8,128)(2,1)S(1)} %collective-permute-done.refs_2_), channel_id=1, source_target_pairs={{0,1},{1,0},{2,3},{3,2},{4,5},{5,4},{6,7},{7,6},{8,9},{9,8},{10,11... | collective-permute-start | bytes 1572872 | tf_op jit(solution)/shard_map/ppermute | solution.py:245
  25.1 0.7 collective-permute-start.8
  25.8 0.0 collective-permute-done.5
  25.8 7.3 %adjoint.1 = (f32[4,2,4,64,1024]{4,3,2,1,0:T(8,128)S(1)}, bf16[4,2,32,1024]{3,2,1,0:T(8,128)(2,1)S(1)}) custom-call(s32[9]{0:T(128)S(1)} %stack.43.scalar_ref, bf16[4,1024,1024]{2,1,0:T(8,128)(2,1)} %bitcast.33, bf16[4,2,64,512]{3,2,1,0:T(8,128)(2,1)S(1)} %bitcast.26, bf16[4,2,64,512]{3,2,1,0:T(8,128)(2,1)S(1)} %bitcast.30, ...), custom_call_target="tpu_custom_call" | custom-call | flops 4294967296 | bytes 8388608 | tf_op jit(solution)/shard_map/adjoint/pallas_call | solution.py:138
  33.1 4.6 %collective-permute-done.6.first_ref = bf16[4,2,32,1024]{3,2,1,0:T(8,128)(2,1)S(1)} collective-permute-done((bf16[4,2,32,1024]{3,2,1,0:T(8,128)(2,1)S(1)}, bf16[4,2,32,1024]{3,2,1,0:T(8,128)(2,1)S(1)}, u32[]{:S(2)}, u32[]{:S(2)}) %collective-permute-start.6) | collective-permute-done | bytes 524320 | tf_op jit(solution)/shard_map/ppermute | solution.py:243
  37.7 0.6 pick.1.refs_4_
  38.3 1.6 %collective-permute-start.7 = (bf16[4,2,32,1024]{3,2,1,0:T(8,128)(2,1)S(1)}, bf16[4,2,32,1024]{3,2,1,0:T(8,128)(2,1)S(1)}, u32[]{:S(2)}, u32[]{:S(2)}) collective-permute-start(bf16[4,2,32,1024]{3,2,1,0:T(8,128)(2,1)S(1)} %pick.1.refs_4_), channel_id=1, source_target_pairs={{0,1},{1,0},{2,3},{3,2},{4,5},{5,4},{6,7},{7,6},{8,9},{9,8},{10,11... | collective-permute-start | bytes 1572872 | tf_op jit(solution)/shard_map/ppermute | solution.py:255
  39.9 1.9 %collective-permute-start.12 = (bf16[4,2,32,1024]{3,2,1,0:T(8,128)(2,1)S(1)}, bf16[4,2,32,1024]{3,2,1,0:T(8,128)(2,1)S(1)}, u32[]{:S(2)}, u32[]{:S(2)}) collective-permute-start(bf16[4,2,32,1024]{3,2,1,0:T(8,128)(2,1)S(1)} %get-tuple-element.27), channel_id=1, source_target_pairs={{0,2},{1,3},{6,4},{7,5},{8,10},{9,11},{14,12},{15,13},{16,18},{17,... | collective-permute-start | bytes 1572872 | tf_op jit(solution)/shard_map/ppermute | solution.py:251
  41.8 0.0 collective-permute-done.10.refs_3_
  41.9 0.7 %collective-permute-start.11 = (bf16[4,2,32,1024]{3,2,1,0:T(8,128)(2,1)S(1)}, bf16[4,2,32,1024]{3,2,1,0:T(8,128)(2,1)S(1)}, u32[]{:S(2)}, u32[]{:S(2)}) collective-permute-start(bf16[4,2,32,1024]{3,2,1,0:T(8,128)(2,1)S(1)} %collective-permute-done.10.refs_3_), channel_id=1, source_target_pairs={{2,4},{3,5},{4,2},{5,3},{10,12},{11,13},{12,10},{13,11},{18,20},{1... | collective-permute-start | bytes 1572872 | tf_op jit(solution)/shard_map/ppermute | solution.py:253
  42.6 0.0 collective-permute-done.8.refs_2_
  42.6 1.3 %collective-permute-start.9 = (bf16[4,2,32,1024]{3,2,1,0:T(8,128)(2,1)S(1)}, bf16[4,2,32,1024]{3,2,1,0:T(8,128)(2,1)S(1)}, u32[]{:S(2)}, u32[]{:S(2)}) collective-permute-start(bf16[4,2,32,1024]{3,2,1,0:T(8,128)(2,1)S(1)} %collective-permute-done.8.refs_2_), channel_id=1, source_target_pairs={{2,0},{3,1},{4,6},{5,7},{10,8},{11,9},{12,14},{13,15},{18,16},{19,... | collective-permute-start | bytes 1572872 | tf_op jit(solution)/shard_map/ppermute | solution.py:252
  43.9 1.5 %weigh.2.refs_5_ = f32[8,1024]{1,0:T(8,128)S(1)} custom-call(s32[9]{0:T(128)S(1)} %stack.43.scalar_ref, f32[4,2,8,32,1024]{4,3,2,1,0:T(8,128)S(1)} %bitcast.20, bf16[4,2,32,1024]{3,2,1,0:T(8,128)(2,1)S(1)} %bitcast.25, bf16[4,2,32,1024]{3,2,1,0:T(8,128)(2,1)S(1)} %collective-permute-done.2.refs_1_, ...), custom_call_target="tpu_custom_call" | custom-call | flops 5242880 | bytes 5242880 | tf_op jit(solution)/shard_map/weigh/pallas_call | solution.py:159
  45.3 4.3 %collective-permute-done.7.refs_0_ = bf16[4,2,32,1024]{3,2,1,0:T(8,128)(2,1)S(1)} collective-permute-done((bf16[4,2,32,1024]{3,2,1,0:T(8,128)(2,1)S(1)}, bf16[4,2,32,1024]{3,2,1,0:T(8,128)(2,1)S(1)}, u32[]{:S(2)}, u32[]{:S(2)}) %collective-permute-start.7) | collective-permute-done | bytes 524320 | tf_op jit(solution)/shard_map/ppermute | solution.py:255
  49.7 1.0 %collective-permute-done.12.refs_4_ = bf16[4,2,32,1024]{3,2,1,0:T(8,128)(2,1)S(1)} collective-permute-done((bf16[4,2,32,1024]{3,2,1,0:T(8,128)(2,1)S(1)}, bf16[4,2,32,1024]{3,2,1,0:T(8,128)(2,1)S(1)}, u32[]{:S(2)}, u32[]{:S(2)}) %collective-permute-start.12) | collective-permute-done | bytes 524320 | tf_op jit(solution)/shard_map/ppermute | solution.py:251
  50.6 0.0 collective-permute-done.11.refs_3_
  50.7 4.9 %collective-permute-done.9.refs_1_ = bf16[4,2,32,1024]{3,2,1,0:T(8,128)(2,1)S(1)} collective-permute-done((bf16[4,2,32,1024]{3,2,1,0:T(8,128)(2,1)S(1)}, bf16[4,2,32,1024]{3,2,1,0:T(8,128)(2,1)S(1)}, u32[]{:S(2)}, u32[]{:S(2)}) %collective-permute-start.9) | collective-permute-done | bytes 524320 | tf_op jit(solution)/shard_map/ppermute | solution.py:252
  55.5 1.0 %weigh.3 = f32[1,1024]{1,0:T(1,128)S(1)} custom-call(s32[9]{0:T(128)S(1)} %stack.43.scalar_ref, f32[4,2,8,32,1024]{4,3,2,1,0:T(8,128)S(1)} %bitcast.21, bf16[4,2,32,1024]{3,2,1,0:T(8,128)(2,1)S(1)} %collective-permute-done.7.refs_0_, bf16[4,2,32,1024]{3,2,1,0:T(8,128)(2,1)S(1)} %collective-permute-done.9.refs_1_, ...), custom_call_target="tpu_custom_call" | custom-call | flops 5275648 | bytes 5275648 | tf_op jit(solution)/shard_map/weigh/pallas_call | solution.py:159
  56.6 1.6 %collective-permute-start.13 = (f32[1024]{0:T(1024)S(1)}, f32[1024]{0:T(1024)S(1)}, u32[]{:S(2)}, u32[]{:S(2)}) collective-permute-start(f32[1024]{0:T(1024)S(1)} %bitcast.27), channel_id=1, source_target_pairs={{0,1},{1,0},{2,3},{3,2},{4,5},{5,4},{6,7},{7,6},{8,9},{9,8},{10,11... | collective-permute-start | bytes 12296 | tf_op jit(solution)/shard_map/ppermute | solution.py:275
  58.1 2.1 %collective-permute-done.13 = f32[1024]{0:T(1024)S(1)} collective-permute-done((f32[1024]{0:T(1024)S(1)}, f32[1024]{0:T(1024)S(1)}, u32[]{:S(2)}, u32[]{:S(2)}) %collective-permute-start.13) | collective-permute-done | bytes 4128 | tf_op jit(solution)/shard_map/ppermute | solution.py:275
  60.2 0.0 collective-permute-start.14
  60.2 3.6 %collective-permute-done.14 = f32[1024]{0:T(1024)S(1)} collective-permute-done((f32[1024]{0:T(1024)S(1)}, f32[1024]{0:T(1024)S(1)}, u32[]{:S(2)}, u32[]{:S(2)}) %collective-permute-start.14) | collective-permute-done | bytes 4128 | tf_op jit(solution)/shard_map/ppermute | solution.py:275
  63.8 0.9 %collective-permute-start.15 = (f32[1024]{0:T(1024)S(1)}, f32[1024]{0:T(1024)S(1)}, u32[]{:S(2)}, u32[]{:S(2)}) collective-permute-start(f32[1024]{0:T(1024)S(1)} %add.48), channel_id=1, source_target_pairs={{0,4},{1,5},{2,6},{3,7},{4,0},{5,1},{6,2},{7,3},{8,12},{9,13},{10,... | collective-permute-start | bytes 12296 | tf_op jit(solution)/shard_map/ppermute | solution.py:275
  64.7 3.6 %collective-permute-done.15 = f32[1024]{0:T(1024)S(1)} collective-permute-done((f32[1024]{0:T(1024)S(1)}, f32[1024]{0:T(1024)S(1)}, u32[]{:S(2)}, u32[]{:S(2)}) %collective-permute-start.15) | collective-permute-done | bytes 4128 | tf_op jit(solution)/shard_map/ppermute | solution.py:275
  68.3 0.6 add.49
  (2 shorter events, 0.0 us)
Async XLA Ops:
  3.8 14.9 %collective-permute-start.4 = (bf16[8,64,512]{2,1,0:T(8,128)(2,1)S(1)}, bf16[8,64,512]{2,1,0:T(8,128)(2,1)S(1)}, u32[]{:S(2)}, u32[]{:S(2)}) collective-permute-start(bf16[8,64,512]{2,1,0:T(8,128)(2,1)S(1)} %spectra.1), channel_id=1, source_target_pairs={{0,16},{8,24},{16,0},{24,8},{1,17},{9,25},{17,1},{25,9},{2,18},{10... | collective-permute-start | bytes 1572872 | tf_op jit(solution)/shard_map/ppermute | solution.py:233
  6.8 13.4 %collective-permute-start = (bf16[4,2,32,1024]{3,2,1,0:T(8,128)(2,1)S(1)}, bf16[4,2,32,1024]{3,2,1,0:T(8,128)(2,1)S(1)}, u32[]{:S(2)}, u32[]{:S(2)}) collective-permute-start(bf16[4,2,32,1024]{3,2,1,0:T(8,128)(2,1)S(1)} %bitcast.22), channel_id=1, source_target_pairs={{0,2},{1,3},{2,0},{3,1},{4,6},{5,7},{6,4},{7,5},{8,10},{9,11},{10,... | collective-permute-start | bytes 1572872 | tf_op jit(solution)/shard_map/ppermute | solution.py:238
  8.4 11.8 %collective-permute-start.1 = (bf16[4,2,32,1024]{3,2,1,0:T(8,128)(2,1)S(1)}, bf16[4,2,32,1024]{3,2,1,0:T(8,128)(2,1)S(1)}, u32[]{:S(2)}, u32[]{:S(2)}) collective-permute-start(bf16[4,2,32,1024]{3,2,1,0:T(8,128)(2,1)S(1)} %bitcast.23), channel_id=1, source_target_pairs={{2,4},{3,5},{4,2},{5,3},{10,12},{11,13},{12,10},{13,11},{18,20},{1... | collective-permute-start | bytes 1572872 | tf_op jit(solution)/shard_map/ppermute | solution.py:239
  9.1 13.2 %collective-permute-start.2 = (bf16[4,2,32,1024]{3,2,1,0:T(8,128)(2,1)S(1)}, bf16[4,2,32,1024]{3,2,1,0:T(8,128)(2,1)S(1)}, u32[]{:S(2)}, u32[]{:S(2)}) collective-permute-start(bf16[4,2,32,1024]{3,2,1,0:T(8,128)(2,1)S(1)} %bitcast.24), channel_id=1, source_target_pairs={{0,1},{1,0},{2,3},{3,2},{4,5},{5,4},{6,7},{7,6},{8,9},{9,8},{10,11... | collective-permute-start | bytes 1572872 | tf_op jit(solution)/shard_map/ppermute | solution.py:240
  10.6 11.6 %collective-permute-start.3 = (bf16[8,64,512]{2,1,0:T(8,128)(2,1)S(1)}, bf16[8,64,512]{2,1,0:T(8,128)(2,1)S(1)}, u32[]{:S(2)}, u32[]{:S(2)}) collective-permute-start(bf16[8,64,512]{2,1,0:T(8,128)(2,1)S(1)} %spectra.1), channel_id=1, source_target_pairs={{0,8},{8,0},{16,24},{24,16},{1,9},{9,1},{17,25},{25,17},{2,10},{10... | collective-permute-start | bytes 1572872 | tf_op jit(solution)/shard_map/ppermute | solution.py:234
  18.7 7.1 %collective-permute-start.5 = (bf16[8,64,512]{2,1,0:T(8,128)(2,1)S(1)}, bf16[8,64,512]{2,1,0:T(8,128)(2,1)S(1)}, u32[]{:S(2)}, u32[]{:S(2)}) collective-permute-start(bf16[8,64,512]{2,1,0:T(8,128)(2,1)S(1)} %collective-permute-done.4), channel_id=1, source_target_pairs={{0,8},{8,0},{16,24},{24,16},{1,9},{9,1},{17,25},{25,17},{2,10},{10... | collective-permute-start | bytes 1572872 | tf_op jit(solution)/shard_map/ppermute | solution.py:235
  22.2 15.5 %collective-permute-start.6 = (bf16[4,2,32,1024]{3,2,1,0:T(8,128)(2,1)S(1)}, bf16[4,2,32,1024]{3,2,1,0:T(8,128)(2,1)S(1)}, u32[]{:S(2)}, u32[]{:S(2)}) collective-permute-start(bf16[4,2,32,1024]{3,2,1,0:T(8,128)(2,1)S(1)} %collective-permute-done.1.second_ref), channel_id=1, source_target_pairs={{2,0},{3,1},{4,6},{5,7},{10,8},{11,9},{12,14},{13,15},{18,16},{19,... | collective-permute-start | bytes 1572872 | tf_op jit(solution)/shard_map/ppermute | solution.py:243
  23.5 18.3 %collective-permute-start.10 = (bf16[4,2,32,1024]{3,2,1,0:T(8,128)(2,1)S(1)}, bf16[4,2,32,1024]{3,2,1,0:T(8,128)(2,1)S(1)}, u32[]{:S(2)}, u32[]{:S(2)}) collective-permute-start(bf16[4,2,32,1024]{3,2,1,0:T(8,128)(2,1)S(1)} %collective-permute-done.refs_2_), channel_id=1, source_target_pairs={{0,1},{1,0},{2,3},{3,2},{4,5},{5,4},{6,7},{7,6},{8,9},{9,8},{10,11... | collective-permute-start | bytes 1572872 | tf_op jit(solution)/shard_map/ppermute | solution.py:245
  25.1 17.5 %collective-permute-start.8 = (bf16[4,2,32,1024]{3,2,1,0:T(8,128)(2,1)S(1)}, bf16[4,2,32,1024]{3,2,1,0:T(8,128)(2,1)S(1)}, u32[]{:S(2)}, u32[]{:S(2)}) collective-permute-start(bf16[4,2,32,1024]{3,2,1,0:T(8,128)(2,1)S(1)} %collective-permute-done.refs_2_), channel_id=1, source_target_pairs={{2,4},{3,5},{4,2},{5,3},{10,12},{11,13},{12,10},{13,11},{18,20},{1... | collective-permute-start | bytes 1572872 | tf_op jit(solution)/shard_map/ppermute | solution.py:244
  38.3 11.3 %collective-permute-start.7 = (bf16[4,2,32,1024]{3,2,1,0:T(8,128)(2,1)S(1)}, bf16[4,2,32,1024]{3,2,1,0:T(8,128)(2,1)S(1)}, u32[]{:S(2)}, u32[]{:S(2)}) collective-permute-start(bf16[4,2,32,1024]{3,2,1,0:T(8,128)(2,1)S(1)} %pick.1.refs_4_), channel_id=1, source_target_pairs={{0,1},{1,0},{2,3},{3,2},{4,5},{5,4},{6,7},{7,6},{8,9},{9,8},{10,11... | collective-permute-start | bytes 1572872 | tf_op jit(solution)/shard_map/ppermute | solution.py:255
  39.9 10.7 %collective-permute-start.12 = (bf16[4,2,32,1024]{3,2,1,0:T(8,128)(2,1)S(1)}, bf16[4,2,32,1024]{3,2,1,0:T(8,128)(2,1)S(1)}, u32[]{:S(2)}, u32[]{:S(2)}) collective-permute-start(bf16[4,2,32,1024]{3,2,1,0:T(8,128)(2,1)S(1)} %get-tuple-element.27), channel_id=1, source_target_pairs={{0,2},{1,3},{6,4},{7,5},{8,10},{9,11},{14,12},{15,13},{16,18},{17,... | collective-permute-start | bytes 1572872 | tf_op jit(solution)/shard_map/ppermute | solution.py:251
  41.9 8.8 %collective-permute-start.11 = (bf16[4,2,32,1024]{3,2,1,0:T(8,128)(2,1)S(1)}, bf16[4,2,32,1024]{3,2,1,0:T(8,128)(2,1)S(1)}, u32[]{:S(2)}, u32[]{:S(2)}) collective-permute-start(bf16[4,2,32,1024]{3,2,1,0:T(8,128)(2,1)S(1)} %collective-permute-done.10.refs_3_), channel_id=1, source_target_pairs={{2,4},{3,5},{4,2},{5,3},{10,12},{11,13},{12,10},{13,11},{18,20},{1... | collective-permute-start | bytes 1572872 | tf_op jit(solution)/shard_map/ppermute | solution.py:253
  42.6 12.9 %collective-permute-start.9 = (bf16[4,2,32,1024]{3,2,1,0:T(8,128)(2,1)S(1)}, bf16[4,2,32,1024]{3,2,1,0:T(8,128)(2,1)S(1)}, u32[]{:S(2)}, u32[]{:S(2)}) collective-permute-start(bf16[4,2,32,1024]{3,2,1,0:T(8,128)(2,1)S(1)} %collective-permute-done.8.refs_2_), channel_id=1, source_target_pairs={{2,0},{3,1},{4,6},{5,7},{10,8},{11,9},{12,14},{13,15},{18,16},{19,... | collective-permute-start | bytes 1572872 | tf_op jit(solution)/shard_map/ppermute | solution.py:252
  56.6 3.7 %collective-permute-start.13 = (f32[1024]{0:T(1024)S(1)}, f32[1024]{0:T(1024)S(1)}, u32[]{:S(2)}, u32[]{:S(2)}) collective-permute-start(f32[1024]{0:T(1024)S(1)} %bitcast.27), channel_id=1, source_target_pairs={{0,1},{1,0},{2,3},{3,2},{4,5},{5,4},{6,7},{7,6},{8,9},{9,8},{10,11... | collective-permute-start | bytes 12296 | tf_op jit(solution)/shard_map/ppermute | solution.py:275
  60.2 3.6 %collective-permute-start.14 = (f32[1024]{0:T(1024)S(1)}, f32[1024]{0:T(1024)S(1)}, u32[]{:S(2)}, u32[]{:S(2)}) collective-permute-start(f32[1024]{0:T(1024)S(1)} %add.47), channel_id=1, source_target_pairs={{0,2},{1,3},{2,0},{3,1},{4,6},{5,7},{6,4},{7,5},{8,10},{9,11},{10,... | collective-permute-start | bytes 12296 | tf_op jit(solution)/shard_map/ppermute | solution.py:275
  63.8 4.5 %collective-permute-start.15 = (f32[1024]{0:T(1024)S(1)}, f32[1024]{0:T(1024)S(1)}, u32[]{:S(2)}, u32[]{:S(2)}) collective-permute-start(f32[1024]{0:T(1024)S(1)} %add.48), channel_id=1, source_target_pairs={{0,4},{1,5},{2,6},{3,7},{4,0},{5,1},{6,2},{7,3},{8,12},{9,13},{10,... | collective-permute-start | bytes 12296 | tf_op jit(solution)/shard_map/ppermute | solution.py:275

commit v7 on v6

--- a/solution.py
+++ b/solution.py
@@ -105,14 +105,12 @@
     )
 
 
-def adjoint_kernel(count, half, scalar_ref, green_hbm, *refs):
-    spectra_refs, (out_ref, block_ref, green_ref, arrived) = refs[:count], refs[count:]
+def adjoint_kernel(count, green_hbm_ref, *refs):
+    spectra_refs, (out_ref, green_ref, arrived) = refs[:count], refs[count:]
     freqs, _, rows, _ = spectra_refs[0].shape
-    block = scalar_ref[FAR_Y]
-    group, first = block // 2, pl.multiple_of((block % 2) * half, half)
 
     def fetch(freq):
-        return pltpu.make_async_copy(green_hbm.at[freq], green_ref.at[freq], arrived.at[freq])
+        return pltpu.make_async_copy(green_hbm_ref.at[freq], green_ref.at[freq], arrived.at[freq])
 
     for freq in range(freqs):
         fetch(freq).start()
@@ -122,7 +120,21 @@
         fetch(freq).wait()
         left = complex_rows(spectra_refs, freq)
         sums = jnp.dot(left, green_ref[freq], preferred_element_type=jnp.float32)
-        out_ref[freq] = sums.reshape(2, count, rows, -1)
+        out_ref[freq, :, :count] = sums.reshape(2, count, rows, -1)
+
+
+def adjoint_rest_kernel(count, half, scalar_ref, green_ref, base_ref, *refs):
+    spectra_refs, (out_ref, block_ref) = refs[:count], refs[count:]
+    del base_ref
+    freqs, _, rows, _ = spectra_refs[0].shape
+    block = scalar_ref[FAR_Y]
+    group, first = block // 2, pl.multiple_of((block % 2) * half, half)
+
+    @pl.loop(0, freqs)
+    def _(freq):
+        left = complex_rows(spectra_refs, freq)
+        sums = jnp.dot(left, green_ref[freq], preferred_element_type=jnp.float32)
+        out_ref[freq, :, count:] = sums.reshape(2, count, rows, -1)
         block_ref[freq] = out_ref[freq, :, group, pl.ds(first, half)].astype(block_ref.dtype)
 
 
@@ -130,29 +142,53 @@
     return [pltpu.with_memory_space_constraint(array, pltpu.VMEM) for array in arrays]
 
 
-def adjoint_of(scalars, pieces, green):
+def adjoint_of(pieces, green, groups):
     freqs, _, recv, cells = green.shape
     rows, count = pieces[0].shape[1], len(pieces)
-    half = rows // 2
     green = green.reshape(freqs, 2 * recv, cells)
     return pl.pallas_call(
-        functools.partial(adjoint_kernel, count, half),
-        in_specs=[pl.BlockSpec(memory_space=pltpu.SMEM), pl.BlockSpec(memory_space=pltpu.HBM)]
+        functools.partial(adjoint_kernel, count),
+        in_specs=[pl.BlockSpec(memory_space=pltpu.HBM)]
         + [pl.BlockSpec(memory_space=pltpu.VMEM)] * count,
         out_specs=[pl.BlockSpec(memory_space=pltpu.VMEM)] * 2,
         out_shape=[
-            pltpu.VMEM((freqs, 2, count, rows, cells), jnp.float32),
-            pltpu.VMEM((freqs, 2, half, cells), jnp.bfloat16),
+            pltpu.VMEM((freqs, 2, groups, rows, cells), jnp.float32),
+            pltpu.VMEM(green.shape, green.dtype),
         ],
-        scratch_shapes=[pltpu.VMEM(green.shape, green.dtype), pltpu.SemaphoreType.DMA((freqs,))],
-        compiler_params=pltpu.CompilerParams(vmem_limit_bytes=24 << 20),
+        scratch_shapes=[pltpu.SemaphoreType.DMA((freqs,))],
+        compiler_params=pltpu.CompilerParams(vmem_limit_bytes=4 * count << 20),
         cost_estimate=pl.CostEstimate(
             flops=8 * freqs * count * rows * recv * cells,
             bytes_accessed=4 * freqs * recv * cells,
             transcendentals=0,
         ),
         name="adjoint",
-    )(scalars, in_hbm(green), *in_vmem_all([piece.reshape(freqs, 2, rows, recv) for piece in pieces]))
+    )(in_hbm(green), *in_vmem_all([piece.reshape(freqs, 2, rows, recv) for piece in pieces]))
+
+
+def adjoint_rest(scalars, pieces, green, base):
+    freqs, _, groups, rows, cells = base.shape
+    recv, count = pieces[0].shape[2], len(pieces)
+    half = rows // 2
+    pieces = [piece.reshape(freqs, 2, rows, recv) for piece in pieces]
+    return pl.pallas_call(
+        functools.partial(adjoint_rest_kernel, count, half),
+        in_specs=[pl.BlockSpec(memory_space=pltpu.SMEM)]
+        + [pl.BlockSpec(memory_space=pltpu.VMEM)] * (count + 2),
+        out_specs=[pl.BlockSpec(memory_space=pltpu.VMEM)] * 2,
+        out_shape=[
+            pltpu.VMEM(base.shape, base.dtype),
+            pltpu.VMEM((freqs, 2, half, cells), jnp.bfloat16),
+        ],
+        input_output_aliases={2: 0},
+        compiler_params=pltpu.CompilerParams(vmem_limit_bytes=8 << 20),
+        cost_estimate=pl.CostEstimate(
+            flops=8 * freqs * count * rows * recv * cells,
+            bytes_accessed=4 * freqs * recv * cells,
+            transcendentals=0,
+        ),
+        name="adjoint_rest",
+    )(scalars, *in_vmem_all([green, base, *pieces]))
 
 
 def in_vmem(kernel, scalars, operands, shape, dtype, name):
@@ -213,9 +249,9 @@
     z_pairs = [(r, r ^ 2) for r in range(8)]
     z_middle = [(r, r ^ 6) for r in range(2, 6)]
     z_outward = [(2, 0), (3, 1), (4, 6), (5, 7)]
-    z_inward = [(there, here) for here, there in z_outward]
     core = [(t, t ^ 1) for t in range(4)]
     along_x = [(t, t ^ 2) for t in range(4)]
+    along_both = [(t, t ^ 3) for t in range(4)]
     send, tie = lax.ppermute, lax.optimization_barrier
 
     me_tx, me_rx = lax.axis_index("tx"), lax.axis_index("rx")
@@ -230,26 +266,24 @@
     own = background.transpose(1, 2, 0, 3)
     own, scalars, records = tie((own, scalars, records))
     spectra = spectra_of(records, active, freqs)
+    spectra_both = send(spectra, "tx", along_both)
     spectra_x = send(spectra, "tx", along_x)
     spectra_core = send(spectra, "tx", core)
-    spectra_both = send(spectra_x, "tx", core)
-
-    own, _ = tie((own, spectra))
     near = send(own, "rx", z_pairs)
     across = send(own, "rx", z_middle)
     own_y = send(own, "rx", along_y)
-    near, across, own_y, spectra_core = tie((near, across, own_y, spectra_core))
+    near, across, own_y, spectra = tie((near, across, own_y, spectra))
 
     across_out = send(across, "rx", z_outward)
     far = send(near, "rx", z_middle)
     near_y = send(near, "rx", along_y)
 
-    adjoint, partial = adjoint_of(scalars, [spectra, spectra_core, spectra_x, spectra_both], green)
-    across_out, partial = tie((across_out, partial))
+    adjoint, green_kept = adjoint_of([spectra, spectra_core], green, 4)
+    adjoint, partial = adjoint_rest(scalars, [spectra_x, spectra_both], green_kept, adjoint)
     adjoint = adjoint.reshape((freqs, 2, 8) + own.shape[2:])
 
-    partial = send(partial, "rx", z_inward)
-    far_out = send(far, "rx", z_outward)
+    swap = in_vmem(pick_kernel, scalars, [partial, far], own.shape, own.dtype, "pick")
+    swap = send(swap, "rx", z_pairs)
     far_both = send(near_y, "rx", z_middle)
     mid = in_vmem(pick_kernel, scalars, [across_out, across], own.shape, own.dtype, "pick")
     mid_y = send(mid, "rx", along_y)
@@ -265,7 +299,7 @@
     sums = in_vmem(
         functools.partial(weigh_kernel, ((MID_Y, 1), (FAR, 2), (FAR_Y, 1)), False, True),
         scalars,
-        [adjoint, mid_y, far_out, far, far_both, partial, sums],
+        [adjoint, mid_y, swap, far, far_both, swap, sums],
         (1, cells),
         jnp.float32,
         "weigh",
@@ -280,8 +314,7 @@
     freqs = green.shape[0]
     spectra = spectra_of(records, active, freqs)
     pieces = lax.all_gather(spectra, "tx", axis=0)
-    scalars = jnp.zeros(MIDDLE + 1, jnp.int32)
-    adjoint, _ = adjoint_of(scalars, [pieces[t] for t in range(pieces.shape[0])], green)
+    adjoint, _ = adjoint_of([pieces[t] for t in range(pieces.shape[0])], green, pieces.shape[0])
     freqs, _, groups, rows, cells = adjoint.shape
     adjoint = adjoint.reshape(freqs, 2, groups * rows, cells)
     fields = lax.all_gather(background, "rx", axis=0, tiled=True)

time: 69.2 us -> 71.6 us (1.035)
  starting transfers between devices: 18.4 us -> 21.7 us
  waiting for transfers between devices: 35.7 us -> 33.5 us
  Pallas kernels: 12.7 us -> 14 us
    ppermute x3 -> x2, waiting for transfers between devices: 5.85 us -> 16.6 us  [the longest x1 8.98 us: box_shards(): swap = send(swap, 'rx', z_pairs)]
    ppermute x1, waiting for transfers between devices: 8.07 us -> 0.01 us  [box_shards(): spectra_x = send(spectra, 'tx', along_x)]
    ppermute x1, waiting for transfers between devices: 4.64 us -> 0.01 us  [box_shards(): across_out = send(across, 'rx', z_outward)]
    ppermute x1, waiting for transfers between devices: 1.46 us -> 5.66 us  [box_shards(): near = send(own, 'rx', z_pairs)]
    ppermute x3, starting transfers between devices: 2.48 us -> 5.29 us  [box_shards(): sums = sums + send(sums, 'rx', [(r, r ^ bit) for r in range(8)])]
    ppermute x1, waiting for transfers between devices: 4.33 us -> 2.12 us  [box_shards(): mid_y = send(mid, 'rx', along_y)]
    ppermute x3, waiting for transfers between devices: 9.31 us -> 7.16 us  [box_shards(): sums = sums + send(sums, 'rx', [(r, r ^ bit) for r in range(8)])]
    ppermute x1, starting transfers between devices: 1.59 us -> 3.03 us  [box_shards(): near = send(own, 'rx', z_pairs)]
  transfers between devices with their start and end apart: 16 -> 15, of which waited for: 10 -> 8; matrix products, arithmetic and copies ran while one was open for 0% -> 0% of each run, Pallas kernels for 14% -> 18%
where the time goes in v7:
time: 71.6 us; the launch traced here: 71.4 us
  waiting for transfers between devices  33.5 us (47%)
  starting transfers between devices  21.7 us (30%)
  Pallas kernels  14 us (20%)
  local copies, waits for them, and re-layouts  1.42 us (2%)
    ppermute x1, waiting for transfers between devices, box_shards(): swap = send(swap, 'rx', z_pairs)  8.98 us
    ppermute x1, waiting for transfers between devices, box_shards(): spectra_both = send(spectra, 'tx', along_both)  7.61 us
    ppermute x3, waiting for transfers between devices, box_shards(): sums = sums + send(sums, 'rx', [(r, r ^ bit) for r in range(8)])  7.16 us
    ppermute x1, waiting for transfers between devices, box_shards(): near = send(own, 'rx', z_pairs)  5.66 us
    ppermute x3, starting transfers between devices, box_shards(): sums = sums + send(sums, 'rx', [(r, r ^ bit) for r in range(8)])  5.29 us
    pallas_call x1, Pallas kernels, adjoint_of(): pl.pallas_call(functools.partial(adjoint_kernel, count), in_specs=[pl.Blo...  4.48 us
    ppermute x1, starting transfers between devices, box_shards(): swap = send(swap, 'rx', z_pairs)  4.43 us
    pallas_call x4, Pallas kernels, in_vmem(): pl.pallas_call(kernel, in_specs=[pl.BlockSpec(memory_space=pltpu.SMEM)] +...  3.74 us
  transfers between devices with their start and end apart: 15, of which 8 were waited for; matrix products, arithmetic and copies ran while one was open for 0% of the time, Pallas kernels for 18%

profile of v7, /device:TPU:0, one launch (start us, length us, event | category | flops | bytes accessed | tf_op | source)
XLA Modules:
  0.0 71.4 jit_solution(5572973039923230775)
XLA Ops:
  0.0 1.3 %copy.9 = bf16[32,4,2,1024]{3,0,2,1:T(8,128)(2,1)S(1)} copy(bf16[32,4,2,1024]{3,2,1,0:T(2,128)(2,1)} %param.8) | data formatting | bytes 1048576 | tf_op args[3]
  1.3 0.1 stack.43.scalar_ref
  1.4 3.0 %collective-permute-start = (bf16[4,2,32,1024]{3,2,1,0:T(8,128)(2,1)S(1)}, bf16[4,2,32,1024]{3,2,1,0:T(8,128)(2,1)S(1)}, u32[]{:S(2)}, u32[]{:S(2)}) collective-permute-start(bf16[4,2,32,1024]{3,2,1,0:T(8,128)(2,1)S(1)} %bitcast.23), channel_id=1, source_target_pairs={{0,2},{1,3},{2,0},{3,1},{4,6},{5,7},{6,4},{7,5},{8,10},{9,11},{10,... | collective-permute-start | bytes 1572872 | tf_op jit(solution)/shard_map/ppermute | solution.py:272
  4.5 0.7 collective-permute-start.1
  5.1 1.6 %collective-permute-start.2 = (bf16[4,2,32,1024]{3,2,1,0:T(8,128)(2,1)S(1)}, bf16[4,2,32,1024]{3,2,1,0:T(8,128)(2,1)S(1)}, u32[]{:S(2)}, u32[]{:S(2)}) collective-permute-start(bf16[4,2,32,1024]{3,2,1,0:T(8,128)(2,1)S(1)} %bitcast.25), channel_id=1, source_target_pairs={{0,1},{1,0},{2,3},{3,2},{4,5},{5,4},{6,7},{7,6},{8,9},{9,8},{10,11... | collective-permute-start | bytes 1572872 | tf_op jit(solution)/shard_map/ppermute | solution.py:274
  6.7 2.3 %spectra.1 = bf16[8,64,512]{2,1,0:T(8,128)(2,1)S(1)} custom-call(bf16[128,640]{1,0:T(8,128)(2,1)} %constant.38.clone.table_hbm, s32[8,64]{1,0:T(8,128)} %bitcast.33, bf16[40,64,512]{2,1,0:T(8,128)(2,1)} %records_hbm), custom_call_target="tpu_custom_call" | custom-call | flops 335544320 | bytes 3145728 | tf_op jit(solution)/shard_map/spectra/pallas_call | solution.py:78
  9.1 0.1 collective-permute-start.3
  9.2 1.6 %collective-permute-start.4 = (bf16[8,64,512]{2,1,0:T(8,128)(2,1)S(1)}, bf16[8,64,512]{2,1,0:T(8,128)(2,1)S(1)}, u32[]{:S(2)}, u32[]{:S(2)}) collective-permute-start(bf16[8,64,512]{2,1,0:T(8,128)(2,1)S(1)} %spectra.1), channel_id=1, source_target_pairs={{0,16},{8,24},{16,0},{24,8},{1,17},{9,25},{17,1},{25,9},{2,18},{10... | collective-permute-start | bytes 1572872 | tf_op jit(solution)/shard_map/ppermute | solution.py:270
  10.7 5.7 %collective-permute-done.refs_2_ = bf16[4,2,32,1024]{3,2,1,0:T(8,128)(2,1)S(1)} collective-permute-done((bf16[4,2,32,1024]{3,2,1,0:T(8,128)(2,1)S(1)}, bf16[4,2,32,1024]{3,2,1,0:T(8,128)(2,1)S(1)}, u32[]{:S(2)}, u32[]{:S(2)}) %collective-permute-start) | collective-permute-done | bytes 524320 | tf_op jit(solution)/shard_map/ppermute | solution.py:272
  16.4 0.2 collective-permute-start.5
  16.6 0.0 collective-permute-done.1.second_ref
  16.6 2.0 %collective-permute-done.2.refs_1_ = bf16[4,2,32,1024]{3,2,1,0:T(8,128)(2,1)S(1)} collective-permute-done((bf16[4,2,32,1024]{3,2,1,0:T(8,128)(2,1)S(1)}, bf16[4,2,32,1024]{3,2,1,0:T(8,128)(2,1)S(1)}, u32[]{:S(2)}, u32[]{:S(2)}) %collective-permute-start.2) | collective-permute-done | bytes 524320 | tf_op jit(solution)/shard_map/ppermute | solution.py:274
  18.6 0.7 collective-permute-start.8
  19.3 1.3 %collective-permute-start.6 = (bf16[4,2,32,1024]{3,2,1,0:T(8,128)(2,1)S(1)}, bf16[4,2,32,1024]{3,2,1,0:T(8,128)(2,1)S(1)}, u32[]{:S(2)}, u32[]{:S(2)}) collective-permute-start(bf16[4,2,32,1024]{3,2,1,0:T(8,128)(2,1)S(1)} %collective-permute-done.1.second_ref), channel_id=1, source_target_pairs={{2,0},{3,1},{4,6},{5,7},{10,8},{11,9},{12,14},{13,15},{18,16},{19,... | collective-permute-start | bytes 1572872 | tf_op jit(solution)/shard_map/ppermute | solution.py:277
  20.6 0.0 collective-permute-done.3
  20.6 1.6 %collective-permute-start.10 = (bf16[4,2,32,1024]{3,2,1,0:T(8,128)(2,1)S(1)}, bf16[4,2,32,1024]{3,2,1,0:T(8,128)(2,1)S(1)}, u32[]{:S(2)}, u32[]{:S(2)}) collective-permute-start(bf16[4,2,32,1024]{3,2,1,0:T(8,128)(2,1)S(1)} %collective-permute-done.refs_2_), channel_id=1, source_target_pairs={{0,1},{1,0},{2,3},{3,2},{4,5},{5,4},{6,7},{7,6},{8,9},{9,8},{10,11... | collective-permute-start | bytes 1572872 | tf_op jit(solution)/shard_map/ppermute | solution.py:279
  22.2 4.5 %adjoint.1 = (f32[4,2,4,64,1024]{4,3,2,1,0:T(8,128)S(1)}, bf16[4,1024,1024]{2,1,0:T(8,128)(2,1)S(1)}) custom-call(bf16[4,1024,1024]{2,1,0:T(8,128)(2,1)} %bitcast.32, bf16[4,2,64,512]{3,2,1,0:T(8,128)(2,1)S(1)} %bitcast.22, bf16[4,2,64,512]{3,2,1,0:T(8,128)(2,1)S(1)} %bitcast.29), custom_call_target="tpu_custom_call" | custom-call | flops 2147483648 | bytes 8388608 | tf_op jit(solution)/shard_map/adjoint/pallas_call | solution.py:149
  26.7 0.0 collective-permute-done.4
  26.7 7.6 %collective-permute-done.5 = bf16[8,64,512]{2,1,0:T(8,128)(2,1)S(1)} collective-permute-done((bf16[8,64,512]{2,1,0:T(8,128)(2,1)S(1)}, bf16[8,64,512]{2,1,0:T(8,128)(2,1)S(1)}, u32[]{:S(2)}, u32[]{:S(2)}) %collective-permute-start.5) | collective-permute-done | bytes 524320 | tf_op jit(solution)/shard_map/ppermute | solution.py:269
  34.3 3.4 %adjoint_rest.1 = (f32[4,2,4,64,1024]{4,3,2,1,0:T(8,128)S(1)}, bf16[4,2,32,1024]{3,2,1,0:T(8,128)(2,1)S(1)}) custom-call(s32[9]{0:T(128)S(1)} %stack.43.scalar_ref, bf16[4,1024,1024]{2,1,0:T(8,128)(2,1)S(1)} %get-tuple-element.20.green_ref, f32[4,2,4,64,1024]{4,3,2,1,0:T(8,128)S(1)} %get-tuple-element.21.base_ref, ...), custom_call_target="tpu_custom_call", output_to_operand_aliasing={{0}: (2, {})} | custom-call | flops 2147483648 | bytes 8388608 | tf_op jit(solution)/shard_map/adjoint_rest/pallas_call | solution.py:174
  37.7 0.0 collective-permute-done.8.second_ref.refs_2_
  37.7 0.6 pick.3
  38.3 4.4 %collective-permute-start.9 = (bf16[4,2,32,1024]{3,2,1,0:T(8,128)(2,1)S(1)}, bf16[4,2,32,1024]{3,2,1,0:T(8,128)(2,1)S(1)}, u32[]{:S(2)}, u32[]{:S(2)}) collective-permute-start(bf16[4,2,32,1024]{3,2,1,0:T(8,128)(2,1)S(1)} %pick.3), channel_id=1, source_target_pairs={{0,2},{1,3},{2,0},{3,1},{4,6},{5,7},{6,4},{7,5},{8,10},{9,11},{10,... | collective-permute-start | bytes 1572872 | tf_op jit(solution)/shard_map/ppermute | solution.py:286
  42.8 0.0 collective-permute-done.6.first_ref
  42.8 0.6 pick.2.refs_4_
  43.4 0.6 collective-permute-start.7
  43.9 0.0 collective-permute-done.10.refs_3_
  43.9 0.7 collective-permute-start.11
  44.6 1.5 %weigh.2.refs_5_ = f32[8,1024]{1,0:T(8,128)S(1)} custom-call(s32[9]{0:T(128)S(1)} %stack.43.scalar_ref, f32[4,2,8,32,1024]{4,3,2,1,0:T(8,128)S(1)} %bitcast.20, bf16[4,2,32,1024]{3,2,1,0:T(8,128)(2,1)S(1)} %bitcast.26, bf16[4,2,32,1024]{3,2,1,0:T(8,128)(2,1)S(1)} %collective-permute-done.2.refs_1_, ...), custom_call_target="tpu_custom_call" | custom-call | flops 5242880 | bytes 5242880 | tf_op jit(solution)/shard_map/weigh/pallas_call | solution.py:195
  46.2 9.0 %collective-permute-done.9.refs_1_.refs_4_ = bf16[4,2,32,1024]{3,2,1,0:T(8,128)(2,1)S(1)} collective-permute-done((bf16[4,2,32,1024]{3,2,1,0:T(8,128)(2,1)S(1)}, bf16[4,2,32,1024]{3,2,1,0:T(8,128)(2,1)S(1)}, u32[]{:S(2)}, u32[]{:S(2)}) %collective-permute-start.9) | collective-permute-done | bytes 524320 | tf_op jit(solution)/shard_map/ppermute | solution.py:286
  55.1 2.1 %collective-permute-done.7.refs_0_ = bf16[4,2,32,1024]{3,2,1,0:T(8,128)(2,1)S(1)} collective-permute-done((bf16[4,2,32,1024]{3,2,1,0:T(8,128)(2,1)S(1)}, bf16[4,2,32,1024]{3,2,1,0:T(8,128)(2,1)S(1)}, u32[]{:S(2)}, u32[]{:S(2)}) %collective-permute-start.7) | collective-permute-done | bytes 524320 | tf_op jit(solution)/shard_map/ppermute | solution.py:289
  57.3 0.0 collective-permute-done.11.refs_3_
  57.3 1.0 %weigh.3 = f32[1,1024]{1,0:T(1,128)S(1)} custom-call(s32[9]{0:T(128)S(1)} %stack.43.scalar_ref, f32[4,2,8,32,1024]{4,3,2,1,0:T(8,128)S(1)} %bitcast.21, bf16[4,2,32,1024]{3,2,1,0:T(8,128)(2,1)S(1)} %collective-permute-done.7.refs_0_, bf16[4,2,32,1024]{3,2,1,0:T(8,128)(2,1)S(1)} %collective-permute-done.9.refs_1_.refs_4_, ...), custom_call_target="tpu_custom_call" | custom-call | flops 5275648 | bytes 5275648 | tf_op jit(solution)/shard_map/weigh/pallas_call | solution.py:195
  58.3 0.9 %collective-permute-start.12 = (f32[1024]{0:T(1024)S(1)}, f32[1024]{0:T(1024)S(1)}, u32[]{:S(2)}, u32[]{:S(2)}) collective-permute-start(f32[1024]{0:T(1024)S(1)} %bitcast.30), channel_id=1, source_target_pairs={{0,1},{1,0},{2,3},{3,2},{4,5},{5,4},{6,7},{7,6},{8,9},{9,8},{10,11... | collective-permute-start | bytes 12296 | tf_op jit(solution)/shard_map/ppermute | solution.py:309
  59.2 2.8 %collective-permute-done.12 = f32[1024]{0:T(1024)S(1)} collective-permute-done((f32[1024]{0:T(1024)S(1)}, f32[1024]{0:T(1024)S(1)}, u32[]{:S(2)}, u32[]{:S(2)}) %collective-permute-start.12) | collective-permute-done | bytes 4128 | tf_op jit(solution)/shard_map/ppermute | solution.py:309
  62.0 2.7 %collective-permute-start.13 = (f32[1024]{0:T(1024)S(1)}, f32[1024]{0:T(1024)S(1)}, u32[]{:S(2)}, u32[]{:S(2)}) collective-permute-start(f32[1024]{0:T(1024)S(1)} %add.47), channel_id=1, source_target_pairs={{0,2},{1,3},{2,0},{3,1},{4,6},{5,7},{6,4},{7,5},{8,10},{9,11},{10,... | collective-permute-start | bytes 12296 | tf_op jit(solution)/shard_map/ppermute | solution.py:309
  64.7 1.6 %collective-permute-done.13 = f32[1024]{0:T(1024)S(1)} collective-permute-done((f32[1024]{0:T(1024)S(1)}, f32[1024]{0:T(1024)S(1)}, u32[]{:S(2)}, u32[]{:S(2)}) %collective-permute-start.13) | collective-permute-done | bytes 4128 | tf_op jit(solution)/shard_map/ppermute | solution.py:309
  66.3 1.8 %collective-permute-start.14 = (f32[1024]{0:T(1024)S(1)}, f32[1024]{0:T(1024)S(1)}, u32[]{:S(2)}, u32[]{:S(2)}) collective-permute-start(f32[1024]{0:T(1024)S(1)} %add.48), channel_id=1, source_target_pairs={{0,4},{1,5},{2,6},{3,7},{4,0},{5,1},{6,2},{7,3},{8,12},{9,13},{10,... | collective-permute-start | bytes 12296 | tf_op jit(solution)/shard_map/ppermute | solution.py:309
  68.0 2.8 %collective-permute-done.14 = f32[1024]{0:T(1024)S(1)} collective-permute-done((f32[1024]{0:T(1024)S(1)}, f32[1024]{0:T(1024)S(1)}, u32[]{:S(2)}, u32[]{:S(2)}) %collective-permute-start.14) | collective-permute-done | bytes 4128 | tf_op jit(solution)/shard_map/ppermute | solution.py:309
  70.8 0.6 add.49
  (2 shorter events, 0.0 us)
Async XLA Ops:
  1.4 15.0 %collective-permute-start = (bf16[4,2,32,1024]{3,2,1,0:T(8,128)(2,1)S(1)}, bf16[4,2,32,1024]{3,2,1,0:T(8,128)(2,1)S(1)}, u32[]{:S(2)}, u32[]{:S(2)}) collective-permute-start(bf16[4,2,32,1024]{3,2,1,0:T(8,128)(2,1)S(1)} %bitcast.23), channel_id=1, source_target_pairs={{0,2},{1,3},{2,0},{3,1},{4,6},{5,7},{6,4},{7,5},{8,10},{9,11},{10,... | collective-permute-start | bytes 1572872 | tf_op jit(solution)/shard_map/ppermute | solution.py:272
  4.5 12.1 %collective-permute-start.1 = (bf16[4,2,32,1024]{3,2,1,0:T(8,128)(2,1)S(1)}, bf16[4,2,32,1024]{3,2,1,0:T(8,128)(2,1)S(1)}, u32[]{:S(2)}, u32[]{:S(2)}) collective-permute-start(bf16[4,2,32,1024]{3,2,1,0:T(8,128)(2,1)S(1)} %bitcast.24), channel_id=1, source_target_pairs={{2,4},{3,5},{4,2},{5,3},{10,12},{11,13},{12,10},{13,11},{18,20},{1... | collective-permute-start | bytes 1572872 | tf_op jit(solution)/shard_map/ppermute | solution.py:273
  5.1 13.4 %collective-permute-start.2 = (bf16[4,2,32,1024]{3,2,1,0:T(8,128)(2,1)S(1)}, bf16[4,2,32,1024]{3,2,1,0:T(8,128)(2,1)S(1)}, u32[]{:S(2)}, u32[]{:S(2)}) collective-permute-start(bf16[4,2,32,1024]{3,2,1,0:T(8,128)(2,1)S(1)} %bitcast.25), channel_id=1, source_target_pairs={{0,1},{1,0},{2,3},{3,2},{4,5},{5,4},{6,7},{7,6},{8,9},{9,8},{10,11... | collective-permute-start | bytes 1572872 | tf_op jit(solution)/shard_map/ppermute | solution.py:274
  9.1 11.5 %collective-permute-start.3 = (bf16[8,64,512]{2,1,0:T(8,128)(2,1)S(1)}, bf16[8,64,512]{2,1,0:T(8,128)(2,1)S(1)}, u32[]{:S(2)}, u32[]{:S(2)}) collective-permute-start(bf16[8,64,512]{2,1,0:T(8,128)(2,1)S(1)} %spectra.1), channel_id=1, source_target_pairs={{0,8},{8,0},{16,24},{24,16},{1,9},{9,1},{17,25},{25,17},{2,10},{10... | collective-permute-start | bytes 1572872 | tf_op jit(solution)/shard_map/ppermute | solution.py:271
  9.2 17.5 %collective-permute-start.4 = (bf16[8,64,512]{2,1,0:T(8,128)(2,1)S(1)}, bf16[8,64,512]{2,1,0:T(8,128)(2,1)S(1)}, u32[]{:S(2)}, u32[]{:S(2)}) collective-permute-start(bf16[8,64,512]{2,1,0:T(8,128)(2,1)S(1)} %spectra.1), channel_id=1, source_target_pairs={{0,16},{8,24},{16,0},{24,8},{1,17},{9,25},{17,1},{25,9},{2,18},{10... | collective-permute-start | bytes 1572872 | tf_op jit(solution)/shard_map/ppermute | solution.py:270
  16.4 17.9 %collective-permute-start.5 = (bf16[8,64,512]{2,1,0:T(8,128)(2,1)S(1)}, bf16[8,64,512]{2,1,0:T(8,128)(2,1)S(1)}, u32[]{:S(2)}, u32[]{:S(2)}) collective-permute-start(bf16[8,64,512]{2,1,0:T(8,128)(2,1)S(1)} %spectra.1), channel_id=1, source_target_pairs={{0,24},{8,16},{16,8},{24,0},{1,25},{9,17},{17,9},{25,1},{2,26},{10... | collective-permute-start | bytes 1572872 | tf_op jit(solution)/shard_map/ppermute | solution.py:269
  18.6 19.1 %collective-permute-start.8 = (bf16[4,2,32,1024]{3,2,1,0:T(8,128)(2,1)S(1)}, bf16[4,2,32,1024]{3,2,1,0:T(8,128)(2,1)S(1)}, u32[]{:S(2)}, u32[]{:S(2)}) collective-permute-start(bf16[4,2,32,1024]{3,2,1,0:T(8,128)(2,1)S(1)} %collective-permute-done.refs_2_), channel_id=1, source_target_pairs={{2,4},{3,5},{4,2},{5,3},{10,12},{11,13},{12,10},{13,11},{18,20},{1... | collective-permute-start | bytes 1572872 | tf_op jit(solution)/shard_map/ppermute | solution.py:278
  19.3 23.5 %collective-permute-start.6 = (bf16[4,2,32,1024]{3,2,1,0:T(8,128)(2,1)S(1)}, bf16[4,2,32,1024]{3,2,1,0:T(8,128)(2,1)S(1)}, u32[]{:S(2)}, u32[]{:S(2)}) collective-permute-start(bf16[4,2,32,1024]{3,2,1,0:T(8,128)(2,1)S(1)} %collective-permute-done.1.second_ref), channel_id=1, source_target_pairs={{2,0},{3,1},{4,6},{5,7},{10,8},{11,9},{12,14},{13,15},{18,16},{19,... | collective-permute-start | bytes 1572872 | tf_op jit(solution)/shard_map/ppermute | solution.py:277
  20.6 23.3 %collective-permute-start.10 = (bf16[4,2,32,1024]{3,2,1,0:T(8,128)(2,1)S(1)}, bf16[4,2,32,1024]{3,2,1,0:T(8,128)(2,1)S(1)}, u32[]{:S(2)}, u32[]{:S(2)}) collective-permute-start(bf16[4,2,32,1024]{3,2,1,0:T(8,128)(2,1)S(1)} %collective-permute-done.refs_2_), channel_id=1, source_target_pairs={{0,1},{1,0},{2,3},{3,2},{4,5},{5,4},{6,7},{7,6},{8,9},{9,8},{10,11... | collective-permute-start | bytes 1572872 | tf_op jit(solution)/shard_map/ppermute | solution.py:279
  38.3 16.8 %collective-permute-start.9 = (bf16[4,2,32,1024]{3,2,1,0:T(8,128)(2,1)S(1)}, bf16[4,2,32,1024]{3,2,1,0:T(8,128)(2,1)S(1)}, u32[]{:S(2)}, u32[]{:S(2)}) collective-permute-start(bf16[4,2,32,1024]{3,2,1,0:T(8,128)(2,1)S(1)} %pick.3), channel_id=1, source_target_pairs={{0,2},{1,3},{2,0},{3,1},{4,6},{5,7},{6,4},{7,5},{8,10},{9,11},{10,... | collective-permute-start | bytes 1572872 | tf_op jit(solution)/shard_map/ppermute | solution.py:286
  43.4 13.9 %collective-permute-start.7 = (bf16[4,2,32,1024]{3,2,1,0:T(8,128)(2,1)S(1)}, bf16[4,2,32,1024]{3,2,1,0:T(8,128)(2,1)S(1)}, u32[]{:S(2)}, u32[]{:S(2)}) collective-permute-start(bf16[4,2,32,1024]{3,2,1,0:T(8,128)(2,1)S(1)} %pick.2.refs_4_), channel_id=1, source_target_pairs={{0,1},{1,0},{2,3},{3,2},{4,5},{5,4},{6,7},{7,6},{8,9},{9,8},{10,11... | collective-permute-start | bytes 1572872 | tf_op jit(solution)/shard_map/ppermute | solution.py:289
  43.9 13.3 %collective-permute-start.11 = (bf16[4,2,32,1024]{3,2,1,0:T(8,128)(2,1)S(1)}, bf16[4,2,32,1024]{3,2,1,0:T(8,128)(2,1)S(1)}, u32[]{:S(2)}, u32[]{:S(2)}) collective-permute-start(bf16[4,2,32,1024]{3,2,1,0:T(8,128)(2,1)S(1)} %collective-permute-done.10.refs_3_), channel_id=1, source_target_pairs={{2,4},{3,5},{4,2},{5,3},{10,12},{11,13},{12,10},{13,11},{18,20},{1... | collective-permute-start | bytes 1572872 | tf_op jit(solution)/shard_map/ppermute | solution.py:287
  58.3 3.7 %collective-permute-start.12 = (f32[1024]{0:T(1024)S(1)}, f32[1024]{0:T(1024)S(1)}, u32[]{:S(2)}, u32[]{:S(2)}) collective-permute-start(f32[1024]{0:T(1024)S(1)} %bitcast.30), channel_id=1, source_target_pairs={{0,1},{1,0},{2,3},{3,2},{4,5},{5,4},{6,7},{7,6},{8,9},{9,8},{10,11... | collective-permute-start | bytes 12296 | tf_op jit(solution)/shard_map/ppermute | solution.py:309
  62.0 4.3 %collective-permute-start.13 = (f32[1024]{0:T(1024)S(1)}, f32[1024]{0:T(1024)S(1)}, u32[]{:S(2)}, u32[]{:S(2)}) collective-permute-start(f32[1024]{0:T(1024)S(1)} %add.47), channel_id=1, source_target_pairs={{0,2},{1,3},{2,0},{3,1},{4,6},{5,7},{6,4},{7,5},{8,10},{9,11},{10,... | collective-permute-start | bytes 12296 | tf_op jit(solution)/shard_map/ppermute | solution.py:309
  66.3 4.5 %collective-permute-start.14 = (f32[1024]{0:T(1024)S(1)}, f32[1024]{0:T(1024)S(1)}, u32[]{:S(2)}, u32[]{:S(2)}) collective-permute-start(f32[1024]{0:T(1024)S(1)} %add.48), channel_id=1, source_target_pairs={{0,4},{1,5},{2,6},{3,7},{4,0},{5,1},{6,2},{7,3},{8,12},{9,13},{10,... | collective-permute-start | bytes 12296 | tf_op jit(solution)/shard_map/ppermute | solution.py:309

commit v8 on v7

--- a/solution.py
+++ b/solution.py
@@ -209,6 +209,7 @@
 
 
 OWN, OWN_Y, NEAR, NEAR_Y, MID, MID_Y, FAR, FAR_Y, MIDDLE = range(9)
+RECEIVED = -1
 
 
 def weigh_kernel(terms, first, last, scalar_ref, adjoint_ref, *refs):
@@ -217,19 +218,16 @@
     freqs, parts, _, cells = refs[0].shape
     middle = scalar_ref[MIDDLE] != 0
     for number, choices in terms:
-        block = scalar_ref[number]
         field_refs = [refs.pop(0) for _ in range(choices)]
-        extra_ref = refs.pop(0) if number == FAR_Y else None
+        block = refs.pop(0) if number == RECEIVED else adjoint_ref.at[:, :, scalar_ref[number]]
         for freq in range(freqs):
             for part in range(parts):
-                weights = adjoint_ref[freq, part, block]
-                if extra_ref is not None:
-                    weights = weights + extra_ref[freq, part].astype(jnp.float32)
                 field = field_refs[0][freq, part].astype(jnp.float32)
                 if choices == 2:
                     other = field_refs[1][freq, part].astype(jnp.float32)
                     field = jnp.where(middle, other, field)
-                sums = sums + jnp.sum((weights * field).reshape(-1, 8, cells), axis=0)
+                products = block[freq, part].astype(jnp.float32) * field
+                sums = sums + jnp.sum(products.reshape(-1, 8, cells), axis=0)
     out_ref[...] = jnp.sum(sums, axis=0, keepdims=True) if last else sums
 
 
@@ -251,7 +249,6 @@
     z_outward = [(2, 0), (3, 1), (4, 6), (5, 7)]
     core = [(t, t ^ 1) for t in range(4)]
     along_x = [(t, t ^ 2) for t in range(4)]
-    along_both = [(t, t ^ 3) for t in range(4)]
     send, tie = lax.ppermute, lax.optimization_barrier
 
     me_tx, me_rx = lax.axis_index("tx"), lax.axis_index("rx")
@@ -266,7 +263,6 @@
     own = background.transpose(1, 2, 0, 3)
     own, scalars, records = tie((own, scalars, records))
     spectra = spectra_of(records, active, freqs)
-    spectra_both = send(spectra, "tx", along_both)
     spectra_x = send(spectra, "tx", along_x)
     spectra_core = send(spectra, "tx", core)
     near = send(own, "rx", z_pairs)
@@ -279,6 +275,8 @@
     near_y = send(near, "rx", along_y)
 
     adjoint, green_kept = adjoint_of([spectra, spectra_core], green, 4)
+    spectra_both = send(spectra_x, "tx", core)
+    across_out, far, near_y, spectra_both = tie((across_out, far, near_y, spectra_both))
     adjoint, partial = adjoint_rest(scalars, [spectra_x, spectra_both], green_kept, adjoint)
     adjoint = adjoint.reshape((freqs, 2, 8) + own.shape[2:])
 
@@ -288,18 +286,19 @@
     mid = in_vmem(pick_kernel, scalars, [across_out, across], own.shape, own.dtype, "pick")
     mid_y = send(mid, "rx", along_y)
 
+    early = (OWN, OWN_Y, NEAR, NEAR_Y, MID, MID_Y, FAR_Y)
     sums = in_vmem(
-        functools.partial(weigh_kernel, ((OWN, 1), (OWN_Y, 1), (NEAR, 1), (NEAR_Y, 1), (MID, 1)), True, False),
+        functools.partial(weigh_kernel, tuple((number, 1) for number in early), True, False),
         scalars,
-        [adjoint, own, own_y, near, near_y, mid],
+        [adjoint, own, own_y, near, near_y, mid, mid_y, far_both],
         (8, cells),
         jnp.float32,
         "weigh",
     )
     sums = in_vmem(
-        functools.partial(weigh_kernel, ((MID_Y, 1), (FAR, 2), (FAR_Y, 1)), False, True),
+        functools.partial(weigh_kernel, ((FAR, 2), (RECEIVED, 1)), False, True),
         scalars,
-        [adjoint, mid_y, swap, far, far_both, swap, sums],
+        [adjoint, swap, far, far_both, swap, sums],
         (1, cells),
         jnp.float32,
         "weigh",

time: 71.6 us -> 70.2 us (0.980)
  waiting for transfers between devices: 33.5 us -> 29.8 us
  starting transfers between devices: 21.7 us -> 23.8 us
    ppermute x1, waiting for transfers between devices: 0.01 us -> 7.65 us  [box_shards(): across_out = send(across, 'rx', z_outward)]
    ppermute x1, waiting for transfers between devices: 7.61 us -> 0.01 us  [box_shards(): spectra_both = send(spectra_x, 'tx', core)]
    ppermute x1, starting transfers between devices: 4.43 us -> 6.79 us  [box_shards(): swap = send(swap, 'rx', z_pairs)]
    ppermute x1, waiting for transfers between devices: 8.98 us -> 6.72 us  [box_shards(): swap = send(swap, 'rx', z_pairs)]
    ppermute x1, waiting for transfers between devices: 2.12 us -> 0.01 us  [box_shards(): mid_y = send(mid, 'rx', along_y)]
    ppermute x1, starting transfers between devices: 0.56 us -> 1.58 us  [box_shards(): mid_y = send(mid, 'rx', along_y)]
    ppermute x3, starting transfers between devices: 5.29 us -> 4.37 us  [box_shards(): sums = sums + send(sums, 'rx', [(r, r ^ bit) for r in range(8)])]
where the time goes in v8:
time: 70.2 us; the launch traced here: 70 us
  waiting for transfers between devices  29.8 us (42%)
  starting transfers between devices  23.8 us (34%)
  Pallas kernels  14.2 us (20%)
  local copies, waits for them, and re-layouts  1.42 us (2%)
    ppermute x1, waiting for transfers between devices, box_shards(): across_out = send(across, 'rx', z_outward)  7.65 us
    ppermute x3, waiting for transfers between devices, box_shards(): sums = sums + send(sums, 'rx', [(r, r ^ bit) for r in range(8)])  7.41 us
    ppermute x1, starting transfers between devices, box_shards(): swap = send(swap, 'rx', z_pairs)  6.79 us
    ppermute x1, waiting for transfers between devices, box_shards(): swap = send(swap, 'rx', z_pairs)  6.72 us
    ppermute x1, waiting for transfers between devices, box_shards(): near = send(own, 'rx', z_pairs)  5.74 us
    pallas_call x1, Pallas kernels, adjoint_of(): pl.pallas_call(functools.partial(adjoint_kernel, count), in_specs=[pl.Blo...  4.47 us
    ppermute x3, starting transfers between devices, box_shards(): sums = sums + send(sums, 'rx', [(r, r ^ bit) for r in range(8)])  4.37 us
    pallas_call x4, Pallas kernels, in_vmem(): pl.pallas_call(kernel, in_specs=[pl.BlockSpec(memory_space=pltpu.SMEM)] +...  3.95 us
  transfers between devices with their start and end apart: 15, of which 8 were waited for; matrix products, arithmetic and copies ran while one was open for 0% of the time, Pallas kernels for 18%

profile of v8, /device:TPU:0, one launch (start us, length us, event | category | flops | bytes accessed | tf_op | source)
XLA Modules:
  0.0 70.0 jit_solution(1821490852417310769)
XLA Ops:
  0.0 1.3 %copy.9 = bf16[32,4,2,1024]{3,0,2,1:T(8,128)(2,1)S(1)} copy(bf16[32,4,2,1024]{3,2,1,0:T(2,128)(2,1)} %param.8) | data formatting | bytes 1048576 | tf_op args[3]
  1.3 0.1 stack.43.scalar_ref
  1.4 3.0 %collective-permute-start = (bf16[4,2,32,1024]{3,2,1,0:T(8,128)(2,1)S(1)}, bf16[4,2,32,1024]{3,2,1,0:T(8,128)(2,1)S(1)}, u32[]{:S(2)}, u32[]{:S(2)}) collective-permute-start(bf16[4,2,32,1024]{3,2,1,0:T(8,128)(2,1)S(1)} %bitcast.23), channel_id=1, source_target_pairs={{0,2},{1,3},{2,0},{3,1},{4,6},{5,7},{6,4},{7,5},{8,10},{9,11},{10,... | collective-permute-start | bytes 1572872 | tf_op jit(solution)/shard_map/ppermute | solution.py:268
  4.5 0.7 collective-permute-start.1
  5.1 1.6 %collective-permute-start.2 = (bf16[4,2,32,1024]{3,2,1,0:T(8,128)(2,1)S(1)}, bf16[4,2,32,1024]{3,2,1,0:T(8,128)(2,1)S(1)}, u32[]{:S(2)}, u32[]{:S(2)}) collective-permute-start(bf16[4,2,32,1024]{3,2,1,0:T(8,128)(2,1)S(1)} %bitcast.25), channel_id=1, source_target_pairs={{0,1},{1,0},{2,3},{3,2},{4,5},{5,4},{6,7},{7,6},{8,9},{9,8},{10,11... | collective-permute-start | bytes 1572872 | tf_op jit(solution)/shard_map/ppermute | solution.py:270
  6.7 2.3 %spectra.1 = bf16[8,64,512]{2,1,0:T(8,128)(2,1)S(1)} custom-call(bf16[128,640]{1,0:T(8,128)(2,1)} %constant.38.clone.table_hbm, s32[8,64]{1,0:T(8,128)} %bitcast.33, bf16[40,64,512]{2,1,0:T(8,128)(2,1)} %records_hbm), custom_call_target="tpu_custom_call" | custom-call | flops 335544320 | bytes 3145728 | tf_op jit(solution)/shard_map/spectra/pallas_call | solution.py:78
  9.1 1.6 %collective-permute-start.4 = (bf16[8,64,512]{2,1,0:T(8,128)(2,1)S(1)}, bf16[8,64,512]{2,1,0:T(8,128)(2,1)S(1)}, u32[]{:S(2)}, u32[]{:S(2)}) collective-permute-start(bf16[8,64,512]{2,1,0:T(8,128)(2,1)S(1)} %spectra.1), channel_id=1, source_target_pairs={{0,16},{8,24},{16,0},{24,8},{1,17},{9,25},{17,1},{25,9},{2,18},{10... | collective-permute-start | bytes 1572872 | tf_op jit(solution)/shard_map/ppermute | solution.py:266
  10.6 0.0 collective-permute-start.3
  10.6 5.7 %collective-permute-done.refs_2_ = bf16[4,2,32,1024]{3,2,1,0:T(8,128)(2,1)S(1)} collective-permute-done((bf16[4,2,32,1024]{3,2,1,0:T(8,128)(2,1)S(1)}, bf16[4,2,32,1024]{3,2,1,0:T(8,128)(2,1)S(1)}, u32[]{:S(2)}, u32[]{:S(2)}) %collective-permute-start) | collective-permute-done | bytes 524320 | tf_op jit(solution)/shard_map/ppermute | solution.py:268
  16.4 0.0 collective-permute-done.1.second_ref
  16.4 2.2 %collective-permute-done.2.refs_1_ = bf16[4,2,32,1024]{3,2,1,0:T(8,128)(2,1)S(1)} collective-permute-done((bf16[4,2,32,1024]{3,2,1,0:T(8,128)(2,1)S(1)}, bf16[4,2,32,1024]{3,2,1,0:T(8,128)(2,1)S(1)}, u32[]{:S(2)}, u32[]{:S(2)}) %collective-permute-start.2) | collective-permute-done | bytes 524320 | tf_op jit(solution)/shard_map/ppermute | solution.py:270
  18.6 1.3 %collective-permute-start.5 = (bf16[4,2,32,1024]{3,2,1,0:T(8,128)(2,1)S(1)}, bf16[4,2,32,1024]{3,2,1,0:T(8,128)(2,1)S(1)}, u32[]{:S(2)}, u32[]{:S(2)}) collective-permute-start(bf16[4,2,32,1024]{3,2,1,0:T(8,128)(2,1)S(1)} %collective-permute-done.1.second_ref), channel_id=1, source_target_pairs={{2,0},{3,1},{4,6},{5,7},{10,8},{11,9},{12,14},{13,15},{18,16},{19,... | collective-permute-start | bytes 1572872 | tf_op jit(solution)/shard_map/ppermute | solution.py:273
  19.9 0.7 collective-permute-start.6
  20.6 1.6 %collective-permute-start.7 = (bf16[4,2,32,1024]{3,2,1,0:T(8,128)(2,1)S(1)}, bf16[4,2,32,1024]{3,2,1,0:T(8,128)(2,1)S(1)}, u32[]{:S(2)}, u32[]{:S(2)}) collective-permute-start(bf16[4,2,32,1024]{3,2,1,0:T(8,128)(2,1)S(1)} %collective-permute-done.refs_2_), channel_id=1, source_target_pairs={{0,1},{1,0},{2,3},{3,2},{4,5},{5,4},{6,7},{7,6},{8,9},{9,8},{10,11... | collective-permute-start | bytes 1572872 | tf_op jit(solution)/shard_map/ppermute | solution.py:275
  22.2 0.1 collective-permute-done.4
  22.2 0.0 collective-permute-start.8
  22.2 0.0 collective-permute-done.3
  22.3 4.5 %adjoint.1 = (f32[4,2,4,64,1024]{4,3,2,1,0:T(8,128)S(1)}, bf16[4,1024,1024]{2,1,0:T(8,128)(2,1)S(1)}) custom-call(bf16[4,1024,1024]{2,1,0:T(8,128)(2,1)} %bitcast.32, bf16[4,2,64,512]{3,2,1,0:T(8,128)(2,1)S(1)} %bitcast.22, bf16[4,2,64,512]{3,2,1,0:T(8,128)(2,1)S(1)} %bitcast.29), custom_call_target="tpu_custom_call" | custom-call | flops 2147483648 | bytes 8388608 | tf_op jit(solution)/shard_map/adjoint/pallas_call | solution.py:149
  26.7 7.6 %collective-permute-done.5.first_ref = bf16[4,2,32,1024]{3,2,1,0:T(8,128)(2,1)S(1)} collective-permute-done((bf16[4,2,32,1024]{3,2,1,0:T(8,128)(2,1)S(1)}, bf16[4,2,32,1024]{3,2,1,0:T(8,128)(2,1)S(1)}, u32[]{:S(2)}, u32[]{:S(2)}) %collective-permute-start.5) | collective-permute-done | bytes 524320 | tf_op jit(solution)/shard_map/ppermute | solution.py:273
  34.4 0.0 collective-permute-done.6.second_ref.refs_1_
  34.4 0.0 collective-permute-done.7.refs_3_
  34.4 0.0 collective-permute-done.8
  34.4 0.6 pick.3.refs_4_
  35.0 1.6 %collective-permute-start.11 = (bf16[4,2,32,1024]{3,2,1,0:T(8,128)(2,1)S(1)}, bf16[4,2,32,1024]{3,2,1,0:T(8,128)(2,1)S(1)}, u32[]{:S(2)}, u32[]{:S(2)}) collective-permute-start(bf16[4,2,32,1024]{3,2,1,0:T(8,128)(2,1)S(1)} %pick.3.refs_4_), channel_id=1, source_target_pairs={{0,1},{1,0},{2,3},{3,2},{4,5},{5,4},{6,7},{7,6},{8,9},{9,8},{10,11... | collective-permute-start | bytes 1572872 | tf_op jit(solution)/shard_map/ppermute | solution.py:287
  36.6 0.7 collective-permute-start.10
  37.3 3.4 %adjoint_rest.1 = (f32[4,2,4,64,1024]{4,3,2,1,0:T(8,128)S(1)}, bf16[4,2,32,1024]{3,2,1,0:T(8,128)(2,1)S(1)}) custom-call(s32[9]{0:T(128)S(1)} %stack.43.scalar_ref, bf16[4,1024,1024]{2,1,0:T(8,128)(2,1)S(1)} %get-tuple-element.24.green_ref, f32[4,2,4,64,1024]{4,3,2,1,0:T(8,128)S(1)} %get-tuple-element.25.base_ref, ...), custom_call_target="tpu_custom_call", output_to_operand_aliasing={{0}: (2, {})} | custom-call | flops 2147483648 | bytes 8388608 | tf_op jit(solution)/shard_map/adjoint_rest/pallas_call | solution.py:174
  40.7 0.6 pick.2
  41.3 6.8 %collective-permute-start.9 = (bf16[4,2,32,1024]{3,2,1,0:T(8,128)(2,1)S(1)}, bf16[4,2,32,1024]{3,2,1,0:T(8,128)(2,1)S(1)}, u32[]{:S(2)}, u32[]{:S(2)}) collective-permute-start(bf16[4,2,32,1024]{3,2,1,0:T(8,128)(2,1)S(1)} %pick.2), channel_id=1, source_target_pairs={{0,2},{1,3},{2,0},{3,1},{4,6},{5,7},{6,4},{7,5},{8,10},{9,11},{10,... | collective-permute-start | bytes 1572872 | tf_op jit(solution)/shard_map/ppermute | solution.py:284
  48.1 0.0 collective-permute-done.11.refs_5_
  48.1 0.0 collective-permute-done.10.refs_6_.refs_2_
  48.1 1.9 %weigh.2.refs_4_ = f32[8,1024]{1,0:T(8,128)S(1)} custom-call(s32[9]{0:T(128)S(1)} %stack.43.scalar_ref, f32[4,2,8,32,1024]{4,3,2,1,0:T(8,128)S(1)} %bitcast.20, bf16[4,2,32,1024]{3,2,1,0:T(8,128)(2,1)S(1)} %bitcast.26, bf16[4,2,32,1024]{3,2,1,0:T(8,128)(2,1)S(1)} %collective-permute-done.2.refs_1_, ...), custom_call_target="tpu_custom_call" | custom-call | flops 7340032 | bytes 7340032 | tf_op jit(solution)/shard_map/weigh/pallas_call | solution.py:195
  50.1 6.7 %collective-permute-done.9.refs_0_.refs_3_ = bf16[4,2,32,1024]{3,2,1,0:T(8,128)(2,1)S(1)} collective-permute-done((bf16[4,2,32,1024]{3,2,1,0:T(8,128)(2,1)S(1)}, bf16[4,2,32,1024]{3,2,1,0:T(8,128)(2,1)S(1)}, u32[]{:S(2)}, u32[]{:S(2)}) %collective-permute-start.9) | collective-permute-done | bytes 524320 | tf_op jit(solution)/shard_map/ppermute | solution.py:284
  56.8 0.8 %weigh.3 = f32[1,1024]{1,0:T(1,128)S(1)} custom-call(s32[9]{0:T(128)S(1)} %stack.43.scalar_ref, f32[4,2,8,32,1024]{4,3,2,1,0:T(8,128)S(1)} %bitcast.21, bf16[4,2,32,1024]{3,2,1,0:T(8,128)(2,1)S(1)} %collective-permute-done.9.refs_0_.refs_3_, bf16[4,2,32,1024]{3,2,1,0:T(8,128)(2,1)S(1)} %collective-permute-done.6.second_ref.refs_1_, ...), custom_call_target="tpu_custom_call" | custom-call | flops 4227072 | bytes 4227072 | tf_op jit(solution)/shard_map/weigh/pallas_call | solution.py:195
  57.6 0.6 collective-permute-start.12
  58.2 3.1 %collective-permute-done.12 = f32[1024]{0:T(1024)S(1)} collective-permute-done((f32[1024]{0:T(1024)S(1)}, f32[1024]{0:T(1024)S(1)}, u32[]{:S(2)}, u32[]{:S(2)}) %collective-permute-start.12) | collective-permute-done | bytes 4128 | tf_op jit(solution)/shard_map/ppermute | solution.py:308
  61.3 1.7 %collective-permute-start.13 = (f32[1024]{0:T(1024)S(1)}, f32[1024]{0:T(1024)S(1)}, u32[]{:S(2)}, u32[]{:S(2)}) collective-permute-start(f32[1024]{0:T(1024)S(1)} %add.47), channel_id=1, source_target_pairs={{0,2},{1,3},{2,0},{3,1},{4,6},{5,7},{6,4},{7,5},{8,10},{9,11},{10,... | collective-permute-start | bytes 12296 | tf_op jit(solution)/shard_map/ppermute | solution.py:308
  63.0 1.9 %collective-permute-done.13 = f32[1024]{0:T(1024)S(1)} collective-permute-done((f32[1024]{0:T(1024)S(1)}, f32[1024]{0:T(1024)S(1)}, u32[]{:S(2)}, u32[]{:S(2)}) %collective-permute-start.13) | collective-permute-done | bytes 4128 | tf_op jit(solution)/shard_map/ppermute | solution.py:308
  64.9 2.1 %collective-permute-start.14 = (f32[1024]{0:T(1024)S(1)}, f32[1024]{0:T(1024)S(1)}, u32[]{:S(2)}, u32[]{:S(2)}) collective-permute-start(f32[1024]{0:T(1024)S(1)} %add.48), channel_id=1, source_target_pairs={{0,4},{1,5},{2,6},{3,7},{4,0},{5,1},{6,2},{7,3},{8,12},{9,13},{10,... | collective-permute-start | bytes 12296 | tf_op jit(solution)/shard_map/ppermute | solution.py:308
  67.0 2.4 %collective-permute-done.14 = f32[1024]{0:T(1024)S(1)} collective-permute-done((f32[1024]{0:T(1024)S(1)}, f32[1024]{0:T(1024)S(1)}, u32[]{:S(2)}, u32[]{:S(2)}) %collective-permute-start.14) | collective-permute-done | bytes 4128 | tf_op jit(solution)/shard_map/ppermute | solution.py:308
  69.4 0.6 add.49
  (2 shorter events, 0.0 us)
Async XLA Ops:
  1.4 15.0 %collective-permute-start = (bf16[4,2,32,1024]{3,2,1,0:T(8,128)(2,1)S(1)}, bf16[4,2,32,1024]{3,2,1,0:T(8,128)(2,1)S(1)}, u32[]{:S(2)}, u32[]{:S(2)}) collective-permute-start(bf16[4,2,32,1024]{3,2,1,0:T(8,128)(2,1)S(1)} %bitcast.23), channel_id=1, source_target_pairs={{0,2},{1,3},{2,0},{3,1},{4,6},{5,7},{6,4},{7,5},{8,10},{9,11},{10,... | collective-permute-start | bytes 1572872 | tf_op jit(solution)/shard_map/ppermute | solution.py:268
  4.5 11.9 %collective-permute-start.1 = (bf16[4,2,32,1024]{3,2,1,0:T(8,128)(2,1)S(1)}, bf16[4,2,32,1024]{3,2,1,0:T(8,128)(2,1)S(1)}, u32[]{:S(2)}, u32[]{:S(2)}) collective-permute-start(bf16[4,2,32,1024]{3,2,1,0:T(8,128)(2,1)S(1)} %bitcast.24), channel_id=1, source_target_pairs={{2,4},{3,5},{4,2},{5,3},{10,12},{11,13},{12,10},{13,11},{18,20},{1... | collective-permute-start | bytes 1572872 | tf_op jit(solution)/shard_map/ppermute | solution.py:269
  5.1 13.4 %collective-permute-start.2 = (bf16[4,2,32,1024]{3,2,1,0:T(8,128)(2,1)S(1)}, bf16[4,2,32,1024]{3,2,1,0:T(8,128)(2,1)S(1)}, u32[]{:S(2)}, u32[]{:S(2)}) collective-permute-start(bf16[4,2,32,1024]{3,2,1,0:T(8,128)(2,1)S(1)} %bitcast.25), channel_id=1, source_target_pairs={{0,1},{1,0},{2,3},{3,2},{4,5},{5,4},{6,7},{7,6},{8,9},{9,8},{10,11... | collective-permute-start | bytes 1572872 | tf_op jit(solution)/shard_map/ppermute | solution.py:270
  9.1 13.2 %collective-permute-start.4 = (bf16[8,64,512]{2,1,0:T(8,128)(2,1)S(1)}, bf16[8,64,512]{2,1,0:T(8,128)(2,1)S(1)}, u32[]{:S(2)}, u32[]{:S(2)}) collective-permute-start(bf16[8,64,512]{2,1,0:T(8,128)(2,1)S(1)} %spectra.1), channel_id=1, source_target_pairs={{0,16},{8,24},{16,0},{24,8},{1,17},{9,25},{17,1},{25,9},{2,18},{10... | collective-permute-start | bytes 1572872 | tf_op jit(solution)/shard_map/ppermute | solution.py:266
  10.6 11.6 %collective-permute-start.3 = (bf16[8,64,512]{2,1,0:T(8,128)(2,1)S(1)}, bf16[8,64,512]{2,1,0:T(8,128)(2,1)S(1)}, u32[]{:S(2)}, u32[]{:S(2)}) collective-permute-start(bf16[8,64,512]{2,1,0:T(8,128)(2,1)S(1)} %spectra.1), channel_id=1, source_target_pairs={{0,8},{8,0},{16,24},{24,16},{1,9},{9,1},{17,25},{25,17},{2,10},{10... | collective-permute-start | bytes 1572872 | tf_op jit(solution)/shard_map/ppermute | solution.py:267
  18.6 15.8 %collective-permute-start.5 = (bf16[4,2,32,1024]{3,2,1,0:T(8,128)(2,1)S(1)}, bf16[4,2,32,1024]{3,2,1,0:T(8,128)(2,1)S(1)}, u32[]{:S(2)}, u32[]{:S(2)}) collective-permute-start(bf16[4,2,32,1024]{3,2,1,0:T(8,128)(2,1)S(1)} %collective-permute-done.1.second_ref), channel_id=1, source_target_pairs={{2,0},{3,1},{4,6},{5,7},{10,8},{11,9},{12,14},{13,15},{18,16},{19,... | collective-permute-start | bytes 1572872 | tf_op jit(solution)/shard_map/ppermute | solution.py:273
  19.9 14.5 %collective-permute-start.6 = (bf16[4,2,32,1024]{3,2,1,0:T(8,128)(2,1)S(1)}, bf16[4,2,32,1024]{3,2,1,0:T(8,128)(2,1)S(1)}, u32[]{:S(2)}, u32[]{:S(2)}) collective-permute-start(bf16[4,2,32,1024]{3,2,1,0:T(8,128)(2,1)S(1)} %collective-permute-done.refs_2_), channel_id=1, source_target_pairs={{2,4},{3,5},{4,2},{5,3},{10,12},{11,13},{12,10},{13,11},{18,20},{1... | collective-permute-start | bytes 1572872 | tf_op jit(solution)/shard_map/ppermute | solution.py:274
  20.6 13.8 %collective-permute-start.7 = (bf16[4,2,32,1024]{3,2,1,0:T(8,128)(2,1)S(1)}, bf16[4,2,32,1024]{3,2,1,0:T(8,128)(2,1)S(1)}, u32[]{:S(2)}, u32[]{:S(2)}) collective-permute-start(bf16[4,2,32,1024]{3,2,1,0:T(8,128)(2,1)S(1)} %collective-permute-done.refs_2_), channel_id=1, source_target_pairs={{0,1},{1,0},{2,3},{3,2},{4,5},{5,4},{6,7},{7,6},{8,9},{9,8},{10,11... | collective-permute-start | bytes 1572872 | tf_op jit(solution)/shard_map/ppermute | solution.py:275
  22.2 12.1 %collective-permute-start.8 = (bf16[8,64,512]{2,1,0:T(8,128)(2,1)S(1)}, bf16[8,64,512]{2,1,0:T(8,128)(2,1)S(1)}, u32[]{:S(2)}, u32[]{:S(2)}) collective-permute-start(bf16[8,64,512]{2,1,0:T(8,128)(2,1)S(1)} %collective-permute-done.4), channel_id=1, source_target_pairs={{0,8},{8,0},{16,24},{24,16},{1,9},{9,1},{17,25},{25,17},{2,10},{10... | collective-permute-start | bytes 1572872 | tf_op jit(solution)/shard_map/ppermute | solution.py:278
  35.0 13.1 %collective-permute-start.11 = (bf16[4,2,32,1024]{3,2,1,0:T(8,128)(2,1)S(1)}, bf16[4,2,32,1024]{3,2,1,0:T(8,128)(2,1)S(1)}, u32[]{:S(2)}, u32[]{:S(2)}) collective-permute-start(bf16[4,2,32,1024]{3,2,1,0:T(8,128)(2,1)S(1)} %pick.3.refs_4_), channel_id=1, source_target_pairs={{0,1},{1,0},{2,3},{3,2},{4,5},{5,4},{6,7},{7,6},{8,9},{9,8},{10,11... | collective-permute-start | bytes 1572872 | tf_op jit(solution)/shard_map/ppermute | solution.py:287
  36.6 11.5 %collective-permute-start.10 = (bf16[4,2,32,1024]{3,2,1,0:T(8,128)(2,1)S(1)}, bf16[4,2,32,1024]{3,2,1,0:T(8,128)(2,1)S(1)}, u32[]{:S(2)}, u32[]{:S(2)}) collective-permute-start(bf16[4,2,32,1024]{3,2,1,0:T(8,128)(2,1)S(1)} %collective-permute-done.7.refs_3_), channel_id=1, source_target_pairs={{2,4},{3,5},{4,2},{5,3},{10,12},{11,13},{12,10},{13,11},{18,20},{1... | collective-permute-start | bytes 1572872 | tf_op jit(solution)/shard_map/ppermute | solution.py:285
  41.3 15.5 %collective-permute-start.9 = (bf16[4,2,32,1024]{3,2,1,0:T(8,128)(2,1)S(1)}, bf16[4,2,32,1024]{3,2,1,0:T(8,128)(2,1)S(1)}, u32[]{:S(2)}, u32[]{:S(2)}) collective-permute-start(bf16[4,2,32,1024]{3,2,1,0:T(8,128)(2,1)S(1)} %pick.2), channel_id=1, source_target_pairs={{0,2},{1,3},{2,0},{3,1},{4,6},{5,7},{6,4},{7,5},{8,10},{9,11},{10,... | collective-permute-start | bytes 1572872 | tf_op jit(solution)/shard_map/ppermute | solution.py:284
  57.6 3.7 %collective-permute-start.12 = (f32[1024]{0:T(1024)S(1)}, f32[1024]{0:T(1024)S(1)}, u32[]{:S(2)}, u32[]{:S(2)}) collective-permute-start(f32[1024]{0:T(1024)S(1)} %bitcast.30), channel_id=1, source_target_pairs={{0,1},{1,0},{2,3},{3,2},{4,5},{5,4},{6,7},{7,6},{8,9},{9,8},{10,11... | collective-permute-start | bytes 12296 | tf_op jit(solution)/shard_map/ppermute | solution.py:308
  61.3 3.6 %collective-permute-start.13 = (f32[1024]{0:T(1024)S(1)}, f32[1024]{0:T(1024)S(1)}, u32[]{:S(2)}, u32[]{:S(2)}) collective-permute-start(f32[1024]{0:T(1024)S(1)} %add.47), channel_id=1, source_target_pairs={{0,2},{1,3},{2,0},{3,1},{4,6},{5,7},{6,4},{7,5},{8,10},{9,11},{10,... | collective-permute-start | bytes 12296 | tf_op jit(solution)/shard_map/ppermute | solution.py:308
  64.9 4.5 %collective-permute-start.14 = (f32[1024]{0:T(1024)S(1)}, f32[1024]{0:T(1024)S(1)}, u32[]{:S(2)}, u32[]{:S(2)}) collective-permute-start(f32[1024]{0:T(1024)S(1)} %add.48), channel_id=1, source_target_pairs={{0,4},{1,5},{2,6},{3,7},{4,0},{5,1},{6,2},{7,3},{8,12},{9,13},{10,... | collective-permute-start | bytes 12296 | tf_op jit(solution)/shard_map/ppermute | solution.py:308

commit v9 on v8

--- a/solution.py
+++ b/solution.py
@@ -226,6 +226,8 @@
                 if choices == 2:
                     other = field_refs[1][freq, part].astype(jnp.float32)
                     field = jnp.where(middle, other, field)
+                if number in (FAR_Y, RECEIVED):
+                    field = jnp.where(middle, field, 0.0)
                 products = block[freq, part].astype(jnp.float32) * field
                 sums = sums + jnp.sum(products.reshape(-1, 8, cells), axis=0)
     out_ref[...] = jnp.sum(sums, axis=0, keepdims=True) if last else sums
@@ -245,8 +247,8 @@
     freqs, _, _, cells = green.shape
     along_y = [(r, r ^ 1) for r in range(8)]
     z_pairs = [(r, r ^ 2) for r in range(8)]
-    z_middle = [(r, r ^ 6) for r in range(2, 6)]
-    z_outward = [(2, 0), (3, 1), (4, 6), (5, 7)]
+    z_middle = [(t * 8 + r, t * 8 + (r ^ 6)) for t in range(4) for r in range(2, 6)]
+    z_middle += [(t * 8 + r, (t ^ 1) * 8 + r) for t in range(4) for r in (0, 1, 6, 7)]
     core = [(t, t ^ 1) for t in range(4)]
     along_x = [(t, t ^ 2) for t in range(4)]
     send, tie = lax.ppermute, lax.optimization_barrier
@@ -266,12 +268,12 @@
     spectra_x = send(spectra, "tx", along_x)
     spectra_core = send(spectra, "tx", core)
     near = send(own, "rx", z_pairs)
-    across = send(own, "rx", z_middle)
+    across = send(own, ("tx", "rx"), z_middle)
     own_y = send(own, "rx", along_y)
     near, across, own_y, spectra = tie((near, across, own_y, spectra))
 
-    across_out = send(across, "rx", z_outward)
-    far = send(near, "rx", z_middle)
+    across_out = send(across, "rx", z_pairs)
+    far = send(near, ("tx", "rx"), z_middle)
     near_y = send(near, "rx", along_y)
 
     adjoint, green_kept = adjoint_of([spectra, spectra_core], green, 4)
@@ -282,7 +284,7 @@
 
     swap = in_vmem(pick_kernel, scalars, [partial, far], own.shape, own.dtype, "pick")
     swap = send(swap, "rx", z_pairs)
-    far_both = send(near_y, "rx", z_middle)
+    far_both = send(near_y, ("tx", "rx"), z_middle)
     mid = in_vmem(pick_kernel, scalars, [across_out, across], own.shape, own.dtype, "pick")
     mid_y = send(mid, "rx", along_y)
 

time: 70.2 us -> 69.2 us (0.986)
  starting transfers between devices: 23.8 us -> 12.9 us
  waiting for transfers between devices: 29.8 us -> 39.8 us
    ppermute x1, waiting for transfers between devices: 0.01 us -> 7.13 us  [box_shards(): mid_y = send(mid, 'rx', along_y)]
    ppermute x1, starting transfers between devices: 6.79 us -> 0.85 us  [box_shards(): swap = send(swap, 'rx', z_pairs)]
    ppermute x3, starting transfers between devices: 4.37 us -> 0.86 us  [box_shards(): sums = sums + send(sums, 'rx', [(r, r ^ bit) for r in range(8)])]
    ppermute x3, waiting for transfers between devices: 7.41 us -> 10.9 us  [box_shards(): sums = sums + send(sums, 'rx', [(r, r ^ bit) for r in range(8)])]
    ppermute x1, waiting for transfers between devices: 0.01 us -> 2.7 us  [box_shards(): near_y = send(near, 'rx', along_y)]
    ppermute x4, waiting for transfers between devices: 7.66 us -> 5.41 us  [the longest x1 5.4 us: box_shards(): across_out = send(across, 'rx', z_pairs)]
    ppermute x1, waiting for transfers between devices: 6.72 us -> 4.5 us  [box_shards(): swap = send(swap, 'rx', z_pairs)]
    ppermute x4, starting transfers between devices: 3.34 us -> 1.93 us  [the longest x1 1.92 us: box_shards(): across_out = send(across, 'rx', z_pairs)]
  transfers between devices with their start and end apart: 15 -> 15, of which waited for: 8 -> 10; matrix products, arithmetic and copies ran while one was open for 0% -> 0% of each run, Pallas kernels for 18% -> 18%
where the time goes in v9:
time: 69.2 us; the launch traced here: 69 us
  waiting for transfers between devices  39.8 us (58%)
  Pallas kernels  14.3 us (21%)
  starting transfers between devices  12.9 us (19%)
  local copies, waits for them, and re-layouts  1.42 us (2%)
    ppermute x3, waiting for transfers between devices, box_shards(): sums = sums + send(sums, 'rx', [(r, r ^ bit) for r in range(8)])  10.9 us
    ppermute x1, waiting for transfers between devices, box_shards(): mid_y = send(mid, 'rx', along_y)  7.13 us
    ppermute x1, waiting for transfers between devices, box_shards(): near = send(own, 'rx', z_pairs)  6.49 us
    ppermute x1, waiting for transfers between devices, box_shards(): across_out = send(across, 'rx', z_pairs)  5.4 us
    ppermute x1, waiting for transfers between devices, box_shards(): swap = send(swap, 'rx', z_pairs)  4.5 us
    pallas_call x1, Pallas kernels, adjoint_of(): pl.pallas_call(functools.partial(adjoint_kernel, count), in_specs=[pl.Blo...  4.47 us
    pallas_call x4, Pallas kernels, in_vmem(): pl.pallas_call(kernel, in_specs=[pl.BlockSpec(memory_space=pltpu.SMEM)] +...  4 us
    pallas_call x1, Pallas kernels, adjoint_rest(): pl.pallas_call(functools.partial(adjoint_rest_kernel, count, half), in_sp...  3.44 us
  transfers between devices with their start and end apart: 15, of which 10 were waited for; matrix products, arithmetic and copies ran while one was open for 0% of the time, Pallas kernels for 18%

profile of v9, /device:TPU:0, one launch (start us, length us, event | category | flops | bytes accessed | tf_op | source)
XLA Modules:
  0.0 69.0 jit_solution(15725182245351357868)
XLA Ops:
  0.0 1.3 %copy.9 = bf16[32,4,2,1024]{3,0,2,1:T(8,128)(2,1)S(1)} copy(bf16[32,4,2,1024]{3,2,1,0:T(2,128)(2,1)} %param.8) | data formatting | bytes 1048576 | tf_op args[3]
  1.3 0.1 stack.43.scalar_ref
  1.4 3.0 %collective-permute-start = (bf16[4,2,32,1024]{3,2,1,0:T(8,128)(2,1)S(1)}, bf16[4,2,32,1024]{3,2,1,0:T(8,128)(2,1)S(1)}, u32[]{:S(2)}, u32[]{:S(2)}) collective-permute-start(bf16[4,2,32,1024]{3,2,1,0:T(8,128)(2,1)S(1)} %bitcast.23), channel_id=1, source_target_pairs={{0,2},{1,3},{2,0},{3,1},{4,6},{5,7},{6,4},{7,5},{8,10},{9,11},{10,... | collective-permute-start | bytes 1572872 | tf_op jit(solution)/shard_map/ppermute | solution.py:270
  4.5 0.0 collective-permute-start.1
  4.5 1.5 %collective-permute-start.2 = (bf16[4,2,32,1024]{3,2,1,0:T(8,128)(2,1)S(1)}, bf16[4,2,32,1024]{3,2,1,0:T(8,128)(2,1)S(1)}, u32[]{:S(2)}, u32[]{:S(2)}) collective-permute-start(bf16[4,2,32,1024]{3,2,1,0:T(8,128)(2,1)S(1)} %bitcast.25), channel_id=1, source_target_pairs={{0,1},{1,0},{2,3},{3,2},{4,5},{5,4},{6,7},{7,6},{8,9},{9,8},{10,11... | collective-permute-start | bytes 1572872 | tf_op jit(solution)/shard_map/ppermute | solution.py:272
  6.0 2.3 %spectra.1 = bf16[8,64,512]{2,1,0:T(8,128)(2,1)S(1)} custom-call(bf16[128,640]{1,0:T(8,128)(2,1)} %constant.38.clone.table_hbm, s32[8,64]{1,0:T(8,128)} %bitcast.33, bf16[40,64,512]{2,1,0:T(8,128)(2,1)} %records_hbm), custom_call_target="tpu_custom_call" | custom-call | flops 335544320 | bytes 3145728 | tf_op jit(solution)/shard_map/spectra/pallas_call | solution.py:78
  8.3 1.6 %collective-permute-start.4 = (bf16[8,64,512]{2,1,0:T(8,128)(2,1)S(1)}, bf16[8,64,512]{2,1,0:T(8,128)(2,1)S(1)}, u32[]{:S(2)}, u32[]{:S(2)}) collective-permute-start(bf16[8,64,512]{2,1,0:T(8,128)(2,1)S(1)} %spectra.1), channel_id=1, source_target_pairs={{0,16},{8,24},{16,0},{24,8},{1,17},{9,25},{17,1},{25,9},{2,18},{10... | collective-permute-start | bytes 1572872 | tf_op jit(solution)/shard_map/ppermute | solution.py:268
  9.9 0.0 collective-permute-start.3
  9.9 6.5 %collective-permute-done.refs_2_ = bf16[4,2,32,1024]{3,2,1,0:T(8,128)(2,1)S(1)} collective-permute-done((bf16[4,2,32,1024]{3,2,1,0:T(8,128)(2,1)S(1)}, bf16[4,2,32,1024]{3,2,1,0:T(8,128)(2,1)S(1)}, u32[]{:S(2)}, u32[]{:S(2)}) %collective-permute-start) | collective-permute-done | bytes 524320 | tf_op jit(solution)/shard_map/ppermute | solution.py:270
  16.4 0.0 collective-permute-done.1.second_ref
  16.4 2.4 %collective-permute-done.2.refs_1_ = bf16[4,2,32,1024]{3,2,1,0:T(8,128)(2,1)S(1)} collective-permute-done((bf16[4,2,32,1024]{3,2,1,0:T(8,128)(2,1)S(1)}, bf16[4,2,32,1024]{3,2,1,0:T(8,128)(2,1)S(1)}, u32[]{:S(2)}, u32[]{:S(2)}) %collective-permute-start.2) | collective-permute-done | bytes 524320 | tf_op jit(solution)/shard_map/ppermute | solution.py:272
  18.8 1.9 %collective-permute-start.5 = (bf16[4,2,32,1024]{3,2,1,0:T(8,128)(2,1)S(1)}, bf16[4,2,32,1024]{3,2,1,0:T(8,128)(2,1)S(1)}, u32[]{:S(2)}, u32[]{:S(2)}) collective-permute-start(bf16[4,2,32,1024]{3,2,1,0:T(8,128)(2,1)S(1)} %collective-permute-done.1.second_ref), channel_id=1, source_target_pairs={{0,2},{1,3},{2,0},{3,1},{4,6},{5,7},{6,4},{7,5},{8,10},{9,11},{10,... | collective-permute-start | bytes 1572872 | tf_op jit(solution)/shard_map/ppermute | solution.py:275
  20.7 0.0 collective-permute-start.6
  20.7 1.5 %collective-permute-start.7 = (bf16[4,2,32,1024]{3,2,1,0:T(8,128)(2,1)S(1)}, bf16[4,2,32,1024]{3,2,1,0:T(8,128)(2,1)S(1)}, u32[]{:S(2)}, u32[]{:S(2)}) collective-permute-start(bf16[4,2,32,1024]{3,2,1,0:T(8,128)(2,1)S(1)} %collective-permute-done.refs_2_), channel_id=1, source_target_pairs={{0,1},{1,0},{2,3},{3,2},{4,5},{5,4},{6,7},{7,6},{8,9},{9,8},{10,11... | collective-permute-start | bytes 1572872 | tf_op jit(solution)/shard_map/ppermute | solution.py:277
  22.2 0.2 collective-permute-done.4
  22.4 0.0 collective-permute-start.8
  22.5 0.0 collective-permute-done.3
  22.5 4.5 %adjoint.1 = (f32[4,2,4,64,1024]{4,3,2,1,0:T(8,128)S(1)}, bf16[4,1024,1024]{2,1,0:T(8,128)(2,1)S(1)}) custom-call(bf16[4,1024,1024]{2,1,0:T(8,128)(2,1)} %bitcast.32, bf16[4,2,64,512]{3,2,1,0:T(8,128)(2,1)S(1)} %bitcast.22, bf16[4,2,64,512]{3,2,1,0:T(8,128)(2,1)S(1)} %bitcast.29), custom_call_target="tpu_custom_call" | custom-call | flops 2147483648 | bytes 8388608 | tf_op jit(solution)/shard_map/adjoint/pallas_call | solution.py:149
  26.9 5.4 %collective-permute-done.5.first_ref = bf16[4,2,32,1024]{3,2,1,0:T(8,128)(2,1)S(1)} collective-permute-done((bf16[4,2,32,1024]{3,2,1,0:T(8,128)(2,1)S(1)}, bf16[4,2,32,1024]{3,2,1,0:T(8,128)(2,1)S(1)}, u32[]{:S(2)}, u32[]{:S(2)}) %collective-permute-start.5) | collective-permute-done | bytes 524320 | tf_op jit(solution)/shard_map/ppermute | solution.py:275
  32.4 0.0 collective-permute-done.6.second_ref.refs_1_
  32.4 2.7 %collective-permute-done.7.refs_3_ = bf16[4,2,32,1024]{3,2,1,0:T(8,128)(2,1)S(1)} collective-permute-done((bf16[4,2,32,1024]{3,2,1,0:T(8,128)(2,1)S(1)}, bf16[4,2,32,1024]{3,2,1,0:T(8,128)(2,1)S(1)}, u32[]{:S(2)}, u32[]{:S(2)}) %collective-permute-start.7) | collective-permute-done | bytes 524320 | tf_op jit(solution)/shard_map/ppermute | solution.py:277
  35.1 0.0 collective-permute-done.8
  35.1 0.6 pick.3.refs_4_
  35.7 1.6 %collective-permute-start.11 = (bf16[4,2,32,1024]{3,2,1,0:T(8,128)(2,1)S(1)}, bf16[4,2,32,1024]{3,2,1,0:T(8,128)(2,1)S(1)}, u32[]{:S(2)}, u32[]{:S(2)}) collective-permute-start(bf16[4,2,32,1024]{3,2,1,0:T(8,128)(2,1)S(1)} %pick.3.refs_4_), channel_id=1, source_target_pairs={{0,1},{1,0},{2,3},{3,2},{4,5},{5,4},{6,7},{7,6},{8,9},{9,8},{10,11... | collective-permute-start | bytes 1572872 | tf_op jit(solution)/shard_map/ppermute | solution.py:289
  37.2 0.0 collective-permute-start.10
  37.2 3.4 %adjoint_rest.1 = (f32[4,2,4,64,1024]{4,3,2,1,0:T(8,128)S(1)}, bf16[4,2,32,1024]{3,2,1,0:T(8,128)(2,1)S(1)}) custom-call(s32[9]{0:T(128)S(1)} %stack.43.scalar_ref, bf16[4,1024,1024]{2,1,0:T(8,128)(2,1)S(1)} %get-tuple-element.24.green_ref, f32[4,2,4,64,1024]{4,3,2,1,0:T(8,128)S(1)} %get-tuple-element.25.base_ref, ...), custom_call_target="tpu_custom_call", output_to_operand_aliasing={{0}: (2, {})} | custom-call | flops 2147483648 | bytes 8388608 | tf_op jit(solution)/shard_map/adjoint_rest/pallas_call | solution.py:174
  40.7 0.6 pick.2
  41.3 0.9 %collective-permute-start.9 = (bf16[4,2,32,1024]{3,2,1,0:T(8,128)(2,1)S(1)}, bf16[4,2,32,1024]{3,2,1,0:T(8,128)(2,1)S(1)}, u32[]{:S(2)}, u32[]{:S(2)}) collective-permute-start(bf16[4,2,32,1024]{3,2,1,0:T(8,128)(2,1)S(1)} %pick.2), channel_id=1, source_target_pairs={{0,2},{1,3},{2,0},{3,1},{4,6},{5,7},{6,4},{7,5},{8,10},{9,11},{10,... | collective-permute-start | bytes 1572872 | tf_op jit(solution)/shard_map/ppermute | solution.py:286
  42.1 7.1 %collective-permute-done.11.refs_5_ = bf16[4,2,32,1024]{3,2,1,0:T(8,128)(2,1)S(1)} collective-permute-done((bf16[4,2,32,1024]{3,2,1,0:T(8,128)(2,1)S(1)}, bf16[4,2,32,1024]{3,2,1,0:T(8,128)(2,1)S(1)}, u32[]{:S(2)}, u32[]{:S(2)}) %collective-permute-start.11) | collective-permute-done | bytes 524320 | tf_op jit(solution)/shard_map/ppermute | solution.py:289
  49.3 0.0 collective-permute-done.10.refs_6_.refs_2_
  49.3 1.9 %weigh.2.refs_4_ = f32[8,1024]{1,0:T(8,128)S(1)} custom-call(s32[9]{0:T(128)S(1)} %stack.43.scalar_ref, f32[4,2,8,32,1024]{4,3,2,1,0:T(8,128)S(1)} %bitcast.20, bf16[4,2,32,1024]{3,2,1,0:T(8,128)(2,1)S(1)} %bitcast.26, bf16[4,2,32,1024]{3,2,1,0:T(8,128)(2,1)S(1)} %collective-permute-done.2.refs_1_, ...), custom_call_target="tpu_custom_call" | custom-call | flops 7340032 | bytes 7340032 | tf_op jit(solution)/shard_map/weigh/pallas_call | solution.py:195
  51.2 4.5 %collective-permute-done.9.refs_0_.refs_3_ = bf16[4,2,32,1024]{3,2,1,0:T(8,128)(2,1)S(1)} collective-permute-done((bf16[4,2,32,1024]{3,2,1,0:T(8,128)(2,1)S(1)}, bf16[4,2,32,1024]{3,2,1,0:T(8,128)(2,1)S(1)}, u32[]{:S(2)}, u32[]{:S(2)}) %collective-permute-start.9) | collective-permute-done | bytes 524320 | tf_op jit(solution)/shard_map/ppermute | solution.py:286
  55.7 0.9 %weigh.3 = f32[1,1024]{1,0:T(1,128)S(1)} custom-call(s32[9]{0:T(128)S(1)} %stack.43.scalar_ref, f32[4,2,8,32,1024]{4,3,2,1,0:T(8,128)S(1)} %bitcast.21, bf16[4,2,32,1024]{3,2,1,0:T(8,128)(2,1)S(1)} %collective-permute-done.9.refs_0_.refs_3_, bf16[4,2,32,1024]{3,2,1,0:T(8,128)(2,1)S(1)} %collective-permute-done.6.second_ref.refs_1_, ...), custom_call_target="tpu_custom_call" | custom-call | flops 4227072 | bytes 4227072 | tf_op jit(solution)/shard_map/weigh/pallas_call | solution.py:195
  56.6 0.6 collective-permute-start.12
  57.2 3.1 %collective-permute-done.12 = f32[1024]{0:T(1024)S(1)} collective-permute-done((f32[1024]{0:T(1024)S(1)}, f32[1024]{0:T(1024)S(1)}, u32[]{:S(2)}, u32[]{:S(2)}) %collective-permute-start.12) | collective-permute-done | bytes 4128 | tf_op jit(solution)/shard_map/ppermute | solution.py:310
  60.3 0.3 collective-permute-start.13
  60.6 3.3 %collective-permute-done.13 = f32[1024]{0:T(1024)S(1)} collective-permute-done((f32[1024]{0:T(1024)S(1)}, f32[1024]{0:T(1024)S(1)}, u32[]{:S(2)}, u32[]{:S(2)}) %collective-permute-start.13) | collective-permute-done | bytes 4128 | tf_op jit(solution)/shard_map/ppermute | solution.py:310
  63.9 0.0 collective-permute-start.14
  63.9 4.5 %collective-permute-done.14 = f32[1024]{0:T(1024)S(1)} collective-permute-done((f32[1024]{0:T(1024)S(1)}, f32[1024]{0:T(1024)S(1)}, u32[]{:S(2)}, u32[]{:S(2)}) %collective-permute-start.14) | collective-permute-done | bytes 4128 | tf_op jit(solution)/shard_map/ppermute | solution.py:310
  68.4 0.6 add.49
  (2 shorter events, 0.0 us)
Async XLA Ops:
  1.4 15.0 %collective-permute-start = (bf16[4,2,32,1024]{3,2,1,0:T(8,128)(2,1)S(1)}, bf16[4,2,32,1024]{3,2,1,0:T(8,128)(2,1)S(1)}, u32[]{:S(2)}, u32[]{:S(2)}) collective-permute-start(bf16[4,2,32,1024]{3,2,1,0:T(8,128)(2,1)S(1)} %bitcast.23), channel_id=1, source_target_pairs={{0,2},{1,3},{2,0},{3,1},{4,6},{5,7},{6,4},{7,5},{8,10},{9,11},{10,... | collective-permute-start | bytes 1572872 | tf_op jit(solution)/shard_map/ppermute | solution.py:270
  4.5 11.9 %collective-permute-start.1 = (bf16[4,2,32,1024]{3,2,1,0:T(8,128)(2,1)S(1)}, bf16[4,2,32,1024]{3,2,1,0:T(8,128)(2,1)S(1)}, u32[]{:S(2)}, u32[]{:S(2)}) collective-permute-start(bf16[4,2,32,1024]{3,2,1,0:T(8,128)(2,1)S(1)} %bitcast.24), channel_id=1, source_target_pairs={{2,4},{3,5},{4,2},{5,3},{10,12},{11,13},{12,10},{13,11},{18,20},{1... | collective-permute-start | bytes 1572872 | tf_op jit(solution)/shard_map/ppermute | solution.py:271
  4.5 14.3 %collective-permute-start.2 = (bf16[4,2,32,1024]{3,2,1,0:T(8,128)(2,1)S(1)}, bf16[4,2,32,1024]{3,2,1,0:T(8,128)(2,1)S(1)}, u32[]{:S(2)}, u32[]{:S(2)}) collective-permute-start(bf16[4,2,32,1024]{3,2,1,0:T(8,128)(2,1)S(1)} %bitcast.25), channel_id=1, source_target_pairs={{0,1},{1,0},{2,3},{3,2},{4,5},{5,4},{6,7},{7,6},{8,9},{9,8},{10,11... | collective-permute-start | bytes 1572872 | tf_op jit(solution)/shard_map/ppermute | solution.py:272
  8.3 14.1 %collective-permute-start.4 = (bf16[8,64,512]{2,1,0:T(8,128)(2,1)S(1)}, bf16[8,64,512]{2,1,0:T(8,128)(2,1)S(1)}, u32[]{:S(2)}, u32[]{:S(2)}) collective-permute-start(bf16[8,64,512]{2,1,0:T(8,128)(2,1)S(1)} %spectra.1), channel_id=1, source_target_pairs={{0,16},{8,24},{16,0},{24,8},{1,17},{9,25},{17,1},{25,9},{2,18},{10... | collective-permute-start | bytes 1572872 | tf_op jit(solution)/shard_map/ppermute | solution.py:268
  9.9 12.6 %collective-permute-start.3 = (bf16[8,64,512]{2,1,0:T(8,128)(2,1)S(1)}, bf16[8,64,512]{2,1,0:T(8,128)(2,1)S(1)}, u32[]{:S(2)}, u32[]{:S(2)}) collective-permute-start(bf16[8,64,512]{2,1,0:T(8,128)(2,1)S(1)} %spectra.1), channel_id=1, source_target_pairs={{0,8},{8,0},{16,24},{24,16},{1,9},{9,1},{17,25},{25,17},{2,10},{10... | collective-permute-start | bytes 1572872 | tf_op jit(solution)/shard_map/ppermute | solution.py:269
  18.8 13.6 %collective-permute-start.5 = (bf16[4,2,32,1024]{3,2,1,0:T(8,128)(2,1)S(1)}, bf16[4,2,32,1024]{3,2,1,0:T(8,128)(2,1)S(1)}, u32[]{:S(2)}, u32[]{:S(2)}) collective-permute-start(bf16[4,2,32,1024]{3,2,1,0:T(8,128)(2,1)S(1)} %collective-permute-done.1.second_ref), channel_id=1, source_target_pairs={{0,2},{1,3},{2,0},{3,1},{4,6},{5,7},{6,4},{7,5},{8,10},{9,11},{10,... | collective-permute-start | bytes 1572872 | tf_op jit(solution)/shard_map/ppermute | solution.py:275
  20.7 11.6 %collective-permute-start.6 = (bf16[4,2,32,1024]{3,2,1,0:T(8,128)(2,1)S(1)}, bf16[4,2,32,1024]{3,2,1,0:T(8,128)(2,1)S(1)}, u32[]{:S(2)}, u32[]{:S(2)}) collective-permute-start(bf16[4,2,32,1024]{3,2,1,0:T(8,128)(2,1)S(1)} %collective-permute-done.refs_2_), channel_id=1, source_target_pairs={{2,4},{3,5},{4,2},{5,3},{10,12},{11,13},{12,10},{13,11},{18,20},{1... | collective-permute-start | bytes 1572872 | tf_op jit(solution)/shard_map/ppermute | solution.py:276
  20.7 14.3 %collective-permute-start.7 = (bf16[4,2,32,1024]{3,2,1,0:T(8,128)(2,1)S(1)}, bf16[4,2,32,1024]{3,2,1,0:T(8,128)(2,1)S(1)}, u32[]{:S(2)}, u32[]{:S(2)}) collective-permute-start(bf16[4,2,32,1024]{3,2,1,0:T(8,128)(2,1)S(1)} %collective-permute-done.refs_2_), channel_id=1, source_target_pairs={{0,1},{1,0},{2,3},{3,2},{4,5},{5,4},{6,7},{7,6},{8,9},{9,8},{10,11... | collective-permute-start | bytes 1572872 | tf_op jit(solution)/shard_map/ppermute | solution.py:277
  22.4 12.6 %collective-permute-start.8 = (bf16[8,64,512]{2,1,0:T(8,128)(2,1)S(1)}, bf16[8,64,512]{2,1,0:T(8,128)(2,1)S(1)}, u32[]{:S(2)}, u32[]{:S(2)}) collective-permute-start(bf16[8,64,512]{2,1,0:T(8,128)(2,1)S(1)} %collective-permute-done.4), channel_id=1, source_target_pairs={{0,8},{8,0},{16,24},{24,16},{1,9},{9,1},{17,25},{25,17},{2,10},{10... | collective-permute-start | bytes 1572872 | tf_op jit(solution)/shard_map/ppermute | solution.py:280
  35.7 13.6 %collective-permute-start.11 = (bf16[4,2,32,1024]{3,2,1,0:T(8,128)(2,1)S(1)}, bf16[4,2,32,1024]{3,2,1,0:T(8,128)(2,1)S(1)}, u32[]{:S(2)}, u32[]{:S(2)}) collective-permute-start(bf16[4,2,32,1024]{3,2,1,0:T(8,128)(2,1)S(1)} %pick.3.refs_4_), channel_id=1, source_target_pairs={{0,1},{1,0},{2,3},{3,2},{4,5},{5,4},{6,7},{7,6},{8,9},{9,8},{10,11... | collective-permute-start | bytes 1572872 | tf_op jit(solution)/shard_map/ppermute | solution.py:289
  37.2 12.0 %collective-permute-start.10 = (bf16[4,2,32,1024]{3,2,1,0:T(8,128)(2,1)S(1)}, bf16[4,2,32,1024]{3,2,1,0:T(8,128)(2,1)S(1)}, u32[]{:S(2)}, u32[]{:S(2)}) collective-permute-start(bf16[4,2,32,1024]{3,2,1,0:T(8,128)(2,1)S(1)} %collective-permute-done.7.refs_3_), channel_id=1, source_target_pairs={{2,4},{3,5},{4,2},{5,3},{10,12},{11,13},{12,10},{13,11},{18,20},{1... | collective-permute-start | bytes 1572872 | tf_op jit(solution)/shard_map/ppermute | solution.py:287
  41.3 14.4 %collective-permute-start.9 = (bf16[4,2,32,1024]{3,2,1,0:T(8,128)(2,1)S(1)}, bf16[4,2,32,1024]{3,2,1,0:T(8,128)(2,1)S(1)}, u32[]{:S(2)}, u32[]{:S(2)}) collective-permute-start(bf16[4,2,32,1024]{3,2,1,0:T(8,128)(2,1)S(1)} %pick.2), channel_id=1, source_target_pairs={{0,2},{1,3},{2,0},{3,1},{4,6},{5,7},{6,4},{7,5},{8,10},{9,11},{10,... | collective-permute-start | bytes 1572872 | tf_op jit(solution)/shard_map/ppermute | solution.py:286
  56.6 3.7 %collective-permute-start.12 = (f32[1024]{0:T(1024)S(1)}, f32[1024]{0:T(1024)S(1)}, u32[]{:S(2)}, u32[]{:S(2)}) collective-permute-start(f32[1024]{0:T(1024)S(1)} %bitcast.30), channel_id=1, source_target_pairs={{0,1},{1,0},{2,3},{3,2},{4,5},{5,4},{6,7},{7,6},{8,9},{9,8},{10,11... | collective-permute-start | bytes 12296 | tf_op jit(solution)/shard_map/ppermute | solution.py:310
  60.3 3.6 %collective-permute-start.13 = (f32[1024]{0:T(1024)S(1)}, f32[1024]{0:T(1024)S(1)}, u32[]{:S(2)}, u32[]{:S(2)}) collective-permute-start(f32[1024]{0:T(1024)S(1)} %add.47), channel_id=1, source_target_pairs={{0,2},{1,3},{2,0},{3,1},{4,6},{5,7},{6,4},{7,5},{8,10},{9,11},{10,... | collective-permute-start | bytes 12296 | tf_op jit(solution)/shard_map/ppermute | solution.py:310
  63.9 4.5 %collective-permute-start.14 = (f32[1024]{0:T(1024)S(1)}, f32[1024]{0:T(1024)S(1)}, u32[]{:S(2)}, u32[]{:S(2)}) collective-permute-start(f32[1024]{0:T(1024)S(1)} %add.48), channel_id=1, source_target_pairs={{0,4},{1,5},{2,6},{3,7},{4,0},{5,1},{6,2},{7,3},{8,12},{9,13},{10,... | collective-permute-start | bytes 12296 | tf_op jit(solution)/shard_map/ppermute | solution.py:310

commit v10 on v9

--- a/solution.py
+++ b/solution.py
@@ -278,8 +278,8 @@
 
     adjoint, green_kept = adjoint_of([spectra, spectra_core], green, 4)
     spectra_both = send(spectra_x, "tx", core)
-    across_out, far, near_y, spectra_both = tie((across_out, far, near_y, spectra_both))
     adjoint, partial = adjoint_rest(scalars, [spectra_x, spectra_both], green_kept, adjoint)
+    across_out, near_y, partial = tie((across_out, near_y, partial))
     adjoint = adjoint.reshape((freqs, 2, 8) + own.shape[2:])
 
     swap = in_vmem(pick_kernel, scalars, [partial, far], own.shape, own.dtype, "pick")

time: 69.2 us -> 66.9 us (0.967)
  waiting for transfers between devices: 39.8 us -> 32.9 us
  starting transfers between devices: 12.9 us -> 17.5 us
    ppermute x1, waiting for transfers between devices: 0.21 us -> 8.6 us  [box_shards(): spectra_x = send(spectra, 'tx', along_x)]
    ppermute x1, waiting for transfers between devices: 6.49 us -> 1.46 us  [box_shards(): near = send(own, 'rx', z_pairs)]
    ppermute x1, waiting for transfers between devices: 5.4 us -> 2.45 us  [box_shards(): across_out = send(across, 'rx', z_pairs)]
    ppermute x1, waiting for transfers between devices: 2.7 us -> 0.01 us  [box_shards(): near_y = send(near, 'rx', along_y)]
    ppermute x1, starting transfers between devices: 0.85 us -> 3.39 us  [box_shards(): swap = send(swap, 'rx', z_pairs)]
    ppermute x1, waiting for transfers between devices: 4.5 us -> 1.99 us  [box_shards(): swap = send(swap, 'rx', z_pairs)]
    ppermute x3, starting transfers between devices: 0.86 us -> 3.07 us  [box_shards(): sums = sums + send(sums, 'rx', [(r, r ^ bit) for r in range(8)])]
    ppermute x3, waiting for transfers between devices: 10.9 us -> 8.72 us  [box_shards(): sums = sums + send(sums, 'rx', [(r, r ^ bit) for r in range(8)])]
  transfers between devices with their start and end apart: 15 -> 15, of which waited for: 10 -> 9; matrix products, arithmetic and copies ran while one was open for 0% -> 0% of each run, Pallas kernels for 18% -> 16%
where the time goes in v10:
time: 66.9 us; the launch traced here: 66.8 us
  waiting for transfers between devices  32.9 us (49%)
  starting transfers between devices  17.5 us (26%)
  Pallas kernels  14.2 us (21%)
  local copies, waits for them, and re-layouts  1.42 us (2%)
    ppermute x3, waiting for transfers between devices, box_shards(): sums = sums + send(sums, 'rx', [(r, r ^ bit) for r in range(8)])  8.72 us
    ppermute x1, waiting for transfers between devices, box_shards(): spectra_x = send(spectra, 'tx', along_x)  8.6 us
    ppermute x1, waiting for transfers between devices, box_shards(): mid_y = send(mid, 'rx', along_y)  7.16 us
    pallas_call x1, Pallas kernels, adjoint_of(): pl.pallas_call(functools.partial(adjoint_kernel, count), in_specs=[pl.Blo...  4.48 us
    pallas_call x4, Pallas kernels, in_vmem(): pl.pallas_call(kernel, in_specs=[pl.BlockSpec(memory_space=pltpu.SMEM)] +...  3.95 us
    pallas_call x1, Pallas kernels, adjoint_rest(): pl.pallas_call(functools.partial(adjoint_rest_kernel, count, half), in_sp...  3.44 us
    ppermute x1, starting transfers between devices, box_shards(): swap = send(swap, 'rx', z_pairs)  3.39 us
    ppermute x3, starting transfers between devices, box_shards(): sums = sums + send(sums, 'rx', [(r, r ^ bit) for r in range(8)])  3.07 us
  transfers between devices with their start and end apart: 15, of which 9 were waited for; matrix products, arithmetic and copies ran while one was open for 0% of the time, Pallas kernels for 16%

profile of v10, /device:TPU:0, one launch (start us, length us, event | category | flops | bytes accessed | tf_op | source)
XLA Modules:
  0.0 66.8 jit_solution(6751336606186600395)
XLA Ops:
  0.0 1.3 %copy.9 = bf16[32,4,2,1024]{3,0,2,1:T(8,128)(2,1)S(1)} copy(bf16[32,4,2,1024]{3,2,1,0:T(2,128)(2,1)} %param.8) | data formatting | bytes 1048576 | tf_op args[3]
  1.3 0.1 stack.43.scalar_ref
  1.4 2.3 %spectra.1 = bf16[8,64,512]{2,1,0:T(8,128)(2,1)S(1)} custom-call(bf16[128,640]{1,0:T(8,128)(2,1)} %constant.38.clone.table_hbm, s32[8,64]{1,0:T(8,128)} %bitcast.33, bf16[40,64,512]{2,1,0:T(8,128)(2,1)} %records_hbm), custom_call_target="tpu_custom_call" | custom-call | flops 335544320 | bytes 3145728 | tf_op jit(solution)/shard_map/spectra/pallas_call | solution.py:78
  3.8 3.0 %collective-permute-start.4 = (bf16[8,64,512]{2,1,0:T(8,128)(2,1)S(1)}, bf16[8,64,512]{2,1,0:T(8,128)(2,1)S(1)}, u32[]{:S(2)}, u32[]{:S(2)}) collective-permute-start(bf16[8,64,512]{2,1,0:T(8,128)(2,1)S(1)} %spectra.1), channel_id=1, source_target_pairs={{0,16},{8,24},{16,0},{24,8},{1,17},{9,25},{17,1},{25,9},{2,18},{10... | collective-permute-start | bytes 1572872 | tf_op jit(solution)/shard_map/ppermute | solution.py:268
  6.8 1.6 %collective-permute-start = (bf16[4,2,32,1024]{3,2,1,0:T(8,128)(2,1)S(1)}, bf16[4,2,32,1024]{3,2,1,0:T(8,128)(2,1)S(1)}, u32[]{:S(2)}, u32[]{:S(2)}) collective-permute-start(bf16[4,2,32,1024]{3,2,1,0:T(8,128)(2,1)S(1)} %bitcast.23), channel_id=1, source_target_pairs={{0,2},{1,3},{2,0},{3,1},{4,6},{5,7},{6,4},{7,5},{8,10},{9,11},{10,... | collective-permute-start | bytes 1572872 | tf_op jit(solution)/shard_map/ppermute | solution.py:270
  8.4 0.0 collective-permute-start.1
  8.4 1.5 %collective-permute-start.2 = (bf16[4,2,32,1024]{3,2,1,0:T(8,128)(2,1)S(1)}, bf16[4,2,32,1024]{3,2,1,0:T(8,128)(2,1)S(1)}, u32[]{:S(2)}, u32[]{:S(2)}) collective-permute-start(bf16[4,2,32,1024]{3,2,1,0:T(8,128)(2,1)S(1)} %bitcast.25), channel_id=1, source_target_pairs={{0,1},{1,0},{2,3},{3,2},{4,5},{5,4},{6,7},{7,6},{8,9},{9,8},{10,11... | collective-permute-start | bytes 1572872 | tf_op jit(solution)/shard_map/ppermute | solution.py:272
  9.9 0.2 collective-permute-start.3
  10.1 8.6 %collective-permute-done.4 = bf16[8,64,512]{2,1,0:T(8,128)(2,1)S(1)} collective-permute-done((bf16[8,64,512]{2,1,0:T(8,128)(2,1)S(1)}, bf16[8,64,512]{2,1,0:T(8,128)(2,1)S(1)}, u32[]{:S(2)}, u32[]{:S(2)}) %collective-permute-start.4) | collective-permute-done | bytes 524320 | tf_op jit(solution)/shard_map/ppermute | solution.py:268
  18.7 0.0 collective-permute-start.5
  18.7 1.5 %collective-permute-done.refs_2_ = bf16[4,2,32,1024]{3,2,1,0:T(8,128)(2,1)S(1)} collective-permute-done((bf16[4,2,32,1024]{3,2,1,0:T(8,128)(2,1)S(1)}, bf16[4,2,32,1024]{3,2,1,0:T(8,128)(2,1)S(1)}, u32[]{:S(2)}, u32[]{:S(2)}) %collective-permute-start) | collective-permute-done | bytes 524320 | tf_op jit(solution)/shard_map/ppermute | solution.py:270
  20.2 0.0 collective-permute-done.1.second_ref
  20.2 2.5 %collective-permute-done.2.refs_1_ = bf16[4,2,32,1024]{3,2,1,0:T(8,128)(2,1)S(1)} collective-permute-done((bf16[4,2,32,1024]{3,2,1,0:T(8,128)(2,1)S(1)}, bf16[4,2,32,1024]{3,2,1,0:T(8,128)(2,1)S(1)}, u32[]{:S(2)}, u32[]{:S(2)}) %collective-permute-start.2) | collective-permute-done | bytes 524320 | tf_op jit(solution)/shard_map/ppermute | solution.py:272
  22.7 1.6 %collective-permute-start.6 = (bf16[4,2,32,1024]{3,2,1,0:T(8,128)(2,1)S(1)}, bf16[4,2,32,1024]{3,2,1,0:T(8,128)(2,1)S(1)}, u32[]{:S(2)}, u32[]{:S(2)}) collective-permute-start(bf16[4,2,32,1024]{3,2,1,0:T(8,128)(2,1)S(1)} %collective-permute-done.1.second_ref), channel_id=1, source_target_pairs={{0,2},{1,3},{2,0},{3,1},{4,6},{5,7},{6,4},{7,5},{8,10},{9,11},{10,... | collective-permute-start | bytes 1572872 | tf_op jit(solution)/shard_map/ppermute | solution.py:275
  24.3 1.5 %collective-permute-start.7 = (bf16[4,2,32,1024]{3,2,1,0:T(8,128)(2,1)S(1)}, bf16[4,2,32,1024]{3,2,1,0:T(8,128)(2,1)S(1)}, u32[]{:S(2)}, u32[]{:S(2)}) collective-permute-start(bf16[4,2,32,1024]{3,2,1,0:T(8,128)(2,1)S(1)} %collective-permute-done.refs_2_), channel_id=1, source_target_pairs={{0,1},{1,0},{2,3},{3,2},{4,5},{5,4},{6,7},{7,6},{8,9},{9,8},{10,11... | collective-permute-start | bytes 1572872 | tf_op jit(solution)/shard_map/ppermute | solution.py:277
  25.9 0.0 collective-permute-start.8
  25.9 0.0 collective-permute-done.3
  25.9 4.5 %adjoint.1 = (f32[4,2,4,64,1024]{4,3,2,1,0:T(8,128)S(1)}, bf16[4,1024,1024]{2,1,0:T(8,128)(2,1)S(1)}) custom-call(bf16[4,1024,1024]{2,1,0:T(8,128)(2,1)} %bitcast.32, bf16[4,2,64,512]{3,2,1,0:T(8,128)(2,1)S(1)} %bitcast.22, bf16[4,2,64,512]{3,2,1,0:T(8,128)(2,1)S(1)} %bitcast.29), custom_call_target="tpu_custom_call" | custom-call | flops 2147483648 | bytes 8388608 | tf_op jit(solution)/shard_map/adjoint/pallas_call | solution.py:149
  30.4 0.0 collective-permute-done.5
  30.4 3.4 %adjoint_rest.1 = (f32[4,2,4,64,1024]{4,3,2,1,0:T(8,128)S(1)}, bf16[4,2,32,1024]{3,2,1,0:T(8,128)(2,1)S(1)}) custom-call(s32[9]{0:T(128)S(1)} %stack.43.scalar_ref, bf16[4,1024,1024]{2,1,0:T(8,128)(2,1)S(1)} %get-tuple-element.23.green_ref, f32[4,2,4,64,1024]{4,3,2,1,0:T(8,128)S(1)} %get-tuple-element.24.base_ref, ...), custom_call_target="tpu_custom_call", output_to_operand_aliasing={{0}: (2, {})} | custom-call | flops 2147483648 | bytes 8388608 | tf_op jit(solution)/shard_map/adjoint_rest/pallas_call | solution.py:174
  33.8 2.4 %collective-permute-done.6.first_ref = bf16[4,2,32,1024]{3,2,1,0:T(8,128)(2,1)S(1)} collective-permute-done((bf16[4,2,32,1024]{3,2,1,0:T(8,128)(2,1)S(1)}, bf16[4,2,32,1024]{3,2,1,0:T(8,128)(2,1)S(1)}, u32[]{:S(2)}, u32[]{:S(2)}) %collective-permute-start.6) | collective-permute-done | bytes 524320 | tf_op jit(solution)/shard_map/ppermute | solution.py:275
  36.3 0.0 collective-permute-done.7.refs_3_
  36.3 0.6 pick.3.refs_4_
  36.9 1.6 %collective-permute-start.11 = (bf16[4,2,32,1024]{3,2,1,0:T(8,128)(2,1)S(1)}, bf16[4,2,32,1024]{3,2,1,0:T(8,128)(2,1)S(1)}, u32[]{:S(2)}, u32[]{:S(2)}) collective-permute-start(bf16[4,2,32,1024]{3,2,1,0:T(8,128)(2,1)S(1)} %pick.3.refs_4_), channel_id=1, source_target_pairs={{0,1},{1,0},{2,3},{3,2},{4,5},{5,4},{6,7},{7,6},{8,9},{9,8},{10,11... | collective-permute-start | bytes 1572872 | tf_op jit(solution)/shard_map/ppermute | solution.py:289
  38.4 0.0 collective-permute-start.10
  38.4 0.0 collective-permute-done.8.second_ref.refs_1_
  38.4 0.6 pick.2
  39.0 3.4 %collective-permute-start.9 = (bf16[4,2,32,1024]{3,2,1,0:T(8,128)(2,1)S(1)}, bf16[4,2,32,1024]{3,2,1,0:T(8,128)(2,1)S(1)}, u32[]{:S(2)}, u32[]{:S(2)}) collective-permute-start(bf16[4,2,32,1024]{3,2,1,0:T(8,128)(2,1)S(1)} %pick.2), channel_id=1, source_target_pairs={{0,2},{1,3},{2,0},{3,1},{4,6},{5,7},{6,4},{7,5},{8,10},{9,11},{10,... | collective-permute-start | bytes 1572872 | tf_op jit(solution)/shard_map/ppermute | solution.py:286
  42.4 7.2 %collective-permute-done.11.refs_5_ = bf16[4,2,32,1024]{3,2,1,0:T(8,128)(2,1)S(1)} collective-permute-done((bf16[4,2,32,1024]{3,2,1,0:T(8,128)(2,1)S(1)}, bf16[4,2,32,1024]{3,2,1,0:T(8,128)(2,1)S(1)}, u32[]{:S(2)}, u32[]{:S(2)}) %collective-permute-start.11) | collective-permute-done | bytes 524320 | tf_op jit(solution)/shard_map/ppermute | solution.py:289
  49.6 0.0 collective-permute-done.10.refs_6_.refs_2_
  49.6 1.9 %weigh.2.refs_4_ = f32[8,1024]{1,0:T(8,128)S(1)} custom-call(s32[9]{0:T(128)S(1)} %stack.43.scalar_ref, f32[4,2,8,32,1024]{4,3,2,1,0:T(8,128)S(1)} %bitcast.20, bf16[4,2,32,1024]{3,2,1,0:T(8,128)(2,1)S(1)} %bitcast.26, bf16[4,2,32,1024]{3,2,1,0:T(8,128)(2,1)S(1)} %collective-permute-done.2.refs_1_, ...), custom_call_target="tpu_custom_call" | custom-call | flops 7340032 | bytes 7340032 | tf_op jit(solution)/shard_map/weigh/pallas_call | solution.py:195
  51.4 2.0 %collective-permute-done.9.refs_0_.refs_3_ = bf16[4,2,32,1024]{3,2,1,0:T(8,128)(2,1)S(1)} collective-permute-done((bf16[4,2,32,1024]{3,2,1,0:T(8,128)(2,1)S(1)}, bf16[4,2,32,1024]{3,2,1,0:T(8,128)(2,1)S(1)}, u32[]{:S(2)}, u32[]{:S(2)}) %collective-permute-start.9) | collective-permute-done | bytes 524320 | tf_op jit(solution)/shard_map/ppermute | solution.py:286
  53.4 0.9 %weigh.3 = f32[1,1024]{1,0:T(1,128)S(1)} custom-call(s32[9]{0:T(128)S(1)} %stack.43.scalar_ref, f32[4,2,8,32,1024]{4,3,2,1,0:T(8,128)S(1)} %bitcast.21, bf16[4,2,32,1024]{3,2,1,0:T(8,128)(2,1)S(1)} %collective-permute-done.9.refs_0_.refs_3_, bf16[4,2,32,1024]{3,2,1,0:T(8,128)(2,1)S(1)} %collective-permute-done.8.second_ref.refs_1_, ...), custom_call_target="tpu_custom_call" | custom-call | flops 4227072 | bytes 4227072 | tf_op jit(solution)/shard_map/weigh/pallas_call | solution.py:195
  54.4 0.6 collective-permute-start.12
  54.9 3.1 %collective-permute-done.12 = f32[1024]{0:T(1024)S(1)} collective-permute-done((f32[1024]{0:T(1024)S(1)}, f32[1024]{0:T(1024)S(1)}, u32[]{:S(2)}, u32[]{:S(2)}) %collective-permute-start.12) | collective-permute-done | bytes 4128 | tf_op jit(solution)/shard_map/ppermute | solution.py:310
  58.0 0.8 %collective-permute-start.13 = (f32[1024]{0:T(1024)S(1)}, f32[1024]{0:T(1024)S(1)}, u32[]{:S(2)}, u32[]{:S(2)}) collective-permute-start(f32[1024]{0:T(1024)S(1)} %add.47), channel_id=1, source_target_pairs={{0,2},{1,3},{2,0},{3,1},{4,6},{5,7},{6,4},{7,5},{8,10},{9,11},{10,... | collective-permute-start | bytes 12296 | tf_op jit(solution)/shard_map/ppermute | solution.py:310
  58.8 2.8 %collective-permute-done.13 = f32[1024]{0:T(1024)S(1)} collective-permute-done((f32[1024]{0:T(1024)S(1)}, f32[1024]{0:T(1024)S(1)}, u32[]{:S(2)}, u32[]{:S(2)}) %collective-permute-start.13) | collective-permute-done | bytes 4128 | tf_op jit(solution)/shard_map/ppermute | solution.py:310
  61.6 1.7 %collective-permute-start.14 = (f32[1024]{0:T(1024)S(1)}, f32[1024]{0:T(1024)S(1)}, u32[]{:S(2)}, u32[]{:S(2)}) collective-permute-start(f32[1024]{0:T(1024)S(1)} %add.48), channel_id=1, source_target_pairs={{0,4},{1,5},{2,6},{3,7},{4,0},{5,1},{6,2},{7,3},{8,12},{9,13},{10,... | collective-permute-start | bytes 12296 | tf_op jit(solution)/shard_map/ppermute | solution.py:310
  63.4 2.8 %collective-permute-done.14 = f32[1024]{0:T(1024)S(1)} collective-permute-done((f32[1024]{0:T(1024)S(1)}, f32[1024]{0:T(1024)S(1)}, u32[]{:S(2)}, u32[]{:S(2)}) %collective-permute-start.14) | collective-permute-done | bytes 4128 | tf_op jit(solution)/shard_map/ppermute | solution.py:310
  66.2 0.6 add.49
  (2 shorter events, 0.0 us)
Async XLA Ops:
  3.8 14.9 %collective-permute-start.4 = (bf16[8,64,512]{2,1,0:T(8,128)(2,1)S(1)}, bf16[8,64,512]{2,1,0:T(8,128)(2,1)S(1)}, u32[]{:S(2)}, u32[]{:S(2)}) collective-permute-start(bf16[8,64,512]{2,1,0:T(8,128)(2,1)S(1)} %spectra.1), channel_id=1, source_target_pairs={{0,16},{8,24},{16,0},{24,8},{1,17},{9,25},{17,1},{25,9},{2,18},{10... | collective-permute-start | bytes 1572872 | tf_op jit(solution)/shard_map/ppermute | solution.py:268
  6.8 13.4 %collective-permute-start = (bf16[4,2,32,1024]{3,2,1,0:T(8,128)(2,1)S(1)}, bf16[4,2,32,1024]{3,2,1,0:T(8,128)(2,1)S(1)}, u32[]{:S(2)}, u32[]{:S(2)}) collective-permute-start(bf16[4,2,32,1024]{3,2,1,0:T(8,128)(2,1)S(1)} %bitcast.23), channel_id=1, source_target_pairs={{0,2},{1,3},{2,0},{3,1},{4,6},{5,7},{6,4},{7,5},{8,10},{9,11},{10,... | collective-permute-start | bytes 1572872 | tf_op jit(solution)/shard_map/ppermute | solution.py:270
  8.4 11.8 %collective-permute-start.1 = (bf16[4,2,32,1024]{3,2,1,0:T(8,128)(2,1)S(1)}, bf16[4,2,32,1024]{3,2,1,0:T(8,128)(2,1)S(1)}, u32[]{:S(2)}, u32[]{:S(2)}) collective-permute-start(bf16[4,2,32,1024]{3,2,1,0:T(8,128)(2,1)S(1)} %bitcast.24), channel_id=1, source_target_pairs={{2,4},{3,5},{4,2},{5,3},{10,12},{11,13},{12,10},{13,11},{18,20},{1... | collective-permute-start | bytes 1572872 | tf_op jit(solution)/shard_map/ppermute | solution.py:271
  8.4 14.3 %collective-permute-start.2 = (bf16[4,2,32,1024]{3,2,1,0:T(8,128)(2,1)S(1)}, bf16[4,2,32,1024]{3,2,1,0:T(8,128)(2,1)S(1)}, u32[]{:S(2)}, u32[]{:S(2)}) collective-permute-start(bf16[4,2,32,1024]{3,2,1,0:T(8,128)(2,1)S(1)} %bitcast.25), channel_id=1, source_target_pairs={{0,1},{1,0},{2,3},{3,2},{4,5},{5,4},{6,7},{7,6},{8,9},{9,8},{10,11... | collective-permute-start | bytes 1572872 | tf_op jit(solution)/shard_map/ppermute | solution.py:272
  9.9 16.0 %collective-permute-start.3 = (bf16[8,64,512]{2,1,0:T(8,128)(2,1)S(1)}, bf16[8,64,512]{2,1,0:T(8,128)(2,1)S(1)}, u32[]{:S(2)}, u32[]{:S(2)}) collective-permute-start(bf16[8,64,512]{2,1,0:T(8,128)(2,1)S(1)} %spectra.1), channel_id=1, source_target_pairs={{0,8},{8,0},{16,24},{24,16},{1,9},{9,1},{17,25},{25,17},{2,10},{10... | collective-permute-start | bytes 1572872 | tf_op jit(solution)/shard_map/ppermute | solution.py:269
  18.7 11.6 %collective-permute-start.5 = (bf16[8,64,512]{2,1,0:T(8,128)(2,1)S(1)}, bf16[8,64,512]{2,1,0:T(8,128)(2,1)S(1)}, u32[]{:S(2)}, u32[]{:S(2)}) collective-permute-start(bf16[8,64,512]{2,1,0:T(8,128)(2,1)S(1)} %collective-permute-done.4), channel_id=1, source_target_pairs={{0,8},{8,0},{16,24},{24,16},{1,9},{9,1},{17,25},{25,17},{2,10},{10... | collective-permute-start | bytes 1572872 | tf_op jit(solution)/shard_map/ppermute | solution.py:280
  22.7 13.6 %collective-permute-start.6 = (bf16[4,2,32,1024]{3,2,1,0:T(8,128)(2,1)S(1)}, bf16[4,2,32,1024]{3,2,1,0:T(8,128)(2,1)S(1)}, u32[]{:S(2)}, u32[]{:S(2)}) collective-permute-start(bf16[4,2,32,1024]{3,2,1,0:T(8,128)(2,1)S(1)} %collective-permute-done.1.second_ref), channel_id=1, source_target_pairs={{0,2},{1,3},{2,0},{3,1},{4,6},{5,7},{6,4},{7,5},{8,10},{9,11},{10,... | collective-permute-start | bytes 1572872 | tf_op jit(solution)/shard_map/ppermute | solution.py:275
  24.3 11.9 %collective-permute-start.7 = (bf16[4,2,32,1024]{3,2,1,0:T(8,128)(2,1)S(1)}, bf16[4,2,32,1024]{3,2,1,0:T(8,128)(2,1)S(1)}, u32[]{:S(2)}, u32[]{:S(2)}) collective-permute-start(bf16[4,2,32,1024]{3,2,1,0:T(8,128)(2,1)S(1)} %collective-permute-done.refs_2_), channel_id=1, source_target_pairs={{0,1},{1,0},{2,3},{3,2},{4,5},{5,4},{6,7},{7,6},{8,9},{9,8},{10,11... | collective-permute-start | bytes 1572872 | tf_op jit(solution)/shard_map/ppermute | solution.py:277
  25.9 12.6 %collective-permute-start.8 = (bf16[4,2,32,1024]{3,2,1,0:T(8,128)(2,1)S(1)}, bf16[4,2,32,1024]{3,2,1,0:T(8,128)(2,1)S(1)}, u32[]{:S(2)}, u32[]{:S(2)}) collective-permute-start(bf16[4,2,32,1024]{3,2,1,0:T(8,128)(2,1)S(1)} %collective-permute-done.refs_2_), channel_id=1, source_target_pairs={{2,4},{3,5},{4,2},{5,3},{10,12},{11,13},{12,10},{13,11},{18,20},{1... | collective-permute-start | bytes 1572872 | tf_op jit(solution)/shard_map/ppermute | solution.py:276
  36.9 12.7 %collective-permute-start.11 = (bf16[4,2,32,1024]{3,2,1,0:T(8,128)(2,1)S(1)}, bf16[4,2,32,1024]{3,2,1,0:T(8,128)(2,1)S(1)}, u32[]{:S(2)}, u32[]{:S(2)}) collective-permute-start(bf16[4,2,32,1024]{3,2,1,0:T(8,128)(2,1)S(1)} %pick.3.refs_4_), channel_id=1, source_target_pairs={{0,1},{1,0},{2,3},{3,2},{4,5},{5,4},{6,7},{7,6},{8,9},{9,8},{10,11... | collective-permute-start | bytes 1572872 | tf_op jit(solution)/shard_map/ppermute | solution.py:289
  38.4 11.2 %collective-permute-start.10 = (bf16[4,2,32,1024]{3,2,1,0:T(8,128)(2,1)S(1)}, bf16[4,2,32,1024]{3,2,1,0:T(8,128)(2,1)S(1)}, u32[]{:S(2)}, u32[]{:S(2)}) collective-permute-start(bf16[4,2,32,1024]{3,2,1,0:T(8,128)(2,1)S(1)} %collective-permute-done.7.refs_3_), channel_id=1, source_target_pairs={{2,4},{3,5},{4,2},{5,3},{10,12},{11,13},{12,10},{13,11},{18,20},{1... | collective-permute-start | bytes 1572872 | tf_op jit(solution)/shard_map/ppermute | solution.py:287
  39.0 14.4 %collective-permute-start.9 = (bf16[4,2,32,1024]{3,2,1,0:T(8,128)(2,1)S(1)}, bf16[4,2,32,1024]{3,2,1,0:T(8,128)(2,1)S(1)}, u32[]{:S(2)}, u32[]{:S(2)}) collective-permute-start(bf16[4,2,32,1024]{3,2,1,0:T(8,128)(2,1)S(1)} %pick.2), channel_id=1, source_target_pairs={{0,2},{1,3},{2,0},{3,1},{4,6},{5,7},{6,4},{7,5},{8,10},{9,11},{10,... | collective-permute-start | bytes 1572872 | tf_op jit(solution)/shard_map/ppermute | solution.py:286
  54.4 3.7 %collective-permute-start.12 = (f32[1024]{0:T(1024)S(1)}, f32[1024]{0:T(1024)S(1)}, u32[]{:S(2)}, u32[]{:S(2)}) collective-permute-start(f32[1024]{0:T(1024)S(1)} %bitcast.30), channel_id=1, source_target_pairs={{0,1},{1,0},{2,3},{3,2},{4,5},{5,4},{6,7},{7,6},{8,9},{9,8},{10,11... | collective-permute-start | bytes 12296 | tf_op jit(solution)/shard_map/ppermute | solution.py:310
  58.0 3.6 %collective-permute-start.13 = (f32[1024]{0:T(1024)S(1)}, f32[1024]{0:T(1024)S(1)}, u32[]{:S(2)}, u32[]{:S(2)}) collective-permute-start(f32[1024]{0:T(1024)S(1)} %add.47), channel_id=1, source_target_pairs={{0,2},{1,3},{2,0},{3,1},{4,6},{5,7},{6,4},{7,5},{8,10},{9,11},{10,... | collective-permute-start | bytes 12296 | tf_op jit(solution)/shard_map/ppermute | solution.py:310
  61.6 4.5 %collective-permute-start.14 = (f32[1024]{0:T(1024)S(1)}, f32[1024]{0:T(1024)S(1)}, u32[]{:S(2)}, u32[]{:S(2)}) collective-permute-start(f32[1024]{0:T(1024)S(1)} %add.48), channel_id=1, source_target_pairs={{0,4},{1,5},{2,6},{3,7},{4,0},{5,1},{6,2},{7,3},{8,12},{9,13},{10,... | collective-permute-start | bytes 12296 | tf_op jit(solution)/shard_map/ppermute | solution.py:310

commit v11 on v10

--- a/solution.py
+++ b/solution.py
@@ -249,6 +249,8 @@
     z_pairs = [(r, r ^ 2) for r in range(8)]
     z_middle = [(t * 8 + r, t * 8 + (r ^ 6)) for t in range(4) for r in range(2, 6)]
     z_middle += [(t * 8 + r, (t ^ 1) * 8 + r) for t in range(4) for r in (0, 1, 6, 7)]
+    z_middle_x = [(t * 8 + r, t * 8 + (r ^ 6)) for t in range(4) for r in range(2, 6)]
+    z_middle_x += [(t * 8 + r, (t ^ 2) * 8 + r) for t in range(4) for r in (0, 1, 6, 7)]
     core = [(t, t ^ 1) for t in range(4)]
     along_x = [(t, t ^ 2) for t in range(4)]
     send, tie = lax.ppermute, lax.optimization_barrier
@@ -273,18 +275,17 @@
     near, across, own_y, spectra = tie((near, across, own_y, spectra))
 
     across_out = send(across, "rx", z_pairs)
-    far = send(near, ("tx", "rx"), z_middle)
+    far = send(near, ("tx", "rx"), z_middle_x)
     near_y = send(near, "rx", along_y)
 
     adjoint, green_kept = adjoint_of([spectra, spectra_core], green, 4)
     spectra_both = send(spectra_x, "tx", core)
     adjoint, partial = adjoint_rest(scalars, [spectra_x, spectra_both], green_kept, adjoint)
-    across_out, near_y, partial = tie((across_out, near_y, partial))
     adjoint = adjoint.reshape((freqs, 2, 8) + own.shape[2:])
 
     swap = in_vmem(pick_kernel, scalars, [partial, far], own.shape, own.dtype, "pick")
     swap = send(swap, "rx", z_pairs)
-    far_both = send(near_y, ("tx", "rx"), z_middle)
+    far_both = send(near_y, ("tx", "rx"), z_middle_x)
     mid = in_vmem(pick_kernel, scalars, [across_out, across], own.shape, own.dtype, "pick")
     mid_y = send(mid, "rx", along_y)
 
@@ -306,8 +307,8 @@
         "weigh",
     )
     sums = sums.reshape(cells)
-    for bit in (1, 2, 4):
-        sums = sums + send(sums, "rx", [(r, r ^ bit) for r in range(8)])
+    for bits in ((3, 2, 1), (4,)):
+        sums = sums + sum(send(sums, "rx", [(r, r ^ bit) for r in range(8)]) for bit in bits)
     return sums
 
 

time: 66.9 us -> 64.1 us (0.958)
  waiting for transfers between devices: 32.9 us -> 28.1 us
  starting transfers between devices: 17.5 us -> 19.4 us
    ppermute x1, waiting for transfers between devices: 8.6 us -> 0.21 us  [box_shards(): spectra_x = send(spectra, 'tx', along_x)]
    ppermute x1, waiting for transfers between devices: 1.46 us -> 6.49 us  [box_shards(): near = send(own, 'rx', z_pairs)]
    ppermute x5 -> x6, starting transfers between devices: 3.07 us -> 7.84 us  [the longest x4 4.85 us: box_shards(): send(sums, 'rx', [(r, r ^ bit) for r in range(8)])]
    ppermute x1, starting transfers between devices: 3.39 us -> 0.43 us  [box_shards(): swap = send(swap, 'rx', z_pairs)]
    ppermute x1, waiting for transfers between devices: 7.16 us -> 5.16 us  [box_shards(): mid_y = send(mid, 'rx', along_y)]
    ppermute x1, waiting for transfers between devices: 2.45 us -> 3.93 us  [box_shards(): across_out = send(across, 'rx', z_pairs)]
    ppermute x1, starting transfers between devices: 1.59 us -> 3.03 us  [box_shards(): near = send(own, 'rx', z_pairs)]
    ppermute x1, starting transfers between devices: 2.99 us -> 1.55 us  [box_shards(): spectra_x = send(spectra, 'tx', along_x)]
  transfers between devices with their start and end apart: 15 -> 16, of which waited for: 9 -> 10; matrix products, arithmetic and copies ran while one was open for 0% -> 0% of each run, Pallas kernels for 16% -> 21%
where the time goes in v11:
time: 64.1 us; the launch traced here: 63.9 us
  waiting for transfers between devices  28.1 us (44%)
  starting transfers between devices  19.4 us (30%)
  Pallas kernels  14.3 us (22%)
  local copies, waits for them, and re-layouts  1.42 us (2%)
    ppermute x1, waiting for transfers between devices, box_shards(): near = send(own, 'rx', z_pairs)  6.49 us
    ppermute x4, waiting for transfers between devices, box_shards(): send(sums, 'rx', [(r, r ^ bit) for r in range(8)])  5.29 us
    ppermute x1, waiting for transfers between devices, box_shards(): mid_y = send(mid, 'rx', along_y)  5.16 us
    ppermute x4, starting transfers between devices, box_shards(): send(sums, 'rx', [(r, r ^ bit) for r in range(8)])  4.85 us
    pallas_call x1, Pallas kernels, adjoint_of(): pl.pallas_call(functools.partial(adjoint_kernel, count), in_specs=[pl.Blo...  4.47 us
    pallas_call x4, Pallas kernels, in_vmem(): pl.pallas_call(kernel, in_specs=[pl.BlockSpec(memory_space=pltpu.SMEM)] +...  4.03 us
    ppermute x1, waiting for transfers between devices, box_shards(): across_out = send(across, 'rx', z_pairs)  3.93 us
    pallas_call x1, Pallas kernels, adjoint_rest(): pl.pallas_call(functools.partial(adjoint_rest_kernel, count, half), in_sp...  3.45 us
  transfers between devices with their start and end apart: 16, of which 10 were waited for; matrix products, arithmetic and copies ran while one was open for 0% of the time, Pallas kernels for 21%

profile of v11, /device:TPU:0, one launch (start us, length us, event | category | flops | bytes accessed | tf_op | source)
XLA Modules:
  0.0 63.9 jit_solution(715205462513212746)
XLA Ops:
  0.0 1.3 %copy.9 = bf16[32,4,2,1024]{3,0,2,1:T(8,128)(2,1)S(1)} copy(bf16[32,4,2,1024]{3,2,1,0:T(2,128)(2,1)} %param.8) | data formatting | bytes 1048576 | tf_op args[3]
  1.3 0.1 stack.43.scalar_ref
  1.4 3.0 %collective-permute-start = (bf16[4,2,32,1024]{3,2,1,0:T(8,128)(2,1)S(1)}, bf16[4,2,32,1024]{3,2,1,0:T(8,128)(2,1)S(1)}, u32[]{:S(2)}, u32[]{:S(2)}) collective-permute-start(bf16[4,2,32,1024]{3,2,1,0:T(8,128)(2,1)S(1)} %bitcast.23), channel_id=1, source_target_pairs={{0,2},{1,3},{2,0},{3,1},{4,6},{5,7},{6,4},{7,5},{8,10},{9,11},{10,... | collective-permute-start | bytes 1572872 | tf_op jit(solution)/shard_map/ppermute | solution.py:272
  4.5 0.0 collective-permute-start.1
  4.5 1.5 %collective-permute-start.2 = (bf16[4,2,32,1024]{3,2,1,0:T(8,128)(2,1)S(1)}, bf16[4,2,32,1024]{3,2,1,0:T(8,128)(2,1)S(1)}, u32[]{:S(2)}, u32[]{:S(2)}) collective-permute-start(bf16[4,2,32,1024]{3,2,1,0:T(8,128)(2,1)S(1)} %bitcast.25), channel_id=1, source_target_pairs={{0,1},{1,0},{2,3},{3,2},{4,5},{5,4},{6,7},{7,6},{8,9},{9,8},{10,11... | collective-permute-start | bytes 1572872 | tf_op jit(solution)/shard_map/ppermute | solution.py:274
  6.0 2.3 %spectra.1 = bf16[8,64,512]{2,1,0:T(8,128)(2,1)S(1)} custom-call(bf16[128,640]{1,0:T(8,128)(2,1)} %constant.38.clone.table_hbm, s32[8,64]{1,0:T(8,128)} %bitcast.35, bf16[40,64,512]{2,1,0:T(8,128)(2,1)} %records_hbm), custom_call_target="tpu_custom_call" | custom-call | flops 335544320 | bytes 3145728 | tf_op jit(solution)/shard_map/spectra/pallas_call | solution.py:78
  8.3 1.6 %collective-permute-start.4 = (bf16[8,64,512]{2,1,0:T(8,128)(2,1)S(1)}, bf16[8,64,512]{2,1,0:T(8,128)(2,1)S(1)}, u32[]{:S(2)}, u32[]{:S(2)}) collective-permute-start(bf16[8,64,512]{2,1,0:T(8,128)(2,1)S(1)} %spectra.1), channel_id=1, source_target_pairs={{0,16},{8,24},{16,0},{24,8},{1,17},{9,25},{17,1},{25,9},{2,18},{10... | collective-permute-start | bytes 1572872 | tf_op jit(solution)/shard_map/ppermute | solution.py:270
  9.9 0.0 collective-permute-start.3
  9.9 6.5 %collective-permute-done.refs_2_ = bf16[4,2,32,1024]{3,2,1,0:T(8,128)(2,1)S(1)} collective-permute-done((bf16[4,2,32,1024]{3,2,1,0:T(8,128)(2,1)S(1)}, bf16[4,2,32,1024]{3,2,1,0:T(8,128)(2,1)S(1)}, u32[]{:S(2)}, u32[]{:S(2)}) %collective-permute-start) | collective-permute-done | bytes 524320 | tf_op jit(solution)/shard_map/ppermute | solution.py:272
  16.4 0.0 collective-permute-done.1.second_ref
  16.4 2.4 %collective-permute-done.2.refs_1_ = bf16[4,2,32,1024]{3,2,1,0:T(8,128)(2,1)S(1)} collective-permute-done((bf16[4,2,32,1024]{3,2,1,0:T(8,128)(2,1)S(1)}, bf16[4,2,32,1024]{3,2,1,0:T(8,128)(2,1)S(1)}, u32[]{:S(2)}, u32[]{:S(2)}) %collective-permute-start.2) | collective-permute-done | bytes 524320 | tf_op jit(solution)/shard_map/ppermute | solution.py:274
  18.8 1.9 %collective-permute-start.10 = (bf16[4,2,32,1024]{3,2,1,0:T(8,128)(2,1)S(1)}, bf16[4,2,32,1024]{3,2,1,0:T(8,128)(2,1)S(1)}, u32[]{:S(2)}, u32[]{:S(2)}) collective-permute-start(bf16[4,2,32,1024]{3,2,1,0:T(8,128)(2,1)S(1)} %collective-permute-done.1.second_ref), channel_id=1, source_target_pairs={{0,2},{1,3},{2,0},{3,1},{4,6},{5,7},{6,4},{7,5},{8,10},{9,11},{10,... | collective-permute-start | bytes 1572872 | tf_op jit(solution)/shard_map/ppermute | solution.py:277
  20.7 1.5 %collective-permute-start.8 = (bf16[4,2,32,1024]{3,2,1,0:T(8,128)(2,1)S(1)}, bf16[4,2,32,1024]{3,2,1,0:T(8,128)(2,1)S(1)}, u32[]{:S(2)}, u32[]{:S(2)}) collective-permute-start(bf16[4,2,32,1024]{3,2,1,0:T(8,128)(2,1)S(1)} %collective-permute-done.refs_2_), channel_id=1, source_target_pairs={{0,1},{1,0},{2,3},{3,2},{4,5},{5,4},{6,7},{7,6},{8,9},{9,8},{10,11... | collective-permute-start | bytes 1572872 | tf_op jit(solution)/shard_map/ppermute | solution.py:279
  22.2 0.2 collective-permute-done.4
  22.4 0.0 collective-permute-start.5
  22.4 1.5 %collective-permute-start.6 = (bf16[4,2,32,1024]{3,2,1,0:T(8,128)(2,1)S(1)}, bf16[4,2,32,1024]{3,2,1,0:T(8,128)(2,1)S(1)}, u32[]{:S(2)}, u32[]{:S(2)}) collective-permute-start(bf16[4,2,32,1024]{3,2,1,0:T(8,128)(2,1)S(1)} %collective-permute-done.refs_2_), channel_id=1, source_target_pairs={{2,4},{3,5},{4,2},{5,3},{10,12},{11,13},{12,10},{13,11},{18,20},{1... | collective-permute-start | bytes 1572872 | tf_op jit(solution)/shard_map/ppermute | solution.py:278
  23.9 0.0 collective-permute-done.3
  23.9 4.5 %adjoint.1 = (f32[4,2,4,64,1024]{4,3,2,1,0:T(8,128)S(1)}, bf16[4,1024,1024]{2,1,0:T(8,128)(2,1)S(1)}) custom-call(bf16[4,1024,1024]{2,1,0:T(8,128)(2,1)} %bitcast.34, bf16[4,2,64,512]{3,2,1,0:T(8,128)(2,1)S(1)} %bitcast.22, bf16[4,2,64,512]{3,2,1,0:T(8,128)(2,1)S(1)} %bitcast.29), custom_call_target="tpu_custom_call" | custom-call | flops 2147483648 | bytes 8388608 | tf_op jit(solution)/shard_map/adjoint/pallas_call | solution.py:149
  28.4 3.9 %collective-permute-done.10.first_ref = bf16[4,2,32,1024]{3,2,1,0:T(8,128)(2,1)S(1)} collective-permute-done((bf16[4,2,32,1024]{3,2,1,0:T(8,128)(2,1)S(1)}, bf16[4,2,32,1024]{3,2,1,0:T(8,128)(2,1)S(1)}, u32[]{:S(2)}, u32[]{:S(2)}) %collective-permute-start.10) | collective-permute-done | bytes 524320 | tf_op jit(solution)/shard_map/ppermute | solution.py:277
  32.4 0.6 pick.3.refs_4_
  32.9 1.6 %collective-permute-start.11 = (bf16[4,2,32,1024]{3,2,1,0:T(8,128)(2,1)S(1)}, bf16[4,2,32,1024]{3,2,1,0:T(8,128)(2,1)S(1)}, u32[]{:S(2)}, u32[]{:S(2)}) collective-permute-start(bf16[4,2,32,1024]{3,2,1,0:T(8,128)(2,1)S(1)} %pick.3.refs_4_), channel_id=1, source_target_pairs={{0,1},{1,0},{2,3},{3,2},{4,5},{5,4},{6,7},{7,6},{8,9},{9,8},{10,11... | collective-permute-start | bytes 1572872 | tf_op jit(solution)/shard_map/ppermute | solution.py:290
  34.5 0.0 collective-permute-done.8.refs_3_
  34.5 1.5 %collective-permute-start.9 = (bf16[4,2,32,1024]{3,2,1,0:T(8,128)(2,1)S(1)}, bf16[4,2,32,1024]{3,2,1,0:T(8,128)(2,1)S(1)}, u32[]{:S(2)}, u32[]{:S(2)}) collective-permute-start(bf16[4,2,32,1024]{3,2,1,0:T(8,128)(2,1)S(1)} %collective-permute-done.8.refs_3_), channel_id=1, source_target_pairs={{2,4},{3,5},{4,2},{5,3},{10,12},{11,13},{12,10},{13,11},{18,20},{1... | collective-permute-start | bytes 1572872 | tf_op jit(solution)/shard_map/ppermute | solution.py:288
  36.0 0.0 collective-permute-done.5
  36.0 3.4 %adjoint_rest.1 = (f32[4,2,4,64,1024]{4,3,2,1,0:T(8,128)S(1)}, bf16[4,2,32,1024]{3,2,1,0:T(8,128)(2,1)S(1)}) custom-call(s32[9]{0:T(128)S(1)} %stack.43.scalar_ref, bf16[4,1024,1024]{2,1,0:T(8,128)(2,1)S(1)} %get-tuple-element.20.green_ref, f32[4,2,4,64,1024]{4,3,2,1,0:T(8,128)S(1)} %get-tuple-element.21.base_ref, ...), custom_call_target="tpu_custom_call", output_to_operand_aliasing={{0}: (2, {})} | custom-call | flops 2147483648 | bytes 8388608 | tf_op jit(solution)/shard_map/adjoint_rest/pallas_call | solution.py:174
  39.5 0.0 collective-permute-done.6.second_ref.refs_1_
  39.5 0.6 pick.2
  40.1 0.4 collective-permute-start.7
  40.5 5.2 %collective-permute-done.11.refs_5_ = bf16[4,2,32,1024]{3,2,1,0:T(8,128)(2,1)S(1)} collective-permute-done((bf16[4,2,32,1024]{3,2,1,0:T(8,128)(2,1)S(1)}, bf16[4,2,32,1024]{3,2,1,0:T(8,128)(2,1)S(1)}, u32[]{:S(2)}, u32[]{:S(2)}) %collective-permute-start.11) | collective-permute-done | bytes 524320 | tf_op jit(solution)/shard_map/ppermute | solution.py:290
  45.7 2.3 %collective-permute-done.9.refs_6_.refs_2_ = bf16[4,2,32,1024]{3,2,1,0:T(8,128)(2,1)S(1)} collective-permute-done((bf16[4,2,32,1024]{3,2,1,0:T(8,128)(2,1)S(1)}, bf16[4,2,32,1024]{3,2,1,0:T(8,128)(2,1)S(1)}, u32[]{:S(2)}, u32[]{:S(2)}) %collective-permute-start.9) | collective-permute-done | bytes 524320 | tf_op jit(solution)/shard_map/ppermute | solution.py:288
  48.0 1.9 %weigh.2.refs_4_ = f32[8,1024]{1,0:T(8,128)S(1)} custom-call(s32[9]{0:T(128)S(1)} %stack.43.scalar_ref, f32[4,2,8,32,1024]{4,3,2,1,0:T(8,128)S(1)} %bitcast.20, bf16[4,2,32,1024]{3,2,1,0:T(8,128)(2,1)S(1)} %bitcast.26, bf16[4,2,32,1024]{3,2,1,0:T(8,128)(2,1)S(1)} %collective-permute-done.2.refs_1_, ...), custom_call_target="tpu_custom_call" | custom-call | flops 7340032 | bytes 7340032 | tf_op jit(solution)/shard_map/weigh/pallas_call | solution.py:195
  50.0 2.3 %collective-permute-done.7.refs_0_.refs_3_ = bf16[4,2,32,1024]{3,2,1,0:T(8,128)(2,1)S(1)} collective-permute-done((bf16[4,2,32,1024]{3,2,1,0:T(8,128)(2,1)S(1)}, bf16[4,2,32,1024]{3,2,1,0:T(8,128)(2,1)S(1)}, u32[]{:S(2)}, u32[]{:S(2)}) %collective-permute-start.7) | collective-permute-done | bytes 524320 | tf_op jit(solution)/shard_map/ppermute | solution.py:287
  52.3 0.9 %weigh.3 = f32[1,1024]{1,0:T(1,128)S(1)} custom-call(s32[9]{0:T(128)S(1)} %stack.43.scalar_ref, f32[4,2,8,32,1024]{4,3,2,1,0:T(8,128)S(1)} %bitcast.21, bf16[4,2,32,1024]{3,2,1,0:T(8,128)(2,1)S(1)} %collective-permute-done.7.refs_0_.refs_3_, bf16[4,2,32,1024]{3,2,1,0:T(8,128)(2,1)S(1)} %collective-permute-done.6.second_ref.refs_1_, ...), custom_call_target="tpu_custom_call" | custom-call | flops 4227072 | bytes 4227072 | tf_op jit(solution)/shard_map/weigh/pallas_call | solution.py:195
  53.2 0.7 %collective-permute-start.12 = (f32[1024]{0:T(1024)S(1)}, f32[1024]{0:T(1024)S(1)}, u32[]{:S(2)}, u32[]{:S(2)}) collective-permute-start(f32[1024]{0:T(1024)S(1)} %bitcast.30), channel_id=1, source_target_pairs={{0,3},{1,2},{2,1},{3,0},{4,7},{5,6},{6,5},{7,4},{8,11},{9,10},{10,... | collective-permute-start | bytes 12296 | tf_op jit(solution)/shard_map/ppermute | solution.py:311
  53.8 1.4 %collective-permute-start.13 = (f32[1024]{0:T(1024)S(1)}, f32[1024]{0:T(1024)S(1)}, u32[]{:S(2)}, u32[]{:S(2)}) collective-permute-start(f32[1024]{0:T(1024)S(1)} %bitcast.31), channel_id=1, source_target_pairs={{0,2},{1,3},{2,0},{3,1},{4,6},{5,7},{6,4},{7,5},{8,10},{9,11},{10,... | collective-permute-start | bytes 12296 | tf_op jit(solution)/shard_map/ppermute | solution.py:311
  55.2 1.5 %collective-permute-start.14 = (f32[1024]{0:T(1024)S(1)}, f32[1024]{0:T(1024)S(1)}, u32[]{:S(2)}, u32[]{:S(2)}) collective-permute-start(f32[1024]{0:T(1024)S(1)} %bitcast.32), channel_id=1, source_target_pairs={{0,1},{1,0},{2,3},{3,2},{4,5},{5,4},{6,7},{7,6},{8,9},{9,8},{10,11... | collective-permute-start | bytes 12296 | tf_op jit(solution)/shard_map/ppermute | solution.py:311
  56.7 1.0 %collective-permute-done.12 = f32[1024]{0:T(1024)S(1)} collective-permute-done((f32[1024]{0:T(1024)S(1)}, f32[1024]{0:T(1024)S(1)}, u32[]{:S(2)}, u32[]{:S(2)}) %collective-permute-start.12) | collective-permute-done | bytes 4128 | tf_op jit(solution)/shard_map/ppermute | solution.py:311
  57.7 0.0 collective-permute-done.13
  57.8 1.1 %collective-permute-done.14 = f32[1024]{0:T(1024)S(1)} collective-permute-done((f32[1024]{0:T(1024)S(1)}, f32[1024]{0:T(1024)S(1)}, u32[]{:S(2)}, u32[]{:S(2)}) %collective-permute-start.14) | collective-permute-done | bytes 4128 | tf_op jit(solution)/shard_map/ppermute | solution.py:311
  58.8 1.3 %collective-permute-start.15 = (f32[1024]{0:T(1024)S(1)}, f32[1024]{0:T(1024)S(1)}, u32[]{:S(2)}, u32[]{:S(2)}) collective-permute-start(f32[1024]{0:T(1024)S(1)} %add_add_fusion), channel_id=1, source_target_pairs={{0,4},{1,5},{2,6},{3,7},{4,0},{5,1},{6,2},{7,3},{8,12},{9,13},{10,... | collective-permute-start | bytes 12296 | tf_op jit(solution)/shard_map/ppermute | solution.py:311
  60.1 3.2 %collective-permute-done.15 = f32[1024]{0:T(1024)S(1)} collective-permute-done((f32[1024]{0:T(1024)S(1)}, f32[1024]{0:T(1024)S(1)}, u32[]{:S(2)}, u32[]{:S(2)}) %collective-permute-start.15) | collective-permute-done | bytes 4128 | tf_op jit(solution)/shard_map/ppermute | solution.py:311
  63.3 0.6 add.53
  (1 shorter events, 0.0 us)
Async XLA Ops:
  1.4 15.0 %collective-permute-start = (bf16[4,2,32,1024]{3,2,1,0:T(8,128)(2,1)S(1)}, bf16[4,2,32,1024]{3,2,1,0:T(8,128)(2,1)S(1)}, u32[]{:S(2)}, u32[]{:S(2)}) collective-permute-start(bf16[4,2,32,1024]{3,2,1,0:T(8,128)(2,1)S(1)} %bitcast.23), channel_id=1, source_target_pairs={{0,2},{1,3},{2,0},{3,1},{4,6},{5,7},{6,4},{7,5},{8,10},{9,11},{10,... | collective-permute-start | bytes 1572872 | tf_op jit(solution)/shard_map/ppermute | solution.py:272
  4.5 11.9 %collective-permute-start.1 = (bf16[4,2,32,1024]{3,2,1,0:T(8,128)(2,1)S(1)}, bf16[4,2,32,1024]{3,2,1,0:T(8,128)(2,1)S(1)}, u32[]{:S(2)}, u32[]{:S(2)}) collective-permute-start(bf16[4,2,32,1024]{3,2,1,0:T(8,128)(2,1)S(1)} %bitcast.24), channel_id=1, source_target_pairs={{2,4},{3,5},{4,2},{5,3},{10,12},{11,13},{12,10},{13,11},{18,20},{1... | collective-permute-start | bytes 1572872 | tf_op jit(solution)/shard_map/ppermute | solution.py:273
  4.5 14.3 %collective-permute-start.2 = (bf16[4,2,32,1024]{3,2,1,0:T(8,128)(2,1)S(1)}, bf16[4,2,32,1024]{3,2,1,0:T(8,128)(2,1)S(1)}, u32[]{:S(2)}, u32[]{:S(2)}) collective-permute-start(bf16[4,2,32,1024]{3,2,1,0:T(8,128)(2,1)S(1)} %bitcast.25), channel_id=1, source_target_pairs={{0,1},{1,0},{2,3},{3,2},{4,5},{5,4},{6,7},{7,6},{8,9},{9,8},{10,11... | collective-permute-start | bytes 1572872 | tf_op jit(solution)/shard_map/ppermute | solution.py:274
  8.3 14.1 %collective-permute-start.4 = (bf16[8,64,512]{2,1,0:T(8,128)(2,1)S(1)}, bf16[8,64,512]{2,1,0:T(8,128)(2,1)S(1)}, u32[]{:S(2)}, u32[]{:S(2)}) collective-permute-start(bf16[8,64,512]{2,1,0:T(8,128)(2,1)S(1)} %spectra.1), channel_id=1, source_target_pairs={{0,16},{8,24},{16,0},{24,8},{1,17},{9,25},{17,1},{25,9},{2,18},{10... | collective-permute-start | bytes 1572872 | tf_op jit(solution)/shard_map/ppermute | solution.py:270
  9.9 14.1 %collective-permute-start.3 = (bf16[8,64,512]{2,1,0:T(8,128)(2,1)S(1)}, bf16[8,64,512]{2,1,0:T(8,128)(2,1)S(1)}, u32[]{:S(2)}, u32[]{:S(2)}) collective-permute-start(bf16[8,64,512]{2,1,0:T(8,128)(2,1)S(1)} %spectra.1), channel_id=1, source_target_pairs={{0,8},{8,0},{16,24},{24,16},{1,9},{9,1},{17,25},{25,17},{2,10},{10... | collective-permute-start | bytes 1572872 | tf_op jit(solution)/shard_map/ppermute | solution.py:271
  18.8 13.6 %collective-permute-start.10 = (bf16[4,2,32,1024]{3,2,1,0:T(8,128)(2,1)S(1)}, bf16[4,2,32,1024]{3,2,1,0:T(8,128)(2,1)S(1)}, u32[]{:S(2)}, u32[]{:S(2)}) collective-permute-start(bf16[4,2,32,1024]{3,2,1,0:T(8,128)(2,1)S(1)} %collective-permute-done.1.second_ref), channel_id=1, source_target_pairs={{0,2},{1,3},{2,0},{3,1},{4,6},{5,7},{6,4},{7,5},{8,10},{9,11},{10,... | collective-permute-start | bytes 1572872 | tf_op jit(solution)/shard_map/ppermute | solution.py:277
  20.7 13.8 %collective-permute-start.8 = (bf16[4,2,32,1024]{3,2,1,0:T(8,128)(2,1)S(1)}, bf16[4,2,32,1024]{3,2,1,0:T(8,128)(2,1)S(1)}, u32[]{:S(2)}, u32[]{:S(2)}) collective-permute-start(bf16[4,2,32,1024]{3,2,1,0:T(8,128)(2,1)S(1)} %collective-permute-done.refs_2_), channel_id=1, source_target_pairs={{0,1},{1,0},{2,3},{3,2},{4,5},{5,4},{6,7},{7,6},{8,9},{9,8},{10,11... | collective-permute-start | bytes 1572872 | tf_op jit(solution)/shard_map/ppermute | solution.py:279
  22.4 13.6 %collective-permute-start.5 = (bf16[8,64,512]{2,1,0:T(8,128)(2,1)S(1)}, bf16[8,64,512]{2,1,0:T(8,128)(2,1)S(1)}, u32[]{:S(2)}, u32[]{:S(2)}) collective-permute-start(bf16[8,64,512]{2,1,0:T(8,128)(2,1)S(1)} %collective-permute-done.4), channel_id=1, source_target_pairs={{0,8},{8,0},{16,24},{24,16},{1,9},{9,1},{17,25},{25,17},{2,10},{10... | collective-permute-start | bytes 1572872 | tf_op jit(solution)/shard_map/ppermute | solution.py:282
  22.4 17.0 %collective-permute-start.6 = (bf16[4,2,32,1024]{3,2,1,0:T(8,128)(2,1)S(1)}, bf16[4,2,32,1024]{3,2,1,0:T(8,128)(2,1)S(1)}, u32[]{:S(2)}, u32[]{:S(2)}) collective-permute-start(bf16[4,2,32,1024]{3,2,1,0:T(8,128)(2,1)S(1)} %collective-permute-done.refs_2_), channel_id=1, source_target_pairs={{2,4},{3,5},{4,2},{5,3},{10,12},{11,13},{12,10},{13,11},{18,20},{1... | collective-permute-start | bytes 1572872 | tf_op jit(solution)/shard_map/ppermute | solution.py:278
  32.9 12.7 %collective-permute-start.11 = (bf16[4,2,32,1024]{3,2,1,0:T(8,128)(2,1)S(1)}, bf16[4,2,32,1024]{3,2,1,0:T(8,128)(2,1)S(1)}, u32[]{:S(2)}, u32[]{:S(2)}) collective-permute-start(bf16[4,2,32,1024]{3,2,1,0:T(8,128)(2,1)S(1)} %pick.3.refs_4_), channel_id=1, source_target_pairs={{0,1},{1,0},{2,3},{3,2},{4,5},{5,4},{6,7},{7,6},{8,9},{9,8},{10,11... | collective-permute-start | bytes 1572872 | tf_op jit(solution)/shard_map/ppermute | solution.py:290
  34.5 13.5 %collective-permute-start.9 = (bf16[4,2,32,1024]{3,2,1,0:T(8,128)(2,1)S(1)}, bf16[4,2,32,1024]{3,2,1,0:T(8,128)(2,1)S(1)}, u32[]{:S(2)}, u32[]{:S(2)}) collective-permute-start(bf16[4,2,32,1024]{3,2,1,0:T(8,128)(2,1)S(1)} %collective-permute-done.8.refs_3_), channel_id=1, source_target_pairs={{2,4},{3,5},{4,2},{5,3},{10,12},{11,13},{12,10},{13,11},{18,20},{1... | collective-permute-start | bytes 1572872 | tf_op jit(solution)/shard_map/ppermute | solution.py:288
  40.1 12.2 %collective-permute-start.7 = (bf16[4,2,32,1024]{3,2,1,0:T(8,128)(2,1)S(1)}, bf16[4,2,32,1024]{3,2,1,0:T(8,128)(2,1)S(1)}, u32[]{:S(2)}, u32[]{:S(2)}) collective-permute-start(bf16[4,2,32,1024]{3,2,1,0:T(8,128)(2,1)S(1)} %pick.2), channel_id=1, source_target_pairs={{0,2},{1,3},{2,0},{3,1},{4,6},{5,7},{6,4},{7,5},{8,10},{9,11},{10,... | collective-permute-start | bytes 1572872 | tf_op jit(solution)/shard_map/ppermute | solution.py:287
  53.2 4.6 %collective-permute-start.12 = (f32[1024]{0:T(1024)S(1)}, f32[1024]{0:T(1024)S(1)}, u32[]{:S(2)}, u32[]{:S(2)}) collective-permute-start(f32[1024]{0:T(1024)S(1)} %bitcast.30), channel_id=1, source_target_pairs={{0,3},{1,2},{2,1},{3,0},{4,7},{5,6},{6,5},{7,4},{8,11},{9,10},{10,... | collective-permute-start | bytes 12296 | tf_op jit(solution)/shard_map/ppermute | solution.py:311
  53.8 3.9 %collective-permute-start.13 = (f32[1024]{0:T(1024)S(1)}, f32[1024]{0:T(1024)S(1)}, u32[]{:S(2)}, u32[]{:S(2)}) collective-permute-start(f32[1024]{0:T(1024)S(1)} %bitcast.31), channel_id=1, source_target_pairs={{0,2},{1,3},{2,0},{3,1},{4,6},{5,7},{6,4},{7,5},{8,10},{9,11},{10,... | collective-permute-start | bytes 12296 | tf_op jit(solution)/shard_map/ppermute | solution.py:311
  55.2 3.6 %collective-permute-start.14 = (f32[1024]{0:T(1024)S(1)}, f32[1024]{0:T(1024)S(1)}, u32[]{:S(2)}, u32[]{:S(2)}) collective-permute-start(f32[1024]{0:T(1024)S(1)} %bitcast.32), channel_id=1, source_target_pairs={{0,1},{1,0},{2,3},{3,2},{4,5},{5,4},{6,7},{7,6},{8,9},{9,8},{10,11... | collective-permute-start | bytes 12296 | tf_op jit(solution)/shard_map/ppermute | solution.py:311
  58.8 4.5 %collective-permute-start.15 = (f32[1024]{0:T(1024)S(1)}, f32[1024]{0:T(1024)S(1)}, u32[]{:S(2)}, u32[]{:S(2)}) collective-permute-start(f32[1024]{0:T(1024)S(1)} %add_add_fusion), channel_id=1, source_target_pairs={{0,4},{1,5},{2,6},{3,7},{4,0},{5,1},{6,2},{7,3},{8,12},{9,13},{10,... | collective-permute-start | bytes 12296 | tf_op jit(solution)/shard_map/ppermute | solution.py:311

commit v12 on v11

--- a/solution.py
+++ b/solution.py
@@ -278,8 +278,8 @@
     far = send(near, ("tx", "rx"), z_middle_x)
     near_y = send(near, "rx", along_y)
 
+    spectra_both = send(spectra_x, "tx", core)
     adjoint, green_kept = adjoint_of([spectra, spectra_core], green, 4)
-    spectra_both = send(spectra_x, "tx", core)
     adjoint, partial = adjoint_rest(scalars, [spectra_x, spectra_both], green_kept, adjoint)
     adjoint = adjoint.reshape((freqs, 2, 8) + own.shape[2:])
 
@@ -289,19 +289,18 @@
     mid = in_vmem(pick_kernel, scalars, [across_out, across], own.shape, own.dtype, "pick")
     mid_y = send(mid, "rx", along_y)
 
-    early = (OWN, OWN_Y, NEAR, NEAR_Y, MID, MID_Y, FAR_Y)
     sums = in_vmem(
-        functools.partial(weigh_kernel, tuple((number, 1) for number in early), True, False),
+        functools.partial(weigh_kernel, ((OWN, 1), (OWN_Y, 1), (NEAR, 1), (NEAR_Y, 1), (MID, 1)), True, False),
         scalars,
-        [adjoint, own, own_y, near, near_y, mid, mid_y, far_both],
+        [adjoint, own, own_y, near, near_y, mid],
         (8, cells),
         jnp.float32,
         "weigh",
     )
     sums = in_vmem(
-        functools.partial(weigh_kernel, ((FAR, 2), (RECEIVED, 1)), False, True),
+        functools.partial(weigh_kernel, ((MID_Y, 1), (FAR, 2), (FAR_Y, 1), (RECEIVED, 1)), False, True),
         scalars,
-        [adjoint, swap, far, far_both, swap, sums],
+        [adjoint, mid_y, swap, far, far_both, far_both, swap, sums],
         (1, cells),
         jnp.float32,
         "weigh",

time: 64.1 us -> 63.6 us (level)
    ppermute x1, waiting for transfers between devices: 0.21 us -> 8.6 us  [box_shards(): spectra_x = send(spectra, 'tx', along_x)]
    ppermute x1, waiting for transfers between devices: 2.3 us -> 7.9 us  [box_shards(): swap = send(swap, 'rx', z_pairs)]
    ppermute x1, waiting for transfers between devices: 6.49 us -> 1.46 us  [box_shards(): near = send(own, 'rx', z_pairs)]
    ppermute x1, waiting for transfers between devices: 5.16 us -> 0.68 us  [box_shards(): mid_y = send(mid, 'rx', along_y)]
    ppermute x1, waiting for transfers between devices: 3.93 us -> 0.01 us  [box_shards(): across_out = send(across, 'rx', z_pairs)]
    ppermute x1, waiting for transfers between devices: 0.01 us -> 2.17 us  [box_shards(): far = send(near, ('tx', 'rx'), z_middle_x)]
    ppermute x1, starting transfers between devices: 3.03 us -> 1.59 us  [box_shards(): near = send(own, 'rx', z_pairs)]
    ppermute x1, starting transfers between devices: 1.55 us -> 2.99 us  [box_shards(): spectra_x = send(spectra, 'tx', along_x)]
  transfers between devices with their start and end apart: 16 -> 16, of which waited for: 10 -> 11; matrix products, arithmetic and copies ran while one was open for 0% -> 0% of each run, Pallas kernels for 21% -> 17%
where the time goes in v12:
time: 63.6 us; the launch traced here: 63.4 us
  waiting for transfers between devices  28.5 us (45%)
  starting transfers between devices  18.8 us (30%)
  Pallas kernels  14.1 us (22%)
  local copies, waits for them, and re-layouts  1.42 us (2%)
    ppermute x1, waiting for transfers between devices, box_shards(): spectra_x = send(spectra, 'tx', along_x)  8.6 us
    ppermute x1, waiting for transfers between devices, box_shards(): swap = send(swap, 'rx', z_pairs)  7.9 us
    ppermute x4, starting transfers between devices, box_shards(): send(sums, 'rx', [(r, r ^ bit) for r in range(8)])  6.29 us
    pallas_call x1, Pallas kernels, adjoint_of(): pl.pallas_call(functools.partial(adjoint_kernel, count), in_specs=[pl.Blo...  4.47 us
    ppermute x4, waiting for transfers between devices, box_shards(): send(sums, 'rx', [(r, r ^ bit) for r in range(8)])  3.87 us
    pallas_call x4, Pallas kernels, in_vmem(): pl.pallas_call(kernel, in_specs=[pl.BlockSpec(memory_space=pltpu.SMEM)] +...  3.82 us
    pallas_call x1, Pallas kernels, adjoint_rest(): pl.pallas_call(functools.partial(adjoint_rest_kernel, count, half), in_sp...  3.44 us
    ppermute x1, starting transfers between devices, box_shards(): spectra_x = send(spectra, 'tx', along_x)  2.99 us
  transfers between devices with their start and end apart: 16, of which 11 were waited for; matrix products, arithmetic and copies ran while one was open for 0% of the time, Pallas kernels for 17%

profile of v12, /device:TPU:0, one launch (start us, length us, event | category | flops | bytes accessed | tf_op | source)
XLA Modules:
  0.0 63.4 jit_solution(16500722693085769306)
XLA Ops:
  0.0 1.3 %copy.9 = bf16[32,4,2,1024]{3,0,2,1:T(8,128)(2,1)S(1)} copy(bf16[32,4,2,1024]{3,2,1,0:T(2,128)(2,1)} %param.8) | data formatting | bytes 1048576 | tf_op args[3]
  1.3 0.1 stack.43.scalar_ref
  1.4 2.3 %spectra.1 = bf16[8,64,512]{2,1,0:T(8,128)(2,1)S(1)} custom-call(bf16[128,640]{1,0:T(8,128)(2,1)} %constant.38.clone.table_hbm, s32[8,64]{1,0:T(8,128)} %bitcast.35, bf16[40,64,512]{2,1,0:T(8,128)(2,1)} %records_hbm), custom_call_target="tpu_custom_call" | custom-call | flops 335544320 | bytes 3145728 | tf_op jit(solution)/shard_map/spectra/pallas_call | solution.py:78
  3.8 3.0 %collective-permute-start.4 = (bf16[8,64,512]{2,1,0:T(8,128)(2,1)S(1)}, bf16[8,64,512]{2,1,0:T(8,128)(2,1)S(1)}, u32[]{:S(2)}, u32[]{:S(2)}) collective-permute-start(bf16[8,64,512]{2,1,0:T(8,128)(2,1)S(1)} %spectra.1), channel_id=1, source_target_pairs={{0,16},{8,24},{16,0},{24,8},{1,17},{9,25},{17,1},{25,9},{2,18},{10... | collective-permute-start | bytes 1572872 | tf_op jit(solution)/shard_map/ppermute | solution.py:270
  6.8 1.6 %collective-permute-start = (bf16[4,2,32,1024]{3,2,1,0:T(8,128)(2,1)S(1)}, bf16[4,2,32,1024]{3,2,1,0:T(8,128)(2,1)S(1)}, u32[]{:S(2)}, u32[]{:S(2)}) collective-permute-start(bf16[4,2,32,1024]{3,2,1,0:T(8,128)(2,1)S(1)} %bitcast.23), channel_id=1, source_target_pairs={{0,2},{1,3},{2,0},{3,1},{4,6},{5,7},{6,4},{7,5},{8,10},{9,11},{10,... | collective-permute-start | bytes 1572872 | tf_op jit(solution)/shard_map/ppermute | solution.py:272
  8.4 0.0 collective-permute-start.1
  8.4 1.5 %collective-permute-start.2 = (bf16[4,2,32,1024]{3,2,1,0:T(8,128)(2,1)S(1)}, bf16[4,2,32,1024]{3,2,1,0:T(8,128)(2,1)S(1)}, u32[]{:S(2)}, u32[]{:S(2)}) collective-permute-start(bf16[4,2,32,1024]{3,2,1,0:T(8,128)(2,1)S(1)} %bitcast.25), channel_id=1, source_target_pairs={{0,1},{1,0},{2,3},{3,2},{4,5},{5,4},{6,7},{7,6},{8,9},{9,8},{10,11... | collective-permute-start | bytes 1572872 | tf_op jit(solution)/shard_map/ppermute | solution.py:274
  9.9 0.2 collective-permute-start.3
  10.1 8.6 %collective-permute-done.4 = bf16[8,64,512]{2,1,0:T(8,128)(2,1)S(1)} collective-permute-done((bf16[8,64,512]{2,1,0:T(8,128)(2,1)S(1)}, bf16[8,64,512]{2,1,0:T(8,128)(2,1)S(1)}, u32[]{:S(2)}, u32[]{:S(2)}) %collective-permute-start.4) | collective-permute-done | bytes 524320 | tf_op jit(solution)/shard_map/ppermute | solution.py:270
  18.7 0.0 collective-permute-start.5
  18.7 1.5 %collective-permute-done.refs_2_ = bf16[4,2,32,1024]{3,2,1,0:T(8,128)(2,1)S(1)} collective-permute-done((bf16[4,2,32,1024]{3,2,1,0:T(8,128)(2,1)S(1)}, bf16[4,2,32,1024]{3,2,1,0:T(8,128)(2,1)S(1)}, u32[]{:S(2)}, u32[]{:S(2)}) %collective-permute-start) | collective-permute-done | bytes 524320 | tf_op jit(solution)/shard_map/ppermute | solution.py:272
  20.2 0.0 collective-permute-done.1.second_ref
  20.2 2.5 %collective-permute-done.2.refs_1_ = bf16[4,2,32,1024]{3,2,1,0:T(8,128)(2,1)S(1)} collective-permute-done((bf16[4,2,32,1024]{3,2,1,0:T(8,128)(2,1)S(1)}, bf16[4,2,32,1024]{3,2,1,0:T(8,128)(2,1)S(1)}, u32[]{:S(2)}, u32[]{:S(2)}) %collective-permute-start.2) | collective-permute-done | bytes 524320 | tf_op jit(solution)/shard_map/ppermute | solution.py:274
  22.7 0.5 collective-permute-start.8
  23.2 1.4 %collective-permute-start.6 = (bf16[4,2,32,1024]{3,2,1,0:T(8,128)(2,1)S(1)}, bf16[4,2,32,1024]{3,2,1,0:T(8,128)(2,1)S(1)}, u32[]{:S(2)}, u32[]{:S(2)}) collective-permute-start(bf16[4,2,32,1024]{3,2,1,0:T(8,128)(2,1)S(1)} %collective-permute-done.1.second_ref), channel_id=1, source_target_pairs={{0,2},{1,3},{2,0},{3,1},{4,6},{5,7},{6,4},{7,5},{8,10},{9,11},{10,... | collective-permute-start | bytes 1572872 | tf_op jit(solution)/shard_map/ppermute | solution.py:277
  24.6 1.5 %collective-permute-start.10 = (bf16[4,2,32,1024]{3,2,1,0:T(8,128)(2,1)S(1)}, bf16[4,2,32,1024]{3,2,1,0:T(8,128)(2,1)S(1)}, u32[]{:S(2)}, u32[]{:S(2)}) collective-permute-start(bf16[4,2,32,1024]{3,2,1,0:T(8,128)(2,1)S(1)} %collective-permute-done.refs_2_), channel_id=1, source_target_pairs={{0,1},{1,0},{2,3},{3,2},{4,5},{5,4},{6,7},{7,6},{8,9},{9,8},{10,11... | collective-permute-start | bytes 1572872 | tf_op jit(solution)/shard_map/ppermute | solution.py:279
  26.1 0.0 collective-permute-done.3
  26.1 4.5 %adjoint.1 = (f32[4,2,4,64,1024]{4,3,2,1,0:T(8,128)S(1)}, bf16[4,1024,1024]{2,1,0:T(8,128)(2,1)S(1)}) custom-call(bf16[4,1024,1024]{2,1,0:T(8,128)(2,1)} %bitcast.34, bf16[4,2,64,512]{3,2,1,0:T(8,128)(2,1)S(1)} %bitcast.22, bf16[4,2,64,512]{3,2,1,0:T(8,128)(2,1)S(1)} %bitcast.29), custom_call_target="tpu_custom_call" | custom-call | flops 2147483648 | bytes 8388608 | tf_op jit(solution)/shard_map/adjoint/pallas_call | solution.py:149
  30.6 0.0 collective-permute-done.5
  30.6 3.4 %adjoint_rest.1 = (f32[4,2,4,64,1024]{4,3,2,1,0:T(8,128)S(1)}, bf16[4,2,32,1024]{3,2,1,0:T(8,128)(2,1)S(1)}) custom-call(s32[9]{0:T(128)S(1)} %stack.43.scalar_ref, bf16[4,1024,1024]{2,1,0:T(8,128)(2,1)S(1)} %get-tuple-element.20.green_ref, f32[4,2,4,64,1024]{4,3,2,1,0:T(8,128)S(1)} %get-tuple-element.21.base_ref, ...), custom_call_target="tpu_custom_call", output_to_operand_aliasing={{0}: (2, {})} | custom-call | flops 2147483648 | bytes 8388608 | tf_op jit(solution)/shard_map/adjoint_rest/pallas_call | solution.py:174
  34.1 2.2 %collective-permute-done.8.second_ref.refs_2_ = bf16[4,2,32,1024]{3,2,1,0:T(8,128)(2,1)S(1)} collective-permute-done((bf16[4,2,32,1024]{3,2,1,0:T(8,128)(2,1)S(1)}, bf16[4,2,32,1024]{3,2,1,0:T(8,128)(2,1)S(1)}, u32[]{:S(2)}, u32[]{:S(2)}) %collective-permute-start.8) | collective-permute-done | bytes 524320 | tf_op jit(solution)/shard_map/ppermute | solution.py:278
  36.3 0.6 pick.3
  36.9 0.1 collective-permute-start.9
  36.9 0.0 collective-permute-done.6.first_ref
  36.9 0.6 pick.2.refs_4_
  37.5 1.6 %collective-permute-start.7 = (bf16[4,2,32,1024]{3,2,1,0:T(8,128)(2,1)S(1)}, bf16[4,2,32,1024]{3,2,1,0:T(8,128)(2,1)S(1)}, u32[]{:S(2)}, u32[]{:S(2)}) collective-permute-start(bf16[4,2,32,1024]{3,2,1,0:T(8,128)(2,1)S(1)} %pick.2.refs_4_), channel_id=1, source_target_pairs={{0,1},{1,0},{2,3},{3,2},{4,5},{5,4},{6,7},{7,6},{8,9},{9,8},{10,11... | collective-permute-start | bytes 1572872 | tf_op jit(solution)/shard_map/ppermute | solution.py:290
  39.1 0.0 collective-permute-done.10.refs_3_
  39.1 1.1 %collective-permute-start.11 = (bf16[4,2,32,1024]{3,2,1,0:T(8,128)(2,1)S(1)}, bf16[4,2,32,1024]{3,2,1,0:T(8,128)(2,1)S(1)}, u32[]{:S(2)}, u32[]{:S(2)}) collective-permute-start(bf16[4,2,32,1024]{3,2,1,0:T(8,128)(2,1)S(1)} %collective-permute-done.10.refs_3_), channel_id=1, source_target_pairs={{2,4},{3,5},{4,2},{5,3},{10,12},{11,13},{12,10},{13,11},{18,20},{1... | collective-permute-start | bytes 1572872 | tf_op jit(solution)/shard_map/ppermute | solution.py:288
  40.2 1.5 %weigh.2.refs_6_ = f32[8,1024]{1,0:T(8,128)S(1)} custom-call(s32[9]{0:T(128)S(1)} %stack.43.scalar_ref, f32[4,2,8,32,1024]{4,3,2,1,0:T(8,128)S(1)} %bitcast.20, bf16[4,2,32,1024]{3,2,1,0:T(8,128)(2,1)S(1)} %bitcast.26, bf16[4,2,32,1024]{3,2,1,0:T(8,128)(2,1)S(1)} %collective-permute-done.2.refs_1_, ...), custom_call_target="tpu_custom_call" | custom-call | flops 5242880 | bytes 5242880 | tf_op jit(solution)/shard_map/weigh/pallas_call | solution.py:195
  41.7 7.9 %collective-permute-done.9.refs_1_.refs_5_ = bf16[4,2,32,1024]{3,2,1,0:T(8,128)(2,1)S(1)} collective-permute-done((bf16[4,2,32,1024]{3,2,1,0:T(8,128)(2,1)S(1)}, bf16[4,2,32,1024]{3,2,1,0:T(8,128)(2,1)S(1)}, u32[]{:S(2)}, u32[]{:S(2)}) %collective-permute-start.9) | collective-permute-done | bytes 524320 | tf_op jit(solution)/shard_map/ppermute | solution.py:287
  49.6 0.7 %collective-permute-done.7.refs_0_ = bf16[4,2,32,1024]{3,2,1,0:T(8,128)(2,1)S(1)} collective-permute-done((bf16[4,2,32,1024]{3,2,1,0:T(8,128)(2,1)S(1)}, bf16[4,2,32,1024]{3,2,1,0:T(8,128)(2,1)S(1)}, u32[]{:S(2)}, u32[]{:S(2)}) %collective-permute-start.7) | collective-permute-done | bytes 524320 | tf_op jit(solution)/shard_map/ppermute | solution.py:290
  50.3 1.2 %collective-permute-done.11.refs_3_.refs_4_ = bf16[4,2,32,1024]{3,2,1,0:T(8,128)(2,1)S(1)} collective-permute-done((bf16[4,2,32,1024]{3,2,1,0:T(8,128)(2,1)S(1)}, bf16[4,2,32,1024]{3,2,1,0:T(8,128)(2,1)S(1)}, u32[]{:S(2)}, u32[]{:S(2)}) %collective-permute-start.11) | collective-permute-done | bytes 524320 | tf_op jit(solution)/shard_map/ppermute | solution.py:288
  51.5 1.1 %weigh.3 = f32[1,1024]{1,0:T(1,128)S(1)} custom-call(s32[9]{0:T(128)S(1)} %stack.43.scalar_ref, f32[4,2,8,32,1024]{4,3,2,1,0:T(8,128)S(1)} %bitcast.21, bf16[4,2,32,1024]{3,2,1,0:T(8,128)(2,1)S(1)} %collective-permute-done.7.refs_0_, bf16[4,2,32,1024]{3,2,1,0:T(8,128)(2,1)S(1)} %collective-permute-done.9.refs_1_.refs_5_, ...), custom_call_target="tpu_custom_call" | custom-call | flops 6324224 | bytes 6324224 | tf_op jit(solution)/shard_map/weigh/pallas_call | solution.py:195
  52.7 1.7 %collective-permute-start.12 = (f32[1024]{0:T(1024)S(1)}, f32[1024]{0:T(1024)S(1)}, u32[]{:S(2)}, u32[]{:S(2)}) collective-permute-start(f32[1024]{0:T(1024)S(1)} %bitcast.30), channel_id=1, source_target_pairs={{0,3},{1,2},{2,1},{3,0},{4,7},{5,6},{6,5},{7,4},{8,11},{9,10},{10,... | collective-permute-start | bytes 12296 | tf_op jit(solution)/shard_map/ppermute | solution.py:310
  54.4 0.3 collective-permute-start.13
  54.7 1.5 %collective-permute-start.14 = (f32[1024]{0:T(1024)S(1)}, f32[1024]{0:T(1024)S(1)}, u32[]{:S(2)}, u32[]{:S(2)}) collective-permute-start(f32[1024]{0:T(1024)S(1)} %bitcast.32), channel_id=1, source_target_pairs={{0,1},{1,0},{2,3},{3,2},{4,5},{5,4},{6,7},{7,6},{8,9},{9,8},{10,11... | collective-permute-start | bytes 12296 | tf_op jit(solution)/shard_map/ppermute | solution.py:310
  56.2 1.0 %collective-permute-done.12 = f32[1024]{0:T(1024)S(1)} collective-permute-done((f32[1024]{0:T(1024)S(1)}, f32[1024]{0:T(1024)S(1)}, u32[]{:S(2)}, u32[]{:S(2)}) %collective-permute-start.12) | collective-permute-done | bytes 4128 | tf_op jit(solution)/shard_map/ppermute | solution.py:310
  57.2 0.8 %collective-permute-done.13 = f32[1024]{0:T(1024)S(1)} collective-permute-done((f32[1024]{0:T(1024)S(1)}, f32[1024]{0:T(1024)S(1)}, u32[]{:S(2)}, u32[]{:S(2)}) %collective-permute-start.13) | collective-permute-done | bytes 4128 | tf_op jit(solution)/shard_map/ppermute | solution.py:310
  58.0 0.3 collective-permute-done.14
  58.3 2.7 %collective-permute-start.15 = (f32[1024]{0:T(1024)S(1)}, f32[1024]{0:T(1024)S(1)}, u32[]{:S(2)}, u32[]{:S(2)}) collective-permute-start(f32[1024]{0:T(1024)S(1)} %add_add_fusion), channel_id=1, source_target_pairs={{0,4},{1,5},{2,6},{3,7},{4,0},{5,1},{6,2},{7,3},{8,12},{9,13},{10,... | collective-permute-start | bytes 12296 | tf_op jit(solution)/shard_map/ppermute | solution.py:310
  61.0 1.8 %collective-permute-done.15 = f32[1024]{0:T(1024)S(1)} collective-permute-done((f32[1024]{0:T(1024)S(1)}, f32[1024]{0:T(1024)S(1)}, u32[]{:S(2)}, u32[]{:S(2)}) %collective-permute-start.15) | collective-permute-done | bytes 4128 | tf_op jit(solution)/shard_map/ppermute | solution.py:310
  62.8 0.6 add.53
  (1 shorter events, 0.0 us)
Async XLA Ops:
  3.8 14.9 %collective-permute-start.4 = (bf16[8,64,512]{2,1,0:T(8,128)(2,1)S(1)}, bf16[8,64,512]{2,1,0:T(8,128)(2,1)S(1)}, u32[]{:S(2)}, u32[]{:S(2)}) collective-permute-start(bf16[8,64,512]{2,1,0:T(8,128)(2,1)S(1)} %spectra.1), channel_id=1, source_target_pairs={{0,16},{8,24},{16,0},{24,8},{1,17},{9,25},{17,1},{25,9},{2,18},{10... | collective-permute-start | bytes 1572872 | tf_op jit(solution)/shard_map/ppermute | solution.py:270
  6.8 13.4 %collective-permute-start = (bf16[4,2,32,1024]{3,2,1,0:T(8,128)(2,1)S(1)}, bf16[4,2,32,1024]{3,2,1,0:T(8,128)(2,1)S(1)}, u32[]{:S(2)}, u32[]{:S(2)}) collective-permute-start(bf16[4,2,32,1024]{3,2,1,0:T(8,128)(2,1)S(1)} %bitcast.23), channel_id=1, source_target_pairs={{0,2},{1,3},{2,0},{3,1},{4,6},{5,7},{6,4},{7,5},{8,10},{9,11},{10,... | collective-permute-start | bytes 1572872 | tf_op jit(solution)/shard_map/ppermute | solution.py:272
  8.4 11.8 %collective-permute-start.1 = (bf16[4,2,32,1024]{3,2,1,0:T(8,128)(2,1)S(1)}, bf16[4,2,32,1024]{3,2,1,0:T(8,128)(2,1)S(1)}, u32[]{:S(2)}, u32[]{:S(2)}) collective-permute-start(bf16[4,2,32,1024]{3,2,1,0:T(8,128)(2,1)S(1)} %bitcast.24), channel_id=1, source_target_pairs={{2,4},{3,5},{4,2},{5,3},{10,12},{11,13},{12,10},{13,11},{18,20},{1... | collective-permute-start | bytes 1572872 | tf_op jit(solution)/shard_map/ppermute | solution.py:273
  8.4 14.3 %collective-permute-start.2 = (bf16[4,2,32,1024]{3,2,1,0:T(8,128)(2,1)S(1)}, bf16[4,2,32,1024]{3,2,1,0:T(8,128)(2,1)S(1)}, u32[]{:S(2)}, u32[]{:S(2)}) collective-permute-start(bf16[4,2,32,1024]{3,2,1,0:T(8,128)(2,1)S(1)} %bitcast.25), channel_id=1, source_target_pairs={{0,1},{1,0},{2,3},{3,2},{4,5},{5,4},{6,7},{7,6},{8,9},{9,8},{10,11... | collective-permute-start | bytes 1572872 | tf_op jit(solution)/shard_map/ppermute | solution.py:274
  9.9 16.3 %collective-permute-start.3 = (bf16[8,64,512]{2,1,0:T(8,128)(2,1)S(1)}, bf16[8,64,512]{2,1,0:T(8,128)(2,1)S(1)}, u32[]{:S(2)}, u32[]{:S(2)}) collective-permute-start(bf16[8,64,512]{2,1,0:T(8,128)(2,1)S(1)} %spectra.1), channel_id=1, source_target_pairs={{0,8},{8,0},{16,24},{24,16},{1,9},{9,1},{17,25},{25,17},{2,10},{10... | collective-permute-start | bytes 1572872 | tf_op jit(solution)/shard_map/ppermute | solution.py:271
  18.7 11.9 %collective-permute-start.5 = (bf16[8,64,512]{2,1,0:T(8,128)(2,1)S(1)}, bf16[8,64,512]{2,1,0:T(8,128)(2,1)S(1)}, u32[]{:S(2)}, u32[]{:S(2)}) collective-permute-start(bf16[8,64,512]{2,1,0:T(8,128)(2,1)S(1)} %collective-permute-done.4), channel_id=1, source_target_pairs={{0,8},{8,0},{16,24},{24,16},{1,9},{9,1},{17,25},{25,17},{2,10},{10... | collective-permute-start | bytes 1572872 | tf_op jit(solution)/shard_map/ppermute | solution.py:281
  22.7 13.6 %collective-permute-start.8 = (bf16[4,2,32,1024]{3,2,1,0:T(8,128)(2,1)S(1)}, bf16[4,2,32,1024]{3,2,1,0:T(8,128)(2,1)S(1)}, u32[]{:S(2)}, u32[]{:S(2)}) collective-permute-start(bf16[4,2,32,1024]{3,2,1,0:T(8,128)(2,1)S(1)} %collective-permute-done.refs_2_), channel_id=1, source_target_pairs={{2,4},{3,5},{4,2},{5,3},{10,12},{11,13},{12,10},{13,11},{18,20},{1... | collective-permute-start | bytes 1572872 | tf_op jit(solution)/shard_map/ppermute | solution.py:278
  23.2 13.7 %collective-permute-start.6 = (bf16[4,2,32,1024]{3,2,1,0:T(8,128)(2,1)S(1)}, bf16[4,2,32,1024]{3,2,1,0:T(8,128)(2,1)S(1)}, u32[]{:S(2)}, u32[]{:S(2)}) collective-permute-start(bf16[4,2,32,1024]{3,2,1,0:T(8,128)(2,1)S(1)} %collective-permute-done.1.second_ref), channel_id=1, source_target_pairs={{0,2},{1,3},{2,0},{3,1},{4,6},{5,7},{6,4},{7,5},{8,10},{9,11},{10,... | collective-permute-start | bytes 1572872 | tf_op jit(solution)/shard_map/ppermute | solution.py:277
  24.6 14.5 %collective-permute-start.10 = (bf16[4,2,32,1024]{3,2,1,0:T(8,128)(2,1)S(1)}, bf16[4,2,32,1024]{3,2,1,0:T(8,128)(2,1)S(1)}, u32[]{:S(2)}, u32[]{:S(2)}) collective-permute-start(bf16[4,2,32,1024]{3,2,1,0:T(8,128)(2,1)S(1)} %collective-permute-done.refs_2_), channel_id=1, source_target_pairs={{0,1},{1,0},{2,3},{3,2},{4,5},{5,4},{6,7},{7,6},{8,9},{9,8},{10,11... | collective-permute-start | bytes 1572872 | tf_op jit(solution)/shard_map/ppermute | solution.py:279
  36.9 12.7 %collective-permute-start.9 = (bf16[4,2,32,1024]{3,2,1,0:T(8,128)(2,1)S(1)}, bf16[4,2,32,1024]{3,2,1,0:T(8,128)(2,1)S(1)}, u32[]{:S(2)}, u32[]{:S(2)}) collective-permute-start(bf16[4,2,32,1024]{3,2,1,0:T(8,128)(2,1)S(1)} %pick.3), channel_id=1, source_target_pairs={{0,2},{1,3},{2,0},{3,1},{4,6},{5,7},{6,4},{7,5},{8,10},{9,11},{10,... | collective-permute-start | bytes 1572872 | tf_op jit(solution)/shard_map/ppermute | solution.py:287
  37.5 12.7 %collective-permute-start.7 = (bf16[4,2,32,1024]{3,2,1,0:T(8,128)(2,1)S(1)}, bf16[4,2,32,1024]{3,2,1,0:T(8,128)(2,1)S(1)}, u32[]{:S(2)}, u32[]{:S(2)}) collective-permute-start(bf16[4,2,32,1024]{3,2,1,0:T(8,128)(2,1)S(1)} %pick.2.refs_4_), channel_id=1, source_target_pairs={{0,1},{1,0},{2,3},{3,2},{4,5},{5,4},{6,7},{7,6},{8,9},{9,8},{10,11... | collective-permute-start | bytes 1572872 | tf_op jit(solution)/shard_map/ppermute | solution.py:290
  39.1 12.4 %collective-permute-start.11 = (bf16[4,2,32,1024]{3,2,1,0:T(8,128)(2,1)S(1)}, bf16[4,2,32,1024]{3,2,1,0:T(8,128)(2,1)S(1)}, u32[]{:S(2)}, u32[]{:S(2)}) collective-permute-start(bf16[4,2,32,1024]{3,2,1,0:T(8,128)(2,1)S(1)} %collective-permute-done.10.refs_3_), channel_id=1, source_target_pairs={{2,4},{3,5},{4,2},{5,3},{10,12},{11,13},{12,10},{13,11},{18,20},{1... | collective-permute-start | bytes 1572872 | tf_op jit(solution)/shard_map/ppermute | solution.py:288
  52.7 4.6 %collective-permute-start.12 = (f32[1024]{0:T(1024)S(1)}, f32[1024]{0:T(1024)S(1)}, u32[]{:S(2)}, u32[]{:S(2)}) collective-permute-start(f32[1024]{0:T(1024)S(1)} %bitcast.30), channel_id=1, source_target_pairs={{0,3},{1,2},{2,1},{3,0},{4,7},{5,6},{6,5},{7,4},{8,11},{9,10},{10,... | collective-permute-start | bytes 12296 | tf_op jit(solution)/shard_map/ppermute | solution.py:310
  54.4 3.6 %collective-permute-start.13 = (f32[1024]{0:T(1024)S(1)}, f32[1024]{0:T(1024)S(1)}, u32[]{:S(2)}, u32[]{:S(2)}) collective-permute-start(f32[1024]{0:T(1024)S(1)} %bitcast.31), channel_id=1, source_target_pairs={{0,2},{1,3},{2,0},{3,1},{4,6},{5,7},{6,4},{7,5},{8,10},{9,11},{10,... | collective-permute-start | bytes 12296 | tf_op jit(solution)/shard_map/ppermute | solution.py:310
  54.7 3.6 %collective-permute-start.14 = (f32[1024]{0:T(1024)S(1)}, f32[1024]{0:T(1024)S(1)}, u32[]{:S(2)}, u32[]{:S(2)}) collective-permute-start(f32[1024]{0:T(1024)S(1)} %bitcast.32), channel_id=1, source_target_pairs={{0,1},{1,0},{2,3},{3,2},{4,5},{5,4},{6,7},{7,6},{8,9},{9,8},{10,11... | collective-permute-start | bytes 12296 | tf_op jit(solution)/shard_map/ppermute | solution.py:310
  58.3 4.5 %collective-permute-start.15 = (f32[1024]{0:T(1024)S(1)}, f32[1024]{0:T(1024)S(1)}, u32[]{:S(2)}, u32[]{:S(2)}) collective-permute-start(f32[1024]{0:T(1024)S(1)} %add_add_fusion), channel_id=1, source_target_pairs={{0,4},{1,5},{2,6},{3,7},{4,0},{5,1},{6,2},{7,3},{8,12},{9,13},{10,... | collective-permute-start | bytes 12296 | tf_op jit(solution)/shard_map/ppermute | solution.py:310

commit v13 on v12

--- a/solution.py
+++ b/solution.py
@@ -258,6 +258,7 @@
     me_tx, me_rx = lax.axis_index("tx"), lax.axis_index("rx")
     me_z, me_y = me_rx // 2, me_rx % 2
     lower = me_z < 2
+    middle = (me_z == 1) | (me_z == 2)
     mid_z, far_z = jnp.where(lower, 2, 1), jnp.where(lower, 3, 0)
     scalars = jnp.stack(
         [(z ^ me_tx) * 2 + y for z in (me_z, me_z ^ 1, mid_z, far_z) for y in (me_y, 1 - me_y)]
@@ -283,10 +284,10 @@
     adjoint, partial = adjoint_rest(scalars, [spectra_x, spectra_both], green_kept, adjoint)
     adjoint = adjoint.reshape((freqs, 2, 8) + own.shape[2:])
 
-    swap = in_vmem(pick_kernel, scalars, [partial, far], own.shape, own.dtype, "pick")
+    swap = jnp.where(middle, far, partial)
     swap = send(swap, "rx", z_pairs)
-    far_both = send(near_y, ("tx", "rx"), z_middle_x)
-    mid = in_vmem(pick_kernel, scalars, [across_out, across], own.shape, own.dtype, "pick")
+    far_both = send(near_y, ("tx", "rx"), z_middle)
+    mid = jnp.where(middle, across, across_out)
     mid_y = send(mid, "rx", along_y)
 
     sums = in_vmem(

time: 63.6 us -> 62.4 us (0.981)
  starting transfers between devices: 18.8 us -> 17 us
  waiting for transfers between devices: 28.5 us -> 30 us
  Pallas kernels: 14.1 us -> 13 us
    ppermute x1, waiting for transfers between devices: 0.01 us -> 1.35 us  [box_shards(): across_out = send(across, 'rx', z_pairs)]
    ppermute x1, waiting for transfers between devices: 1.23 us -> 0.01 us  [box_shards(): far_both = send(near_y, ('tx', 'rx'), z_middle)]
    ppermute x1, waiting for transfers between devices: 7.9 us -> 9.12 us  [box_shards(): swap = send(swap, 'rx', z_pairs)]
    pallas_call x4 -> x2, Pallas kernels: 3.82 us -> 2.7 us  [in_vmem(): pl.pallas_call(kernel, in_specs=[pl.BlockSpec(memory_space=pltpu.SMEM)] +...]
    ppermute x1, starting transfers between devices: 1.06 us -> 0.01 us  [box_shards(): far_both = send(near_y, ('tx', 'rx'), z_middle)]
    ppermute x1, starting transfers between devices: 1.58 us -> 0.57 us  [box_shards(): mid_y = send(mid, 'rx', along_y)]
  transfers between devices with their start and end apart: 16 -> 16, of which waited for: 11 -> 11; matrix products, arithmetic and copies ran while one was open for 0% -> 0% of each run, Pallas kernels for 17% -> 15%
where the time goes in v13:
time: 62.4 us; the launch traced here: 62.2 us
  waiting for transfers between devices  30 us (48%)
  starting transfers between devices  17 us (27%)
  Pallas kernels  13 us (21%)
  local copies, waits for them, and re-layouts  1.42 us (2%)
  other arithmetic  0.71 us (1%)
    ppermute x1, waiting for transfers between devices, box_shards(): swap = send(swap, 'rx', z_pairs)  9.12 us
    ppermute x1, waiting for transfers between devices, box_shards(): spectra_x = send(spectra, 'tx', along_x)  8.6 us
    ppermute x4, starting transfers between devices, box_shards(): send(sums, 'rx', [(r, r ^ bit) for r in range(8)])  6.64 us
    pallas_call x1, Pallas kernels, adjoint_of(): pl.pallas_call(functools.partial(adjoint_kernel, count), in_specs=[pl.Blo...  4.47 us
    ppermute x4, waiting for transfers between devices, box_shards(): send(sums, 'rx', [(r, r ^ bit) for r in range(8)])  3.82 us
    pallas_call x1, Pallas kernels, adjoint_rest(): pl.pallas_call(functools.partial(adjoint_rest_kernel, count, half), in_sp...  3.44 us
    ppermute x1, starting transfers between devices, box_shards(): spectra_x = send(spectra, 'tx', along_x)  2.99 us
    pallas_call x2, Pallas kernels, in_vmem(): pl.pallas_call(kernel, in_specs=[pl.BlockSpec(memory_space=pltpu.SMEM)] +...  2.7 us
  transfers between devices with their start and end apart: 16, of which 11 were waited for; matrix products, arithmetic and copies ran while one was open for 0% of the time, Pallas kernels for 15%

profile of v13, /device:TPU:0, one launch (start us, length us, event | category | flops | bytes accessed | tf_op | source)
XLA Modules:
  0.0 62.2 jit_solution(16965718136994167191)
XLA Ops:
  0.0 1.3 %copy.9 = bf16[32,4,2,1024]{3,0,2,1:T(8,128)(2,1)S(1)} copy(bf16[32,4,2,1024]{3,2,1,0:T(2,128)(2,1)} %param.8) | data formatting | bytes 1048576 | tf_op args[3]
  1.3 0.1 stack.43.scalar_ref
  1.4 2.3 %spectra.1 = bf16[8,64,512]{2,1,0:T(8,128)(2,1)S(1)} custom-call(bf16[128,640]{1,0:T(8,128)(2,1)} %constant.38.clone.table_hbm, s32[8,64]{1,0:T(8,128)} %bitcast.35, bf16[40,64,512]{2,1,0:T(8,128)(2,1)} %records_hbm), custom_call_target="tpu_custom_call" | custom-call | flops 335544320 | bytes 3145728 | tf_op jit(solution)/shard_map/spectra/pallas_call | solution.py:78
  3.8 3.0 %collective-permute-start.4 = (bf16[8,64,512]{2,1,0:T(8,128)(2,1)S(1)}, bf16[8,64,512]{2,1,0:T(8,128)(2,1)S(1)}, u32[]{:S(2)}, u32[]{:S(2)}) collective-permute-start(bf16[8,64,512]{2,1,0:T(8,128)(2,1)S(1)} %spectra.1), channel_id=1, source_target_pairs={{0,16},{8,24},{16,0},{24,8},{1,17},{9,25},{17,1},{25,9},{2,18},{10... | collective-permute-start | bytes 1572872 | tf_op jit(solution)/shard_map/ppermute | solution.py:271
  6.8 1.6 %collective-permute-start = (bf16[4,2,32,1024]{3,2,1,0:T(8,128)(2,1)S(1)}, bf16[4,2,32,1024]{3,2,1,0:T(8,128)(2,1)S(1)}, u32[]{:S(2)}, u32[]{:S(2)}) collective-permute-start(bf16[4,2,32,1024]{3,2,1,0:T(8,128)(2,1)S(1)} %bitcast.23), channel_id=1, source_target_pairs={{0,2},{1,3},{2,0},{3,1},{4,6},{5,7},{6,4},{7,5},{8,10},{9,11},{10,... | collective-permute-start | bytes 1572872 | tf_op jit(solution)/shard_map/ppermute | solution.py:273
  8.4 0.0 collective-permute-start.1
  8.4 1.5 %collective-permute-start.2 = (bf16[4,2,32,1024]{3,2,1,0:T(8,128)(2,1)S(1)}, bf16[4,2,32,1024]{3,2,1,0:T(8,128)(2,1)S(1)}, u32[]{:S(2)}, u32[]{:S(2)}) collective-permute-start(bf16[4,2,32,1024]{3,2,1,0:T(8,128)(2,1)S(1)} %bitcast.25), channel_id=1, source_target_pairs={{0,1},{1,0},{2,3},{3,2},{4,5},{5,4},{6,7},{7,6},{8,9},{9,8},{10,11... | collective-permute-start | bytes 1572872 | tf_op jit(solution)/shard_map/ppermute | solution.py:275
  9.9 0.2 collective-permute-start.3
  10.1 8.6 %collective-permute-done.4 = bf16[8,64,512]{2,1,0:T(8,128)(2,1)S(1)} collective-permute-done((bf16[8,64,512]{2,1,0:T(8,128)(2,1)S(1)}, bf16[8,64,512]{2,1,0:T(8,128)(2,1)S(1)}, u32[]{:S(2)}, u32[]{:S(2)}) %collective-permute-start.4) | collective-permute-done | bytes 524320 | tf_op jit(solution)/shard_map/ppermute | solution.py:271
  18.7 0.0 collective-permute-start.5
  18.7 1.5 %collective-permute-done.refs_2_ = bf16[4,2,32,1024]{3,2,1,0:T(8,128)(2,1)S(1)} collective-permute-done((bf16[4,2,32,1024]{3,2,1,0:T(8,128)(2,1)S(1)}, bf16[4,2,32,1024]{3,2,1,0:T(8,128)(2,1)S(1)}, u32[]{:S(2)}, u32[]{:S(2)}) %collective-permute-start) | collective-permute-done | bytes 524320 | tf_op jit(solution)/shard_map/ppermute | solution.py:273
  20.2 0.0 collective-permute-done.1
  20.2 2.5 %collective-permute-done.2.refs_1_ = bf16[4,2,32,1024]{3,2,1,0:T(8,128)(2,1)S(1)} collective-permute-done((bf16[4,2,32,1024]{3,2,1,0:T(8,128)(2,1)S(1)}, bf16[4,2,32,1024]{3,2,1,0:T(8,128)(2,1)S(1)}, u32[]{:S(2)}, u32[]{:S(2)}) %collective-permute-start.2) | collective-permute-done | bytes 524320 | tf_op jit(solution)/shard_map/ppermute | solution.py:275
  22.7 0.5 collective-permute-start.8
  23.2 1.5 %collective-permute-start.10 = (bf16[4,2,32,1024]{3,2,1,0:T(8,128)(2,1)S(1)}, bf16[4,2,32,1024]{3,2,1,0:T(8,128)(2,1)S(1)}, u32[]{:S(2)}, u32[]{:S(2)}) collective-permute-start(bf16[4,2,32,1024]{3,2,1,0:T(8,128)(2,1)S(1)} %collective-permute-done.refs_2_), channel_id=1, source_target_pairs={{0,1},{1,0},{2,3},{3,2},{4,5},{5,4},{6,7},{7,6},{8,9},{9,8},{10,11... | collective-permute-start | bytes 1572872 | tf_op jit(solution)/shard_map/ppermute | solution.py:280
  24.8 1.4 %collective-permute-start.6 = (bf16[4,2,32,1024]{3,2,1,0:T(8,128)(2,1)S(1)}, bf16[4,2,32,1024]{3,2,1,0:T(8,128)(2,1)S(1)}, u32[]{:S(2)}, u32[]{:S(2)}) collective-permute-start(bf16[4,2,32,1024]{3,2,1,0:T(8,128)(2,1)S(1)} %collective-permute-done.1), channel_id=1, source_target_pairs={{0,2},{1,3},{2,0},{3,1},{4,6},{5,7},{6,4},{7,5},{8,10},{9,11},{10,... | collective-permute-start | bytes 1572872 | tf_op jit(solution)/shard_map/ppermute | solution.py:278
  26.1 0.0 collective-permute-done.3
  26.1 4.5 %adjoint.1 = (f32[4,2,4,64,1024]{4,3,2,1,0:T(8,128)S(1)}, bf16[4,1024,1024]{2,1,0:T(8,128)(2,1)S(1)}) custom-call(bf16[4,1024,1024]{2,1,0:T(8,128)(2,1)} %bitcast.34, bf16[4,2,64,512]{3,2,1,0:T(8,128)(2,1)S(1)} %bitcast.22, bf16[4,2,64,512]{3,2,1,0:T(8,128)(2,1)S(1)} %bitcast.29), custom_call_target="tpu_custom_call" | custom-call | flops 2147483648 | bytes 8388608 | tf_op jit(solution)/shard_map/adjoint/pallas_call | solution.py:149
  30.6 0.0 collective-permute-done.5
  30.6 3.4 %adjoint_rest.1 = (f32[4,2,4,64,1024]{4,3,2,1,0:T(8,128)S(1)}, bf16[4,2,32,1024]{3,2,1,0:T(8,128)(2,1)S(1)}) custom-call(s32[9]{0:T(128)S(1)} %stack.43.scalar_ref, bf16[4,1024,1024]{2,1,0:T(8,128)(2,1)S(1)} %get-tuple-element.20.green_ref, f32[4,2,4,64,1024]{4,3,2,1,0:T(8,128)S(1)} %get-tuple-element.21.base_ref, ...), custom_call_target="tpu_custom_call", output_to_operand_aliasing={{0}: (2, {})} | custom-call | flops 2147483648 | bytes 8388608 | tf_op jit(solution)/shard_map/adjoint_rest/pallas_call | solution.py:174
  34.1 2.2 %collective-permute-done.8.refs_2_ = bf16[4,2,32,1024]{3,2,1,0:T(8,128)(2,1)S(1)} collective-permute-done((bf16[4,2,32,1024]{3,2,1,0:T(8,128)(2,1)S(1)}, bf16[4,2,32,1024]{3,2,1,0:T(8,128)(2,1)S(1)}, u32[]{:S(2)}, u32[]{:S(2)}) %collective-permute-start.8) | collective-permute-done | bytes 524320 | tf_op jit(solution)/shard_map/ppermute | solution.py:279
  36.3 0.1 broadcast_select_fusion
  36.3 0.1 collective-permute-start.9
  36.4 1.4 %collective-permute-done.6 = bf16[4,2,32,1024]{3,2,1,0:T(8,128)(2,1)S(1)} collective-permute-done((bf16[4,2,32,1024]{3,2,1,0:T(8,128)(2,1)S(1)}, bf16[4,2,32,1024]{3,2,1,0:T(8,128)(2,1)S(1)}, u32[]{:S(2)}, u32[]{:S(2)}) %collective-permute-start.6) | collective-permute-done | bytes 524320 | tf_op jit(solution)/shard_map/ppermute | solution.py:278
  37.8 0.1 broadcast_select_fusion.1.refs_4_
  37.8 0.6 collective-permute-start.7
  38.4 0.0 collective-permute-done.10.refs_3_
  38.4 0.0 collective-permute-start.11
  38.4 1.5 %weigh.2.refs_6_ = f32[8,1024]{1,0:T(8,128)S(1)} custom-call(s32[9]{0:T(128)S(1)} %stack.43.scalar_ref, f32[4,2,8,32,1024]{4,3,2,1,0:T(8,128)S(1)} %bitcast.20, bf16[4,2,32,1024]{3,2,1,0:T(8,128)(2,1)S(1)} %bitcast.26, bf16[4,2,32,1024]{3,2,1,0:T(8,128)(2,1)S(1)} %collective-permute-done.2.refs_1_, ...), custom_call_target="tpu_custom_call" | custom-call | flops 5242880 | bytes 5242880 | tf_op jit(solution)/shard_map/weigh/pallas_call | solution.py:195
  39.9 9.1 %collective-permute-done.9.refs_1_.refs_5_ = bf16[4,2,32,1024]{3,2,1,0:T(8,128)(2,1)S(1)} collective-permute-done((bf16[4,2,32,1024]{3,2,1,0:T(8,128)(2,1)S(1)}, bf16[4,2,32,1024]{3,2,1,0:T(8,128)(2,1)S(1)}, u32[]{:S(2)}, u32[]{:S(2)}) %collective-permute-start.9) | collective-permute-done | bytes 524320 | tf_op jit(solution)/shard_map/ppermute | solution.py:288
  49.1 0.9 %collective-permute-done.7.refs_0_ = bf16[4,2,32,1024]{3,2,1,0:T(8,128)(2,1)S(1)} collective-permute-done((bf16[4,2,32,1024]{3,2,1,0:T(8,128)(2,1)S(1)}, bf16[4,2,32,1024]{3,2,1,0:T(8,128)(2,1)S(1)}, u32[]{:S(2)}, u32[]{:S(2)}) %collective-permute-start.7) | collective-permute-done | bytes 524320 | tf_op jit(solution)/shard_map/ppermute | solution.py:291
  49.9 0.0 collective-permute-done.11.refs_3_.refs_4_
  50.0 1.2 %weigh.3 = f32[1,1024]{1,0:T(1,128)S(1)} custom-call(s32[9]{0:T(128)S(1)} %stack.43.scalar_ref, f32[4,2,8,32,1024]{4,3,2,1,0:T(8,128)S(1)} %bitcast.21, bf16[4,2,32,1024]{3,2,1,0:T(8,128)(2,1)S(1)} %collective-permute-done.7.refs_0_, bf16[4,2,32,1024]{3,2,1,0:T(8,128)(2,1)S(1)} %collective-permute-done.9.refs_1_.refs_5_, ...), custom_call_target="tpu_custom_call" | custom-call | flops 6324224 | bytes 6324224 | tf_op jit(solution)/shard_map/weigh/pallas_call | solution.py:195
  51.1 2.2 %collective-permute-start.12 = (f32[1024]{0:T(1024)S(1)}, f32[1024]{0:T(1024)S(1)}, u32[]{:S(2)}, u32[]{:S(2)}) collective-permute-start(f32[1024]{0:T(1024)S(1)} %bitcast.30), channel_id=1, source_target_pairs={{0,3},{1,2},{2,1},{3,0},{4,7},{5,6},{6,5},{7,4},{8,11},{9,10},{10,... | collective-permute-start | bytes 12296 | tf_op jit(solution)/shard_map/ppermute | solution.py:311
  53.3 0.1 collective-permute-start.13
  53.5 1.4 %collective-permute-start.14 = (f32[1024]{0:T(1024)S(1)}, f32[1024]{0:T(1024)S(1)}, u32[]{:S(2)}, u32[]{:S(2)}) collective-permute-start(f32[1024]{0:T(1024)S(1)} %bitcast.32), channel_id=1, source_target_pairs={{0,1},{1,0},{2,3},{3,2},{4,5},{5,4},{6,7},{7,6},{8,9},{9,8},{10,11... | collective-permute-start | bytes 12296 | tf_op jit(solution)/shard_map/ppermute | solution.py:311
  54.9 0.8 %collective-permute-done.12 = f32[1024]{0:T(1024)S(1)} collective-permute-done((f32[1024]{0:T(1024)S(1)}, f32[1024]{0:T(1024)S(1)}, u32[]{:S(2)}, u32[]{:S(2)}) %collective-permute-start.12) | collective-permute-done | bytes 4128 | tf_op jit(solution)/shard_map/ppermute | solution.py:311
  55.7 1.3 %collective-permute-done.13 = f32[1024]{0:T(1024)S(1)} collective-permute-done((f32[1024]{0:T(1024)S(1)}, f32[1024]{0:T(1024)S(1)}, u32[]{:S(2)}, u32[]{:S(2)}) %collective-permute-start.13) | collective-permute-done | bytes 4128 | tf_op jit(solution)/shard_map/ppermute | solution.py:311
  57.0 0.1 collective-permute-done.14
  57.1 2.9 %collective-permute-start.15 = (f32[1024]{0:T(1024)S(1)}, f32[1024]{0:T(1024)S(1)}, u32[]{:S(2)}, u32[]{:S(2)}) collective-permute-start(f32[1024]{0:T(1024)S(1)} %add_add_fusion), channel_id=1, source_target_pairs={{0,4},{1,5},{2,6},{3,7},{4,0},{5,1},{6,2},{7,3},{8,12},{9,13},{10,... | collective-permute-start | bytes 12296 | tf_op jit(solution)/shard_map/ppermute | solution.py:311
  60.0 1.6 %collective-permute-done.15 = f32[1024]{0:T(1024)S(1)} collective-permute-done((f32[1024]{0:T(1024)S(1)}, f32[1024]{0:T(1024)S(1)}, u32[]{:S(2)}, u32[]{:S(2)}) %collective-permute-start.15) | collective-permute-done | bytes 4128 | tf_op jit(solution)/shard_map/ppermute | solution.py:311
  61.6 0.6 add.53
  (1 shorter events, 0.0 us)
Async XLA Ops:
  3.8 14.9 %collective-permute-start.4 = (bf16[8,64,512]{2,1,0:T(8,128)(2,1)S(1)}, bf16[8,64,512]{2,1,0:T(8,128)(2,1)S(1)}, u32[]{:S(2)}, u32[]{:S(2)}) collective-permute-start(bf16[8,64,512]{2,1,0:T(8,128)(2,1)S(1)} %spectra.1), channel_id=1, source_target_pairs={{0,16},{8,24},{16,0},{24,8},{1,17},{9,25},{17,1},{25,9},{2,18},{10... | collective-permute-start | bytes 1572872 | tf_op jit(solution)/shard_map/ppermute | solution.py:271
  6.8 13.4 %collective-permute-start = (bf16[4,2,32,1024]{3,2,1,0:T(8,128)(2,1)S(1)}, bf16[4,2,32,1024]{3,2,1,0:T(8,128)(2,1)S(1)}, u32[]{:S(2)}, u32[]{:S(2)}) collective-permute-start(bf16[4,2,32,1024]{3,2,1,0:T(8,128)(2,1)S(1)} %bitcast.23), channel_id=1, source_target_pairs={{0,2},{1,3},{2,0},{3,1},{4,6},{5,7},{6,4},{7,5},{8,10},{9,11},{10,... | collective-permute-start | bytes 1572872 | tf_op jit(solution)/shard_map/ppermute | solution.py:273
  8.4 11.8 %collective-permute-start.1 = (bf16[4,2,32,1024]{3,2,1,0:T(8,128)(2,1)S(1)}, bf16[4,2,32,1024]{3,2,1,0:T(8,128)(2,1)S(1)}, u32[]{:S(2)}, u32[]{:S(2)}) collective-permute-start(bf16[4,2,32,1024]{3,2,1,0:T(8,128)(2,1)S(1)} %bitcast.24), channel_id=1, source_target_pairs={{2,4},{3,5},{4,2},{5,3},{10,12},{11,13},{12,10},{13,11},{18,20},{1... | collective-permute-start | bytes 1572872 | tf_op jit(solution)/shard_map/ppermute | solution.py:274
  8.4 14.3 %collective-permute-start.2 = (bf16[4,2,32,1024]{3,2,1,0:T(8,128)(2,1)S(1)}, bf16[4,2,32,1024]{3,2,1,0:T(8,128)(2,1)S(1)}, u32[]{:S(2)}, u32[]{:S(2)}) collective-permute-start(bf16[4,2,32,1024]{3,2,1,0:T(8,128)(2,1)S(1)} %bitcast.25), channel_id=1, source_target_pairs={{0,1},{1,0},{2,3},{3,2},{4,5},{5,4},{6,7},{7,6},{8,9},{9,8},{10,11... | collective-permute-start | bytes 1572872 | tf_op jit(solution)/shard_map/ppermute | solution.py:275
  9.9 16.3 %collective-permute-start.3 = (bf16[8,64,512]{2,1,0:T(8,128)(2,1)S(1)}, bf16[8,64,512]{2,1,0:T(8,128)(2,1)S(1)}, u32[]{:S(2)}, u32[]{:S(2)}) collective-permute-start(bf16[8,64,512]{2,1,0:T(8,128)(2,1)S(1)} %spectra.1), channel_id=1, source_target_pairs={{0,8},{8,0},{16,24},{24,16},{1,9},{9,1},{17,25},{25,17},{2,10},{10... | collective-permute-start | bytes 1572872 | tf_op jit(solution)/shard_map/ppermute | solution.py:272
  18.7 11.9 %collective-permute-start.5 = (bf16[8,64,512]{2,1,0:T(8,128)(2,1)S(1)}, bf16[8,64,512]{2,1,0:T(8,128)(2,1)S(1)}, u32[]{:S(2)}, u32[]{:S(2)}) collective-permute-start(bf16[8,64,512]{2,1,0:T(8,128)(2,1)S(1)} %collective-permute-done.4), channel_id=1, source_target_pairs={{0,8},{8,0},{16,24},{24,16},{1,9},{9,1},{17,25},{25,17},{2,10},{10... | collective-permute-start | bytes 1572872 | tf_op jit(solution)/shard_map/ppermute | solution.py:282
  22.7 13.6 %collective-permute-start.8 = (bf16[4,2,32,1024]{3,2,1,0:T(8,128)(2,1)S(1)}, bf16[4,2,32,1024]{3,2,1,0:T(8,128)(2,1)S(1)}, u32[]{:S(2)}, u32[]{:S(2)}) collective-permute-start(bf16[4,2,32,1024]{3,2,1,0:T(8,128)(2,1)S(1)} %collective-permute-done.refs_2_), channel_id=1, source_target_pairs={{2,4},{3,5},{4,2},{5,3},{10,12},{11,13},{12,10},{13,11},{18,20},{1... | collective-permute-start | bytes 1572872 | tf_op jit(solution)/shard_map/ppermute | solution.py:279
  23.2 15.1 %collective-permute-start.10 = (bf16[4,2,32,1024]{3,2,1,0:T(8,128)(2,1)S(1)}, bf16[4,2,32,1024]{3,2,1,0:T(8,128)(2,1)S(1)}, u32[]{:S(2)}, u32[]{:S(2)}) collective-permute-start(bf16[4,2,32,1024]{3,2,1,0:T(8,128)(2,1)S(1)} %collective-permute-done.refs_2_), channel_id=1, source_target_pairs={{0,1},{1,0},{2,3},{3,2},{4,5},{5,4},{6,7},{7,6},{8,9},{9,8},{10,11... | collective-permute-start | bytes 1572872 | tf_op jit(solution)/shard_map/ppermute | solution.py:280
  24.8 13.0 %collective-permute-start.6 = (bf16[4,2,32,1024]{3,2,1,0:T(8,128)(2,1)S(1)}, bf16[4,2,32,1024]{3,2,1,0:T(8,128)(2,1)S(1)}, u32[]{:S(2)}, u32[]{:S(2)}) collective-permute-start(bf16[4,2,32,1024]{3,2,1,0:T(8,128)(2,1)S(1)} %collective-permute-done.1), channel_id=1, source_target_pairs={{0,2},{1,3},{2,0},{3,1},{4,6},{5,7},{6,4},{7,5},{8,10},{9,11},{10,... | collective-permute-start | bytes 1572872 | tf_op jit(solution)/shard_map/ppermute | solution.py:278
  36.3 12.7 %collective-permute-start.9 = (bf16[4,2,32,1024]{3,2,1,0:T(8,128)(2,1)S(1)}, bf16[4,2,32,1024]{3,2,1,0:T(8,128)(2,1)S(1)}, u32[]{:S(2)}, u32[]{:S(2)}) collective-permute-start(bf16[4,2,32,1024]{3,2,1,0:T(8,128)(2,1)S(1)} %broadcast_select_fusion), channel_id=1, source_target_pairs={{0,2},{1,3},{2,0},{3,1},{4,6},{5,7},{6,4},{7,5},{8,10},{9,11},{10,... | collective-permute-start | bytes 1572872 | tf_op jit(solution)/shard_map/ppermute | solution.py:288
  37.8 12.1 %collective-permute-start.7 = (bf16[4,2,32,1024]{3,2,1,0:T(8,128)(2,1)S(1)}, bf16[4,2,32,1024]{3,2,1,0:T(8,128)(2,1)S(1)}, u32[]{:S(2)}, u32[]{:S(2)}) collective-permute-start(bf16[4,2,32,1024]{3,2,1,0:T(8,128)(2,1)S(1)} %broadcast_select_fusion.1.refs_4_), channel_id=1, source_target_pairs={{0,1},{1,0},{2,3},{3,2},{4,5},{5,4},{6,7},{7,6},{8,9},{9,8},{10,11... | collective-permute-start | bytes 1572872 | tf_op jit(solution)/shard_map/ppermute | solution.py:291
  38.4 11.6 %collective-permute-start.11 = (bf16[4,2,32,1024]{3,2,1,0:T(8,128)(2,1)S(1)}, bf16[4,2,32,1024]{3,2,1,0:T(8,128)(2,1)S(1)}, u32[]{:S(2)}, u32[]{:S(2)}) collective-permute-start(bf16[4,2,32,1024]{3,2,1,0:T(8,128)(2,1)S(1)} %collective-permute-done.10.refs_3_), channel_id=1, source_target_pairs={{2,4},{3,5},{4,2},{5,3},{10,12},{11,13},{12,10},{13,11},{18,20},{1... | collective-permute-start | bytes 1572872 | tf_op jit(solution)/shard_map/ppermute | solution.py:289
  51.1 4.6 %collective-permute-start.12 = (f32[1024]{0:T(1024)S(1)}, f32[1024]{0:T(1024)S(1)}, u32[]{:S(2)}, u32[]{:S(2)}) collective-permute-start(f32[1024]{0:T(1024)S(1)} %bitcast.30), channel_id=1, source_target_pairs={{0,3},{1,2},{2,1},{3,0},{4,7},{5,6},{6,5},{7,4},{8,11},{9,10},{10,... | collective-permute-start | bytes 12296 | tf_op jit(solution)/shard_map/ppermute | solution.py:311
  53.3 3.6 %collective-permute-start.13 = (f32[1024]{0:T(1024)S(1)}, f32[1024]{0:T(1024)S(1)}, u32[]{:S(2)}, u32[]{:S(2)}) collective-permute-start(f32[1024]{0:T(1024)S(1)} %bitcast.31), channel_id=1, source_target_pairs={{0,2},{1,3},{2,0},{3,1},{4,6},{5,7},{6,4},{7,5},{8,10},{9,11},{10,... | collective-permute-start | bytes 12296 | tf_op jit(solution)/shard_map/ppermute | solution.py:311
  53.5 3.6 %collective-permute-start.14 = (f32[1024]{0:T(1024)S(1)}, f32[1024]{0:T(1024)S(1)}, u32[]{:S(2)}, u32[]{:S(2)}) collective-permute-start(f32[1024]{0:T(1024)S(1)} %bitcast.32), channel_id=1, source_target_pairs={{0,1},{1,0},{2,3},{3,2},{4,5},{5,4},{6,7},{7,6},{8,9},{9,8},{10,11... | collective-permute-start | bytes 12296 | tf_op jit(solution)/shard_map/ppermute | solution.py:311
  57.1 4.5 %collective-permute-start.15 = (f32[1024]{0:T(1024)S(1)}, f32[1024]{0:T(1024)S(1)}, u32[]{:S(2)}, u32[]{:S(2)}) collective-permute-start(f32[1024]{0:T(1024)S(1)} %add_add_fusion), channel_id=1, source_target_pairs={{0,4},{1,5},{2,6},{3,7},{4,0},{5,1},{6,2},{7,3},{8,12},{9,13},{10,... | collective-permute-start | bytes 12296 | tf_op jit(solution)/shard_map/ppermute | solution.py:311

commit v14 on v13

--- a/solution.py
+++ b/solution.py
@@ -279,8 +279,8 @@
     far = send(near, ("tx", "rx"), z_middle_x)
     near_y = send(near, "rx", along_y)
 
+    adjoint, green_kept = adjoint_of([spectra, spectra_core], green, 4)
     spectra_both = send(spectra_x, "tx", core)
-    adjoint, green_kept = adjoint_of([spectra, spectra_core], green, 4)
     adjoint, partial = adjoint_rest(scalars, [spectra_x, spectra_both], green_kept, adjoint)
     adjoint = adjoint.reshape((freqs, 2, 8) + own.shape[2:])
 

time: 62.4 us -> 62.4 us (level)
  no operation moved by 1% of the time
where the time goes in v14:
time: 62.4 us; the launch traced here: 62.2 us
  waiting for transfers between devices  30 us (48%)
  starting transfers between devices  17 us (27%)
  Pallas kernels  13 us (21%)
  local copies, waits for them, and re-layouts  1.42 us (2%)
  other arithmetic  0.71 us (1%)
    ppermute x1, waiting for transfers between devices, box_shards(): swap = send(swap, 'rx', z_pairs)  9.12 us
    ppermute x1, waiting for transfers between devices, box_shards(): spectra_x = send(spectra, 'tx', along_x)  8.6 us
    ppermute x4, starting transfers between devices, box_shards(): send(sums, 'rx', [(r, r ^ bit) for r in range(8)])  6.64 us
    pallas_call x1, Pallas kernels, adjoint_of(): pl.pallas_call(functools.partial(adjoint_kernel, count), in_specs=[pl.Blo...  4.47 us
    ppermute x4, waiting for transfers between devices, box_shards(): send(sums, 'rx', [(r, r ^ bit) for r in range(8)])  3.82 us
    pallas_call x1, Pallas kernels, adjoint_rest(): pl.pallas_call(functools.partial(adjoint_rest_kernel, count, half), in_sp...  3.44 us
    ppermute x1, starting transfers between devices, box_shards(): spectra_x = send(spectra, 'tx', along_x)  2.99 us
    pallas_call x2, Pallas kernels, in_vmem(): pl.pallas_call(kernel, in_specs=[pl.BlockSpec(memory_space=pltpu.SMEM)] +...  2.7 us
  transfers between devices with their start and end apart: 16, of which 11 were waited for; matrix products, arithmetic and copies ran while one was open for 0% of the time, Pallas kernels for 15%

profile of v14, /device:TPU:0, one launch (start us, length us, event | category | flops | bytes accessed | tf_op | source)
XLA Modules:
  0.0 62.2 jit_solution(16965718136994167191)
XLA Ops:
  0.0 1.3 %copy.9 = bf16[32,4,2,1024]{3,0,2,1:T(8,128)(2,1)S(1)} copy(bf16[32,4,2,1024]{3,2,1,0:T(2,128)(2,1)} %param.8) | data formatting | bytes 1048576 | tf_op args[3]
  1.3 0.1 stack.43.scalar_ref
  1.4 2.3 %spectra.1 = bf16[8,64,512]{2,1,0:T(8,128)(2,1)S(1)} custom-call(bf16[128,640]{1,0:T(8,128)(2,1)} %constant.38.clone.table_hbm, s32[8,64]{1,0:T(8,128)} %bitcast.35, bf16[40,64,512]{2,1,0:T(8,128)(2,1)} %records_hbm), custom_call_target="tpu_custom_call" | custom-call | flops 335544320 | bytes 3145728 | tf_op jit(solution)/shard_map/spectra/pallas_call | solution.py:78
  3.8 3.0 %collective-permute-start.4 = (bf16[8,64,512]{2,1,0:T(8,128)(2,1)S(1)}, bf16[8,64,512]{2,1,0:T(8,128)(2,1)S(1)}, u32[]{:S(2)}, u32[]{:S(2)}) collective-permute-start(bf16[8,64,512]{2,1,0:T(8,128)(2,1)S(1)} %spectra.1), channel_id=1, source_target_pairs={{0,16},{8,24},{16,0},{24,8},{1,17},{9,25},{17,1},{25,9},{2,18},{10... | collective-permute-start | bytes 1572872 | tf_op jit(solution)/shard_map/ppermute | solution.py:271
  6.8 1.6 %collective-permute-start = (bf16[4,2,32,1024]{3,2,1,0:T(8,128)(2,1)S(1)}, bf16[4,2,32,1024]{3,2,1,0:T(8,128)(2,1)S(1)}, u32[]{:S(2)}, u32[]{:S(2)}) collective-permute-start(bf16[4,2,32,1024]{3,2,1,0:T(8,128)(2,1)S(1)} %bitcast.23), channel_id=1, source_target_pairs={{0,2},{1,3},{2,0},{3,1},{4,6},{5,7},{6,4},{7,5},{8,10},{9,11},{10,... | collective-permute-start | bytes 1572872 | tf_op jit(solution)/shard_map/ppermute | solution.py:273
  8.4 0.0 collective-permute-start.1
  8.4 1.5 %collective-permute-start.2 = (bf16[4,2,32,1024]{3,2,1,0:T(8,128)(2,1)S(1)}, bf16[4,2,32,1024]{3,2,1,0:T(8,128)(2,1)S(1)}, u32[]{:S(2)}, u32[]{:S(2)}) collective-permute-start(bf16[4,2,32,1024]{3,2,1,0:T(8,128)(2,1)S(1)} %bitcast.25), channel_id=1, source_target_pairs={{0,1},{1,0},{2,3},{3,2},{4,5},{5,4},{6,7},{7,6},{8,9},{9,8},{10,11... | collective-permute-start | bytes 1572872 | tf_op jit(solution)/shard_map/ppermute | solution.py:275
  9.9 0.2 collective-permute-start.3
  10.1 8.6 %collective-permute-done.4 = bf16[8,64,512]{2,1,0:T(8,128)(2,1)S(1)} collective-permute-done((bf16[8,64,512]{2,1,0:T(8,128)(2,1)S(1)}, bf16[8,64,512]{2,1,0:T(8,128)(2,1)S(1)}, u32[]{:S(2)}, u32[]{:S(2)}) %collective-permute-start.4) | collective-permute-done | bytes 524320 | tf_op jit(solution)/shard_map/ppermute | solution.py:271
  18.7 0.0 collective-permute-start.5
  18.7 1.5 %collective-permute-done.refs_2_ = bf16[4,2,32,1024]{3,2,1,0:T(8,128)(2,1)S(1)} collective-permute-done((bf16[4,2,32,1024]{3,2,1,0:T(8,128)(2,1)S(1)}, bf16[4,2,32,1024]{3,2,1,0:T(8,128)(2,1)S(1)}, u32[]{:S(2)}, u32[]{:S(2)}) %collective-permute-start) | collective-permute-done | bytes 524320 | tf_op jit(solution)/shard_map/ppermute | solution.py:273
  20.2 0.0 collective-permute-done.1
  20.2 2.5 %collective-permute-done.2.refs_1_ = bf16[4,2,32,1024]{3,2,1,0:T(8,128)(2,1)S(1)} collective-permute-done((bf16[4,2,32,1024]{3,2,1,0:T(8,128)(2,1)S(1)}, bf16[4,2,32,1024]{3,2,1,0:T(8,128)(2,1)S(1)}, u32[]{:S(2)}, u32[]{:S(2)}) %collective-permute-start.2) | collective-permute-done | bytes 524320 | tf_op jit(solution)/shard_map/ppermute | solution.py:275
  22.7 0.5 collective-permute-start.8
  23.2 1.5 %collective-permute-start.10 = (bf16[4,2,32,1024]{3,2,1,0:T(8,128)(2,1)S(1)}, bf16[4,2,32,1024]{3,2,1,0:T(8,128)(2,1)S(1)}, u32[]{:S(2)}, u32[]{:S(2)}) collective-permute-start(bf16[4,2,32,1024]{3,2,1,0:T(8,128)(2,1)S(1)} %collective-permute-done.refs_2_), channel_id=1, source_target_pairs={{0,1},{1,0},{2,3},{3,2},{4,5},{5,4},{6,7},{7,6},{8,9},{9,8},{10,11... | collective-permute-start | bytes 1572872 | tf_op jit(solution)/shard_map/ppermute | solution.py:280
  24.8 1.4 %collective-permute-start.6 = (bf16[4,2,32,1024]{3,2,1,0:T(8,128)(2,1)S(1)}, bf16[4,2,32,1024]{3,2,1,0:T(8,128)(2,1)S(1)}, u32[]{:S(2)}, u32[]{:S(2)}) collective-permute-start(bf16[4,2,32,1024]{3,2,1,0:T(8,128)(2,1)S(1)} %collective-permute-done.1), channel_id=1, source_target_pairs={{0,2},{1,3},{2,0},{3,1},{4,6},{5,7},{6,4},{7,5},{8,10},{9,11},{10,... | collective-permute-start | bytes 1572872 | tf_op jit(solution)/shard_map/ppermute | solution.py:278
  26.1 0.0 collective-permute-done.3
  26.1 4.5 %adjoint.1 = (f32[4,2,4,64,1024]{4,3,2,1,0:T(8,128)S(1)}, bf16[4,1024,1024]{2,1,0:T(8,128)(2,1)S(1)}) custom-call(bf16[4,1024,1024]{2,1,0:T(8,128)(2,1)} %bitcast.34, bf16[4,2,64,512]{3,2,1,0:T(8,128)(2,1)S(1)} %bitcast.22, bf16[4,2,64,512]{3,2,1,0:T(8,128)(2,1)S(1)} %bitcast.29), custom_call_target="tpu_custom_call" | custom-call | flops 2147483648 | bytes 8388608 | tf_op jit(solution)/shard_map/adjoint/pallas_call | solution.py:149
  30.6 0.0 collective-permute-done.5
  30.6 3.4 %adjoint_rest.1 = (f32[4,2,4,64,1024]{4,3,2,1,0:T(8,128)S(1)}, bf16[4,2,32,1024]{3,2,1,0:T(8,128)(2,1)S(1)}) custom-call(s32[9]{0:T(128)S(1)} %stack.43.scalar_ref, bf16[4,1024,1024]{2,1,0:T(8,128)(2,1)S(1)} %get-tuple-element.20.green_ref, f32[4,2,4,64,1024]{4,3,2,1,0:T(8,128)S(1)} %get-tuple-element.21.base_ref, ...), custom_call_target="tpu_custom_call", output_to_operand_aliasing={{0}: (2, {})} | custom-call | flops 2147483648 | bytes 8388608 | tf_op jit(solution)/shard_map/adjoint_rest/pallas_call | solution.py:174
  34.1 2.2 %collective-permute-done.8.refs_2_ = bf16[4,2,32,1024]{3,2,1,0:T(8,128)(2,1)S(1)} collective-permute-done((bf16[4,2,32,1024]{3,2,1,0:T(8,128)(2,1)S(1)}, bf16[4,2,32,1024]{3,2,1,0:T(8,128)(2,1)S(1)}, u32[]{:S(2)}, u32[]{:S(2)}) %collective-permute-start.8) | collective-permute-done | bytes 524320 | tf_op jit(solution)/shard_map/ppermute | solution.py:279
  36.3 0.1 broadcast_select_fusion
  36.3 0.1 collective-permute-start.9
  36.4 1.4 %collective-permute-done.6 = bf16[4,2,32,1024]{3,2,1,0:T(8,128)(2,1)S(1)} collective-permute-done((bf16[4,2,32,1024]{3,2,1,0:T(8,128)(2,1)S(1)}, bf16[4,2,32,1024]{3,2,1,0:T(8,128)(2,1)S(1)}, u32[]{:S(2)}, u32[]{:S(2)}) %collective-permute-start.6) | collective-permute-done | bytes 524320 | tf_op jit(solution)/shard_map/ppermute | solution.py:278
  37.8 0.1 broadcast_select_fusion.1.refs_4_
  37.8 0.6 collective-permute-start.7
  38.4 0.0 collective-permute-done.10.refs_3_
  38.4 0.0 collective-permute-start.11
  38.4 1.5 %weigh.2.refs_6_ = f32[8,1024]{1,0:T(8,128)S(1)} custom-call(s32[9]{0:T(128)S(1)} %stack.43.scalar_ref, f32[4,2,8,32,1024]{4,3,2,1,0:T(8,128)S(1)} %bitcast.20, bf16[4,2,32,1024]{3,2,1,0:T(8,128)(2,1)S(1)} %bitcast.26, bf16[4,2,32,1024]{3,2,1,0:T(8,128)(2,1)S(1)} %collective-permute-done.2.refs_1_, ...), custom_call_target="tpu_custom_call" | custom-call | flops 5242880 | bytes 5242880 | tf_op jit(solution)/shard_map/weigh/pallas_call | solution.py:195
  39.9 9.1 %collective-permute-done.9.refs_1_.refs_5_ = bf16[4,2,32,1024]{3,2,1,0:T(8,128)(2,1)S(1)} collective-permute-done((bf16[4,2,32,1024]{3,2,1,0:T(8,128)(2,1)S(1)}, bf16[4,2,32,1024]{3,2,1,0:T(8,128)(2,1)S(1)}, u32[]{:S(2)}, u32[]{:S(2)}) %collective-permute-start.9) | collective-permute-done | bytes 524320 | tf_op jit(solution)/shard_map/ppermute | solution.py:288
  49.1 0.9 %collective-permute-done.7.refs_0_ = bf16[4,2,32,1024]{3,2,1,0:T(8,128)(2,1)S(1)} collective-permute-done((bf16[4,2,32,1024]{3,2,1,0:T(8,128)(2,1)S(1)}, bf16[4,2,32,1024]{3,2,1,0:T(8,128)(2,1)S(1)}, u32[]{:S(2)}, u32[]{:S(2)}) %collective-permute-start.7) | collective-permute-done | bytes 524320 | tf_op jit(solution)/shard_map/ppermute | solution.py:291
  49.9 0.0 collective-permute-done.11.refs_3_.refs_4_
  50.0 1.2 %weigh.3 = f32[1,1024]{1,0:T(1,128)S(1)} custom-call(s32[9]{0:T(128)S(1)} %stack.43.scalar_ref, f32[4,2,8,32,1024]{4,3,2,1,0:T(8,128)S(1)} %bitcast.21, bf16[4,2,32,1024]{3,2,1,0:T(8,128)(2,1)S(1)} %collective-permute-done.7.refs_0_, bf16[4,2,32,1024]{3,2,1,0:T(8,128)(2,1)S(1)} %collective-permute-done.9.refs_1_.refs_5_, ...), custom_call_target="tpu_custom_call" | custom-call | flops 6324224 | bytes 6324224 | tf_op jit(solution)/shard_map/weigh/pallas_call | solution.py:195
  51.1 2.2 %collective-permute-start.12 = (f32[1024]{0:T(1024)S(1)}, f32[1024]{0:T(1024)S(1)}, u32[]{:S(2)}, u32[]{:S(2)}) collective-permute-start(f32[1024]{0:T(1024)S(1)} %bitcast.30), channel_id=1, source_target_pairs={{0,3},{1,2},{2,1},{3,0},{4,7},{5,6},{6,5},{7,4},{8,11},{9,10},{10,... | collective-permute-start | bytes 12296 | tf_op jit(solution)/shard_map/ppermute | solution.py:311
  53.3 0.1 collective-permute-start.13
  53.5 1.4 %collective-permute-start.14 = (f32[1024]{0:T(1024)S(1)}, f32[1024]{0:T(1024)S(1)}, u32[]{:S(2)}, u32[]{:S(2)}) collective-permute-start(f32[1024]{0:T(1024)S(1)} %bitcast.32), channel_id=1, source_target_pairs={{0,1},{1,0},{2,3},{3,2},{4,5},{5,4},{6,7},{7,6},{8,9},{9,8},{10,11... | collective-permute-start | bytes 12296 | tf_op jit(solution)/shard_map/ppermute | solution.py:311
  54.9 0.8 %collective-permute-done.12 = f32[1024]{0:T(1024)S(1)} collective-permute-done((f32[1024]{0:T(1024)S(1)}, f32[1024]{0:T(1024)S(1)}, u32[]{:S(2)}, u32[]{:S(2)}) %collective-permute-start.12) | collective-permute-done | bytes 4128 | tf_op jit(solution)/shard_map/ppermute | solution.py:311
  55.7 1.3 %collective-permute-done.13 = f32[1024]{0:T(1024)S(1)} collective-permute-done((f32[1024]{0:T(1024)S(1)}, f32[1024]{0:T(1024)S(1)}, u32[]{:S(2)}, u32[]{:S(2)}) %collective-permute-start.13) | collective-permute-done | bytes 4128 | tf_op jit(solution)/shard_map/ppermute | solution.py:311
  57.0 0.1 collective-permute-done.14
  57.1 2.9 %collective-permute-start.15 = (f32[1024]{0:T(1024)S(1)}, f32[1024]{0:T(1024)S(1)}, u32[]{:S(2)}, u32[]{:S(2)}) collective-permute-start(f32[1024]{0:T(1024)S(1)} %add_add_fusion), channel_id=1, source_target_pairs={{0,4},{1,5},{2,6},{3,7},{4,0},{5,1},{6,2},{7,3},{8,12},{9,13},{10,... | collective-permute-start | bytes 12296 | tf_op jit(solution)/shard_map/ppermute | solution.py:311
  60.0 1.6 %collective-permute-done.15 = f32[1024]{0:T(1024)S(1)} collective-permute-done((f32[1024]{0:T(1024)S(1)}, f32[1024]{0:T(1024)S(1)}, u32[]{:S(2)}, u32[]{:S(2)}) %collective-permute-start.15) | collective-permute-done | bytes 4128 | tf_op jit(solution)/shard_map/ppermute | solution.py:311
  61.6 0.6 add.53
  (1 shorter events, 0.0 us)
Async XLA Ops:
  3.8 14.9 %collective-permute-start.4 = (bf16[8,64,512]{2,1,0:T(8,128)(2,1)S(1)}, bf16[8,64,512]{2,1,0:T(8,128)(2,1)S(1)}, u32[]{:S(2)}, u32[]{:S(2)}) collective-permute-start(bf16[8,64,512]{2,1,0:T(8,128)(2,1)S(1)} %spectra.1), channel_id=1, source_target_pairs={{0,16},{8,24},{16,0},{24,8},{1,17},{9,25},{17,1},{25,9},{2,18},{10... | collective-permute-start | bytes 1572872 | tf_op jit(solution)/shard_map/ppermute | solution.py:271
  6.8 13.4 %collective-permute-start = (bf16[4,2,32,1024]{3,2,1,0:T(8,128)(2,1)S(1)}, bf16[4,2,32,1024]{3,2,1,0:T(8,128)(2,1)S(1)}, u32[]{:S(2)}, u32[]{:S(2)}) collective-permute-start(bf16[4,2,32,1024]{3,2,1,0:T(8,128)(2,1)S(1)} %bitcast.23), channel_id=1, source_target_pairs={{0,2},{1,3},{2,0},{3,1},{4,6},{5,7},{6,4},{7,5},{8,10},{9,11},{10,... | collective-permute-start | bytes 1572872 | tf_op jit(solution)/shard_map/ppermute | solution.py:273
  8.4 11.8 %collective-permute-start.1 = (bf16[4,2,32,1024]{3,2,1,0:T(8,128)(2,1)S(1)}, bf16[4,2,32,1024]{3,2,1,0:T(8,128)(2,1)S(1)}, u32[]{:S(2)}, u32[]{:S(2)}) collective-permute-start(bf16[4,2,32,1024]{3,2,1,0:T(8,128)(2,1)S(1)} %bitcast.24), channel_id=1, source_target_pairs={{2,4},{3,5},{4,2},{5,3},{10,12},{11,13},{12,10},{13,11},{18,20},{1... | collective-permute-start | bytes 1572872 | tf_op jit(solution)/shard_map/ppermute | solution.py:274
  8.4 14.3 %collective-permute-start.2 = (bf16[4,2,32,1024]{3,2,1,0:T(8,128)(2,1)S(1)}, bf16[4,2,32,1024]{3,2,1,0:T(8,128)(2,1)S(1)}, u32[]{:S(2)}, u32[]{:S(2)}) collective-permute-start(bf16[4,2,32,1024]{3,2,1,0:T(8,128)(2,1)S(1)} %bitcast.25), channel_id=1, source_target_pairs={{0,1},{1,0},{2,3},{3,2},{4,5},{5,4},{6,7},{7,6},{8,9},{9,8},{10,11... | collective-permute-start | bytes 1572872 | tf_op jit(solution)/shard_map/ppermute | solution.py:275
  9.9 16.3 %collective-permute-start.3 = (bf16[8,64,512]{2,1,0:T(8,128)(2,1)S(1)}, bf16[8,64,512]{2,1,0:T(8,128)(2,1)S(1)}, u32[]{:S(2)}, u32[]{:S(2)}) collective-permute-start(bf16[8,64,512]{2,1,0:T(8,128)(2,1)S(1)} %spectra.1), channel_id=1, source_target_pairs={{0,8},{8,0},{16,24},{24,16},{1,9},{9,1},{17,25},{25,17},{2,10},{10... | collective-permute-start | bytes 1572872 | tf_op jit(solution)/shard_map/ppermute | solution.py:272
  18.7 11.9 %collective-permute-start.5 = (bf16[8,64,512]{2,1,0:T(8,128)(2,1)S(1)}, bf16[8,64,512]{2,1,0:T(8,128)(2,1)S(1)}, u32[]{:S(2)}, u32[]{:S(2)}) collective-permute-start(bf16[8,64,512]{2,1,0:T(8,128)(2,1)S(1)} %collective-permute-done.4), channel_id=1, source_target_pairs={{0,8},{8,0},{16,24},{24,16},{1,9},{9,1},{17,25},{25,17},{2,10},{10... | collective-permute-start | bytes 1572872 | tf_op jit(solution)/shard_map/ppermute | solution.py:283
  22.7 13.6 %collective-permute-start.8 = (bf16[4,2,32,1024]{3,2,1,0:T(8,128)(2,1)S(1)}, bf16[4,2,32,1024]{3,2,1,0:T(8,128)(2,1)S(1)}, u32[]{:S(2)}, u32[]{:S(2)}) collective-permute-start(bf16[4,2,32,1024]{3,2,1,0:T(8,128)(2,1)S(1)} %collective-permute-done.refs_2_), channel_id=1, source_target_pairs={{2,4},{3,5},{4,2},{5,3},{10,12},{11,13},{12,10},{13,11},{18,20},{1... | collective-permute-start | bytes 1572872 | tf_op jit(solution)/shard_map/ppermute | solution.py:279
  23.2 15.1 %collective-permute-start.10 = (bf16[4,2,32,1024]{3,2,1,0:T(8,128)(2,1)S(1)}, bf16[4,2,32,1024]{3,2,1,0:T(8,128)(2,1)S(1)}, u32[]{:S(2)}, u32[]{:S(2)}) collective-permute-start(bf16[4,2,32,1024]{3,2,1,0:T(8,128)(2,1)S(1)} %collective-permute-done.refs_2_), channel_id=1, source_target_pairs={{0,1},{1,0},{2,3},{3,2},{4,5},{5,4},{6,7},{7,6},{8,9},{9,8},{10,11... | collective-permute-start | bytes 1572872 | tf_op jit(solution)/shard_map/ppermute | solution.py:280
  24.8 13.0 %collective-permute-start.6 = (bf16[4,2,32,1024]{3,2,1,0:T(8,128)(2,1)S(1)}, bf16[4,2,32,1024]{3,2,1,0:T(8,128)(2,1)S(1)}, u32[]{:S(2)}, u32[]{:S(2)}) collective-permute-start(bf16[4,2,32,1024]{3,2,1,0:T(8,128)(2,1)S(1)} %collective-permute-done.1), channel_id=1, source_target_pairs={{0,2},{1,3},{2,0},{3,1},{4,6},{5,7},{6,4},{7,5},{8,10},{9,11},{10,... | collective-permute-start | bytes 1572872 | tf_op jit(solution)/shard_map/ppermute | solution.py:278
  36.3 12.7 %collective-permute-start.9 = (bf16[4,2,32,1024]{3,2,1,0:T(8,128)(2,1)S(1)}, bf16[4,2,32,1024]{3,2,1,0:T(8,128)(2,1)S(1)}, u32[]{:S(2)}, u32[]{:S(2)}) collective-permute-start(bf16[4,2,32,1024]{3,2,1,0:T(8,128)(2,1)S(1)} %broadcast_select_fusion), channel_id=1, source_target_pairs={{0,2},{1,3},{2,0},{3,1},{4,6},{5,7},{6,4},{7,5},{8,10},{9,11},{10,... | collective-permute-start | bytes 1572872 | tf_op jit(solution)/shard_map/ppermute | solution.py:288
  37.8 12.1 %collective-permute-start.7 = (bf16[4,2,32,1024]{3,2,1,0:T(8,128)(2,1)S(1)}, bf16[4,2,32,1024]{3,2,1,0:T(8,128)(2,1)S(1)}, u32[]{:S(2)}, u32[]{:S(2)}) collective-permute-start(bf16[4,2,32,1024]{3,2,1,0:T(8,128)(2,1)S(1)} %broadcast_select_fusion.1.refs_4_), channel_id=1, source_target_pairs={{0,1},{1,0},{2,3},{3,2},{4,5},{5,4},{6,7},{7,6},{8,9},{9,8},{10,11... | collective-permute-start | bytes 1572872 | tf_op jit(solution)/shard_map/ppermute | solution.py:291
  38.4 11.6 %collective-permute-start.11 = (bf16[4,2,32,1024]{3,2,1,0:T(8,128)(2,1)S(1)}, bf16[4,2,32,1024]{3,2,1,0:T(8,128)(2,1)S(1)}, u32[]{:S(2)}, u32[]{:S(2)}) collective-permute-start(bf16[4,2,32,1024]{3,2,1,0:T(8,128)(2,1)S(1)} %collective-permute-done.10.refs_3_), channel_id=1, source_target_pairs={{2,4},{3,5},{4,2},{5,3},{10,12},{11,13},{12,10},{13,11},{18,20},{1... | collective-permute-start | bytes 1572872 | tf_op jit(solution)/shard_map/ppermute | solution.py:289
  51.1 4.6 %collective-permute-start.12 = (f32[1024]{0:T(1024)S(1)}, f32[1024]{0:T(1024)S(1)}, u32[]{:S(2)}, u32[]{:S(2)}) collective-permute-start(f32[1024]{0:T(1024)S(1)} %bitcast.30), channel_id=1, source_target_pairs={{0,3},{1,2},{2,1},{3,0},{4,7},{5,6},{6,5},{7,4},{8,11},{9,10},{10,... | collective-permute-start | bytes 12296 | tf_op jit(solution)/shard_map/ppermute | solution.py:311
  53.3 3.6 %collective-permute-start.13 = (f32[1024]{0:T(1024)S(1)}, f32[1024]{0:T(1024)S(1)}, u32[]{:S(2)}, u32[]{:S(2)}) collective-permute-start(f32[1024]{0:T(1024)S(1)} %bitcast.31), channel_id=1, source_target_pairs={{0,2},{1,3},{2,0},{3,1},{4,6},{5,7},{6,4},{7,5},{8,10},{9,11},{10,... | collective-permute-start | bytes 12296 | tf_op jit(solution)/shard_map/ppermute | solution.py:311
  53.5 3.6 %collective-permute-start.14 = (f32[1024]{0:T(1024)S(1)}, f32[1024]{0:T(1024)S(1)}, u32[]{:S(2)}, u32[]{:S(2)}) collective-permute-start(f32[1024]{0:T(1024)S(1)} %bitcast.32), channel_id=1, source_target_pairs={{0,1},{1,0},{2,3},{3,2},{4,5},{5,4},{6,7},{7,6},{8,9},{9,8},{10,11... | collective-permute-start | bytes 12296 | tf_op jit(solution)/shard_map/ppermute | solution.py:311
  57.1 4.5 %collective-permute-start.15 = (f32[1024]{0:T(1024)S(1)}, f32[1024]{0:T(1024)S(1)}, u32[]{:S(2)}, u32[]{:S(2)}) collective-permute-start(f32[1024]{0:T(1024)S(1)} %add_add_fusion), channel_id=1, source_target_pairs={{0,4},{1,5},{2,6},{3,7},{4,0},{5,1},{6,2},{7,3},{8,12},{9,13},{10,... | collective-permute-start | bytes 12296 | tf_op jit(solution)/shard_map/ppermute | solution.py:311

commit v15 on v13

--- a/solution.py
+++ b/solution.py
@@ -266,7 +266,7 @@
     ).astype(jnp.int32)
 
     own = background.transpose(1, 2, 0, 3)
-    own, scalars, records = tie((own, scalars, records))
+    own, scalars = tie((own, scalars))
     spectra = spectra_of(records, active, freqs)
     spectra_x = send(spectra, "tx", along_x)
     spectra_core = send(spectra, "tx", core)

time: 62.4 us -> 62.4 us (level)
    ppermute x1, waiting for transfers between devices: 8.6 us -> 7.16 us  [box_shards(): spectra_x = send(spectra, 'tx', along_x)]
    ppermute x1, waiting for transfers between devices: 1.46 us -> 2.89 us  [box_shards(): near = send(own, 'rx', z_pairs)]
  transfers between devices with their start and end apart: 16 -> 16, of which waited for: 11 -> 11; matrix products, arithmetic and copies ran while one was open for 0% -> 2% of each run, Pallas kernels for 15% -> 15%
where the time goes in v15:
time: 62.4 us; the launch traced here: 62.2 us
  waiting for transfers between devices  30 us (48%)
  starting transfers between devices  17.1 us (27%)
  Pallas kernels  12.9 us (21%)
  local copies, waits for them, and re-layouts  1.42 us (2%)
  other arithmetic  0.73 us (1%)
    ppermute x1, waiting for transfers between devices, box_shards(): swap = send(swap, 'rx', z_pairs)  9.17 us
    ppermute x1, waiting for transfers between devices, box_shards(): spectra_x = send(spectra, 'tx', along_x)  7.16 us
    ppermute x4, starting transfers between devices, box_shards(): send(sums, 'rx', [(r, r ^ bit) for r in range(8)])  6.66 us
    pallas_call x1, Pallas kernels, adjoint_of(): pl.pallas_call(functools.partial(adjoint_kernel, count), in_specs=[pl.Blo...  4.49 us
    ppermute x4, waiting for transfers between devices, box_shards(): send(sums, 'rx', [(r, r ^ bit) for r in range(8)])  3.82 us
    pallas_call x1, Pallas kernels, adjoint_rest(): pl.pallas_call(functools.partial(adjoint_rest_kernel, count, half), in_sp...  3.44 us
    ppermute x1, starting transfers between devices, box_shards(): spectra_x = send(spectra, 'tx', along_x)  3.01 us
    ppermute x1, waiting for transfers between devices, box_shards(): near = send(own, 'rx', z_pairs)  2.89 us
  transfers between devices with their start and end apart: 16, of which 11 were waited for; matrix products, arithmetic and copies ran while one was open for 2% of the time, Pallas kernels for 15%

profile of v15, /device:TPU:0, one launch (start us, length us, event | category | flops | bytes accessed | tf_op | source)
XLA Modules:
  0.0 62.2 jit_solution(3168050403038499923)
XLA Ops:
  0.0 2.3 %spectra.1 = bf16[8,64,512]{2,1,0:T(8,128)(2,1)S(1)} custom-call(bf16[128,640]{1,0:T(8,128)(2,1)} %constant.38.clone.table_hbm, s32[8,64]{1,0:T(8,128)} %bitcast.35, bf16[40,64,512]{2,1,0:T(8,128)(2,1)} %records_hbm.1), custom_call_target="tpu_custom_call" | custom-call | flops 335544320 | bytes 3145728 | tf_op jit(solution)/shard_map/spectra/pallas_call | solution.py:78
  2.3 3.0 %collective-permute-start.4 = (bf16[8,64,512]{2,1,0:T(8,128)(2,1)S(1)}, bf16[8,64,512]{2,1,0:T(8,128)(2,1)S(1)}, u32[]{:S(2)}, u32[]{:S(2)}) collective-permute-start(bf16[8,64,512]{2,1,0:T(8,128)(2,1)S(1)} %spectra.1), channel_id=1, source_target_pairs={{0,16},{8,24},{16,0},{24,8},{1,17},{9,25},{17,1},{25,9},{2,18},{10... | collective-permute-start | bytes 1572872 | tf_op jit(solution)/shard_map/ppermute | solution.py:271
  5.4 1.3 %copy.9 = bf16[32,4,2,1024]{3,0,2,1:T(8,128)(2,1)S(1)} copy(bf16[32,4,2,1024]{3,2,1,0:T(2,128)(2,1)} %param.8) | data formatting | bytes 1048576 | tf_op args[3]
  6.7 0.1 stack.43.scalar_ref
  6.8 1.6 %collective-permute-start = (bf16[4,2,32,1024]{3,2,1,0:T(8,128)(2,1)S(1)}, bf16[4,2,32,1024]{3,2,1,0:T(8,128)(2,1)S(1)}, u32[]{:S(2)}, u32[]{:S(2)}) collective-permute-start(bf16[4,2,32,1024]{3,2,1,0:T(8,128)(2,1)S(1)} %bitcast.23), channel_id=1, source_target_pairs={{0,2},{1,3},{2,0},{3,1},{4,6},{5,7},{6,4},{7,5},{8,10},{9,11},{10,... | collective-permute-start | bytes 1572872 | tf_op jit(solution)/shard_map/ppermute | solution.py:273
  8.4 0.0 collective-permute-start.1
  8.4 1.5 %collective-permute-start.2 = (bf16[4,2,32,1024]{3,2,1,0:T(8,128)(2,1)S(1)}, bf16[4,2,32,1024]{3,2,1,0:T(8,128)(2,1)S(1)}, u32[]{:S(2)}, u32[]{:S(2)}) collective-permute-start(bf16[4,2,32,1024]{3,2,1,0:T(8,128)(2,1)S(1)} %bitcast.25), channel_id=1, source_target_pairs={{0,1},{1,0},{2,3},{3,2},{4,5},{5,4},{6,7},{7,6},{8,9},{9,8},{10,11... | collective-permute-start | bytes 1572872 | tf_op jit(solution)/shard_map/ppermute | solution.py:275
  9.9 0.2 collective-permute-start.3
  10.1 7.2 %collective-permute-done.4 = bf16[8,64,512]{2,1,0:T(8,128)(2,1)S(1)} collective-permute-done((bf16[8,64,512]{2,1,0:T(8,128)(2,1)S(1)}, bf16[8,64,512]{2,1,0:T(8,128)(2,1)S(1)}, u32[]{:S(2)}, u32[]{:S(2)}) %collective-permute-start.4) | collective-permute-done | bytes 524320 | tf_op jit(solution)/shard_map/ppermute | solution.py:271
  17.3 0.0 collective-permute-start.5
  17.3 2.9 %collective-permute-done.refs_2_ = bf16[4,2,32,1024]{3,2,1,0:T(8,128)(2,1)S(1)} collective-permute-done((bf16[4,2,32,1024]{3,2,1,0:T(8,128)(2,1)S(1)}, bf16[4,2,32,1024]{3,2,1,0:T(8,128)(2,1)S(1)}, u32[]{:S(2)}, u32[]{:S(2)}) %collective-permute-start) | collective-permute-done | bytes 524320 | tf_op jit(solution)/shard_map/ppermute | solution.py:273
  20.2 0.0 collective-permute-done.1
  20.2 2.5 %collective-permute-done.2.refs_1_ = bf16[4,2,32,1024]{3,2,1,0:T(8,128)(2,1)S(1)} collective-permute-done((bf16[4,2,32,1024]{3,2,1,0:T(8,128)(2,1)S(1)}, bf16[4,2,32,1024]{3,2,1,0:T(8,128)(2,1)S(1)}, u32[]{:S(2)}, u32[]{:S(2)}) %collective-permute-start.2) | collective-permute-done | bytes 524320 | tf_op jit(solution)/shard_map/ppermute | solution.py:275
  22.7 0.5 collective-permute-start.8
  23.2 1.5 %collective-permute-start.10 = (bf16[4,2,32,1024]{3,2,1,0:T(8,128)(2,1)S(1)}, bf16[4,2,32,1024]{3,2,1,0:T(8,128)(2,1)S(1)}, u32[]{:S(2)}, u32[]{:S(2)}) collective-permute-start(bf16[4,2,32,1024]{3,2,1,0:T(8,128)(2,1)S(1)} %collective-permute-done.refs_2_), channel_id=1, source_target_pairs={{0,1},{1,0},{2,3},{3,2},{4,5},{5,4},{6,7},{7,6},{8,9},{9,8},{10,11... | collective-permute-start | bytes 1572872 | tf_op jit(solution)/shard_map/ppermute | solution.py:280
  24.8 1.4 %collective-permute-start.6 = (bf16[4,2,32,1024]{3,2,1,0:T(8,128)(2,1)S(1)}, bf16[4,2,32,1024]{3,2,1,0:T(8,128)(2,1)S(1)}, u32[]{:S(2)}, u32[]{:S(2)}) collective-permute-start(bf16[4,2,32,1024]{3,2,1,0:T(8,128)(2,1)S(1)} %collective-permute-done.1), channel_id=1, source_target_pairs={{0,2},{1,3},{2,0},{3,1},{4,6},{5,7},{6,4},{7,5},{8,10},{9,11},{10,... | collective-permute-start | bytes 1572872 | tf_op jit(solution)/shard_map/ppermute | solution.py:278
  26.1 0.0 collective-permute-done.3
  26.1 4.5 %adjoint.1 = (f32[4,2,4,64,1024]{4,3,2,1,0:T(8,128)S(1)}, bf16[4,1024,1024]{2,1,0:T(8,128)(2,1)S(1)}) custom-call(bf16[4,1024,1024]{2,1,0:T(8,128)(2,1)} %bitcast.34, bf16[4,2,64,512]{3,2,1,0:T(8,128)(2,1)S(1)} %bitcast.22, bf16[4,2,64,512]{3,2,1,0:T(8,128)(2,1)S(1)} %bitcast.29), custom_call_target="tpu_custom_call" | custom-call | flops 2147483648 | bytes 8388608 | tf_op jit(solution)/shard_map/adjoint/pallas_call | solution.py:149
  30.6 0.0 collective-permute-done.5
  30.7 3.4 %adjoint_rest.1 = (f32[4,2,4,64,1024]{4,3,2,1,0:T(8,128)S(1)}, bf16[4,2,32,1024]{3,2,1,0:T(8,128)(2,1)S(1)}) custom-call(s32[9]{0:T(128)S(1)} %stack.43.scalar_ref, bf16[4,1024,1024]{2,1,0:T(8,128)(2,1)S(1)} %get-tuple-element.18.green_ref, f32[4,2,4,64,1024]{4,3,2,1,0:T(8,128)S(1)} %get-tuple-element.19.base_ref, ...), custom_call_target="tpu_custom_call", output_to_operand_aliasing={{0}: (2, {})} | custom-call | flops 2147483648 | bytes 8388608 | tf_op jit(solution)/shard_map/adjoint_rest/pallas_call | solution.py:174
  34.1 2.1 %collective-permute-done.8.refs_2_ = bf16[4,2,32,1024]{3,2,1,0:T(8,128)(2,1)S(1)} collective-permute-done((bf16[4,2,32,1024]{3,2,1,0:T(8,128)(2,1)S(1)}, bf16[4,2,32,1024]{3,2,1,0:T(8,128)(2,1)S(1)}, u32[]{:S(2)}, u32[]{:S(2)}) %collective-permute-start.8) | collective-permute-done | bytes 524320 | tf_op jit(solution)/shard_map/ppermute | solution.py:279
  36.2 0.1 broadcast_select_fusion
  36.3 0.1 collective-permute-start.9
  36.4 1.4 %collective-permute-done.6 = bf16[4,2,32,1024]{3,2,1,0:T(8,128)(2,1)S(1)} collective-permute-done((bf16[4,2,32,1024]{3,2,1,0:T(8,128)(2,1)S(1)}, bf16[4,2,32,1024]{3,2,1,0:T(8,128)(2,1)S(1)}, u32[]{:S(2)}, u32[]{:S(2)}) %collective-permute-start.6) | collective-permute-done | bytes 524320 | tf_op jit(solution)/shard_map/ppermute | solution.py:278
  37.8 0.1 broadcast_select_fusion.1.refs_4_
  37.8 0.6 collective-permute-start.7
  38.4 0.0 collective-permute-done.10.refs_3_
  38.4 0.0 collective-permute-start.11
  38.4 1.5 %weigh.2.refs_6_ = f32[8,1024]{1,0:T(8,128)S(1)} custom-call(s32[9]{0:T(128)S(1)} %stack.43.scalar_ref, f32[4,2,8,32,1024]{4,3,2,1,0:T(8,128)S(1)} %bitcast.20, bf16[4,2,32,1024]{3,2,1,0:T(8,128)(2,1)S(1)} %bitcast.26, bf16[4,2,32,1024]{3,2,1,0:T(8,128)(2,1)S(1)} %collective-permute-done.2.refs_1_, ...), custom_call_target="tpu_custom_call" | custom-call | flops 5242880 | bytes 5242880 | tf_op jit(solution)/shard_map/weigh/pallas_call | solution.py:195
  39.9 9.2 %collective-permute-done.9.refs_1_.refs_5_ = bf16[4,2,32,1024]{3,2,1,0:T(8,128)(2,1)S(1)} collective-permute-done((bf16[4,2,32,1024]{3,2,1,0:T(8,128)(2,1)S(1)}, bf16[4,2,32,1024]{3,2,1,0:T(8,128)(2,1)S(1)}, u32[]{:S(2)}, u32[]{:S(2)}) %collective-permute-start.9) | collective-permute-done | bytes 524320 | tf_op jit(solution)/shard_map/ppermute | solution.py:288
  49.1 0.9 %collective-permute-done.7.refs_0_ = bf16[4,2,32,1024]{3,2,1,0:T(8,128)(2,1)S(1)} collective-permute-done((bf16[4,2,32,1024]{3,2,1,0:T(8,128)(2,1)S(1)}, bf16[4,2,32,1024]{3,2,1,0:T(8,128)(2,1)S(1)}, u32[]{:S(2)}, u32[]{:S(2)}) %collective-permute-start.7) | collective-permute-done | bytes 524320 | tf_op jit(solution)/shard_map/ppermute | solution.py:291
  50.0 0.0 collective-permute-done.11.refs_3_.refs_4_
  50.0 1.2 %weigh.3 = f32[1,1024]{1,0:T(1,128)S(1)} custom-call(s32[9]{0:T(128)S(1)} %stack.43.scalar_ref, f32[4,2,8,32,1024]{4,3,2,1,0:T(8,128)S(1)} %bitcast.21, bf16[4,2,32,1024]{3,2,1,0:T(8,128)(2,1)S(1)} %collective-permute-done.7.refs_0_, bf16[4,2,32,1024]{3,2,1,0:T(8,128)(2,1)S(1)} %collective-permute-done.9.refs_1_.refs_5_, ...), custom_call_target="tpu_custom_call" | custom-call | flops 6324224 | bytes 6324224 | tf_op jit(solution)/shard_map/weigh/pallas_call | solution.py:195
  51.1 2.2 %collective-permute-start.12 = (f32[1024]{0:T(1024)S(1)}, f32[1024]{0:T(1024)S(1)}, u32[]{:S(2)}, u32[]{:S(2)}) collective-permute-start(f32[1024]{0:T(1024)S(1)} %bitcast.30), channel_id=1, source_target_pairs={{0,3},{1,2},{2,1},{3,0},{4,7},{5,6},{6,5},{7,4},{8,11},{9,10},{10,... | collective-permute-start | bytes 12296 | tf_op jit(solution)/shard_map/ppermute | solution.py:311
  53.4 0.1 collective-permute-start.13
  53.5 1.4 %collective-permute-start.14 = (f32[1024]{0:T(1024)S(1)}, f32[1024]{0:T(1024)S(1)}, u32[]{:S(2)}, u32[]{:S(2)}) collective-permute-start(f32[1024]{0:T(1024)S(1)} %bitcast.32), channel_id=1, source_target_pairs={{0,1},{1,0},{2,3},{3,2},{4,5},{5,4},{6,7},{7,6},{8,9},{9,8},{10,11... | collective-permute-start | bytes 12296 | tf_op jit(solution)/shard_map/ppermute | solution.py:311
  54.9 0.8 %collective-permute-done.12 = f32[1024]{0:T(1024)S(1)} collective-permute-done((f32[1024]{0:T(1024)S(1)}, f32[1024]{0:T(1024)S(1)}, u32[]{:S(2)}, u32[]{:S(2)}) %collective-permute-start.12) | collective-permute-done | bytes 4128 | tf_op jit(solution)/shard_map/ppermute | solution.py:311
  55.7 1.3 %collective-permute-done.13 = f32[1024]{0:T(1024)S(1)} collective-permute-done((f32[1024]{0:T(1024)S(1)}, f32[1024]{0:T(1024)S(1)}, u32[]{:S(2)}, u32[]{:S(2)}) %collective-permute-start.13) | collective-permute-done | bytes 4128 | tf_op jit(solution)/shard_map/ppermute | solution.py:311
  57.0 0.1 collective-permute-done.14
  57.1 2.9 %collective-permute-start.15 = (f32[1024]{0:T(1024)S(1)}, f32[1024]{0:T(1024)S(1)}, u32[]{:S(2)}, u32[]{:S(2)}) collective-permute-start(f32[1024]{0:T(1024)S(1)} %add_add_fusion), channel_id=1, source_target_pairs={{0,4},{1,5},{2,6},{3,7},{4,0},{5,1},{6,2},{7,3},{8,12},{9,13},{10,... | collective-permute-start | bytes 12296 | tf_op jit(solution)/shard_map/ppermute | solution.py:311
  60.0 1.6 %collective-permute-done.15 = f32[1024]{0:T(1024)S(1)} collective-permute-done((f32[1024]{0:T(1024)S(1)}, f32[1024]{0:T(1024)S(1)}, u32[]{:S(2)}, u32[]{:S(2)}) %collective-permute-start.15) | collective-permute-done | bytes 4128 | tf_op jit(solution)/shard_map/ppermute | solution.py:311
  61.6 0.6 add.53
  (1 shorter events, 0.0 us)
Async XLA Ops:
  2.3 14.9 %collective-permute-start.4 = (bf16[8,64,512]{2,1,0:T(8,128)(2,1)S(1)}, bf16[8,64,512]{2,1,0:T(8,128)(2,1)S(1)}, u32[]{:S(2)}, u32[]{:S(2)}) collective-permute-start(bf16[8,64,512]{2,1,0:T(8,128)(2,1)S(1)} %spectra.1), channel_id=1, source_target_pairs={{0,16},{8,24},{16,0},{24,8},{1,17},{9,25},{17,1},{25,9},{2,18},{10... | collective-permute-start | bytes 1572872 | tf_op jit(solution)/shard_map/ppermute | solution.py:271
  6.8 13.4 %collective-permute-start = (bf16[4,2,32,1024]{3,2,1,0:T(8,128)(2,1)S(1)}, bf16[4,2,32,1024]{3,2,1,0:T(8,128)(2,1)S(1)}, u32[]{:S(2)}, u32[]{:S(2)}) collective-permute-start(bf16[4,2,32,1024]{3,2,1,0:T(8,128)(2,1)S(1)} %bitcast.23), channel_id=1, source_target_pairs={{0,2},{1,3},{2,0},{3,1},{4,6},{5,7},{6,4},{7,5},{8,10},{9,11},{10,... | collective-permute-start | bytes 1572872 | tf_op jit(solution)/shard_map/ppermute | solution.py:273
  8.4 11.8 %collective-permute-start.1 = (bf16[4,2,32,1024]{3,2,1,0:T(8,128)(2,1)S(1)}, bf16[4,2,32,1024]{3,2,1,0:T(8,128)(2,1)S(1)}, u32[]{:S(2)}, u32[]{:S(2)}) collective-permute-start(bf16[4,2,32,1024]{3,2,1,0:T(8,128)(2,1)S(1)} %bitcast.24), channel_id=1, source_target_pairs={{2,4},{3,5},{4,2},{5,3},{10,12},{11,13},{12,10},{13,11},{18,20},{1... | collective-permute-start | bytes 1572872 | tf_op jit(solution)/shard_map/ppermute | solution.py:274
  8.4 14.3 %collective-permute-start.2 = (bf16[4,2,32,1024]{3,2,1,0:T(8,128)(2,1)S(1)}, bf16[4,2,32,1024]{3,2,1,0:T(8,128)(2,1)S(1)}, u32[]{:S(2)}, u32[]{:S(2)}) collective-permute-start(bf16[4,2,32,1024]{3,2,1,0:T(8,128)(2,1)S(1)} %bitcast.25), channel_id=1, source_target_pairs={{0,1},{1,0},{2,3},{3,2},{4,5},{5,4},{6,7},{7,6},{8,9},{9,8},{10,11... | collective-permute-start | bytes 1572872 | tf_op jit(solution)/shard_map/ppermute | solution.py:275
  9.9 16.3 %collective-permute-start.3 = (bf16[8,64,512]{2,1,0:T(8,128)(2,1)S(1)}, bf16[8,64,512]{2,1,0:T(8,128)(2,1)S(1)}, u32[]{:S(2)}, u32[]{:S(2)}) collective-permute-start(bf16[8,64,512]{2,1,0:T(8,128)(2,1)S(1)} %spectra.1), channel_id=1, source_target_pairs={{0,8},{8,0},{16,24},{24,16},{1,9},{9,1},{17,25},{25,17},{2,10},{10... | collective-permute-start | bytes 1572872 | tf_op jit(solution)/shard_map/ppermute | solution.py:272
  17.3 13.4 %collective-permute-start.5 = (bf16[8,64,512]{2,1,0:T(8,128)(2,1)S(1)}, bf16[8,64,512]{2,1,0:T(8,128)(2,1)S(1)}, u32[]{:S(2)}, u32[]{:S(2)}) collective-permute-start(bf16[8,64,512]{2,1,0:T(8,128)(2,1)S(1)} %collective-permute-done.4), channel_id=1, source_target_pairs={{0,8},{8,0},{16,24},{24,16},{1,9},{9,1},{17,25},{25,17},{2,10},{10... | collective-permute-start | bytes 1572872 | tf_op jit(solution)/shard_map/ppermute | solution.py:282
  22.7 13.6 %collective-permute-start.8 = (bf16[4,2,32,1024]{3,2,1,0:T(8,128)(2,1)S(1)}, bf16[4,2,32,1024]{3,2,1,0:T(8,128)(2,1)S(1)}, u32[]{:S(2)}, u32[]{:S(2)}) collective-permute-start(bf16[4,2,32,1024]{3,2,1,0:T(8,128)(2,1)S(1)} %collective-permute-done.refs_2_), channel_id=1, source_target_pairs={{2,4},{3,5},{4,2},{5,3},{10,12},{11,13},{12,10},{13,11},{18,20},{1... | collective-permute-start | bytes 1572872 | tf_op jit(solution)/shard_map/ppermute | solution.py:279
  23.2 15.1 %collective-permute-start.10 = (bf16[4,2,32,1024]{3,2,1,0:T(8,128)(2,1)S(1)}, bf16[4,2,32,1024]{3,2,1,0:T(8,128)(2,1)S(1)}, u32[]{:S(2)}, u32[]{:S(2)}) collective-permute-start(bf16[4,2,32,1024]{3,2,1,0:T(8,128)(2,1)S(1)} %collective-permute-done.refs_2_), channel_id=1, source_target_pairs={{0,1},{1,0},{2,3},{3,2},{4,5},{5,4},{6,7},{7,6},{8,9},{9,8},{10,11... | collective-permute-start | bytes 1572872 | tf_op jit(solution)/shard_map/ppermute | solution.py:280
  24.8 13.0 %collective-permute-start.6 = (bf16[4,2,32,1024]{3,2,1,0:T(8,128)(2,1)S(1)}, bf16[4,2,32,1024]{3,2,1,0:T(8,128)(2,1)S(1)}, u32[]{:S(2)}, u32[]{:S(2)}) collective-permute-start(bf16[4,2,32,1024]{3,2,1,0:T(8,128)(2,1)S(1)} %collective-permute-done.1), channel_id=1, source_target_pairs={{0,2},{1,3},{2,0},{3,1},{4,6},{5,7},{6,4},{7,5},{8,10},{9,11},{10,... | collective-permute-start | bytes 1572872 | tf_op jit(solution)/shard_map/ppermute | solution.py:278
  36.3 12.7 %collective-permute-start.9 = (bf16[4,2,32,1024]{3,2,1,0:T(8,128)(2,1)S(1)}, bf16[4,2,32,1024]{3,2,1,0:T(8,128)(2,1)S(1)}, u32[]{:S(2)}, u32[]{:S(2)}) collective-permute-start(bf16[4,2,32,1024]{3,2,1,0:T(8,128)(2,1)S(1)} %broadcast_select_fusion), channel_id=1, source_target_pairs={{0,2},{1,3},{2,0},{3,1},{4,6},{5,7},{6,4},{7,5},{8,10},{9,11},{10,... | collective-permute-start | bytes 1572872 | tf_op jit(solution)/shard_map/ppermute | solution.py:288
  37.8 12.1 %collective-permute-start.7 = (bf16[4,2,32,1024]{3,2,1,0:T(8,128)(2,1)S(1)}, bf16[4,2,32,1024]{3,2,1,0:T(8,128)(2,1)S(1)}, u32[]{:S(2)}, u32[]{:S(2)}) collective-permute-start(bf16[4,2,32,1024]{3,2,1,0:T(8,128)(2,1)S(1)} %broadcast_select_fusion.1.refs_4_), channel_id=1, source_target_pairs={{0,1},{1,0},{2,3},{3,2},{4,5},{5,4},{6,7},{7,6},{8,9},{9,8},{10,11... | collective-permute-start | bytes 1572872 | tf_op jit(solution)/shard_map/ppermute | solution.py:291
  38.4 11.6 %collective-permute-start.11 = (bf16[4,2,32,1024]{3,2,1,0:T(8,128)(2,1)S(1)}, bf16[4,2,32,1024]{3,2,1,0:T(8,128)(2,1)S(1)}, u32[]{:S(2)}, u32[]{:S(2)}) collective-permute-start(bf16[4,2,32,1024]{3,2,1,0:T(8,128)(2,1)S(1)} %collective-permute-done.10.refs_3_), channel_id=1, source_target_pairs={{2,4},{3,5},{4,2},{5,3},{10,12},{11,13},{12,10},{13,11},{18,20},{1... | collective-permute-start | bytes 1572872 | tf_op jit(solution)/shard_map/ppermute | solution.py:289
  51.1 4.6 %collective-permute-start.12 = (f32[1024]{0:T(1024)S(1)}, f32[1024]{0:T(1024)S(1)}, u32[]{:S(2)}, u32[]{:S(2)}) collective-permute-start(f32[1024]{0:T(1024)S(1)} %bitcast.30), channel_id=1, source_target_pairs={{0,3},{1,2},{2,1},{3,0},{4,7},{5,6},{6,5},{7,4},{8,11},{9,10},{10,... | collective-permute-start | bytes 12296 | tf_op jit(solution)/shard_map/ppermute | solution.py:311
  53.4 3.6 %collective-permute-start.13 = (f32[1024]{0:T(1024)S(1)}, f32[1024]{0:T(1024)S(1)}, u32[]{:S(2)}, u32[]{:S(2)}) collective-permute-start(f32[1024]{0:T(1024)S(1)} %bitcast.31), channel_id=1, source_target_pairs={{0,2},{1,3},{2,0},{3,1},{4,6},{5,7},{6,4},{7,5},{8,10},{9,11},{10,... | collective-permute-start | bytes 12296 | tf_op jit(solution)/shard_map/ppermute | solution.py:311
  53.5 3.6 %collective-permute-start.14 = (f32[1024]{0:T(1024)S(1)}, f32[1024]{0:T(1024)S(1)}, u32[]{:S(2)}, u32[]{:S(2)}) collective-permute-start(f32[1024]{0:T(1024)S(1)} %bitcast.32), channel_id=1, source_target_pairs={{0,1},{1,0},{2,3},{3,2},{4,5},{5,4},{6,7},{7,6},{8,9},{9,8},{10,11... | collective-permute-start | bytes 12296 | tf_op jit(solution)/shard_map/ppermute | solution.py:311
  57.1 4.5 %collective-permute-start.15 = (f32[1024]{0:T(1024)S(1)}, f32[1024]{0:T(1024)S(1)}, u32[]{:S(2)}, u32[]{:S(2)}) collective-permute-start(f32[1024]{0:T(1024)S(1)} %add_add_fusion), channel_id=1, source_target_pairs={{0,4},{1,5},{2,6},{3,7},{4,0},{5,1},{6,2},{7,3},{8,12},{9,13},{10,... | collective-permute-start | bytes 12296 | tf_op jit(solution)/shard_map/ppermute | solution.py:311
